TPU v7x, 128 devices: a whole 4x4x4 slice. The times are simulated.
128 devices in a mesh: cols: 8 (over y, core), rows: 16 (over z, x).
Axes of the slice: x: 4, y: 4, z: 4, core: 2. Of those that a mesh axis runs over, the one named last changes fastest.
Arguments:
- sensitivity: float32 [8, 6144, 2048], P('cols', 'rows'), may hold values from -470 to 470, as said below
Outputs:
- rotated: float32 [8, 6144, 2048], P(None, 'rows', 'cols')
- frame: float32 [2048, 2048], P('rows', 'cols')
- column_scale: float32 [2048], P('cols')
Inputs may be any that keep to these rules, and one draw needn't show every extreme that they name: `sensitivity`: Real-valued sensitivities.
All inputs are finite; a program needn't handle non-finite values.
Results may differ from a plain program's by a relative error of at most 0.00018.
Values sent between devices are 32-bit elements; how exact they have to be, the bound alone decides.
No kernel may reach another device: no remote copies, remote signals or barrier semaphores. Data moves between devices by JAX's collectives and lax.ppermute only.
A program may use at most 64 MiB of HBM per device.

v0:
```python
import jax
import jax.numpy as jnp
from jax import lax
from jax.sharding import PartitionSpec as P

N = 2048
ROUNDS = 4


def passed_along(value, axis, steps):
    count = lax.axis_size(axis)
    pairs = [(source, (source + steps) % count) for source in range(count)]
    return lax.ppermute(value, axis, pairs)


def product(left, right):
    return jnp.dot(left, right, precision=lax.Precision.HIGHEST, preferred_element_type=jnp.float32)


def inner_gram(left, right):
    return lax.dot_general(
        left,
        right,
        (((0,), (0,)), ((), ())),
        precision=lax.Precision.HIGHEST,
        preferred_element_type=jnp.float32,
    )


def cayley_rotation(gram):
    order = gram.shape[0]
    diagonal = jnp.diagonal(gram)
    spread = diagonal[None, :] - diagonal[:, None]
    totals = diagonal[None, :] + diagonal[:, None]
    skew = gram * spread / (2.0 * spread * spread + 0.5 * totals * totals)
    identity = jnp.eye(order, dtype=jnp.float32)
    raised = identity + skew
    numerator = product(raised, raised)
    denominator = identity - product(skew, skew)
    factor = jnp.linalg.cholesky(denominator)
    partial_solve = lax.linalg.triangular_solve(factor, numerator.T, left_side=True, lower=True)
    solved = lax.linalg.triangular_solve(
        factor, partial_solve, left_side=True, lower=True, transpose_a=True
    )
    return solved.T


def pass_lower(lower_block, basis_low, sweep_round):
    if sweep_round > 0:
        return passed_along((lower_block, basis_low), "cols", 1)
    return (lower_block, basis_low)


def body(sensitivity):
    col_count = lax.axis_size("cols")
    row_count = lax.axis_size("rows")
    regrouped = lax.all_to_all(sensitivity, "cols", split_axis=2, concat_axis=0, tiled=True)
    pair_width = regrouped.shape[2]
    block_width = pair_width // 2
    local_rows = regrouped.shape[0] * regrouped.shape[1]
    flattened = regrouped.reshape(local_rows, pair_width)
    upper_block = flattened[:, :block_width]
    lower_block = flattened[:, block_width:]
    basis_rows = N // row_count
    row_start = lax.axis_index("rows") * basis_rows
    col_start = lax.axis_index("cols") * pair_width
    row_ids = row_start + jnp.arange(basis_rows, dtype=jnp.int32)[:, None]
    col_ids = col_start + jnp.arange(pair_width, dtype=jnp.int32)[None, :]
    basis_pair = (row_ids == col_ids).astype(jnp.float32)
    basis_up = basis_pair[:, :block_width]
    basis_low = basis_pair[:, block_width:]
    gram = None
    weights = None
    turned = None
    for sweep_round in range(ROUNDS):
        lower_block, basis_low = pass_lower(lower_block, basis_low, sweep_round)
        paired = jnp.concatenate([upper_block, lower_block], axis=1)
        gram = lax.psum(inner_gram(paired, paired), "rows")
        weights = cayley_rotation(gram)
        turned = product(paired, weights)
        framed = product(jnp.concatenate([basis_up, basis_low], axis=1), weights)
        upper_block = turned[:, :block_width]
        lower_block = turned[:, block_width:]
        basis_up = framed[:, :block_width]
        basis_low = framed[:, block_width:]
    squares = lax.psum(jnp.sum(turned * turned, axis=0), "rows")
    column_scale = jnp.sqrt(squares / (local_rows * row_count))
    rotated = turned.reshape(col_count, local_rows // col_count, pair_width)
    frame = jnp.concatenate([basis_up, basis_low], axis=1)
    return (rotated, frame, column_scale)


def solution(mesh):
    in_specs = (P("cols", "rows", None),)
    out_specs = (P(None, "rows", "cols"), P("rows", "cols"), P("cols"))
    return jax.shard_map(body, mesh=mesh, in_specs=in_specs, out_specs=out_specs, check_vma=False)
```

profile of v0, /device:TPU:1, one launch (start us, length us, event | category | flops | bytes accessed | tf_op | source)
XLA Modules:
  0.0 824.6 jit_solution(12071564501459900061)
XLA Ops:
  7.2 7.7 copy.32
  14.9 43.7 %all_to_all.15 = f32[1,384,2048]{1,0,2:T(1,128)S(1)} all-to-all(f32[1,384,2048]{1,0,2:T(1,128)S(1)} %copy.32), channel_id=1, replica_groups=mesh['cols'=8,'rows'=16] {'cols'}, dimensions={2} | all-to-all | bytes 6291456 | tf_op jit(solution)/shard_map/all_to_all | solution.py:57
  62.8 7.8 fusion.8
  70.9 83.6 %all-reduce.6.cloned.1.call-done = f32[256,256]{0,1:T(8,128)} async-done(((f32[256,256]{0,1:T(8,128)}), f32[256,256]{0,1:T(8,128)}) %all-reduce.6.cloned.1.call-update) | async-done | bytes 262160 | tf_op jit(solution)/shard_map/psum | solution.py:78
  163.1 11.7 %cholesky.214 = f32[128,128]{1,0:T(8,128)S(1)} custom-call(f32[128,128]{1,0:T(8,128)S(1)} %cholesky.346), custom_call_target="Cholesky" | custom-call | tf_op jit(solution)/shard_map/jit(cholesky)/cholesky | solution.py:40
  174.8 10.4 %custom-call.31 = f32[1,128,128]{1,2,0:T(8,128)} custom-call(f32[1,128,128]{2,1,0:T(8,128)S(1)} %get-tuple-element.133), custom_call_target="InvertDiagBlocksLowerTriangular" | custom-call | tf_op jit(solution)/shard_map/jit(cholesky)/cholesky | solution.py:40
  188.8 11.7 %cholesky.231 = f32[128,128]{1,0:T(8,128)S(1)} custom-call(f32[128,128]{1,0:T(8,128)S(1)} %convolution_subtract_fusion.15), custom_call_target="Cholesky" | custom-call | tf_op jit(solution)/shard_map/jit(cholesky)/cholesky | solution.py:40
  204.9 6.1 while.16
  211.7 20.5 %custom-call.33 = f32[2,128,128]{1,2,0:T(8,128)S(1)} custom-call(f32[2,128,128]{2,1,0:T(8,128)} %copy-done.9), custom_call_target="InvertDiagBlocksLowerTriangular" | custom-call | tf_op jit(solution)/shard_map/triangular_solve/custom-call.4 | solution.py:42
  242.6 17.4 %collective-permute-done = f32[3072,128]{0,1:T(8,128)S(1)} collective-permute-done((f32[3072,128]{0,1:T(8,128)S(1)}, f32[3072,128]{0,1:T(8,128)S(1)}, u32[]{:S(2)}, u32[]{:S(2)}) %collective-permute-start) | collective-permute-done | bytes 1572896 | tf_op jit(solution)/shard_map/ppermute | solution.py:13
  263.6 83.0 %all-reduce.8.cloned.1.call-done = f32[256,256]{0,1:T(8,128)} async-done(((f32[256,256]{0,1:T(8,128)}), f32[256,256]{0,1:T(8,128)}) %all-reduce.8.cloned.1.call-update) | async-done | bytes 262160 | tf_op jit(solution)/shard_map/psum | solution.py:78
  351.1 11.7 %cholesky.248 = f32[128,128]{1,0:T(8,128)S(1)} custom-call(f32[128,128]{1,0:T(8,128)S(1)} %cholesky.349), custom_call_target="Cholesky" | custom-call | tf_op jit(solution)/shard_map/jit(cholesky)/cholesky | solution.py:40
  362.8 9.8 %custom-call.34 = f32[1,128,128]{1,2,0:T(8,128)S(1)} custom-call(f32[1,128,128]{2,1,0:T(8,128)S(1)} %get-tuple-element.129), custom_call_target="InvertDiagBlocksLowerTriangular" | custom-call | tf_op jit(solution)/shard_map/jit(cholesky)/cholesky | solution.py:40
  373.1 11.7 %cholesky.265 = f32[128,128]{1,0:T(8,128)S(1)} custom-call(f32[128,128]{1,0:T(8,128)S(1)} %convolution_subtract_fusion.14), custom_call_target="Cholesky" | custom-call | tf_op jit(solution)/shard_map/jit(cholesky)/cholesky | solution.py:40
  387.6 4.3 while.17
  391.8 19.7 %custom-call.36 = f32[2,128,128]{1,2,0:T(8,128)S(1)} custom-call(f32[2,128,128]{2,1,0:T(8,128)S(1)} %get-tuple-element.61), custom_call_target="InvertDiagBlocksLowerTriangular" | custom-call | tf_op jit(solution)/shard_map/triangular_solve/custom-call.4 | solution.py:42
  420.4 17.4 %collective-permute-done.1 = f32[3072,128]{0,1:T(8,128)S(1)} collective-permute-done((f32[3072,128]{0,1:T(8,128)S(1)}, f32[3072,128]{0,1:T(8,128)S(1)}, u32[]{:S(2)}, u32[]{:S(2)}) %collective-permute-start.1) | collective-permute-done | bytes 1572896 | tf_op jit(solution)/shard_map/ppermute | solution.py:13
  442.9 82.7 %all-reduce.10.cloned.1.call-done = f32[256,256]{0,1:T(8,128)} async-done(((f32[256,256]{0,1:T(8,128)}), f32[256,256]{0,1:T(8,128)}) %all-reduce.10.cloned.1.call-update) | async-done | bytes 262160 | tf_op jit(solution)/shard_map/psum | solution.py:78
  530.1 11.7 %cholesky.282 = f32[128,128]{1,0:T(8,128)S(1)} custom-call(f32[128,128]{1,0:T(8,128)S(1)} %cholesky.352), custom_call_target="Cholesky" | custom-call | tf_op jit(solution)/shard_map/jit(cholesky)/cholesky | solution.py:40
  541.9 9.8 %custom-call.37 = f32[1,128,128]{1,2,0:T(8,128)S(1)} custom-call(f32[1,128,128]{2,1,0:T(8,128)S(1)} %get-tuple-element.125), custom_call_target="InvertDiagBlocksLowerTriangular" | custom-call | tf_op jit(solution)/shard_map/jit(cholesky)/cholesky | solution.py:40
  552.2 11.7 %cholesky.299 = f32[128,128]{1,0:T(8,128)S(1)} custom-call(f32[128,128]{1,0:T(8,128)S(1)} %convolution_subtract_fusion.13), custom_call_target="Cholesky" | custom-call | tf_op jit(solution)/shard_map/jit(cholesky)/cholesky | solution.py:40
  566.6 4.0 while.18
  570.6 19.8 %custom-call.39 = f32[2,128,128]{1,2,0:T(8,128)S(1)} custom-call(f32[2,128,128]{2,1,0:T(8,128)S(1)} %get-tuple-element.63), custom_call_target="InvertDiagBlocksLowerTriangular" | custom-call | tf_op jit(solution)/shard_map/triangular_solve/custom-call.4 | solution.py:42
  600.9 17.9 %collective-permute-done.3 = f32[128,128]{1,0:T(8,128)S(1)} collective-permute-done((f32[128,128]{1,0:T(8,128)S(1)}, f32[128,128]{1,0:T(8,128)S(1)}, u32[]{:S(2)}, u32[]{:S(2)}) %collective-permute-start.3) | collective-permute-done | bytes 65568 | tf_op jit(solution)/shard_map/ppermute | solution.py:13
  621.7 5.3 fusion.3
  627.5 81.5 %all-reduce.12.cloned.1.call-done = f32[256,256]{0,1:T(8,128)} async-done(((f32[256,256]{0,1:T(8,128)}), f32[256,256]{0,1:T(8,128)}) %all-reduce.12.cloned.1.call-update) | async-done | bytes 262160 | tf_op jit(solution)/shard_map/psum | solution.py:78
  713.5 11.9 %cholesky.316 = f32[128,128]{1,0:T(8,128)S(1)} custom-call(f32[128,128]{1,0:T(8,128)S(1)} %cholesky.355), custom_call_target="Cholesky" | custom-call | tf_op jit(solution)/shard_map/jit(cholesky)/cholesky | solution.py:40
  725.4 9.8 %custom-call.40 = f32[1,128,128]{1,2,0:T(8,128)S(1)} custom-call(f32[1,128,128]{2,1,0:T(8,128)S(1)} %get-tuple-element.121), custom_call_target="InvertDiagBlocksLowerTriangular" | custom-call | tf_op jit(solution)/shard_map/jit(cholesky)/cholesky | solution.py:40
  735.7 11.7 %cholesky.333 = f32[128,128]{1,0:T(8,128)S(1)} custom-call(f32[128,128]{1,0:T(8,128)S(1)} %convolution_subtract_fusion.12), custom_call_target="Cholesky" | custom-call | tf_op jit(solution)/shard_map/jit(cholesky)/cholesky | solution.py:40
  754.1 19.9 %custom-call.42 = f32[2,128,128]{1,2,0:T(8,128)S(1)} custom-call(f32[2,128,128]{2,1,0:T(8,128)S(1)} %get-tuple-element.65), custom_call_target="InvertDiagBlocksLowerTriangular" | custom-call | tf_op jit(solution)/shard_map/triangular_solve/custom-call.4 | solution.py:42
  776.4 8.4 %multiply_reduce_fusion = (f32[256]{0:T(256)S(1)}, f32[3072,256]{1,0:T(8,128)}) fusion(f32[128,256]{1,0:T(8,128)S(1)} %fusion.74, f32[128,256]{1,0:T(8,128)S(1)} %fusion.72, f32[3072,128]{0,1:T(8,128)} %collective-permute-done.2, f32[3072,128]{0,1:T(8,128)S(1)} %get-tuple-element.106), kind=kOutput, calls=%fused_computation.18 | convolution fusion | flops 2418343680 | bytes 6554624 | tf_op jit(solution)/shard_map/dot_general | solution.py:17
  784.8 31.2 %psum.39 = f32[256]{0:T(256)S(1)} all-reduce(f32[256]{0:T(256)S(1)} %get-tuple-element.142), channel_id=1, replica_groups=mesh['cols'=8,'rows'=16] {'rows'}, use_global_device_ids=true, to_apply=%region_9.13 | all-reduce | flops 256 | bytes 2048 | tf_op jit(solution)/shard_map/psum | solution.py:86
  (168 shorter events, 106.6 us)
Async XLA Ops:
  7.2 147.4 %all-reduce.6.cloned.1.call-start = ((), (), s32[]{:S(2)}) async-start(), calls=%async_computation.1 | async-start | bytes 524288 | tf_op jit(solution)/shard_map/psum | solution.py:78
  70.6 276.0 %all-reduce.8.cloned.1.call-start = ((), (), s32[]{:S(2)}) async-start(), calls=%async_computation.2 | async-start | bytes 524288 | tf_op jit(solution)/shard_map/psum | solution.py:78
  154.5 77.6 %copy-start.1 = (f32[256,256]{0,1:T(8,128)S(1)}, f32[256,256]{0,1:T(8,128)}, u32[]{:S(2)}) copy-start(f32[256,256]{0,1:T(8,128)} %all-reduce.6.cloned.1.call-done) | copy-start | bytes 786436
  162.4 0.7 copy-start.8
  211.0 0.7 copy-start.9
  239.5 20.4 %collective-permute-start = (f32[3072,128]{0,1:T(8,128)S(1)}, f32[3072,128]{0,1:T(8,128)S(1)}, u32[]{:S(2)}, u32[]{:S(2)}) collective-permute-start(f32[3072,128]{0,1:T(8,128)S(1)} %get-tuple-element.111), channel_id=1, source_target_pairs={{0,16},{16,32},{32,48},{48,64},{64,80},{80,96},{96,112},{112,0},{1... | collective-permute-start | bytes 4718600 | tf_op jit(solution)/shard_map/ppermute | solution.py:13
  260.0 3.6 copy-start.4
  263.4 262.2 %all-reduce.10.cloned.1.call-start = ((), (), s32[]{:S(2)}) async-start(), calls=%async_computation.3 | async-start | bytes 524288 | tf_op jit(solution)/shard_map/psum | solution.py:78
  346.6 64.9 %copy-start.2 = (f32[256,256]{0,1:T(8,128)S(1)}, f32[256,256]{0,1:T(8,128)}, u32[]{:S(2)}) copy-start(f32[256,256]{0,1:T(8,128)} %all-reduce.8.cloned.1.call-done) | copy-start | bytes 786436
  411.5 2.4 copy-start.5
  417.4 20.4 %collective-permute-start.1 = (f32[3072,128]{0,1:T(8,128)S(1)}, f32[3072,128]{0,1:T(8,128)S(1)}, u32[]{:S(2)}, u32[]{:S(2)}) collective-permute-start(f32[3072,128]{0,1:T(8,128)S(1)} %get-tuple-element.109), channel_id=1, source_target_pairs={{0,16},{16,32},{32,48},{48,64},{64,80},{80,96},{96,112},{112,0},{1... | collective-permute-start | bytes 4718600 | tf_op jit(solution)/shard_map/ppermute | solution.py:13
  437.8 1.1 copy-start.6
  442.4 266.6 %all-reduce.12.cloned.1.call-start = ((), (), s32[]{:S(2)}) async-start(), calls=%async_computation.4 | async-start | bytes 524288 | tf_op jit(solution)/shard_map/psum | solution.py:78
  525.6 64.9 %copy-start.3 = (f32[256,256]{0,1:T(8,128)S(1)}, f32[256,256]{0,1:T(8,128)}, u32[]{:S(2)}) copy-start(f32[256,256]{0,1:T(8,128)} %all-reduce.10.cloned.1.call-done) | copy-start | bytes 786436
  590.5 2.4 copy-start.7
  597.4 24.3 %collective-permute-start.2 = (f32[3072,128]{0,1:T(8,128)}, f32[3072,128]{0,1:T(8,128)}, u32[]{:S(2)}, u32[]{:S(2)}) collective-permute-start(f32[3072,128]{0,1:T(8,128)} %get-tuple-element.107), channel_id=1, source_target_pairs={{0,16},{16,32},{32,48},{48,64},{64,80},{80,96},{96,112},{112,0},{1... | collective-permute-start | bytes 4718600 | tf_op jit(solution)/shard_map/ppermute | solution.py:13
  600.8 17.9 %collective-permute-start.3 = (f32[128,128]{1,0:T(8,128)S(1)}, f32[128,128]{1,0:T(8,128)S(1)}, u32[]{:S(2)}, u32[]{:S(2)}) collective-permute-start(f32[128,128]{1,0:T(8,128)S(1)} %get-tuple-element.117), channel_id=1, source_target_pairs={{0,16},{16,32},{32,48},{48,64},{64,80},{80,96},{96,112},{112,0},{1... | collective-permute-start | bytes 196616 | tf_op jit(solution)/shard_map/ppermute | solution.py:13
  619.2 7.8 collective-permute-start.4
  627.5 189.1 %collective-permute-start.5 = (f32[128,128]{1,0:T(8,128)S(1)}, f32[128,128]{1,0:T(8,128)S(1)}, u32[]{:S(2)}, u32[]{:S(2)}) collective-permute-start(f32[128,128]{1,0:T(8,128)S(1)} %get-tuple-element.113), channel_id=1, source_target_pairs={{0,16},{16,32},{32,48},{48,64},{64,80},{80,96},{96,112},{112,0},{1... | collective-permute-start | bytes 196616 | tf_op jit(solution)/shard_map/ppermute | solution.py:13
  709.0 65.1 %copy-start = (f32[256,256]{0,1:T(8,128)S(1)}, f32[256,256]{0,1:T(8,128)}, u32[]{:S(2)}) copy-start(f32[256,256]{0,1:T(8,128)} %all-reduce.12.cloned.1.call-done) | copy-start | bytes 786436
Sparse Core Ops, SparseCore 0:
  70.7 83.7 all-reduce.5
  263.5 83.0 all-reduce.7
  442.5 83.0 all-reduce.9
  627.1 81.7 all-reduce.11
where the time goes:
time: 838 us; the launch traced here: 825 us
  waiting for transfers between devices  384 us (46%)
  other arithmetic  223 us (27%)
  blocking collectives  74.8 us (9%)
  matrix products  62.2 us (7%)
  local copies, waits for them, and re-layouts  47.6 us (6%)
  between operations  20 us (2%)
  starting transfers between devices  12.8 us (2%)
    psum x4, waiting for transfers between devices, body(): gram = lax.psum(inner_gram(paired, paired), 'rows')  331 us
    another operation x27, other arithmetic, cayley_rotation(): factor = jnp.linalg.cholesky(denominator)  139 us
    another operation x9, other arithmetic, cayley_rotation(): lax.linalg.triangular_solve(factor, partial_solve, left_side=True, lower=...  81.7 us
    ppermute x6, waiting for transfers between devices, passed_along(): return lax.ppermute(value, axis, pairs)  52.6 us
    all_to_all x1, blocking collectives, body(): lax.all_to_all(sensitivity, 'cols', split_axis=2, concat_axis=0, tiled=True)  43.7 us
    psum x1, blocking collectives, body(): squares = lax.psum(jnp.sum(turned * turned, axis=0), 'rows')  31.2 us
    dot_general x16, matrix products, product(): jnp.dot(left, right, precision=lax.Precision.HIGHEST, preferred_element_t...  29.5 us
    dot_general x4, matrix products, inner_gram(): lax.dot_general(left, right, (((0,), (0,)), ((), ())), precision=lax.Prec...  19.9 us
  transfers between devices with their start and end apart: 10, of which 7 were waited for; matrix products, arithmetic and copies ran while one was open for 10% of the time, Pallas kernels for 0%

commit v1 on v0

v1 whole, which is shorter than its diff:
```python
import jax
import jax.numpy as jnp
from jax import lax
from jax.experimental import pallas as pl
from jax.experimental.pallas import tpu as pltpu
from jax.sharding import PartitionSpec as P

ROUNDS = 4
BLOCK = 128
PAIR = 256
SIDE = 4
ROWS = 16
COLS = 8
F32 = jnp.float32
VMEM_LIMIT = 48 * 1024 * 1024

TURN_CORE = [(c, c ^ 1) for c in range(COLS)]
NEXT_SLOT = [(c, (c + 1) % COLS) for c in range(COLS)]
NEXT_CHIP = [(c, (c + 2) % COLS) for c in range(COLS)]
ODD_TO_EVEN = [(c, (c + 1) % COLS) for c in range(1, COLS, 2)]
ODD_TO_ODD = [(c, (c + 2) % COLS) for c in range(1, COLS, 2)]
SAME_CORE = [[c for c in range(COLS) if c % 2 == k] for k in range(2)]
ALONG_X = [[(r, r - r % SIDE + (r + k) % SIDE) for r in range(ROWS)] for k in range(1, SIDE)]
ALONG_Z = [[(r, (r + SIDE * k) % ROWS) for r in range(ROWS)] for k in range(1, SIDE)]


def mm(left, right):
    return jnp.dot(left, right, precision=lax.Precision.HIGHEST, preferred_element_type=F32)


def mm_t(left, right):
    return lax.dot_general(
        left, right, (((0,), (0,)), ((), ())), precision=lax.Precision.HIGHEST, preferred_element_type=F32
    )


def call(kernel, grid, in_specs, out_specs, out_shape, scalars=0, scratch=(), flops=0, nbytes=0):
    return pl.pallas_call(
        kernel,
        grid_spec=pltpu.PrefetchScalarGridSpec(
            num_scalar_prefetch=scalars,
            grid=grid,
            in_specs=in_specs,
            out_specs=out_specs,
            scratch_shapes=list(scratch),
        ),
        out_shape=out_shape,
        compiler_params=pltpu.CompilerParams(vmem_limit_bytes=VMEM_LIMIT),
        cost_estimate=pl.CostEstimate(flops=flops, bytes_accessed=nbytes, transcendentals=0),
    )


def shape(*dims):
    return jax.ShapeDtypeStruct(dims, F32)


def whole(*dims):
    return pl.BlockSpec(dims, lambda *_: (0,) * len(dims))


def pack_kernel(x_ref, out_ref):
    out_ref[0, 0, 0] = x_ref[:, :BLOCK]
    out_ref[0, 0, 1] = x_ref[:, BLOCK:]


def pack(x):
    rows = x.shape[0]
    return call(
        pack_kernel,
        (SIDE, 3),
        [pl.BlockSpec((rows, PAIR), lambda y, j: (0, (2 * y + jnp.where(j == 2, COLS - 1, j)) % COLS))],
        pl.BlockSpec((1, 1, 2, rows, BLOCK), lambda y, j: (y, j, 0, 0, 0)),
        shape(SIDE, 3, 2, rows, BLOCK),
        nbytes=2 * 4 * SIDE * 3 * rows * PAIR,
    )(x)


def gram_kernel(core_ref, x_ref, keep_ref, send_ref):
    @pl.when(pl.program_id(0) == 0)
    def _():
        keep_ref[...] = jnp.zeros_like(keep_ref)
        send_ref[...] = jnp.zeros_like(send_ref)

    grams = []
    for slot in range(2):
        paired = jnp.concatenate([x_ref[0, slot, 0], x_ref[0, slot, 1]], axis=1)
        grams.append(mm_t(paired, paired))
    first = core_ref[0] == 0
    keep_ref[...] += jnp.where(first, grams[0], grams[1])
    send_ref[...] += jnp.where(first, grams[1], grams[0])


def first_grams(core, blocks):
    rows = blocks.shape[3]
    return call(
        gram_kernel,
        (SIDE,),
        [pl.BlockSpec((1, 2, 2, rows, BLOCK), lambda i, c: (i, 0, 0, 0, 0))],
        [whole(PAIR, PAIR)] * 2,
        [shape(PAIR, PAIR)] * 2,
        scalars=1,
        flops=2 * 6 * 2 * SIDE * rows * PAIR * PAIR,
        nbytes=4 * SIDE * rows * 2 * PAIR,
    )(core, blocks)


def rotation_of(gram, x_ref, r_ref):
    rows = lax.broadcasted_iota(jnp.int32, (PAIR, PAIR), 0)
    columns = lax.broadcasted_iota(jnp.int32, (PAIR, PAIR), 1)
    eye = (rows == columns).astype(F32)
    on_diagonal = gram * eye
    across = jnp.sum(on_diagonal, axis=0, keepdims=True)
    down = jnp.sum(on_diagonal, axis=1, keepdims=True)
    spread = across - down
    totals = across + down
    skew = gram * spread / (2.0 * spread * spread + 0.5 * totals * totals)
    square = mm(skew, skew)
    bound = jnp.max(jnp.sum(jnp.abs(square), axis=0))
    scale = 2.0 / (2.0 + bound)
    x_ref[...] = scale * (eye + skew)
    r_ref[...] = (1.0 - scale) * eye + scale * square

    def step(size):
        left = r_ref[...]
        x = x_ref[...]
        x_ref[...] = x + mm(x, left)
        r_ref[...] = mm(left, left)
        return size * size

    lax.while_loop(lambda size: size > 3e-4, step, bound / (2.0 + bound))
    x = x_ref[...]
    x = x + mm(x, eye - x + mm(skew, x))
    return 2.0 * x - eye


def first_cayley_kernel(gram_ref, weights_ref, x_ref, r_ref):
    weights_ref[...] = rotation_of(gram_ref[...], x_ref, r_ref)


def first_cayley(gram):
    return call(
        first_cayley_kernel,
        (1,),
        [whole(PAIR, PAIR)],
        whole(PAIR, PAIR),
        shape(PAIR, PAIR),
        scratch=[pltpu.VMEM((PAIR, PAIR), F32)] * 2,
        flops=2 * 6 * 8 * PAIR**3,
        nbytes=8 * PAIR * PAIR,
    )(gram)


def cayley_kernel(core_ref, up_ref, low_ref, z0_ref, z1_ref, z2_ref, z3_ref, wm_ref, wo_ref, weights_ref, gram_ref, x_ref, r_ref):
    mixed = (z0_ref[...] + z1_ref[...]) + (z2_ref[...] + z3_ref[...])
    before = jnp.where(core_ref[0] == 0, wm_ref[:, BLOCK:], wo_ref[:, BLOCK:])
    cross = mm(mixed, before)
    gram_ref[:BLOCK, :BLOCK] = up_ref[...]
    gram_ref[:BLOCK, BLOCK:] = cross
    gram_ref[BLOCK:, :BLOCK] = cross.T
    gram_ref[BLOCK:, BLOCK:] = low_ref[...]
    weights_ref[...] = rotation_of(gram_ref[...], x_ref, r_ref)


def cayley(core, up, low, parts, weights_m, weights_o):
    return call(
        cayley_kernel,
        (1,),
        [whole(BLOCK, BLOCK)] * 2 + [whole(BLOCK, PAIR)] * 4 + [whole(PAIR, PAIR)] * 2,
        [whole(PAIR, PAIR)] * 2,
        [shape(PAIR, PAIR)] * 2,
        scalars=1,
        scratch=[pltpu.VMEM((PAIR, PAIR), F32)] * 2,
        flops=2 * 6 * 8 * PAIR**3,
        nbytes=16 * PAIR * PAIR,
    )(core, up, low, *parts, weights_m, weights_o)


def project_kernel(gram_ref, weights_ref, up_ref, low_ref):
    weights = weights_ref[...]
    turned = mm(gram_ref[...], weights)
    up_ref[...] = mm_t(weights[:, :BLOCK], turned[:, :BLOCK])
    low_ref[...] = mm_t(weights[:, BLOCK:], turned[:, BLOCK:])


def project(gram, weights):
    return call(
        project_kernel,
        (1,),
        [whole(PAIR, PAIR)] * 2,
        [whole(BLOCK, BLOCK)] * 2,
        [shape(BLOCK, BLOCK)] * 2,
        flops=2 * 6 * 2 * PAIR**3,
        nbytes=12 * PAIR * PAIR,
    )(gram, weights)


def scale_kernel(rows, gram_ref, weights_ref, out_ref):
    weights = weights_ref[...]
    squares = jnp.sum(weights * mm(gram_ref[...], weights), axis=0, keepdims=True)
    out_ref[...] = jnp.sqrt(squares / rows)


def scale_of(gram, weights, rows):
    return call(
        lambda *refs: scale_kernel(rows, *refs),
        (1,),
        [whole(PAIR, PAIR)] * 2,
        whole(1, PAIR),
        shape(1, PAIR),
        flops=2 * 6 * PAIR**3,
        nbytes=8 * PAIR * PAIR,
    )(gram, weights)


def main_kernel(step, valid, swap, core_ref, own_ref, other_ref, u0_ref, l0_ref, u1_ref, l1_ref, um_ref, lm_ref,
                out0_ref, out1_ref, lown_ref, keep_ref, send_ref):
    index = pl.program_id(0)

    @pl.when(index == 0)
    def _():
        keep_ref[...] = jnp.zeros_like(keep_ref)
        send_ref[...] = jnp.zeros_like(send_ref)

    first = core_ref[0] == 0
    w0 = jnp.where(first, own_ref[...], other_ref[...])
    w1 = jnp.where(first, other_ref[:, :BLOCK], own_ref[:, :BLOCK])
    pair0 = jnp.concatenate([u0_ref[...], l0_ref[...]], axis=1)
    pair1 = jnp.concatenate([u1_ref[...], l1_ref[...]], axis=1)
    pair_m = jnp.concatenate([um_ref[...], lm_ref[...]], axis=1)
    turned = mm(pair0, w0)
    up0 = turned[:, :BLOCK]
    up1 = mm(pair1, w1)
    lown_ref[...] = turned[:, BLOCK:]
    if swap:
        out0_ref[...] = jnp.where(first, up0, up1)
        out1_ref[...] = jnp.where(first, up1, up0)
    else:
        out0_ref[...] = up0
        out1_ref[...] = up1
    inside = index * step + lax.broadcasted_iota(jnp.int32, up0.shape, 0) < valid
    z0 = mm_t(jnp.where(inside, up0, 0.0), pair_m)
    z1 = mm_t(jnp.where(inside, up1, 0.0), pair0)
    keep_ref[...] += jnp.where(first, z0, z1)
    send_ref[...] += jnp.where(first, z1, z0)


def rotate_main(core, own, other, state, valid, swap):
    rows = state[0].shape[0]
    step = rows // SIDE
    tile = pl.BlockSpec((step, BLOCK), lambda i, c: (i, 0))
    return call(
        lambda *refs: main_kernel(step, valid, swap, *refs),
        (SIDE,),
        [whole(PAIR, PAIR)] * 2 + [tile] * 6,
        [tile] * 3 + [whole(BLOCK, PAIR)] * 2,
        [shape(rows, BLOCK)] * 3 + [shape(BLOCK, PAIR)] * 2,
        scalars=1,
        flops=2 * 6 * rows * (PAIR * (PAIR + BLOCK) + 2 * BLOCK * PAIR),
        nbytes=4 * 9 * rows * BLOCK,
    )(core, own, other, *state)


def ahead_kernel(um_ref, lm_ref, weights_ref, up_ref, low_ref):
    turned = mm(jnp.concatenate([um_ref[...], lm_ref[...]], axis=1), weights_ref[...])
    up_ref[...] = turned[:, :BLOCK]
    low_ref[...] = turned[:, BLOCK:]


def rotate_ahead(upper, lower, weights):
    rows = upper.shape[0]
    tile = pl.BlockSpec((rows // SIDE, BLOCK), lambda i: (i, 0))
    return call(
        ahead_kernel,
        (SIDE,),
        [tile] * 2 + [whole(PAIR, PAIR)],
        [tile] * 2,
        [shape(rows, BLOCK)] * 2,
        flops=2 * 6 * rows * PAIR * PAIR,
        nbytes=4 * 4 * rows * BLOCK,
    )(upper, lower, weights)


def last_ahead_kernel(core_ref, um_ref, lm_ref, weights_ref, lown_ref, keep_ref, send_ref):
    low0 = mm(jnp.concatenate([um_ref[...], lm_ref[...]], axis=1), weights_ref[:, BLOCK:])
    low1 = lown_ref[...]
    first = core_ref[0] == 0
    keep_ref[...] = jnp.where(first, low0, low1)
    send_ref[...] = jnp.where(first, low1, low0)


def rotate_last_ahead(core, upper, lower, weights, lown):
    rows = upper.shape[0]
    tile = pl.BlockSpec((rows // SIDE, BLOCK), lambda i, c: (i, 0))
    return call(
        last_ahead_kernel,
        (SIDE,),
        [tile] * 2 + [whole(PAIR, PAIR)] + [tile],
        [tile] * 2,
        [shape(rows, BLOCK)] * 2,
        scalars=1,
        flops=2 * 6 * rows * PAIR * BLOCK,
        nbytes=4 * 5 * rows * BLOCK,
    )(core, upper, lower, weights, lown)


def final_kernel(core_ref, weights_ref, ku_ref, kl_ref, ru_ref, rl_ref, kub_ref, klb_ref, rub_ref, rlb_ref,
                 out_ref, frame_ref):
    weights = weights_ref[...]
    first = core_ref[0] == 0
    half = kub_ref.shape[0]

    def ordered(keep_up, keep_low, other_up, other_low):
        mine = mm(jnp.concatenate([keep_up[...], keep_low[...]], axis=1), weights)
        theirs = mm(jnp.concatenate([other_up[...], other_low[...]], axis=1), weights)
        return jnp.where(first, mine, theirs), jnp.where(first, theirs, mine)

    out_ref[0], out_ref[1] = ordered(ku_ref, kl_ref, ru_ref, rl_ref)

    @pl.when(pl.program_id(0) == 0)
    def _():
        frame_ref[:half], frame_ref[half:] = ordered(kub_ref, klb_ref, rub_ref, rlb_ref)


def rotate_final(core, weights, blocks, rows, basis_rows):
    tile = pl.BlockSpec((rows, BLOCK), lambda i, c: (i, 0))
    at = SIDE * rows // basis_rows
    basis = pl.BlockSpec((basis_rows, BLOCK), lambda i, c: (at, 0))
    return call(
        final_kernel,
        (SIDE,),
        [whole(PAIR, PAIR)] + [tile] * 4 + [basis] * 4,
        [pl.BlockSpec((2, rows, PAIR), lambda i, c: (i, 0, 0)), whole(2 * basis_rows, PAIR)],
        [shape(COLS, rows, PAIR), shape(2 * basis_rows, PAIR)],
        scalars=1,
        flops=2 * 6 * 2 * SIDE * rows * PAIR * PAIR,
        nbytes=4 * 4 * SIDE * rows * PAIR,
    )(core, weights, *blocks, *blocks)


def swap_core(value):
    return lax.ppermute(value, "cols", TURN_CORE)


def sum_over_rows(value):
    value = value + sum(lax.ppermute(value, "rows", pairs) for pairs in ALONG_X)
    return [value] + [lax.ppermute(value, "rows", pairs) for pairs in ALONG_Z]


def gram_over_rows(gram):
    parts = lax.all_to_all(gram.reshape(ROWS, PAIR // ROWS, PAIR), "rows", 0, 0, tiled=True)
    share = jnp.sum(parts, axis=0)
    spread = jnp.broadcast_to(share[None], (ROWS,) + share.shape)
    return lax.all_to_all(spread, "rows", 0, 0, tiled=True).reshape(PAIR, PAIR)


def body(sensitivity):
    rows = sensitivity.shape[1]
    column = lax.axis_index("cols")
    parity = column % 2
    core = parity.astype(jnp.int32).reshape(1)
    blocks = lax.all_to_all(pack(sensitivity[0]), "cols", 0, 0, axis_index_groups=SAME_CORE, tiled=True)

    keep, send = first_grams(core, blocks)
    gram = gram_over_rows(keep + swap_core(send))

    basis_rows = sensitivity.shape[2] // ROWS // 2
    basis_at = lax.axis_index("rows") * 2 * basis_rows + parity * basis_rows
    row_ids = basis_at + lax.broadcasted_iota(jnp.int32, (basis_rows, BLOCK), 0)
    state = []
    for j, slot in enumerate((column - parity, column - parity + 1, (column - parity + COLS - 1) % COLS)):
        for half in range(2):
            ids = slot * PAIR + half * BLOCK + lax.broadcasted_iota(jnp.int32, (basis_rows, BLOCK), 1)
            data = blocks[:, j, half].reshape(SIDE * rows, BLOCK)
            state.append(jnp.concatenate([data, (row_ids == ids).astype(F32)], axis=0))
    valid = SIDE * rows

    weights = first_cayley(gram)
    for sweep_round in range(ROUNDS - 1):
        last = sweep_round == ROUNDS - 2
        other = swap_core(weights)
        ahead = lax.ppermute(weights, "cols", ODD_TO_EVEN) + lax.ppermute(weights, "cols", ODD_TO_ODD)
        up, low = project(gram, weights)
        low = lax.ppermute(low, "cols", NEXT_SLOT)
        out0, out1, low_out, keep, send = rotate_main(core, weights, other, state, valid, last)
        parts = sum_over_rows(keep + swap_core(send))
        if last:
            keep_low, send_low = rotate_last_ahead(core, state[4], state[5], ahead, low_out)
            held = [out0, keep_low, swap_core(out1), swap_core(send_low)]
        else:
            up_m, low0 = rotate_ahead(state[4], state[5], ahead)
            low_m = lax.ppermute(low_out, "cols", NEXT_CHIP)
            state = [out0, low0, out1, low_out, up_m, low_m]
        weights, gram = cayley(core, up, low, parts, ahead, other)

    column_scale = scale_of(gram, weights, float(rows * COLS * ROWS)).reshape(PAIR)
    rotated, frame = rotate_final(core, weights, held, rows, basis_rows)
    return rotated, frame, column_scale


def solution(mesh):
    in_specs = (P("cols", "rows", None),)
    out_specs = (P(None, "rows", "cols"), P("rows", "cols"), P("cols"))
    return jax.shard_map(body, mesh=mesh, in_specs=in_specs, out_specs=out_specs, check_vma=False)
```

time: 838 us -> 266 us (0.32); the launches traced: 825 us -> 265 us
  waiting for transfers between devices: 384 us -> 124 us
  other arithmetic: 223 us -> 6.46 us
  blocking collectives: 74.8 us -> 0 us
  matrix products: 62.2 us -> 0 us
  Pallas kernels: 0 us -> 58.6 us
  starting transfers between devices: 12.8 us -> 63.7 us
  local copies, waits for them, and re-layouts: 47.6 us -> 11.3 us
  between operations: 20 us -> 1.09 us
    psum x4 -> x0, waiting for transfers between devices: 331 us -> none  [body(): gram = lax.psum(inner_gram(paired, paired), 'rows')]
    another operation x36 -> x0, other arithmetic: 221 us -> none  [the longest x27 139 us: cayley_rotation(): factor = jnp.linalg.cholesky(denominator)]
    all_to_all x0 -> x3, waiting for transfers between devices: none -> 65.2 us  [the longest x1 53.8 us: body(): lax.all_to_all(pack(sensitivity[0]), 'cols', 0, 0, axis_index_groups=SAME...]
    pallas_call x0 -> x17, Pallas kernels: none -> 58.6 us  [the longest x3 21.6 us: rotate_main(): call(lambda *refs: main_kernel(step, valid, swap, *refs), (SIDE,), [whole...]
    dot_general x20 -> x0, matrix products: 49.4 us -> none  [the longest x16 29.5 us: product(): jnp.dot(left, right, precision=lax.Precision.HIGHEST, preferred_element_t...]
    all_to_all x1 -> x0, blocking collectives: 43.7 us -> none  [body(): lax.all_to_all(sensitivity, 'cols', split_axis=2, concat_axis=0, tiled=True)]
    ppermute x6 -> x38, starting transfers between devices: 11.8 us -> 47.5 us  [the longest x9 15.3 us: swap_core(): return lax.ppermute(value, 'cols', TURN_CORE)]
    psum x1 -> x0, blocking collectives: 31.2 us -> none  [body(): squares = lax.psum(jnp.sum(turned * turned, axis=0), 'rows')]
  transfers between devices with their start and end apart: 10 -> 41, of which waited for: 7 -> 23; matrix products, arithmetic and copies ran while one was open for 10% -> 4% of each run, Pallas kernels for 0% -> 6%
where the time goes in v1:
time: 266 us; the launch traced here: 265 us
  waiting for transfers between devices  124 us (47%)
  starting transfers between devices  63.7 us (24%)
  Pallas kernels  58.6 us (22%)
  local copies, waits for them, and re-layouts  11.3 us (4%)
  other arithmetic  6.46 us (2%)
    all_to_all x1, waiting for transfers between devices, body(): lax.all_to_all(pack(sensitivity[0]), 'cols', 0, 0, axis_index_groups=SAME...  53.8 us
    ppermute x3, waiting for transfers between devices, body(): lax.ppermute(weights, 'cols', ODD_TO_ODD)  27.9 us
    pallas_call x3, Pallas kernels, rotate_main(): call(lambda *refs: main_kernel(step, valid, swap, *refs), (SIDE,), [whole...  21.6 us
    ppermute x9, starting transfers between devices, swap_core(): return lax.ppermute(value, 'cols', TURN_CORE)  15.3 us
    ppermute x9, waiting for transfers between devices, sum_over_rows(): lax.ppermute(value, 'rows', pairs)  12.2 us
    ppermute x9, starting transfers between devices, sum_over_rows(): lax.ppermute(value, 'rows', pairs)  9.4 us
    ppermute x9, waiting for transfers between devices, sum_over_rows(): return [value] + [lax.ppermute(value, 'rows', pairs) for pairs in ALONG_Z]  8.95 us
    pallas_call x3, Pallas kernels, cayley(): call(cayley_kernel, (1,), [whole(BLOCK, BLOCK)] * 2 + [whole(BLOCK, PAIR)...  8.15 us
  transfers between devices with their start and end apart: 41, of which 23 were waited for; matrix products, arithmetic and copies ran while one was open for 4% of the time, Pallas kernels for 6%

profile of v1, /device:TPU:1, one launch (start us, length us, event | category | flops | bytes accessed | tf_op | source)
XLA Modules:
  0.0 265.5 jit_solution(15667161047960497230)
XLA Ops:
  2.5 5.1 %shard_map.38 = f32[4,3,2,384,128]{4,3,2,1,0:T(8,128)} custom-call(f32[384,2048]{1,0:T(8,128)S(1)} %bitcast.11), custom_call_target="tpu_custom_call" | custom-call | bytes 9437184 | tf_op jit(solution)/shard_map/pallas_call | solution.py:68
  7.6 5.0 %all-to-all-start = ((f32[4,3,2,384,128]{4,3,2,1,0:T(8,128)}), f32[4,3,2,384,128]{4,3,2,1,0:T(8,128)}, u32[]{:S(2)}, u32[]{:S(2)}) async-start(f32[4,3,2,384,128]{4,3,2,1,0:T(8,128)} %shard_map.38), calls=%async_computation | async-start | bytes 9437184 | tf_op jit(solution)/shard_map/all_to_all | solution.py:361
  13.4 53.8 %all-to-all-done.x_ref = f32[4,3,2,384,128]{4,3,2,1,0:T(8,128)} async-done(((f32[4,3,2,384,128]{4,3,2,1,0:T(8,128)}), f32[4,3,2,384,128]{4,3,2,1,0:T(8,128)}, u32[]{:S(2)}, u32[]{:S(2)}) %all-to-all-start) | async-done | bytes 4718624 | tf_op jit(solution)/shard_map/all_to_all | solution.py:361
  67.2 5.8 %shard_map.39 = (f32[256,256]{1,0:T(8,128)S(1)}, f32[256,256]{1,0:T(8,128)S(1)}) custom-call(s32[1]{0:T(128)} %bitcast.core_ref.refs_0_, f32[4,3,2,384,128]{4,3,2,1,0:T(8,128)} %all-to-all-done.x_ref), custom_call_target="tpu_custom_call" | custom-call | flops 2415919104 | bytes 3145728 | tf_op jit(solution)/shard_map/pallas_call | solution.py:95
  74.6 3.8 %fusion = (f32[4,1,1,384,128]{4,3,2,1,0:T(8,128)S(1)}, f32[4,1,1,384,128]{4,3,2,1,0:T(8,128)}, f32[4,1,1,384,128]{4,3,2,1,0:T(8,128)S(1)}, f32[4,1,1,384,128]{4,...) fusion(f32[4,3,2,384,128]{4,3,2,1,0:T(8,128)} %all-to-all-done.x_ref), kind=kLoop, calls=%fused_computation.22 | loop fusion | bytes 9437184 | tf_op jit(solution)/shard_map/slice | solution.py:373
  79.2 7.7 %all-to-all-start.1 = ((f32[16,16,256]{2,1,0:T(8,128)}), f32[16,16,256]{2,1,0:T(8,128)S(1)}, u32[]{:S(2)}, u32[]{:S(2)}) async-start(f32[16,16,256]{2,1,0:T(8,128)} %bitcast.2), calls=%async_computation.1 | async-start | bytes 524288 | tf_op jit(solution)/shard_map/all_to_all | solution.py:350
  86.9 2.5 pad_maximum_fusion.4
  89.4 6.0 %all-to-all-done.1 = f32[16,16,256]{2,1,0:T(8,128)S(1)} async-done(((f32[16,16,256]{2,1,0:T(8,128)}), f32[16,16,256]{2,1,0:T(8,128)S(1)}, u32[]{:S(2)}, u32[]{:S(2)}) %all-to-all-start.1) | async-done | bytes 262176 | tf_op jit(solution)/shard_map/all_to_all | solution.py:350
  96.2 3.5 %all-to-all-start.2 = ((f32[16,16,256]{2,1,0:T(8,128)}), f32[16,16,256]{2,1,0:T(8,128)S(1)}, u32[]{:S(2)}, u32[]{:S(2)}) async-start(f32[16,16,256]{2,1,0:T(8,128)} %broadcast_in_dim.2), calls=%async_computation.2 | async-start | bytes 524288 | tf_op jit(solution)/shard_map/all_to_all | solution.py:353
  99.7 2.1 pad_maximum_fusion.2
  101.9 5.4 %all-to-all-done.2 = f32[16,16,256]{2,1,0:T(8,128)S(1)} async-done(((f32[16,16,256]{2,1,0:T(8,128)}), f32[16,16,256]{2,1,0:T(8,128)S(1)}, u32[]{:S(2)}, u32[]{:S(2)}) %all-to-all-start.2) | async-done | bytes 262176 | tf_op jit(solution)/shard_map/all_to_all | solution.py:353
  107.2 3.0 %shard_map.40.weights_ref.refs_1_ = f32[256,256]{1,0:T(8,128)S(1)} custom-call(f32[256,256]{1,0:T(8,128)S(1)} %bitcast.12), custom_call_target="tpu_custom_call" | custom-call | flops 1610612736 | bytes 524288 | tf_op jit(solution)/shard_map/pallas_call | solution.py:141
  110.2 2.4 collective-permute-start.2
  113.8 7.2 %shard_map.42 = (f32[1600,128]{1,0:T(8,128)S(1)}, f32[1600,128]{1,0:T(8,128)S(1)}, f32[1600,128]{1,0:T(8,128)S(1)}, f32[128,256]{1,0:T(8,128)S(1)}, f32[128,256]{1,0:T(8,128)S(1)}) custom-call(s32[1]{0:T(128)} %bitcast.core_ref.refs_0_, f32[256,256]{1,0:T(8,128)S(1)} %shard_map.40.weights_ref.refs_1_, f32[256,256]{1,0:T(8,128)S(1)} %collective-permute-done.2.refs_2_.wo_ref, ...), custom_call_target="tpu_custom_call" | custom-call | flops 3145728000 | bytes 7372800 | tf_op jit(solution)/shard_map/pallas_call | solution.py:251
  127.2 4.1 %collective-permute-start.10 = (f32[256,256]{1,0:T(8,128)S(1)}, f32[256,256]{1,0:T(8,128)S(1)}, u32[]{:S(2)}, u32[]{:S(2)}) collective-permute-start(f32[256,256]{1,0:T(8,128)S(1)} %shard_map.40.weights_ref.refs_1_), channel_id=1, source_target_pairs={{16,32},{48,64},{80,96},{112,0},{17,33},{49,65},{81,97},{113,1},{1... | collective-permute-start | bytes 786440 | tf_op jit(solution)/shard_map/ppermute | solution.py:381
  134.8 13.8 %collective-permute-done.11 = f32[256,256]{1,0:T(8,128)S(1)} collective-permute-done((f32[256,256]{1,0:T(8,128)S(1)}, f32[256,256]{1,0:T(8,128)S(1)}, u32[]{:S(2)}, u32[]{:S(2)}) %collective-permute-start.11) | collective-permute-done | bytes 262176 | tf_op jit(solution)/shard_map/ppermute | solution.py:381
  153.6 2.8 %shard_map.43 = (f32[256,256]{1,0:T(8,128)S(1)}, f32[256,256]{1,0:T(8,128)S(1)}) custom-call(s32[1]{0:T(128)} %bitcast.core_ref.refs_0_, f32[128,128]{1,0:T(8,128)S(1)} %get-tuple-element.42.up_ref, f32[128,128]{1,0:T(8,128)S(1)} %collective-permute-done.1.low_ref, f32[128,256]{1,0:T(8,128)S(1)} %add_add_fusion.2.z0_ref, ...), custom_call_target="tpu_custom_call" | custom-call | flops 1610612736 | bytes 1048576 | tf_op jit(solution)/shard_map/pallas_call | solution.py:165
  156.4 3.5 %collective-permute-start.13 = (f32[256,256]{1,0:T(8,128)S(1)}, f32[256,256]{1,0:T(8,128)S(1)}, u32[]{:S(2)}, u32[]{:S(2)}) collective-permute-start(f32[256,256]{1,0:T(8,128)S(1)} %get-tuple-element.47.weights_ref.refs_1_), channel_id=1, source_target_pairs={{0,16},{16,0},{32,48},{48,32},{64,80},{80,64},{96,112},{112,96},{1... | collective-permute-start | bytes 786440 | tf_op jit(solution)/shard_map/ppermute | solution.py:341
  163.8 7.2 %shard_map.46 = (f32[1600,128]{1,0:T(8,128)S(1)}, f32[1600,128]{1,0:T(8,128)S(1)}, f32[1600,128]{1,0:T(8,128)S(1)}, f32[128,256]{1,0:T(8,128)S(1)}, f32[128,256]{1,0:T(8,128)S(1)}) custom-call(s32[1]{0:T(128)} %bitcast.core_ref.refs_0_, f32[256,256]{1,0:T(8,128)S(1)} %get-tuple-element.47.weights_ref.refs_1_, ...), custom_call_target="tpu_custom_call" | custom-call | flops 3145728000 | bytes 7372800 | tf_op jit(solution)/shard_map/pallas_call | solution.py:251
  172.5 2.7 %collective-permute-start.18 = (f32[128,256]{1,0:T(8,128)S(1)}, f32[128,256]{1,0:T(8,128)S(1)}, u32[]{:S(2)}, u32[]{:S(2)}) collective-permute-start(f32[128,256]{1,0:T(8,128)S(1)} %add.150), channel_id=1, source_target_pairs={{0,3},{1,0},{2,1},{3,2},{4,7},{5,4},{6,5},{7,6},{8,11},{9,8},{10,9... | collective-permute-start | bytes 393224 | tf_op jit(solution)/shard_map/ppermute | solution.py:345
  178.3 2.3 collective-permute-done.18
  182.0 3.0 %collective-permute-done.16 = f32[128,256]{1,0:T(8,128)S(1)} collective-permute-done((f32[128,256]{1,0:T(8,128)S(1)}, f32[128,256]{1,0:T(8,128)S(1)}, u32[]{:S(2)}, u32[]{:S(2)}) %collective-permute-start.16) | collective-permute-done | bytes 131104 | tf_op jit(solution)/shard_map/ppermute | solution.py:345
  186.2 14.2 %collective-permute-done.23 = f32[256,256]{1,0:T(8,128)S(1)} collective-permute-done((f32[256,256]{1,0:T(8,128)S(1)}, f32[256,256]{1,0:T(8,128)S(1)}, u32[]{:S(2)}, u32[]{:S(2)}) %collective-permute-start.23) | collective-permute-done | bytes 262176 | tf_op jit(solution)/shard_map/ppermute | solution.py:381
  202.6 2.0 collective-permute-done.12.low_ref
  205.4 2.7 %shard_map.47 = (f32[256,256]{1,0:T(8,128)S(1)}, f32[256,256]{1,0:T(8,128)S(1)}) custom-call(s32[1]{0:T(128)} %bitcast.core_ref.refs_0_, f32[128,128]{1,0:T(8,128)S(1)} %get-tuple-element.48.up_ref, f32[128,128]{1,0:T(8,128)S(1)} %collective-permute-done.12.low_ref, f32[128,256]{1,0:T(8,128)S(1)} %add_add_fusion.1.z0_ref, ...), custom_call_target="tpu_custom_call" | custom-call | flops 1610612736 | bytes 1048576 | tf_op jit(solution)/shard_map/pallas_call | solution.py:165
  217.5 7.2 %shard_map.50 = (f32[1600,128]{1,0:T(8,128)S(1)}, f32[1600,128]{1,0:T(8,128)S(1)}, f32[1600,128]{1,0:T(8,128)S(1)}, f32[128,256]{1,0:T(8,128)S(1)}, f32[128,256]{1,0:T(8,128)S(1)}) custom-call(s32[1]{0:T(128)} %bitcast.core_ref.refs_0_, f32[256,256]{1,0:T(8,128)S(1)} %get-tuple-element.58.weights_ref.refs_1_, ...), custom_call_target="tpu_custom_call" | custom-call | flops 3145728000 | bytes 7372800 | tf_op jit(solution)/shard_map/pallas_call | solution.py:251
  227.9 4.8 %collective-permute-start.37 = (f32[1600,128]{1,0:T(8,128)S(1)}, f32[1600,128]{1,0:T(8,128)S(1)}, u32[]{:S(2)}, u32[]{:S(2)}) collective-permute-start(f32[1600,128]{1,0:T(8,128)S(1)} %get-tuple-element.73), channel_id=1, source_target_pairs={{0,16},{16,0},{32,48},{48,32},{64,80},{80,64},{96,112},{112,96},{1... | collective-permute-start | bytes 2457608 | tf_op jit(solution)/shard_map/ppermute | solution.py:341
  233.3 2.8 %collective-permute-done.27 = f32[128,256]{1,0:T(8,128)S(1)} collective-permute-done((f32[128,256]{1,0:T(8,128)S(1)}, f32[128,256]{1,0:T(8,128)S(1)}, u32[]{:S(2)}, u32[]{:S(2)}) %collective-permute-start.27) | collective-permute-done | bytes 131104 | tf_op jit(solution)/shard_map/ppermute | solution.py:341
  244.0 3.5 %collective-permute-done.28 = f32[128,256]{1,0:T(8,128)S(1)} collective-permute-done((f32[128,256]{1,0:T(8,128)S(1)}, f32[128,256]{1,0:T(8,128)S(1)}, u32[]{:S(2)}, u32[]{:S(2)}) %collective-permute-start.28) | collective-permute-done | bytes 131104 | tf_op jit(solution)/shard_map/ppermute | solution.py:345
  253.4 3.6 %collective-permute-done.31.z1_ref = f32[128,256]{1,0:T(8,128)S(1)} collective-permute-done((f32[128,256]{1,0:T(8,128)S(1)}, f32[128,256]{1,0:T(8,128)S(1)}, u32[]{:S(2)}, u32[]{:S(2)}) %collective-permute-start.31) | collective-permute-done | bytes 131104 | tf_op jit(solution)/shard_map/ppermute | solution.py:346
  257.1 2.7 %shard_map.51 = (f32[256,256]{1,0:T(8,128)S(1)}, f32[256,256]{1,0:T(8,128)S(1)}) custom-call(s32[1]{0:T(128)} %bitcast.core_ref.refs_0_, f32[128,128]{1,0:T(8,128)S(1)} %get-tuple-element.59.up_ref, f32[128,128]{1,0:T(8,128)S(1)} %collective-permute-done.24.low_ref, f32[128,256]{1,0:T(8,128)S(1)} %add_add_fusion.z0_ref, ...), custom_call_target="tpu_custom_call" | custom-call | flops 1610612736 | bytes 1048576 | tf_op jit(solution)/shard_map/pallas_call | solution.py:165
  260.7 4.7 %shard_map.53 = (f32[8,384,256]{2,1,0:T(8,128)}, f32[128,256]{1,0:T(8,128)}) custom-call(s32[1]{0:T(128)} %bitcast.core_ref.refs_0_, f32[256,256]{1,0:T(8,128)S(1)} %get-tuple-element.68.weights_ref.refs_1_, f32[1600,128]{1,0:T(8,128)S(1)} %get-tuple-element.69.ku_ref.kub_ref, f32[1600,128]{1,0:T(8,128)S(1)} %get-tuple-element.71.kl_ref.klb_ref, ...), custom_call_target="tpu_custom_call" | custom-call | flops 2415919104 | bytes 6291456 | tf_op jit(solution)/shard_map/pallas_call | solution.py:328
  (117 shorter events, 63.4 us)
Async XLA Ops:
  7.6 59.6 %all-to-all-start = ((f32[4,3,2,384,128]{4,3,2,1,0:T(8,128)}), f32[4,3,2,384,128]{4,3,2,1,0:T(8,128)}, u32[]{:S(2)}, u32[]{:S(2)}) async-start(f32[4,3,2,384,128]{4,3,2,1,0:T(8,128)} %shard_map.38), calls=%async_computation | async-start | bytes 9437184 | tf_op jit(solution)/shard_map/all_to_all | solution.py:361
  73.0 5.5 %collective-permute-start = (f32[256,256]{1,0:T(8,128)S(1)}, f32[256,256]{1,0:T(8,128)S(1)}, u32[]{:S(2)}, u32[]{:S(2)}) collective-permute-start(f32[256,256]{1,0:T(8,128)S(1)} %get-tuple-element.41), channel_id=1, source_target_pairs={{0,16},{16,0},{32,48},{48,32},{64,80},{80,64},{96,112},{112,96},{1... | collective-permute-start | bytes 786440 | tf_op jit(solution)/shard_map/ppermute | solution.py:341
  79.2 16.2 %all-to-all-start.1 = ((f32[16,16,256]{2,1,0:T(8,128)}), f32[16,16,256]{2,1,0:T(8,128)S(1)}, u32[]{:S(2)}, u32[]{:S(2)}) async-start(f32[16,16,256]{2,1,0:T(8,128)} %bitcast.2), calls=%async_computation.1 | async-start | bytes 524288 | tf_op jit(solution)/shard_map/all_to_all | solution.py:350
  96.2 11.0 %all-to-all-start.2 = ((f32[16,16,256]{2,1,0:T(8,128)}), f32[16,16,256]{2,1,0:T(8,128)S(1)}, u32[]{:S(2)}, u32[]{:S(2)}) async-start(f32[16,16,256]{2,1,0:T(8,128)} %broadcast_in_dim.2), calls=%async_computation.2 | async-start | bytes 524288 | tf_op jit(solution)/shard_map/all_to_all | solution.py:353
  123.0 8.4 %collective-permute-start.5 = (f32[128,256]{1,0:T(8,128)S(1)}, f32[128,256]{1,0:T(8,128)S(1)}, u32[]{:S(2)}, u32[]{:S(2)}) collective-permute-start(f32[128,256]{1,0:T(8,128)S(1)} %add.145), channel_id=1, source_target_pairs={{0,2},{1,3},{2,0},{3,1},{4,6},{5,7},{6,4},{7,5},{8,10},{9,11},{10,... | collective-permute-start | bytes 393224 | tf_op jit(solution)/shard_map/ppermute | solution.py:345
  124.6 7.6 %collective-permute-start.4 = (f32[128,256]{1,0:T(8,128)S(1)}, f32[128,256]{1,0:T(8,128)S(1)}, u32[]{:S(2)}, u32[]{:S(2)}) collective-permute-start(f32[128,256]{1,0:T(8,128)S(1)} %add.145), channel_id=1, source_target_pairs={{0,1},{1,2},{2,3},{3,0},{4,5},{5,6},{6,7},{7,4},{8,9},{9,10},{10,1... | collective-permute-start | bytes 393224 | tf_op jit(solution)/shard_map/ppermute | solution.py:345
  124.6 38.3 %collective-permute-start.14 = (f32[1600,128]{1,0:T(8,128)S(1)}, f32[1600,128]{1,0:T(8,128)S(1)}, u32[]{:S(2)}, u32[]{:S(2)}) collective-permute-start(f32[1600,128]{1,0:T(8,128)S(1)} %get-tuple-element.53.refs_6_), channel_id=1, source_target_pairs={{0,32},{16,48},{32,64},{48,80},{64,96},{80,112},{96,0},{112,16},{1... | collective-permute-start | bytes 2457608 | tf_op jit(solution)/shard_map/ppermute | solution.py:391
  125.0 23.6 %collective-permute-start.11 = (f32[256,256]{1,0:T(8,128)S(1)}, f32[256,256]{1,0:T(8,128)S(1)}, u32[]{:S(2)}, u32[]{:S(2)}) collective-permute-start(f32[256,256]{1,0:T(8,128)S(1)} %shard_map.40.weights_ref.refs_1_), channel_id=1, source_target_pairs={{16,48},{48,80},{80,112},{112,16},{17,49},{49,81},{81,113},{113,17... | collective-permute-start | bytes 786440 | tf_op jit(solution)/shard_map/ppermute | solution.py:381
  127.2 22.4 %collective-permute-start.10 = (f32[256,256]{1,0:T(8,128)S(1)}, f32[256,256]{1,0:T(8,128)S(1)}, u32[]{:S(2)}, u32[]{:S(2)}) collective-permute-start(f32[256,256]{1,0:T(8,128)S(1)} %shard_map.40.weights_ref.refs_1_), channel_id=1, source_target_pairs={{16,32},{48,64},{80,96},{112,0},{17,33},{49,65},{81,97},{113,1},{1... | collective-permute-start | bytes 786440 | tf_op jit(solution)/shard_map/ppermute | solution.py:381
  132.3 20.6 %collective-permute-start.9 = (f32[128,256]{1,0:T(8,128)S(1)}, f32[128,256]{1,0:T(8,128)S(1)}, u32[]{:S(2)}, u32[]{:S(2)}) collective-permute-start(f32[128,256]{1,0:T(8,128)S(1)} %add_add_fusion.2.z0_ref), channel_id=1, source_target_pairs={{0,12},{1,13},{2,14},{3,15},{4,0},{5,1},{6,2},{7,3},{8,4},{9,5},{1... | collective-permute-start | bytes 393224 | tf_op jit(solution)/shard_map/ppermute | solution.py:346
  133.2 19.6 %collective-permute-start.8 = (f32[128,256]{1,0:T(8,128)S(1)}, f32[128,256]{1,0:T(8,128)S(1)}, u32[]{:S(2)}, u32[]{:S(2)}) collective-permute-start(f32[128,256]{1,0:T(8,128)S(1)} %add_add_fusion.2.z0_ref), channel_id=1, source_target_pairs={{0,8},{1,9},{2,10},{3,11},{4,12},{5,13},{6,14},{7,15},{8,0},{9,1},... | collective-permute-start | bytes 393224 | tf_op jit(solution)/shard_map/ppermute | solution.py:346
  148.6 5.0 %collective-permute-start.7 = (f32[128,256]{1,0:T(8,128)S(1)}, f32[128,256]{1,0:T(8,128)S(1)}, u32[]{:S(2)}, u32[]{:S(2)}) collective-permute-start(f32[128,256]{1,0:T(8,128)S(1)} %add_add_fusion.2.z0_ref), channel_id=1, source_target_pairs={{0,4},{1,5},{2,6},{3,7},{4,8},{5,9},{6,10},{7,11},{8,12},{9,13},{1... | collective-permute-start | bytes 393224 | tf_op jit(solution)/shard_map/ppermute | solution.py:346
  156.4 6.5 %collective-permute-start.13 = (f32[256,256]{1,0:T(8,128)S(1)}, f32[256,256]{1,0:T(8,128)S(1)}, u32[]{:S(2)}, u32[]{:S(2)}) collective-permute-start(f32[256,256]{1,0:T(8,128)S(1)} %get-tuple-element.47.weights_ref.refs_1_), channel_id=1, source_target_pairs={{0,16},{16,0},{32,48},{48,32},{64,80},{80,64},{96,112},{112,96},{1... | collective-permute-start | bytes 786440 | tf_op jit(solution)/shard_map/ppermute | solution.py:341
  172.5 8.2 %collective-permute-start.18 = (f32[128,256]{1,0:T(8,128)S(1)}, f32[128,256]{1,0:T(8,128)S(1)}, u32[]{:S(2)}, u32[]{:S(2)}) collective-permute-start(f32[128,256]{1,0:T(8,128)S(1)} %add.150), channel_id=1, source_target_pairs={{0,3},{1,0},{2,1},{3,2},{4,7},{5,4},{6,5},{7,6},{8,11},{9,8},{10,9... | collective-permute-start | bytes 393224 | tf_op jit(solution)/shard_map/ppermute | solution.py:345
  175.3 6.7 %collective-permute-start.17 = (f32[128,256]{1,0:T(8,128)S(1)}, f32[128,256]{1,0:T(8,128)S(1)}, u32[]{:S(2)}, u32[]{:S(2)}) collective-permute-start(f32[128,256]{1,0:T(8,128)S(1)} %add.150), channel_id=1, source_target_pairs={{0,2},{1,3},{2,0},{3,1},{4,6},{5,7},{6,4},{7,5},{8,10},{9,11},{10,... | collective-permute-start | bytes 393224 | tf_op jit(solution)/shard_map/ppermute | solution.py:345
  175.6 9.4 %collective-permute-start.16 = (f32[128,256]{1,0:T(8,128)S(1)}, f32[128,256]{1,0:T(8,128)S(1)}, u32[]{:S(2)}, u32[]{:S(2)}) collective-permute-start(f32[128,256]{1,0:T(8,128)S(1)} %add.150), channel_id=1, source_target_pairs={{0,1},{1,2},{2,3},{3,0},{4,5},{5,6},{6,7},{7,4},{8,9},{9,10},{10,1... | collective-permute-start | bytes 393224 | tf_op jit(solution)/shard_map/ppermute | solution.py:345
  176.4 40.2 %collective-permute-start.26 = (f32[1600,128]{1,0:T(8,128)S(1)}, f32[1600,128]{1,0:T(8,128)S(1)}, u32[]{:S(2)}, u32[]{:S(2)}) collective-permute-start(f32[1600,128]{1,0:T(8,128)S(1)} %get-tuple-element.64.refs_6_), channel_id=1, source_target_pairs={{0,32},{16,48},{32,64},{48,80},{64,96},{80,112},{96,0},{112,16},{1... | collective-permute-start | bytes 2457608 | tf_op jit(solution)/shard_map/ppermute | solution.py:391
  176.4 24.0 %collective-permute-start.23 = (f32[256,256]{1,0:T(8,128)S(1)}, f32[256,256]{1,0:T(8,128)S(1)}, u32[]{:S(2)}, u32[]{:S(2)}) collective-permute-start(f32[256,256]{1,0:T(8,128)S(1)} %get-tuple-element.47.weights_ref.refs_1_), channel_id=1, source_target_pairs={{16,48},{48,80},{80,112},{112,16},{17,49},{49,81},{81,113},{113,17... | collective-permute-start | bytes 786440 | tf_op jit(solution)/shard_map/ppermute | solution.py:381
  180.7 20.8 %collective-permute-start.22 = (f32[256,256]{1,0:T(8,128)S(1)}, f32[256,256]{1,0:T(8,128)S(1)}, u32[]{:S(2)}, u32[]{:S(2)}) collective-permute-start(f32[256,256]{1,0:T(8,128)S(1)} %get-tuple-element.47.weights_ref.refs_1_), channel_id=1, source_target_pairs={{16,32},{48,64},{80,96},{112,0},{17,33},{49,65},{81,97},{113,1},{1... | collective-permute-start | bytes 786440 | tf_op jit(solution)/shard_map/ppermute | solution.py:381
  185.0 19.6 %collective-permute-start.21 = (f32[128,256]{1,0:T(8,128)S(1)}, f32[128,256]{1,0:T(8,128)S(1)}, u32[]{:S(2)}, u32[]{:S(2)}) collective-permute-start(f32[128,256]{1,0:T(8,128)S(1)} %add_add_fusion.1.z0_ref), channel_id=1, source_target_pairs={{0,12},{1,13},{2,14},{3,15},{4,0},{5,1},{6,2},{7,3},{8,4},{9,5},{1... | collective-permute-start | bytes 393224 | tf_op jit(solution)/shard_map/ppermute | solution.py:346
  185.7 19.0 %collective-permute-start.20 = (f32[128,256]{1,0:T(8,128)S(1)}, f32[128,256]{1,0:T(8,128)S(1)}, u32[]{:S(2)}, u32[]{:S(2)}) collective-permute-start(f32[128,256]{1,0:T(8,128)S(1)} %add_add_fusion.1.z0_ref), channel_id=1, source_target_pairs={{0,8},{1,9},{2,10},{3,11},{4,12},{5,13},{6,14},{7,15},{8,0},{9,1},... | collective-permute-start | bytes 393224 | tf_op jit(solution)/shard_map/ppermute | solution.py:346
  200.4 5.0 %collective-permute-start.19 = (f32[128,256]{1,0:T(8,128)S(1)}, f32[128,256]{1,0:T(8,128)S(1)}, u32[]{:S(2)}, u32[]{:S(2)}) collective-permute-start(f32[128,256]{1,0:T(8,128)S(1)} %add_add_fusion.1.z0_ref), channel_id=1, source_target_pairs={{0,4},{1,5},{2,6},{3,7},{4,8},{5,9},{6,10},{7,11},{8,12},{9,13},{1... | collective-permute-start | bytes 393224 | tf_op jit(solution)/shard_map/ppermute | solution.py:346
  208.1 8.5 %collective-permute-start.35 = (f32[256,256]{1,0:T(8,128)S(1)}, f32[256,256]{1,0:T(8,128)S(1)}, u32[]{:S(2)}, u32[]{:S(2)}) collective-permute-start(f32[256,256]{1,0:T(8,128)S(1)} %get-tuple-element.58.weights_ref.refs_1_), channel_id=1, source_target_pairs={{16,48},{48,80},{80,112},{112,16},{17,49},{49,81},{81,113},{113,17... | collective-permute-start | bytes 786440 | tf_op jit(solution)/shard_map/ppermute | solution.py:381
  210.0 6.5 %collective-permute-start.34 = (f32[256,256]{1,0:T(8,128)S(1)}, f32[256,256]{1,0:T(8,128)S(1)}, u32[]{:S(2)}, u32[]{:S(2)}) collective-permute-start(f32[256,256]{1,0:T(8,128)S(1)} %get-tuple-element.58.weights_ref.refs_1_), channel_id=1, source_target_pairs={{16,32},{48,64},{80,96},{112,0},{17,33},{49,65},{81,97},{113,1},{1... | collective-permute-start | bytes 786440 | tf_op jit(solution)/shard_map/ppermute | solution.py:381
  211.6 5.0 %collective-permute-start.25 = (f32[256,256]{1,0:T(8,128)S(1)}, f32[256,256]{1,0:T(8,128)S(1)}, u32[]{:S(2)}, u32[]{:S(2)}) collective-permute-start(f32[256,256]{1,0:T(8,128)S(1)} %get-tuple-element.58.weights_ref.refs_1_), channel_id=1, source_target_pairs={{0,16},{16,0},{32,48},{48,32},{64,80},{80,64},{96,112},{112,96},{1... | collective-permute-start | bytes 786440 | tf_op jit(solution)/shard_map/ppermute | solution.py:341
  227.9 32.8 %collective-permute-start.37 = (f32[1600,128]{1,0:T(8,128)S(1)}, f32[1600,128]{1,0:T(8,128)S(1)}, u32[]{:S(2)}, u32[]{:S(2)}) collective-permute-start(f32[1600,128]{1,0:T(8,128)S(1)} %get-tuple-element.73), channel_id=1, source_target_pairs={{0,16},{16,0},{32,48},{48,32},{64,80},{80,64},{96,112},{112,96},{1... | collective-permute-start | bytes 2457608 | tf_op jit(solution)/shard_map/ppermute | solution.py:341
  232.8 28.0 %collective-permute-start.36 = (f32[1600,128]{1,0:T(8,128)S(1)}, f32[1600,128]{1,0:T(8,128)S(1)}, u32[]{:S(2)}, u32[]{:S(2)}) collective-permute-start(f32[1600,128]{1,0:T(8,128)S(1)} %get-tuple-element.72), channel_id=1, source_target_pairs={{0,16},{16,0},{32,48},{48,32},{64,80},{80,64},{96,112},{112,96},{1... | collective-permute-start | bytes 2457608 | tf_op jit(solution)/shard_map/ppermute | solution.py:341
  238.1 5.9 %collective-permute-start.29 = (f32[128,256]{1,0:T(8,128)S(1)}, f32[128,256]{1,0:T(8,128)S(1)}, u32[]{:S(2)}, u32[]{:S(2)}) collective-permute-start(f32[128,256]{1,0:T(8,128)S(1)} %add.155), channel_id=1, source_target_pairs={{0,2},{1,3},{2,0},{3,1},{4,6},{5,7},{6,4},{7,5},{8,10},{9,11},{10,... | collective-permute-start | bytes 393224 | tf_op jit(solution)/shard_map/ppermute | solution.py:345
  239.4 8.0 %collective-permute-start.28 = (f32[128,256]{1,0:T(8,128)S(1)}, f32[128,256]{1,0:T(8,128)S(1)}, u32[]{:S(2)}, u32[]{:S(2)}) collective-permute-start(f32[128,256]{1,0:T(8,128)S(1)} %add.155), channel_id=1, source_target_pairs={{0,1},{1,2},{2,3},{3,0},{4,5},{5,6},{6,7},{7,4},{8,9},{9,10},{10,1... | collective-permute-start | bytes 393224 | tf_op jit(solution)/shard_map/ppermute | solution.py:345
  240.9 8.8 %collective-permute-start.24 = (f32[128,128]{1,0:T(8,128)S(1)}, f32[128,128]{1,0:T(8,128)S(1)}, u32[]{:S(2)}, u32[]{:S(2)}) collective-permute-start(f32[128,128]{1,0:T(8,128)S(1)} %get-tuple-element.60), channel_id=1, source_target_pairs={{0,16},{16,32},{32,48},{48,64},{64,80},{80,96},{96,112},{112,0},{1... | collective-permute-start | bytes 196616 | tf_op jit(solution)/shard_map/ppermute | solution.py:383
  248.1 5.3 %collective-permute-start.32 = (f32[128,256]{1,0:T(8,128)S(1)}, f32[128,256]{1,0:T(8,128)S(1)}, u32[]{:S(2)}, u32[]{:S(2)}) collective-permute-start(f32[128,256]{1,0:T(8,128)S(1)} %add_add_fusion.z0_ref), channel_id=1, source_target_pairs={{0,8},{1,9},{2,10},{3,11},{4,12},{5,13},{6,14},{7,15},{8,0},{9,1},... | collective-permute-start | bytes 393224 | tf_op jit(solution)/shard_map/ppermute | solution.py:346
  249.7 7.4 %collective-permute-start.31 = (f32[128,256]{1,0:T(8,128)S(1)}, f32[128,256]{1,0:T(8,128)S(1)}, u32[]{:S(2)}, u32[]{:S(2)}) collective-permute-start(f32[128,256]{1,0:T(8,128)S(1)} %add_add_fusion.z0_ref), channel_id=1, source_target_pairs={{0,4},{1,5},{2,6},{3,7},{4,8},{5,9},{6,10},{7,11},{8,12},{9,13},{1... | collective-permute-start | bytes 393224 | tf_op jit(solution)/shard_map/ppermute | solution.py:346
  (22 other events, 292.2 us)

commit v2 on v1

v2 whole, which is shorter than its diff:
```python
import jax
import jax.numpy as jnp
from jax import lax
from jax.experimental import pallas as pl
from jax.experimental.pallas import tpu as pltpu
from jax.sharding import PartitionSpec as P

ROUNDS = 4
BLOCK = 128
PAIR = 256
SIDE = 4
ROWS = 16
COLS = 8
F32 = jnp.float32
VMEM_LIMIT = 48 * 1024 * 1024

TURN_CORE = [(c, c ^ 1) for c in range(COLS)]
NEXT_SLOT = [(c, (c + 1) % COLS) for c in range(COLS)]
CHIPS_ON = [[(c, (c + 2 * k) % COLS) for c in range(COLS)] for k in range(SIDE)]
ODD_TO_EVEN = [(c, (c + 1) % COLS) for c in range(1, COLS, 2)]
EVEN_TO_ODD = [(c, c + 1) for c in range(0, COLS, 2)]
ALONG_X = [[(r, r - r % SIDE + (r + k) % SIDE) for r in range(ROWS)] for k in range(1, SIDE)]
ALONG_Z = [[(r, (r + SIDE * k) % ROWS) for r in range(ROWS)] for k in range(1, SIDE)]


def mm(left, right):
    return jnp.dot(left, right, precision=lax.Precision.HIGHEST, preferred_element_type=F32)


def mm_t(left, right):
    return lax.dot_general(
        left, right, (((0,), (0,)), ((), ())), precision=lax.Precision.HIGHEST, preferred_element_type=F32
    )


def call(kernel, grid, in_specs, out_specs, out_shape, scalars=0, scratch=(), flops=0, nbytes=0):
    return pl.pallas_call(
        kernel,
        grid_spec=pltpu.PrefetchScalarGridSpec(
            num_scalar_prefetch=scalars,
            grid=grid,
            in_specs=in_specs,
            out_specs=out_specs,
            scratch_shapes=list(scratch),
        ),
        out_shape=out_shape,
        compiler_params=pltpu.CompilerParams(vmem_limit_bytes=VMEM_LIMIT),
        cost_estimate=pl.CostEstimate(flops=flops, bytes_accessed=nbytes, transcendentals=0),
    )


def shape(*dims):
    return jax.ShapeDtypeStruct(dims, F32)


def whole(*dims):
    return pl.BlockSpec(dims, lambda *_: (0,) * len(dims))


def pack_main_kernel(chip_ref, *refs):
    for x_ref, out_ref in zip(refs[:SIDE], refs[SIDE:]):
        out_ref[0, 0] = x_ref[:, :BLOCK]
        out_ref[0, 1] = x_ref[:, BLOCK:]


def pack_main(chip, x):
    rows = x.shape[0]

    def columns(k):
        return pl.BlockSpec((rows, PAIR), lambda j, c: (0, 2 * ((c[0] + k) % SIDE) + j))

    return call(
        pack_main_kernel,
        (2,),
        [columns(k) for k in range(SIDE)],
        [pl.BlockSpec((1, 2, rows, BLOCK), lambda j, c: (j, 0, 0, 0))] * SIDE,
        [shape(2, 2, rows, BLOCK)] * SIDE,
        scalars=1,
        nbytes=8 * SIDE * rows * 2 * PAIR,
    )(chip, *[x] * SIDE)


def pack_ahead_kernel(chip_ref, *refs):
    for x_ref, out_ref in zip(refs[:SIDE], refs[SIDE + 1:]):
        out_ref[0] = x_ref[:, :BLOCK]
        out_ref[1] = x_ref[:, BLOCK:]


def pack_ahead(chip, x, before):
    rows = x.shape[0]

    def columns(k):
        return pl.BlockSpec((rows, PAIR), lambda i, c: (0, (2 * ((c[0] + k) % SIDE) + COLS - 1) % COLS))

    return call(
        pack_ahead_kernel,
        (1,),
        [columns(k) for k in range(SIDE)] + [whole(*before.shape)],
        [whole(2, rows, BLOCK)] * SIDE,
        [shape(2, rows, BLOCK)] * SIDE,
        scalars=1,
        nbytes=8 * SIDE * rows * PAIR,
    )(chip, *[x] * SIDE, before)


def gram_kernel(x_ref, out_ref):
    paired = x_ref[...]
    out_ref[:, 0] = mm_t(paired, paired).reshape(ROWS, PAIR // ROWS, PAIR)


def row_grams(x):
    rows = x.shape[0]
    return call(
        gram_kernel,
        (COLS,),
        [pl.BlockSpec((rows, PAIR), lambda s: (0, s))],
        pl.BlockSpec((ROWS, 1, PAIR // ROWS, PAIR), lambda s: (0, s, 0, 0)),
        shape(ROWS, COLS, PAIR // ROWS, PAIR),
        flops=2 * 6 * COLS * rows * PAIR * PAIR,
        nbytes=4 * COLS * (rows * PAIR + PAIR * PAIR),
    )(x)


def rotation_of(gram, x_ref, r_ref):
    rows = lax.broadcasted_iota(jnp.int32, (PAIR, PAIR), 0)
    columns = lax.broadcasted_iota(jnp.int32, (PAIR, PAIR), 1)
    eye = (rows == columns).astype(F32)
    on_diagonal = gram * eye
    across = jnp.sum(on_diagonal, axis=0, keepdims=True)
    down = jnp.sum(on_diagonal, axis=1, keepdims=True)
    spread = across - down
    totals = across + down
    skew = gram * spread / (2.0 * spread * spread + 0.5 * totals * totals)
    square = mm(skew, skew)
    bound = jnp.max(jnp.sum(jnp.abs(square), axis=0))
    scale = 2.0 / (2.0 + bound)
    x_ref[...] = scale * (eye + skew)
    r_ref[...] = (1.0 - scale) * eye + scale * square

    def step(size):
        left = r_ref[...]
        x = x_ref[...]
        x_ref[...] = x + mm(x, left)
        r_ref[...] = mm(left, left)
        return size * size

    lax.while_loop(lambda size: size > 3e-4, step, bound / (2.0 + bound))
    x = x_ref[...]
    x = x + mm(x, eye - x + mm(skew, x))
    return 2.0 * x - eye


def first_cayley_kernel(gram_ref, weights_ref, x_ref, r_ref):
    weights_ref[...] = rotation_of(gram_ref[...], x_ref, r_ref)


def first_cayley(gram):
    return call(
        first_cayley_kernel,
        (1,),
        [whole(PAIR, PAIR)],
        whole(PAIR, PAIR),
        shape(PAIR, PAIR),
        scratch=[pltpu.VMEM((PAIR, PAIR), F32)] * 2,
        flops=2 * 6 * 8 * PAIR**3,
        nbytes=8 * PAIR * PAIR,
    )(gram)


def cayley_kernel(core_ref, up_ref, low_ref, z0_ref, z1_ref, z2_ref, z3_ref, wm_ref, wo_ref, weights_ref, gram_ref, x_ref, r_ref):
    mixed = (z0_ref[...] + z1_ref[...]) + (z2_ref[...] + z3_ref[...])
    before = jnp.where(core_ref[0] == 0, wm_ref[:, BLOCK:], wo_ref[:, BLOCK:])
    cross = mm(mixed, before)
    gram_ref[:BLOCK, :BLOCK] = up_ref[...]
    gram_ref[:BLOCK, BLOCK:] = cross
    gram_ref[BLOCK:, :BLOCK] = cross.T
    gram_ref[BLOCK:, BLOCK:] = low_ref[...]
    weights_ref[...] = rotation_of(gram_ref[...], x_ref, r_ref)


def cayley(core, up, low, parts, weights_m, weights_o):
    return call(
        cayley_kernel,
        (1,),
        [whole(BLOCK, BLOCK)] * 2 + [whole(BLOCK, PAIR)] * 4 + [whole(PAIR, PAIR)] * 2,
        [whole(PAIR, PAIR)] * 2,
        [shape(PAIR, PAIR)] * 2,
        scalars=1,
        scratch=[pltpu.VMEM((PAIR, PAIR), F32)] * 2,
        flops=2 * 6 * 8 * PAIR**3,
        nbytes=16 * PAIR * PAIR,
    )(core, up, low, *parts, weights_m, weights_o)


def project_kernel(gram_ref, weights_ref, up_ref, low_ref):
    weights = weights_ref[...]
    turned = mm(gram_ref[...], weights)
    up_ref[...] = mm_t(weights[:, :BLOCK], turned[:, :BLOCK])
    low_ref[...] = mm_t(weights[:, BLOCK:], turned[:, BLOCK:])


def project(gram, weights):
    return call(
        project_kernel,
        (1,),
        [whole(PAIR, PAIR)] * 2,
        [whole(BLOCK, BLOCK)] * 2,
        [shape(BLOCK, BLOCK)] * 2,
        flops=2 * 6 * 2 * PAIR**3,
        nbytes=12 * PAIR * PAIR,
    )(gram, weights)


def scale_kernel(rows, gram_ref, weights_ref, out_ref):
    weights = weights_ref[...]
    squares = jnp.sum(weights * mm(gram_ref[...], weights), axis=0, keepdims=True)
    out_ref[...] = jnp.sqrt(squares / rows)


def scale_of(gram, weights, rows):
    return call(
        lambda *refs: scale_kernel(rows, *refs),
        (1,),
        [whole(PAIR, PAIR)] * 2,
        whole(1, PAIR),
        shape(1, PAIR),
        flops=2 * 6 * PAIR**3,
        nbytes=8 * PAIR * PAIR,
    )(gram, weights)


def turn(core_ref, own_ref, other_ref, pair0, pair1, pair_m, rows, out0_ref, out1_ref, keep_ref, send_ref):
    @pl.when(pl.program_id(0) == 0)
    def _():
        keep_ref[...] = jnp.zeros_like(keep_ref)
        send_ref[...] = jnp.zeros_like(send_ref)

    first = core_ref[0] == 0
    up0 = mm(pair0, jnp.where(first, own_ref[:, :BLOCK], other_ref[:, :BLOCK]))
    up1 = mm(pair1, jnp.where(first, other_ref[:, :BLOCK], own_ref[:, :BLOCK]))
    out0_ref[0] = up0
    out1_ref[0] = up1
    z0 = mm_t(up0[:rows], pair_m[:rows])
    z1 = mm_t(up1[:rows], pair0[:rows])
    keep_ref[...] += jnp.where(first, z0, z1)
    send_ref[...] += jnp.where(first, z1, z0)


def halves(up_ref, low_ref):
    return jnp.concatenate([up_ref[0], low_ref[0]], axis=1)


def main_kernel(rows, core_ref, own_ref, other_ref, u0_ref, l0_ref, u1_ref, l1_ref, um_ref, lm_ref, *outs):
    turn(core_ref, own_ref, other_ref, halves(u0_ref, l0_ref), halves(u1_ref, l1_ref), halves(um_ref, lm_ref), rows, *outs)


def rotate_main(core, own, other, state, rows):
    step = state[0].shape[1]
    tile = pl.BlockSpec((1, step, BLOCK), lambda i, c: (i, 0, 0))
    return call(
        lambda *refs: main_kernel(rows, *refs),
        (SIDE,),
        [whole(PAIR, PAIR)] * 2 + [tile] * 6,
        [tile] * 2 + [whole(BLOCK, PAIR)] * 2,
        [shape(SIDE, step, BLOCK)] * 2 + [shape(BLOCK, PAIR)] * 2,
        scalars=1,
        flops=2 * 6 * SIDE * step * 4 * BLOCK * PAIR,
        nbytes=4 * 8 * SIDE * step * BLOCK,
    )(core, own, other, *state)


def start_pair(info_ref, step, slot, up, low):
    column = slot * PAIR - info_ref[2] - (step - up.shape[0]) * pl.program_id(0)
    rows = lax.broadcasted_iota(jnp.int32, (step - up.shape[0], PAIR), 0)
    columns = lax.broadcasted_iota(jnp.int32, (step - up.shape[0], PAIR), 1)
    basis = (rows == columns + column).astype(F32)
    return jnp.concatenate([jnp.concatenate([up, low], axis=1), basis], axis=0)


def start_main_kernel(step, info_ref, own_ref, other_ref, main_ref, ahead_ref, *outs):
    slot = 2 * info_ref[1]
    pair0 = start_pair(info_ref, step, slot, main_ref[0, 0, 0], main_ref[0, 0, 1])
    pair1 = start_pair(info_ref, step, slot + 1, main_ref[0, 1, 0], main_ref[0, 1, 1])
    pair_m = jnp.concatenate([ahead_ref[0, 0], ahead_ref[0, 1]], axis=1)
    turn(info_ref, own_ref, other_ref, pair0, pair1, pair_m, pair_m.shape[0], *outs)


def start_ahead_kernel(step, info_ref, weights_ref, other_ref, own_ref, low_in_ref, main_ref, ahead_ref, *outs):
    slot = 2 * info_ref[1]
    pair0 = start_pair(info_ref, step, slot, main_ref[0, 0, 0], main_ref[0, 0, 1])
    pair_m = start_pair(info_ref, step, (slot + COLS - 1) % COLS, ahead_ref[0, 0], ahead_ref[0, 1])
    turn_ahead(info_ref, weights_ref, other_ref, own_ref, pair0, pair_m, *outs)


def start_specs(rows, step):
    main = pl.BlockSpec((1, 2, 2, rows, BLOCK), lambda i, c: (lax.rem(c[1] + SIDE - i, SIDE), 0, 0, 0, 0))
    ahead = pl.BlockSpec((1, 2, rows, BLOCK), lambda i, c: (lax.rem(c[1] + SIDE - i, SIDE), 0, 0, 0))
    return main, ahead, pl.BlockSpec((1, step, BLOCK), lambda i, c: (i, 0, 0))


def start_main(info, own, other, main, ahead, step):
    rows = main.shape[3]
    main_spec, ahead_spec, tile = start_specs(rows, step)
    return call(
        lambda *refs: start_main_kernel(step, *refs),
        (SIDE,),
        [whole(PAIR, PAIR)] * 2 + [main_spec, ahead_spec],
        [tile] * 2 + [whole(BLOCK, PAIR)] * 2,
        [shape(SIDE, step, BLOCK)] * 2 + [shape(BLOCK, PAIR)] * 2,
        scalars=1,
        flops=2 * 6 * SIDE * step * 4 * BLOCK * PAIR,
        nbytes=4 * 8 * SIDE * step * BLOCK,
    )(info, own, other, main, ahead)


def turn_ahead(core_ref, weights_ref, other_ref, own_ref, pair0, pair_m, up_ref, low_ref, pass_ref):
    turned = mm(pair_m, weights_ref[...])
    up_ref[0] = turned[:, :BLOCK]
    low_ref[0] = turned[:, BLOCK:]
    pass_ref[0] = mm(pair0, jnp.where(core_ref[0] == 0, own_ref[:, BLOCK:], other_ref[:, BLOCK:]))


def ahead_kernel(core_ref, weights_ref, other_ref, own_ref, low_in_ref, u0_ref, l0_ref, um_ref, lm_ref, *outs):
    turn_ahead(core_ref, weights_ref, other_ref, own_ref, halves(u0_ref, l0_ref), halves(um_ref, lm_ref), *outs)


def ahead_call(kernel, step, specs, args):
    tile = pl.BlockSpec((1, step, BLOCK), lambda i, c: (i, 0, 0))
    return call(
        kernel,
        (SIDE,),
        [whole(PAIR, PAIR)] * 3 + [whole(BLOCK, BLOCK)] + specs,
        [tile] * 3,
        [shape(SIDE, step, BLOCK)] * 3,
        scalars=1,
        flops=2 * 6 * SIDE * step * 3 * BLOCK * PAIR,
        nbytes=4 * 7 * SIDE * step * BLOCK,
    )(*args)


def rotate_ahead(core, weights, other, own, low, blocks):
    step = blocks[0].shape[1]
    tile = pl.BlockSpec((1, step, BLOCK), lambda i, c: (i, 0, 0))
    return ahead_call(ahead_kernel, step, [tile] * 4, (core, weights, other, own, low, *blocks))


def start_ahead(info, weights, other, own, low, main, ahead, step):
    specs = list(start_specs(main.shape[3], step)[:2])
    kernel = lambda *refs: start_ahead_kernel(step, *refs)
    return ahead_call(kernel, step, specs, (info, weights, other, own, low, main, ahead))


def last_ahead_kernel(core_ref, weights_ref, other_ref, own_ref, before_ref, u0_ref, l0_ref, um_ref, lm_ref,
                      out0_ref, out1_ref, keep_up_ref, keep_low_ref, send_up_ref, send_low_ref):
    first = core_ref[0] == 0
    low0 = mm(halves(um_ref, lm_ref), weights_ref[:, BLOCK:])
    low1 = mm(halves(u0_ref, l0_ref), jnp.where(first, own_ref[:, BLOCK:], other_ref[:, BLOCK:]))
    up0 = out0_ref[0]
    up1 = out1_ref[0]
    keep_up_ref[0] = jnp.where(first, up0, up1)
    send_up_ref[0] = jnp.where(first, up1, up0)
    keep_low_ref[0] = jnp.where(first, low0, low1)
    send_low_ref[0] = jnp.where(first, low1, low0)


def rotate_last_ahead(core, weights, other, own, before, blocks):
    step = blocks[0].shape[1]
    tile = pl.BlockSpec((1, step, BLOCK), lambda i, c: (i, 0, 0))
    return call(
        last_ahead_kernel,
        (SIDE,),
        [whole(PAIR, PAIR)] * 3 + [whole(*before.shape)] + [tile] * 6,
        [tile] * 4,
        [shape(SIDE, step, BLOCK)] * 4,
        scalars=1,
        flops=2 * 6 * SIDE * step * 2 * PAIR * BLOCK,
        nbytes=4 * 10 * SIDE * step * BLOCK,
    )(core, weights, other, own, before, *blocks)


def final_kernel(rows, core_ref, weights_ref, ku_ref, kl_ref, ru_ref, rl_ref, out_ref, frame_ref):
    weights = weights_ref[...]
    first = core_ref[0] == 0
    mine = mm(halves(ku_ref, kl_ref), weights)
    theirs = mm(halves(ru_ref, rl_ref), weights)
    for k, turned in enumerate((jnp.where(first, mine, theirs), jnp.where(first, theirs, mine))):
        out_ref[k] = turned[:rows]
        frame_ref[k] = turned[rows:]


def rotate_final(core, weights, blocks, rows):
    step = blocks[0].shape[1]
    tile = pl.BlockSpec((1, step, BLOCK), lambda i, c: (i, 0, 0))
    share = step - rows
    return call(
        lambda *refs: final_kernel(rows, *refs),
        (SIDE,),
        [whole(PAIR, PAIR)] + [tile] * 4,
        [pl.BlockSpec((2, rows, PAIR), lambda i, c: (i, 0, 0)), pl.BlockSpec((2, share, PAIR), lambda i, c: (0, i, 0))],
        [shape(COLS, rows, PAIR), shape(2, SIDE * share, PAIR)],
        scalars=1,
        flops=2 * 6 * 2 * SIDE * step * PAIR * PAIR,
        nbytes=4 * 4 * SIDE * step * PAIR,
    )(core, weights, *blocks)


def swap_core(value):
    return lax.ppermute(value, "cols", TURN_CORE)


def sum_over_rows(value):
    value = value + sum(lax.ppermute(value, "rows", pairs) for pairs in ALONG_X)
    return [value] + [lax.ppermute(value, "rows", pairs) for pairs in ALONG_Z]


def spread_over_rows(share):
    copies = jnp.broadcast_to(share[None], (ROWS,) + share.shape)
    return lax.all_to_all(copies, "rows", 0, 0, tiled=True).reshape(PAIR, PAIR)


def body(sensitivity):
    x = sensitivity[0]
    rows = x.shape[0]
    column = lax.axis_index("cols")
    parity = column % 2
    basis_rows = x.shape[1] // ROWS // 2
    basis_at = (lax.axis_index("rows") * 2 + parity) * basis_rows
    core = parity.astype(jnp.int32).reshape(1)
    chip = (column // 2).astype(jnp.int32).reshape(1)
    info = jnp.stack([parity, column // 2, basis_at]).astype(jnp.int32)
    step = rows + basis_rows // SIDE

    packed = pack_main(chip, x)
    main = [packed[0]] + [lax.ppermute(packed[k], "cols", CHIPS_ON[k]) for k in range(1, SIDE)]

    parts = lax.all_to_all(row_grams(x), "rows", 0, 0, tiled=True)
    parts = lax.all_to_all(jnp.sum(parts, axis=0), "cols", 0, 0, tiled=True)
    share = jnp.sum(parts, axis=0)

    packed = pack_ahead(chip, x, share)
    ahead = [packed[0]] + [lax.ppermute(packed[k], "cols", CHIPS_ON[k]) for k in range(1, SIDE)]
    gram = spread_over_rows(share)
    weights = first_cayley(gram)

    main = jnp.stack(main)
    ahead = jnp.stack(ahead)
    state = None
    for sweep_round in range(ROUNDS - 1):
        other = swap_core(weights)
        weights_m = lax.ppermute(weights, "cols", ODD_TO_EVEN)
        weights_m = weights_m + lax.ppermute(weights_m, "cols", EVEN_TO_ODD)
        up, low = project(gram, weights)
        low = lax.ppermute(low, "cols", NEXT_SLOT)
        if state is None:
            up0, up1, keep, send = start_main(info, weights, other, main, ahead, step)
        else:
            up0, up1, keep, send = rotate_main(core, weights, other, state, rows)
        parts = sum_over_rows(keep + swap_core(send))
        if sweep_round == ROUNDS - 2:
            blocks = (state[0], state[1], state[4], state[5], up0, up1)
            held = rotate_last_ahead(core, weights_m, other, weights, parts[0], blocks)
            held = [held[0], held[1], swap_core(held[2]), swap_core(held[3])]
        else:
            if state is None:
                up_m, low0, low1 = start_ahead(info, weights_m, other, weights, low, main, ahead, step)
            else:
                blocks = (state[0], state[1], state[4], state[5])
                up_m, low0, low1 = rotate_ahead(core, weights_m, other, weights, low, blocks)
            state = [up0, low0, up1, low1, up_m, lax.ppermute(low1, "cols", CHIPS_ON[1])]
        weights, gram = cayley(core, up, low, parts, weights_m, other)

    column_scale = scale_of(gram, weights, float(rows * COLS * ROWS)).reshape(PAIR)
    rotated, frame = rotate_final(core, weights, held, rows)
    return rotated, frame.reshape(2 * basis_rows, PAIR), column_scale


def solution(mesh):
    in_specs = (P("cols", "rows", None),)
    out_specs = (P(None, "rows", "cols"), P("rows", "cols"), P("cols"))
    return jax.shard_map(body, mesh=mesh, in_specs=in_specs, out_specs=out_specs, check_vma=False)
```

time: 266 us -> 233 us (0.88)
  waiting for transfers between devices: 124 us -> 65.5 us
  blocking collectives: 0 us -> 11.7 us
  Pallas kernels: 58.6 us -> 69.8 us
  starting transfers between devices: 63.7 us -> 71.6 us
  local copies, waits for them, and re-layouts: 11.3 us -> 7.22 us
    all_to_all x3 -> x2, waiting for transfers between devices: 65.2 us -> 23.7 us  [the longest x1 21.6 us: body(): parts = lax.all_to_all(row_grams(x), 'rows', 0, 0, tiled=True)]
    ppermute x8 -> x14, waiting for transfers between devices: 27.9 us -> 5.34 us  [the longest x3 4.58 us: body(): weights_m = lax.ppermute(weights, 'cols', ODD_TO_EVEN)]
    ppermute x9, waiting for transfers between devices: 8.95 us -> 24.8 us  [sum_over_rows(): return [value] + [lax.ppermute(value, 'rows', pairs) for pairs in ALONG_Z]]
    ppermute x8 -> x14, starting transfers between devices: 13.1 us -> 27.2 us  [the longest x3 11.8 us: body(): weights_m = lax.ppermute(weights, 'cols', ODD_TO_EVEN)]
    all_to_all x0 -> x1, blocking collectives: none -> 11.7 us  [body(): parts = lax.all_to_all(jnp.sum(parts, axis=0), 'cols', 0, 0, tiled=True)]
    pallas_call x9 -> x10, Pallas kernels: 43.3 us -> 52.7 us  [the longest x2 14.6 us: rotate_main(): call(lambda *refs: main_kernel(rows, *refs), (SIDE,), [whole(PAIR, PAIR)]...]
    ppermute x9 -> x8, starting transfers between devices: 15.3 us -> 8.78 us  [swap_core(): return lax.ppermute(value, 'cols', TURN_CORE)]
    ppermute x9 -> x8, waiting for transfers between devices: 6.17 us -> 0.02 us  [swap_core(): return lax.ppermute(value, 'cols', TURN_CORE)]
  transfers between devices with their start and end apart: 41 -> 45, of which waited for: 23 -> 19; matrix products, arithmetic and copies ran while one was open for 4% -> 3% of each run, Pallas kernels for 6% -> 23%
where the time goes in v2:
time: 233 us
  starting transfers between devices  71.6 us (31%)
  Pallas kernels  69.8 us (30%)
  waiting for transfers between devices  65.5 us (28%)
  blocking collectives  11.7 us (5%)
  local copies, waits for them, and re-layouts  7.22 us (3%)
  other arithmetic  5.81 us (2%)
    ppermute x9, waiting for transfers between devices, sum_over_rows(): return [value] + [lax.ppermute(value, 'rows', pairs) for pairs in ALONG_Z]  24.8 us
    all_to_all x1, waiting for transfers between devices, body(): parts = lax.all_to_all(row_grams(x), 'rows', 0, 0, tiled=True)  21.6 us
    pallas_call x2, Pallas kernels, rotate_main(): call(lambda *refs: main_kernel(rows, *refs), (SIDE,), [whole(PAIR, PAIR)]...  14.6 us
    ppermute x3, starting transfers between devices, body(): weights_m = lax.ppermute(weights, 'cols', ODD_TO_EVEN)  11.8 us
    all_to_all x1, blocking collectives, body(): parts = lax.all_to_all(jnp.sum(parts, axis=0), 'cols', 0, 0, tiled=True)  11.7 us
    ppermute x9, waiting for transfers between devices, sum_over_rows(): lax.ppermute(value, 'rows', pairs)  11.6 us
    ppermute x9, starting transfers between devices, sum_over_rows(): return [value] + [lax.ppermute(value, 'rows', pairs) for pairs in ALONG_Z]  10.4 us
    pallas_call x2, Pallas kernels, ahead_call(): call(kernel, (SIDE,), [whole(PAIR, PAIR)] * 3 + [whole(BLOCK, BLOCK)] + s...  10.1 us
  transfers between devices with their start and end apart: 45, of which 19 were waited for; matrix products, arithmetic and copies ran while one was open for 3% of the time, Pallas kernels for 23%

profile of v2, /device:TPU:1, one launch (start us, length us, event | category | flops | bytes accessed | tf_op | source)
XLA Modules:
  0.0 232.7 jit_solution(12246057451706113641)
XLA Ops:
  2.5 6.2 %shard_map.38 = f32[16,8,16,256]{3,2,1,0:T(8,128)} custom-call(f32[384,2048]{1,0:T(8,128)S(1)} %bitcast.19), custom_call_target="tpu_custom_call" | custom-call | flops 2415919104 | bytes 5242880 | tf_op jit(solution)/shard_map/pallas_call | solution.py:113
  8.7 8.5 %all-to-all-start = ((f32[16,8,16,256]{3,2,1,0:T(8,128)}), f32[16,8,16,256]{3,2,1,0:T(8,128)}, u32[]{:S(2)}, u32[]{:S(2)}) async-start(f32[16,8,16,256]{3,2,1,0:T(8,128)} %shard_map.38), calls=%async_computation | async-start | bytes 4194304 | tf_op jit(solution)/shard_map/all_to_all | solution.py:436
  17.2 3.0 %shard_map.41 = (f32[2,2,384,128]{3,2,1,0:T(8,128)S(1)}, f32[2,2,384,128]{3,2,1,0:T(8,128)}, f32[2,2,384,128]{3,2,1,0:T(8,128)}, f32[2,2,384,128]{3,2,1,0:T(8,128)}) custom-call(s32[1]{0:T(128)} %bitcast.3.chip_ref, f32[384,2048]{1,0:T(8,128)} %bitcast.15, f32[384,2048]{1,0:T(8,128)} %bitcast.16, f32[384,2048]{1,0:T(8,128)} %bitcast.17, f32[384,2048]{1,0:T(8,128)} %bitcast.18), custom_call_target="tpu_custom_call" | custom-call | bytes 6291456 | tf_op jit(solution)/shard_map/pallas_call | solution.py:72
  26.2 21.6 %all-to-all-done = f32[16,8,16,256]{3,2,1,0:T(8,128)} async-done(((f32[16,8,16,256]{3,2,1,0:T(8,128)}), f32[16,8,16,256]{3,2,1,0:T(8,128)}, u32[]{:S(2)}, u32[]{:S(2)}) %all-to-all-start) | async-done | bytes 2097184 | tf_op jit(solution)/shard_map/all_to_all | solution.py:436
  49.6 11.7 %all_to_all.15 = f32[8,16,256]{2,1,0:T(8,128)S(1)} all-to-all(f32[8,16,256]{2,1,0:T(8,128)S(1)} %reduce_sum.18), channel_id=1, replica_groups=mesh['cols'=8,'rows'=16] {'cols'}, dimensions={0} | all-to-all | bytes 262144 | tf_op jit(solution)/shard_map/all_to_all | solution.py:437
  62.0 6.7 %all-to-all-start.2 = ((f32[16,16,256]{2,1,0:T(8,128)}), f32[16,16,256]{2,1,0:T(8,128)}, u32[]{:S(2)}, u32[]{:S(2)}) async-start(f32[16,16,256]{2,1,0:T(8,128)} %broadcast_in_dim.2), calls=%async_computation.2 | async-start | bytes 524288 | tf_op jit(solution)/shard_map/all_to_all | solution.py:418
  76.3 3.9 %shard_map.39.weights_ref.refs_1_.refs_3_ = f32[256,256]{1,0:T(8,128)S(1)} custom-call(f32[256,256]{1,0:T(8,128)} %bitcast.2.gram_ref), custom_call_target="tpu_custom_call" | custom-call | flops 1610612736 | bytes 524288 | tf_op jit(solution)/shard_map/pallas_call | solution.py:158
  80.3 5.7 %collective-permute-start.15 = (f32[256,256]{1,0:T(8,128)S(1)}, f32[256,256]{1,0:T(8,128)S(1)}, u32[]{:S(2)}, u32[]{:S(2)}) collective-permute-start(f32[256,256]{1,0:T(8,128)S(1)} %shard_map.39.weights_ref.refs_1_.refs_3_), channel_id=1, source_target_pairs={{16,32},{48,64},{80,96},{112,0},{17,33},{49,65},{81,97},{113,1},{1... | collective-permute-start | bytes 786440 | tf_op jit(solution)/shard_map/ppermute | solution.py:450
  86.1 3.6 %pad_maximum_fusion.refs_3_.refs_5_ = f32[4,2,2,384,128]{4,3,2,1,0:T(8,128)} fusion(f32[1,2,2,384,128]{4,3,2,1,0:T(8,128)} %bitcast.8, f32[1,2,2,384,128]{4,3,2,1,0:T(8,128)} %bitcast.7, f32[1,2,2,384,128]{4,3,2,1,0:T(8,128)} %bitcast.6, f32[1,2,2,384,128]{4,3,2,1,0:T(8,128)S(1)} %bitcast.24), kind=kLoop, calls=%fused_computation | loop fusion | flops 2359296 | bytes 6291456 | tf_op jit(solution)/shard_map/stack | solution.py:445
  93.2 7.9 %shard_map.43 = (f32[4,400,128]{2,1,0:T(8,128)S(1)}, f32[4,400,128]{2,1,0:T(8,128)S(1)}, f32[128,256]{1,0:T(8,128)S(1)}, f32[128,256]{1,0:T(8,128)S(1)}) custom-call(s32[3]{0:T(128)S(1)} %pad_add_fusion.refs_0_, f32[256,256]{1,0:T(8,128)S(1)} %shard_map.39.weights_ref.refs_1_.refs_3_, f32[256,256]{1,0:T(8,128)S(1)} %collective-permute-done.1.refs_2_.wo_ref, ...), custom_call_target="tpu_custom_call" | custom-call | flops 2516582400 | bytes 6553600 | tf_op jit(solution)/shard_map/pallas_call | solution.py:304
  109.6 5.6 %shard_map.46 = (f32[4,400,128]{2,1,0:T(8,128)S(1)}, f32[4,400,128]{2,1,0:T(8,128)S(1)}, f32[4,400,128]{2,1,0:T(8,128)S(1)}) custom-call(s32[3]{0:T(128)S(1)} %pad_add_fusion.refs_0_, f32[256,256]{1,0:T(8,128)S(1)} %add.59.wm_ref.refs_1_, f32[256,256]{1,0:T(8,128)S(1)} %collective-permute-done.1.refs_2_.wo_ref, ...), custom_call_target="tpu_custom_call" | custom-call | flops 1887436800 | bytes 5734400 | tf_op jit(solution)/shard_map/pallas_call | solution.py:329
  123.7 2.9 %collective-permute-done.13.z2_ref = f32[128,256]{1,0:T(8,128)S(1)} collective-permute-done((f32[128,256]{1,0:T(8,128)S(1)}, f32[128,256]{1,0:T(8,128)S(1)}, u32[]{:S(2)}, u32[]{:S(2)}) %collective-permute-start.13) | collective-permute-done | bytes 131104 | tf_op jit(solution)/shard_map/ppermute | solution.py:413
  126.6 3.9 %collective-permute-done.12.z1_ref = f32[128,256]{1,0:T(8,128)S(1)} collective-permute-done((f32[128,256]{1,0:T(8,128)S(1)}, f32[128,256]{1,0:T(8,128)S(1)}, u32[]{:S(2)}, u32[]{:S(2)}) %collective-permute-start.12) | collective-permute-done | bytes 131104 | tf_op jit(solution)/shard_map/ppermute | solution.py:413
  130.5 2.7 %shard_map.44 = (f32[256,256]{1,0:T(8,128)S(1)}, f32[256,256]{1,0:T(8,128)S(1)}) custom-call(s32[1]{0:T(128)} %bitcast.core_ref.refs_0_, f32[128,128]{1,0:T(8,128)S(1)} %get-tuple-element.47.up_ref, f32[128,128]{1,0:T(8,128)S(1)} %collective-permute-done.low_ref.refs_4_, f32[128,256]{1,0:T(8,128)S(1)} %add_add_fusion.2.z0_ref, ...), custom_call_target="tpu_custom_call" | custom-call | flops 1610612736 | bytes 1048576 | tf_op jit(solution)/shard_map/pallas_call | solution.py:182
  133.2 3.2 %collective-permute-start.27 = (f32[256,256]{1,0:T(8,128)S(1)}, f32[256,256]{1,0:T(8,128)S(1)}, u32[]{:S(2)}, u32[]{:S(2)}) collective-permute-start(f32[256,256]{1,0:T(8,128)S(1)} %get-tuple-element.60.weights_ref.refs_1_.own_ref), channel_id=1, source_target_pairs={{16,32},{48,64},{80,96},{112,0},{17,33},{49,65},{81,97},{113,1},{1... | collective-permute-start | bytes 786440 | tf_op jit(solution)/shard_map/ppermute | solution.py:450
  136.5 3.2 %collective-permute-done.27 = f32[256,256]{1,0:T(8,128)S(1)} collective-permute-done((f32[256,256]{1,0:T(8,128)S(1)}, f32[256,256]{1,0:T(8,128)S(1)}, u32[]{:S(2)}, u32[]{:S(2)}) %collective-permute-start.27) | collective-permute-done | bytes 262176 | tf_op jit(solution)/shard_map/ppermute | solution.py:450
  141.9 7.4 %shard_map.47 = (f32[4,400,128]{2,1,0:T(8,128)S(1)}, f32[4,400,128]{2,1,0:T(8,128)S(1)}, f32[128,256]{1,0:T(8,128)S(1)}, f32[128,256]{1,0:T(8,128)S(1)}) custom-call(s32[1]{0:T(128)} %bitcast.core_ref.refs_0_, f32[256,256]{1,0:T(8,128)S(1)} %get-tuple-element.60.weights_ref.refs_1_.own_ref, f32[256,256]{1,0:T(8,128)S(1)} %collective-permute-done.18.refs_2_.wo_ref.other_ref, ...), custom_call_target="tpu_custom_call" | custom-call | flops 2516582400 | bytes 6553600 | tf_op jit(solution)/shard_map/pallas_call | solution.py:260
  149.3 3.0 %collective-permute-start.20 = (f32[128,256]{1,0:T(8,128)S(1)}, f32[128,256]{1,0:T(8,128)S(1)}, u32[]{:S(2)}, u32[]{:S(2)}) collective-permute-start(f32[128,256]{1,0:T(8,128)S(1)} %get-tuple-element.69), channel_id=1, source_target_pairs={{0,16},{16,0},{32,48},{48,32},{64,80},{80,64},{96,112},{112,96},{1... | collective-permute-start | bytes 393224 | tf_op jit(solution)/shard_map/ppermute | solution.py:408
  155.7 4.5 %shard_map.50 = (f32[4,400,128]{2,1,0:T(8,128)S(1)}, f32[4,400,128]{2,1,0:T(8,128)S(1)}, f32[4,400,128]{2,1,0:T(8,128)S(1)}) custom-call(s32[1]{0:T(128)} %bitcast.core_ref.refs_0_, f32[256,256]{1,0:T(8,128)S(1)} %add.64.wm_ref.weights_ref, f32[256,256]{1,0:T(8,128)S(1)} %collective-permute-done.18.refs_2_.wo_ref.other_ref, ...), custom_call_target="tpu_custom_call" | custom-call | flops 1887436800 | bytes 5734400 | tf_op jit(solution)/shard_map/pallas_call | solution.py:329
  161.5 2.7 %collective-permute-done.21 = f32[128,256]{1,0:T(8,128)S(1)} collective-permute-done((f32[128,256]{1,0:T(8,128)S(1)}, f32[128,256]{1,0:T(8,128)S(1)}, u32[]{:S(2)}, u32[]{:S(2)}) %collective-permute-start.21) | collective-permute-done | bytes 131104 | tf_op jit(solution)/shard_map/ppermute | solution.py:412
  171.1 3.8 %collective-permute-done.24.z1_ref = f32[128,256]{1,0:T(8,128)S(1)} collective-permute-done((f32[128,256]{1,0:T(8,128)S(1)}, f32[128,256]{1,0:T(8,128)S(1)}, u32[]{:S(2)}, u32[]{:S(2)}) %collective-permute-start.24) | collective-permute-done | bytes 131104 | tf_op jit(solution)/shard_map/ppermute | solution.py:413
  174.9 2.7 %shard_map.48 = (f32[256,256]{1,0:T(8,128)S(1)}, f32[256,256]{1,0:T(8,128)S(1)}) custom-call(s32[1]{0:T(128)} %bitcast.core_ref.refs_0_, f32[128,128]{1,0:T(8,128)S(1)} %get-tuple-element.61.up_ref, f32[128,128]{1,0:T(8,128)S(1)} %collective-permute-done.17.low_ref.low_in_ref, f32[128,256]{1,0:T(8,128)S(1)} %add_add_fusion.1.z0_ref, ...), custom_call_target="tpu_custom_call" | custom-call | flops 1610612736 | bytes 1048576 | tf_op jit(solution)/shard_map/pallas_call | solution.py:182
  178.7 2.9 %collective-permute-start.39 = (f32[256,256]{1,0:T(8,128)S(1)}, f32[256,256]{1,0:T(8,128)S(1)}, u32[]{:S(2)}, u32[]{:S(2)}) collective-permute-start(f32[256,256]{1,0:T(8,128)S(1)} %get-tuple-element.71.weights_ref.refs_1_.own_ref), channel_id=1, source_target_pairs={{16,32},{48,64},{80,96},{112,0},{17,33},{49,65},{81,97},{113,1},{1... | collective-permute-start | bytes 786440 | tf_op jit(solution)/shard_map/ppermute | solution.py:450
  182.5 7.3 %shard_map.51 = (f32[4,400,128]{2,1,0:T(8,128)S(1)}, f32[4,400,128]{2,1,0:T(8,128)S(1)}, f32[128,256]{1,0:T(8,128)S(1)}, f32[128,256]{1,0:T(8,128)S(1)}) custom-call(s32[1]{0:T(128)} %bitcast.core_ref.refs_0_, f32[256,256]{1,0:T(8,128)S(1)} %get-tuple-element.71.weights_ref.refs_1_.own_ref, f32[256,256]{1,0:T(8,128)S(1)} %collective-permute-done.30.refs_2_.wo_ref.other_ref, ...), custom_call_target="tpu_custom_call" | custom-call | flops 2516582400 | bytes 6553600 | tf_op jit(solution)/shard_map/pallas_call | solution.py:260
  192.6 2.9 %collective-permute-start.35 = (f32[128,256]{1,0:T(8,128)S(1)}, f32[128,256]{1,0:T(8,128)S(1)}, u32[]{:S(2)}, u32[]{:S(2)}) collective-permute-start(f32[128,256]{1,0:T(8,128)S(1)} %add.65), channel_id=1, source_target_pairs={{0,3},{1,0},{2,1},{3,2},{4,7},{5,4},{6,5},{7,6},{8,11},{9,8},{10,9... | collective-permute-start | bytes 393224 | tf_op jit(solution)/shard_map/ppermute | solution.py:412
  198.2 2.8 %collective-permute-done.34 = f32[128,256]{1,0:T(8,128)S(1)} collective-permute-done((f32[128,256]{1,0:T(8,128)S(1)}, f32[128,256]{1,0:T(8,128)S(1)}, u32[]{:S(2)}, u32[]{:S(2)}) %collective-permute-start.34) | collective-permute-done | bytes 131104 | tf_op jit(solution)/shard_map/ppermute | solution.py:412
  201.0 3.5 %collective-permute-done.33 = f32[128,256]{1,0:T(8,128)S(1)} collective-permute-done((f32[128,256]{1,0:T(8,128)S(1)}, f32[128,256]{1,0:T(8,128)S(1)}, u32[]{:S(2)}, u32[]{:S(2)}) %collective-permute-start.33) | collective-permute-done | bytes 131104 | tf_op jit(solution)/shard_map/ppermute | solution.py:412
  204.6 5.2 %shard_map.53 = (f32[4,400,128]{2,1,0:T(8,128)S(1)}, f32[4,400,128]{2,1,0:T(8,128)S(1)}, f32[4,400,128]{2,1,0:T(8,128)S(1)}, f32[4,400,128]{2,1,0:T(8,128)S(1)}) custom-call(s32[1]{0:T(128)} %bitcast.core_ref.refs_0_, f32[256,256]{1,0:T(8,128)S(1)} %add.69.wm_ref.weights_ref, f32[256,256]{1,0:T(8,128)S(1)} %collective-permute-done.30.refs_2_.wo_ref.other_ref, ...), custom_call_target="tpu_custom_call" | custom-call | flops 1258291200 | bytes 8192000 | tf_op jit(solution)/shard_map/pallas_call | solution.py:369
  212.5 2.8 %collective-permute-start.38 = (f32[128,256]{1,0:T(8,128)S(1)}, f32[128,256]{1,0:T(8,128)S(1)}, u32[]{:S(2)}, u32[]{:S(2)}) collective-permute-start(f32[128,256]{1,0:T(8,128)S(1)} %add_add_fusion.z0_ref.before_ref), channel_id=1, source_target_pairs={{0,12},{1,13},{2,14},{3,15},{4,0},{5,1},{6,2},{7,3},{8,4},{9,5},{1... | collective-permute-start | bytes 393224 | tf_op jit(solution)/shard_map/ppermute | solution.py:413
  216.5 3.9 %collective-permute-done.38.z3_ref = f32[128,256]{1,0:T(8,128)S(1)} collective-permute-done((f32[128,256]{1,0:T(8,128)S(1)}, f32[128,256]{1,0:T(8,128)S(1)}, u32[]{:S(2)}, u32[]{:S(2)}) %collective-permute-start.38) | collective-permute-done | bytes 131104 | tf_op jit(solution)/shard_map/ppermute | solution.py:413
  221.1 3.5 %collective-permute-done.36.z1_ref = f32[128,256]{1,0:T(8,128)S(1)} collective-permute-done((f32[128,256]{1,0:T(8,128)S(1)}, f32[128,256]{1,0:T(8,128)S(1)}, u32[]{:S(2)}, u32[]{:S(2)}) %collective-permute-start.36) | collective-permute-done | bytes 131104 | tf_op jit(solution)/shard_map/ppermute | solution.py:413
  228.3 4.4 %shard_map.54 = (f32[8,384,256]{2,1,0:T(8,128)}, f32[2,64,256]{2,1,0:T(8,128)}) custom-call(s32[1]{0:T(128)} %bitcast.core_ref.refs_0_, f32[256,256]{1,0:T(8,128)S(1)} %get-tuple-element.81.refs_1_, f32[4,400,128]{2,1,0:T(8,128)S(1)} %get-tuple-element.84.refs_2_, f32[4,400,128]{2,1,0:T(8,128)S(1)} %get-tuple-element.85.refs_3_, ...), custom_call_target="tpu_custom_call" | custom-call | flops 2516582400 | bytes 6553600 | tf_op jit(solution)/shard_map/pallas_call | solution.py:395
  (114 shorter events, 68.1 us)
Async XLA Ops:
  8.7 39.0 %all-to-all-start = ((f32[16,8,16,256]{3,2,1,0:T(8,128)}), f32[16,8,16,256]{3,2,1,0:T(8,128)}, u32[]{:S(2)}, u32[]{:S(2)}) async-start(f32[16,8,16,256]{3,2,1,0:T(8,128)} %shard_map.38), calls=%async_computation | async-start | bytes 4194304 | tf_op jit(solution)/shard_map/all_to_all | solution.py:436
  21.2 51.6 %collective-permute-start.2 = (f32[2,2,384,128]{3,2,1,0:T(8,128)}, f32[2,2,384,128]{3,2,1,0:T(8,128)}, u32[]{:S(2)}, u32[]{:S(2)}) collective-permute-start(f32[2,2,384,128]{3,2,1,0:T(8,128)} %get-tuple-element.50), channel_id=1, source_target_pairs={{0,32},{16,48},{32,64},{48,80},{64,96},{80,112},{96,0},{112,16},{1... | collective-permute-start | bytes 2359304 | tf_op jit(solution)/shard_map/ppermute | solution.py:434
  22.5 57.7 %collective-permute-start.3 = (f32[2,2,384,128]{3,2,1,0:T(8,128)}, f32[2,2,384,128]{3,2,1,0:T(8,128)}, u32[]{:S(2)}, u32[]{:S(2)}) collective-permute-start(f32[2,2,384,128]{3,2,1,0:T(8,128)} %get-tuple-element.51), channel_id=1, source_target_pairs={{0,64},{16,80},{32,96},{48,112},{64,0},{80,16},{96,32},{112,48},{1... | collective-permute-start | bytes 2359304 | tf_op jit(solution)/shard_map/ppermute | solution.py:434
  25.1 60.8 %collective-permute-start.4 = (f32[2,2,384,128]{3,2,1,0:T(8,128)}, f32[2,2,384,128]{3,2,1,0:T(8,128)}, u32[]{:S(2)}, u32[]{:S(2)}) collective-permute-start(f32[2,2,384,128]{3,2,1,0:T(8,128)} %get-tuple-element.52), channel_id=1, source_target_pairs={{0,96},{16,112},{32,0},{48,16},{64,32},{80,48},{96,64},{112,80},{1... | collective-permute-start | bytes 2359304 | tf_op jit(solution)/shard_map/ppermute | solution.py:434
  62.0 14.3 %all-to-all-start.2 = ((f32[16,16,256]{2,1,0:T(8,128)}), f32[16,16,256]{2,1,0:T(8,128)}, u32[]{:S(2)}, u32[]{:S(2)}) async-start(f32[16,16,256]{2,1,0:T(8,128)} %broadcast_in_dim.2), calls=%async_computation.2 | async-start | bytes 524288 | tf_op jit(solution)/shard_map/all_to_all | solution.py:418
  69.8 19.8 %collective-permute-start.5 = (f32[2,384,128]{2,1,0:T(8,128)}, f32[2,384,128]{2,1,0:T(8,128)S(1)}, u32[]{:S(2)}, u32[]{:S(2)}) collective-permute-start(f32[2,384,128]{2,1,0:T(8,128)} %get-tuple-element.54), channel_id=1, source_target_pairs={{0,32},{16,48},{32,64},{48,80},{64,96},{80,112},{96,0},{112,16},{1... | collective-permute-start | bytes 1179656 | tf_op jit(solution)/shard_map/ppermute | solution.py:441
  71.5 18.2 %collective-permute-start.6 = (f32[2,384,128]{2,1,0:T(8,128)}, f32[2,384,128]{2,1,0:T(8,128)S(1)}, u32[]{:S(2)}, u32[]{:S(2)}) collective-permute-start(f32[2,384,128]{2,1,0:T(8,128)} %get-tuple-element.55), channel_id=1, source_target_pairs={{0,64},{16,80},{32,96},{48,112},{64,0},{80,16},{96,32},{112,48},{1... | collective-permute-start | bytes 1179656 | tf_op jit(solution)/shard_map/ppermute | solution.py:441
  72.8 17.6 %collective-permute-start.7 = (f32[2,384,128]{2,1,0:T(8,128)}, f32[2,384,128]{2,1,0:T(8,128)S(1)}, u32[]{:S(2)}, u32[]{:S(2)}) collective-permute-start(f32[2,384,128]{2,1,0:T(8,128)} %get-tuple-element.56), channel_id=1, source_target_pairs={{0,96},{16,112},{32,0},{48,16},{64,32},{80,48},{96,64},{112,80},{1... | collective-permute-start | bytes 1179656 | tf_op jit(solution)/shard_map/ppermute | solution.py:441
  80.3 11.7 %collective-permute-start.15 = (f32[256,256]{1,0:T(8,128)S(1)}, f32[256,256]{1,0:T(8,128)S(1)}, u32[]{:S(2)}, u32[]{:S(2)}) collective-permute-start(f32[256,256]{1,0:T(8,128)S(1)} %shard_map.39.weights_ref.refs_1_.refs_3_), channel_id=1, source_target_pairs={{16,32},{48,64},{80,96},{112,0},{17,33},{49,65},{81,97},{113,1},{1... | collective-permute-start | bytes 786440 | tf_op jit(solution)/shard_map/ppermute | solution.py:450
  86.0 7.2 %collective-permute-start.1 = (f32[256,256]{1,0:T(8,128)S(1)}, f32[256,256]{1,0:T(8,128)S(1)}, u32[]{:S(2)}, u32[]{:S(2)}) collective-permute-start(f32[256,256]{1,0:T(8,128)S(1)} %shard_map.39.weights_ref.refs_1_.refs_3_), channel_id=1, source_target_pairs={{0,16},{16,0},{32,48},{48,32},{64,80},{80,64},{96,112},{112,96},{1... | collective-permute-start | bytes 786440 | tf_op jit(solution)/shard_map/ppermute | solution.py:408
  91.9 17.6 %collective-permute-start.16 = (f32[256,256]{1,0:T(8,128)S(1)}, f32[256,256]{1,0:T(8,128)S(1)}, u32[]{:S(2)}, u32[]{:S(2)}) collective-permute-start(f32[256,256]{1,0:T(8,128)S(1)} %collective-permute-done.15), channel_id=1, source_target_pairs={{0,16},{32,48},{64,80},{96,112},{1,17},{33,49},{65,81},{97,113},{2... | collective-permute-start | bytes 786440 | tf_op jit(solution)/shard_map/ppermute | solution.py:451
  105.8 11.4 %collective-permute-start.11 = (f32[128,256]{1,0:T(8,128)S(1)}, f32[128,256]{1,0:T(8,128)S(1)}, u32[]{:S(2)}, u32[]{:S(2)}) collective-permute-start(f32[128,256]{1,0:T(8,128)S(1)} %add.55), channel_id=1, source_target_pairs={{0,3},{1,0},{2,1},{3,2},{4,7},{5,4},{6,5},{7,6},{8,11},{9,8},{10,9... | collective-permute-start | bytes 393224 | tf_op jit(solution)/shard_map/ppermute | solution.py:412
  108.4 8.8 %collective-permute-start.10 = (f32[128,256]{1,0:T(8,128)S(1)}, f32[128,256]{1,0:T(8,128)S(1)}, u32[]{:S(2)}, u32[]{:S(2)}) collective-permute-start(f32[128,256]{1,0:T(8,128)S(1)} %add.55), channel_id=1, source_target_pairs={{0,2},{1,3},{2,0},{3,1},{4,6},{5,7},{6,4},{7,5},{8,10},{9,11},{10,... | collective-permute-start | bytes 393224 | tf_op jit(solution)/shard_map/ppermute | solution.py:412
  109.0 9.2 %collective-permute-start.9 = (f32[128,256]{1,0:T(8,128)S(1)}, f32[128,256]{1,0:T(8,128)S(1)}, u32[]{:S(2)}, u32[]{:S(2)}) collective-permute-start(f32[128,256]{1,0:T(8,128)S(1)} %add.55), channel_id=1, source_target_pairs={{0,1},{1,2},{2,3},{3,0},{4,5},{5,6},{6,7},{7,4},{8,9},{9,10},{10,1... | collective-permute-start | bytes 393224 | tf_op jit(solution)/shard_map/ppermute | solution.py:412
  116.1 24.9 %collective-permute-start.19 = (f32[4,400,128]{2,1,0:T(8,128)S(1)}, f32[4,400,128]{2,1,0:T(8,128)S(1)}, u32[]{:S(2)}, u32[]{:S(2)}) collective-permute-start(f32[4,400,128]{2,1,0:T(8,128)S(1)} %get-tuple-element.66.refs_6_), channel_id=1, source_target_pairs={{0,32},{16,48},{32,64},{48,80},{64,96},{80,112},{96,0},{112,16},{1... | collective-permute-start | bytes 2457608 | tf_op jit(solution)/shard_map/ppermute | solution.py:469
  120.8 5.8 %collective-permute-start.13 = (f32[128,256]{1,0:T(8,128)S(1)}, f32[128,256]{1,0:T(8,128)S(1)}, u32[]{:S(2)}, u32[]{:S(2)}) collective-permute-start(f32[128,256]{1,0:T(8,128)S(1)} %add_add_fusion.2.z0_ref), channel_id=1, source_target_pairs={{0,8},{1,9},{2,10},{3,11},{4,12},{5,13},{6,14},{7,15},{8,0},{9,1},... | collective-permute-start | bytes 393224 | tf_op jit(solution)/shard_map/ppermute | solution.py:413
  121.4 9.1 %collective-permute-start.12 = (f32[128,256]{1,0:T(8,128)S(1)}, f32[128,256]{1,0:T(8,128)S(1)}, u32[]{:S(2)}, u32[]{:S(2)}) collective-permute-start(f32[128,256]{1,0:T(8,128)S(1)} %add_add_fusion.2.z0_ref), channel_id=1, source_target_pairs={{0,4},{1,5},{2,6},{3,7},{4,8},{5,9},{6,10},{7,11},{8,12},{9,13},{1... | collective-permute-start | bytes 393224 | tf_op jit(solution)/shard_map/ppermute | solution.py:413
  133.2 6.5 %collective-permute-start.27 = (f32[256,256]{1,0:T(8,128)S(1)}, f32[256,256]{1,0:T(8,128)S(1)}, u32[]{:S(2)}, u32[]{:S(2)}) collective-permute-start(f32[256,256]{1,0:T(8,128)S(1)} %get-tuple-element.60.weights_ref.refs_1_.own_ref), channel_id=1, source_target_pairs={{16,32},{48,64},{80,96},{112,0},{17,33},{49,65},{81,97},{113,1},{1... | collective-permute-start | bytes 786440 | tf_op jit(solution)/shard_map/ppermute | solution.py:450
  139.7 13.7 %collective-permute-start.28 = (f32[256,256]{1,0:T(8,128)S(1)}, f32[256,256]{1,0:T(8,128)S(1)}, u32[]{:S(2)}, u32[]{:S(2)}) collective-permute-start(f32[256,256]{1,0:T(8,128)S(1)} %collective-permute-done.27), channel_id=1, source_target_pairs={{0,16},{32,48},{64,80},{96,112},{1,17},{33,49},{65,81},{97,113},{2... | collective-permute-start | bytes 786440 | tf_op jit(solution)/shard_map/ppermute | solution.py:451
  153.5 8.0 %collective-permute-start.23 = (f32[128,256]{1,0:T(8,128)S(1)}, f32[128,256]{1,0:T(8,128)S(1)}, u32[]{:S(2)}, u32[]{:S(2)}) collective-permute-start(f32[128,256]{1,0:T(8,128)S(1)} %add.60), channel_id=1, source_target_pairs={{0,3},{1,0},{2,1},{3,2},{4,7},{5,4},{6,5},{7,6},{8,11},{9,8},{10,9... | collective-permute-start | bytes 393224 | tf_op jit(solution)/shard_map/ppermute | solution.py:412
  154.7 6.8 %collective-permute-start.22 = (f32[128,256]{1,0:T(8,128)S(1)}, f32[128,256]{1,0:T(8,128)S(1)}, u32[]{:S(2)}, u32[]{:S(2)}) collective-permute-start(f32[128,256]{1,0:T(8,128)S(1)} %add.60), channel_id=1, source_target_pairs={{0,2},{1,3},{2,0},{3,1},{4,6},{5,7},{6,4},{7,5},{8,10},{9,11},{10,... | collective-permute-start | bytes 393224 | tf_op jit(solution)/shard_map/ppermute | solution.py:412
  155.7 8.5 %collective-permute-start.21 = (f32[128,256]{1,0:T(8,128)S(1)}, f32[128,256]{1,0:T(8,128)S(1)}, u32[]{:S(2)}, u32[]{:S(2)}) collective-permute-start(f32[128,256]{1,0:T(8,128)S(1)} %add.60), channel_id=1, source_target_pairs={{0,1},{1,2},{2,3},{3,0},{4,5},{5,6},{6,7},{7,4},{8,9},{9,10},{10,1... | collective-permute-start | bytes 393224 | tf_op jit(solution)/shard_map/ppermute | solution.py:412
  160.2 21.3 %collective-permute-start.31 = (f32[4,400,128]{2,1,0:T(8,128)S(1)}, f32[4,400,128]{2,1,0:T(8,128)S(1)}, u32[]{:S(2)}, u32[]{:S(2)}) collective-permute-start(f32[4,400,128]{2,1,0:T(8,128)S(1)} %get-tuple-element.77.refs_6_), channel_id=1, source_target_pairs={{0,32},{16,48},{32,64},{48,80},{64,96},{80,112},{96,0},{112,16},{1... | collective-permute-start | bytes 2457608 | tf_op jit(solution)/shard_map/ppermute | solution.py:469
  166.3 8.7 %collective-permute-start.24 = (f32[128,256]{1,0:T(8,128)S(1)}, f32[128,256]{1,0:T(8,128)S(1)}, u32[]{:S(2)}, u32[]{:S(2)}) collective-permute-start(f32[128,256]{1,0:T(8,128)S(1)} %add_add_fusion.1.z0_ref), channel_id=1, source_target_pairs={{0,4},{1,5},{2,6},{3,7},{4,8},{5,9},{6,10},{7,11},{8,12},{9,13},{1... | collective-permute-start | bytes 393224 | tf_op jit(solution)/shard_map/ppermute | solution.py:413
  178.7 12.7 %collective-permute-start.39 = (f32[256,256]{1,0:T(8,128)S(1)}, f32[256,256]{1,0:T(8,128)S(1)}, u32[]{:S(2)}, u32[]{:S(2)}) collective-permute-start(f32[256,256]{1,0:T(8,128)S(1)} %get-tuple-element.71.weights_ref.refs_1_.own_ref), channel_id=1, source_target_pairs={{16,32},{48,64},{80,96},{112,0},{17,33},{49,65},{81,97},{113,1},{1... | collective-permute-start | bytes 786440 | tf_op jit(solution)/shard_map/ppermute | solution.py:450
  192.6 5.6 %collective-permute-start.35 = (f32[128,256]{1,0:T(8,128)S(1)}, f32[128,256]{1,0:T(8,128)S(1)}, u32[]{:S(2)}, u32[]{:S(2)}) collective-permute-start(f32[128,256]{1,0:T(8,128)S(1)} %add.65), channel_id=1, source_target_pairs={{0,3},{1,0},{2,1},{3,2},{4,7},{5,4},{6,5},{7,6},{8,11},{9,8},{10,9... | collective-permute-start | bytes 393224 | tf_op jit(solution)/shard_map/ppermute | solution.py:412
  196.1 8.4 %collective-permute-start.33 = (f32[128,256]{1,0:T(8,128)S(1)}, f32[128,256]{1,0:T(8,128)S(1)}, u32[]{:S(2)}, u32[]{:S(2)}) collective-permute-start(f32[128,256]{1,0:T(8,128)S(1)} %add.65), channel_id=1, source_target_pairs={{0,1},{1,2},{2,3},{3,0},{4,5},{5,6},{6,7},{7,4},{8,9},{9,10},{10,1... | collective-permute-start | bytes 393224 | tf_op jit(solution)/shard_map/ppermute | solution.py:412
  209.8 18.5 %collective-permute-start.41 = (f32[4,400,128]{2,1,0:T(8,128)S(1)}, f32[4,400,128]{2,1,0:T(8,128)S(1)}, u32[]{:S(2)}, u32[]{:S(2)}) collective-permute-start(f32[4,400,128]{2,1,0:T(8,128)S(1)} %get-tuple-element.86), channel_id=1, source_target_pairs={{0,16},{16,0},{32,48},{48,32},{64,80},{80,64},{96,112},{112,96},{1... | collective-permute-start | bytes 2457608 | tf_op jit(solution)/shard_map/ppermute | solution.py:408
  211.1 17.1 %collective-permute-start.42 = (f32[4,400,128]{2,1,0:T(8,128)S(1)}, f32[4,400,128]{2,1,0:T(8,128)S(1)}, u32[]{:S(2)}, u32[]{:S(2)}) collective-permute-start(f32[4,400,128]{2,1,0:T(8,128)S(1)} %get-tuple-element.87), channel_id=1, source_target_pairs={{0,16},{16,0},{32,48},{48,32},{64,80},{80,64},{96,112},{112,96},{1... | collective-permute-start | bytes 2457608 | tf_op jit(solution)/shard_map/ppermute | solution.py:408
  212.5 7.9 %collective-permute-start.38 = (f32[128,256]{1,0:T(8,128)S(1)}, f32[128,256]{1,0:T(8,128)S(1)}, u32[]{:S(2)}, u32[]{:S(2)}) collective-permute-start(f32[128,256]{1,0:T(8,128)S(1)} %add_add_fusion.z0_ref.before_ref), channel_id=1, source_target_pairs={{0,12},{1,13},{2,14},{3,15},{4,0},{5,1},{6,2},{7,3},{8,4},{9,5},{1... | collective-permute-start | bytes 393224 | tf_op jit(solution)/shard_map/ppermute | solution.py:413
  215.3 5.8 %collective-permute-start.37 = (f32[128,256]{1,0:T(8,128)S(1)}, f32[128,256]{1,0:T(8,128)S(1)}, u32[]{:S(2)}, u32[]{:S(2)}) collective-permute-start(f32[128,256]{1,0:T(8,128)S(1)} %add_add_fusion.z0_ref.before_ref), channel_id=1, source_target_pairs={{0,8},{1,9},{2,10},{3,11},{4,12},{5,13},{6,14},{7,15},{8,0},{9,1},... | collective-permute-start | bytes 393224 | tf_op jit(solution)/shard_map/ppermute | solution.py:413
  215.9 8.7 %collective-permute-start.36 = (f32[128,256]{1,0:T(8,128)S(1)}, f32[128,256]{1,0:T(8,128)S(1)}, u32[]{:S(2)}, u32[]{:S(2)}) collective-permute-start(f32[128,256]{1,0:T(8,128)S(1)} %add_add_fusion.z0_ref.before_ref), channel_id=1, source_target_pairs={{0,4},{1,5},{2,6},{3,7},{4,8},{5,9},{6,10},{7,11},{8,12},{9,13},{1... | collective-permute-start | bytes 393224 | tf_op jit(solution)/shard_map/ppermute | solution.py:413
  (24 other events, 170.2 us)

commit v3 on v2

v3 whole, which is shorter than its diff:
```python
import functools

import jax
import jax.numpy as jnp
from jax import lax
from jax.experimental import pallas as pl
from jax.experimental.pallas import tpu as pltpu
from jax.sharding import PartitionSpec as P

ROUNDS = 4
BLOCK = 128
PAIR = 256
SIDE = 4
ROWS = 16
COLS = 8
F32 = jnp.float32
BF16 = jnp.bfloat16
VMEM_LIMIT = 48 * 1024 * 1024

TURN_CORE = [(c, c ^ 1) for c in range(COLS)]
NEXT_SLOT = [(c, (c + 1) % COLS) for c in range(COLS)]
CHIPS_ON = [[(c, (c + 2 * k) % COLS) for c in range(COLS)] for k in range(SIDE)]
ODD_TO_EVEN = [(c, (c + 1) % COLS) for c in range(1, COLS, 2)]
ODD_TO_ODD = [(c, (c + 2) % COLS) for c in range(1, COLS, 2)]
ALONG_X = [[(r, r - r % SIDE + (r + k) % SIDE) for r in range(ROWS)] for k in range(1, SIDE)]
ALONG_Z = [[(r, (r + SIDE * k) % ROWS) for r in range(ROWS)] for k in range(1, SIDE)]


def mm(left, right):
    return jnp.dot(left, right, precision=lax.Precision.HIGHEST, preferred_element_type=F32)


def mm_t(left, right):
    return lax.dot_general(
        left, right, (((0,), (0,)), ((), ())), precision=lax.Precision.HIGHEST, preferred_element_type=F32
    )


def parts_of(value):
    high = value.astype(BF16)
    return high, (value - high.astype(F32)).astype(BF16)


def dot(left, right, axis):
    return lax.dot_general(left, right, (((axis,), (0,)), ((), ())), preferred_element_type=F32)


def mm3(left, right, axis=1):
    high, low = parts_of(left)
    right_high, right_low = parts_of(right)
    width = right.shape[1]
    if width < PAIR:
        both = dot(high, jnp.concatenate([right_high, right_low], axis=1), axis)
        return both[:, :width] + (both[:, width:] + dot(low, right_high, axis))
    return dot(high, right_high, axis) + (dot(high, right_low, axis) + dot(low, right_high, axis))


def call(kernel, grid, in_specs, out_specs, out_shape, scalars=0, scratch=(), flops=0, nbytes=0):
    return pl.pallas_call(
        kernel,
        grid_spec=pltpu.PrefetchScalarGridSpec(
            num_scalar_prefetch=scalars,
            grid=grid,
            in_specs=in_specs,
            out_specs=out_specs,
            scratch_shapes=list(scratch),
        ),
        out_shape=out_shape,
        compiler_params=pltpu.CompilerParams(vmem_limit_bytes=VMEM_LIMIT),
        cost_estimate=pl.CostEstimate(flops=flops, bytes_accessed=nbytes, transcendentals=0),
    )


def shape(*dims):
    return jax.ShapeDtypeStruct(dims, F32)


def whole(*dims):
    return pl.BlockSpec(dims, lambda *_: (0,) * len(dims))


def pack_main_kernel(info_ref, *refs):
    for x_ref, out_ref in zip(refs[:SIDE], refs[SIDE:]):
        out_ref[0, 0] = x_ref[:, :BLOCK]
        out_ref[0, 1] = x_ref[:, BLOCK:]


def pack_main(info, x):
    rows = x.shape[0]

    def columns(k):
        return pl.BlockSpec((rows, PAIR), lambda j, c: (0, 2 * ((c[1] + k) % SIDE) + j))

    return call(
        pack_main_kernel,
        (2,),
        [columns(k) for k in range(SIDE)],
        [pl.BlockSpec((1, 2, rows, BLOCK), lambda j, c: (j, 0, 0, 0))] * SIDE,
        [shape(2, 2, rows, BLOCK)] * SIDE,
        scalars=1,
        nbytes=8 * SIDE * rows * 2 * PAIR,
    )(info, *[x] * SIDE)


def pack_ahead_kernel(info_ref, *refs):
    for x_ref, out_ref in zip(refs[:SIDE], refs[SIDE + 1:]):
        out_ref[0] = x_ref[:, :BLOCK]
        out_ref[1] = x_ref[:, BLOCK:]


def pack_ahead(info, x, before):
    rows = x.shape[0]

    def columns(k):
        return pl.BlockSpec((rows, PAIR), lambda i, c: (0, (2 * ((c[1] + k) % SIDE) + COLS - 1) % COLS))

    return call(
        pack_ahead_kernel,
        (1,),
        [columns(k) for k in range(SIDE)] + [pl.BlockSpec(memory_space=pl.ANY)],
        [whole(2, rows, BLOCK)] * SIDE,
        [shape(2, rows, BLOCK)] * SIDE,
        scalars=1,
        nbytes=8 * SIDE * rows * PAIR,
    )(info, *[x] * SIDE, before)


def gram_kernel(x_ref, before_ref, out_ref):
    high, low = parts_of(x_ref[...])
    mixed = dot(high, low, 0)
    gram = dot(high, high, 0) + (mixed + mixed.T)
    for k, block in enumerate((gram[:BLOCK, :BLOCK], gram[:BLOCK, BLOCK:], gram[BLOCK:, BLOCK:])):
        out_ref[:, 0, k] = block.reshape(ROWS, BLOCK // ROWS, BLOCK)


def row_grams(x, before):
    rows = x.shape[0]
    return call(
        gram_kernel,
        (COLS,),
        [pl.BlockSpec((rows, PAIR), lambda s: (0, s)), pl.BlockSpec(memory_space=pl.ANY)],
        pl.BlockSpec((ROWS, 1, 3, BLOCK // ROWS, BLOCK), lambda s: (0, s, 0, 0, 0)),
        shape(ROWS, COLS, 3, BLOCK // ROWS, BLOCK),
        flops=2 * 2 * COLS * rows * PAIR * PAIR,
        nbytes=4 * COLS * (rows * PAIR + PAIR * PAIR),
    )(x, before)


def rotation_of(gram, x_ref, r_ref):
    rows = lax.broadcasted_iota(jnp.int32, (PAIR, PAIR), 0)
    columns = lax.broadcasted_iota(jnp.int32, (PAIR, PAIR), 1)
    eye = (rows == columns).astype(F32)
    on_diagonal = gram * eye
    across = jnp.sum(on_diagonal, axis=0, keepdims=True)
    down = jnp.sum(on_diagonal, axis=1, keepdims=True)
    spread = across - down
    totals = across + down
    skew = gram * spread / (2.0 * spread * spread + 0.5 * totals * totals)
    square = mm(skew, skew)
    bound = jnp.max(jnp.sum(jnp.abs(square), axis=0))
    scale = 2.0 / (2.0 + bound)
    x_ref[...] = scale * (eye + skew)
    r_ref[...] = (1.0 - scale) * eye + scale * square

    def step(size):
        left = r_ref[...]
        x = x_ref[...]
        x_ref[...] = x + mm(x, left)
        r_ref[...] = mm(left, left)
        return size * size

    lax.while_loop(lambda size: size > 3e-4, step, bound / (2.0 + bound))
    x = x_ref[...]
    x = x + mm(x, eye - x + mm(skew, x))
    return 2.0 * x - eye


def cayley_kernel(fill, *refs):
    weights_ref, up_ref, low_ref, gram_ref, x_ref, r_ref = refs[-6:]
    up, cross, low = fill(*refs[:-6])
    gram_ref[:BLOCK, :BLOCK] = up
    gram_ref[:BLOCK, BLOCK:] = cross
    gram_ref[BLOCK:, :BLOCK] = cross.T
    gram_ref[BLOCK:, BLOCK:] = low
    weights = rotation_of(gram_ref[...], x_ref, r_ref)
    weights_ref[...] = weights
    up_ref[...] = weights[:, :BLOCK]
    low_ref[...] = weights[:, BLOCK:]


def cayley_call(fill, args):
    return call(
        lambda *refs: cayley_kernel(fill, *refs),
        (1,),
        [whole(*arg.shape) for arg in args],
        [whole(PAIR, PAIR), whole(PAIR, BLOCK), whole(PAIR, BLOCK), whole(PAIR, PAIR)],
        [shape(PAIR, PAIR), shape(PAIR, BLOCK), shape(PAIR, BLOCK), shape(PAIR, PAIR)],
        scratch=[pltpu.VMEM((PAIR, PAIR), F32)] * 2,
        flops=2 * 6 * 8 * PAIR**3,
        nbytes=20 * PAIR * PAIR,
    )(*args)


def first_cayley(blocks):
    return cayley_call(lambda ref: [ref[:, k].reshape(BLOCK, BLOCK) for k in range(3)], (blocks,))


def cayley(up, low, parts):
    def fill(up_ref, low_ref, *part_refs):
        first, second, third, fourth = (ref[...] for ref in part_refs)
        return up_ref[...], (first + second) + (third + fourth), low_ref[...]

    return cayley_call(fill, (up, low, *parts))


def project_kernel(gram_ref, weights_ref, up_ref, low_ref):
    weights = weights_ref[...]
    turned = mm(gram_ref[...], weights)
    up_ref[...] = mm_t(weights[:, :BLOCK], turned[:, :BLOCK])
    low_ref[...] = mm_t(weights[:, BLOCK:], turned[:, BLOCK:])


def project(gram, weights):
    return call(
        project_kernel,
        (1,),
        [whole(PAIR, PAIR)] * 2,
        [whole(BLOCK, BLOCK)] * 2,
        [shape(BLOCK, BLOCK)] * 2,
        flops=2 * 6 * 2 * PAIR**3,
        nbytes=12 * PAIR * PAIR,
    )(gram, weights)


def halves(up_ref, low_ref):
    return jnp.concatenate([up_ref[0], low_ref[0]], axis=1)


def own_turn(info_ref, own_ref, other_ref, pair0, pair1, rows, up0_ref, up1_ref, low1_ref, cross_ref):
    @pl.when(pl.program_id(0) == 0)
    def _():
        cross_ref[...] = jnp.zeros_like(cross_ref)

    first = info_ref[0] == 0
    turned = mm3(pair0, jnp.where(first, own_ref[...], other_ref[...]))
    up1 = mm3(pair1, jnp.where(first, other_ref[:, :BLOCK], own_ref[:, :BLOCK]))
    up0_ref[0] = turned[:, :BLOCK]
    low1_ref[0] = turned[:, BLOCK:]
    up1_ref[0] = up1
    cross_ref[...] += mm3(up1[:rows], turned[:rows, BLOCK:], 0)


def ahead_turn(info_ref, even_ref, odd_ref, cross_ref, up0_ref, pair_m, rows, low0_ref, keep_ref, send_ref, sum_ref):
    @pl.when(pl.program_id(0) == 0)
    def _():
        sum_ref[...] = jnp.zeros_like(sum_ref)

    low0 = mm3(pair_m, even_ref[...] + odd_ref[...])
    low0_ref[0] = low0
    sum_ref[...] += mm3(up0_ref[0, :rows], low0[:rows], 0)

    @pl.when(pl.program_id(0) == SIDE - 1)
    def _():
        first = info_ref[0] == 0
        keep_ref[...] = jnp.where(first, sum_ref[...], cross_ref[...])
        send_ref[...] = jnp.where(first, cross_ref[...], sum_ref[...])


def up_turn(even_ref, odd_ref, pair_m, low1_ref, up_m_ref, pass_ref):
    up_m_ref[0] = mm3(pair_m, even_ref[...] + odd_ref[...])
    pass_ref[0] = low1_ref[0]


def own_kernel(rows, info_ref, own_ref, other_ref, u0_ref, l0_ref, u1_ref, l1_ref, *outs):
    own_turn(info_ref, own_ref, other_ref, halves(u0_ref, l0_ref), halves(u1_ref, l1_ref), rows, *outs)


def ahead_kernel(rows, info_ref, even_ref, odd_ref, cross_ref, up0_ref, um_ref, lm_ref, *outs):
    ahead_turn(info_ref, even_ref, odd_ref, cross_ref, up0_ref, halves(um_ref, lm_ref), rows, *outs)


def up_kernel(info_ref, even_ref, odd_ref, before_ref, low1_ref, um_ref, lm_ref, *outs):
    up_turn(even_ref, odd_ref, halves(um_ref, lm_ref), low1_ref, *outs)


def start_pair(info_ref, step, slot, up, low):
    column = slot * PAIR - info_ref[2] - (step - up.shape[0]) * pl.program_id(0)
    rows = lax.broadcasted_iota(jnp.int32, (step - up.shape[0], PAIR), 0)
    columns = lax.broadcasted_iota(jnp.int32, (step - up.shape[0], PAIR), 1)
    basis = (rows == columns + column).astype(F32)
    return jnp.concatenate([jnp.concatenate([up, low], axis=1), basis], axis=0)


def start_ahead_pair(info_ref, step, ahead_ref):
    slot = (2 * info_ref[1] + COLS - 1) % COLS
    return start_pair(info_ref, step, slot, ahead_ref[0, 0], ahead_ref[0, 1])


def start_own_kernel(step, rows, info_ref, own_ref, other_ref, main_ref, *outs):
    slot = 2 * info_ref[1]
    pair0 = start_pair(info_ref, step, slot, main_ref[0, 0, 0], main_ref[0, 0, 1])
    pair1 = start_pair(info_ref, step, slot + 1, main_ref[0, 1, 0], main_ref[0, 1, 1])
    own_turn(info_ref, own_ref, other_ref, pair0, pair1, rows, *outs)


def start_ahead_kernel(step, rows, info_ref, even_ref, odd_ref, cross_ref, up0_ref, ahead_ref, *outs):
    pair_m = start_ahead_pair(info_ref, step, ahead_ref)
    ahead_turn(info_ref, even_ref, odd_ref, cross_ref, up0_ref, pair_m, rows, *outs)


def start_up_kernel(step, info_ref, even_ref, odd_ref, before_ref, low1_ref, ahead_ref, *outs):
    up_turn(even_ref, odd_ref, start_ahead_pair(info_ref, step, ahead_ref), low1_ref, *outs)


def group_tile(step):
    return pl.BlockSpec((1, step, BLOCK), lambda i, c: (i, 0, 0))


def arrived(value):
    rest = value.shape[1:]
    return pl.BlockSpec((1,) + rest, lambda i, c: (lax.rem(c[1] + SIDE - i, SIDE),) + (0,) * len(rest))


def rotate_own(info, own, other, blocks, rows, step):
    starting = len(blocks) == 1
    kernel = functools.partial(start_own_kernel, step, rows) if starting else functools.partial(own_kernel, rows)
    tile = group_tile(step)
    return call(
        kernel,
        (SIDE,),
        [whole(PAIR, PAIR)] * 2 + ([arrived(blocks[0])] if starting else [tile] * 4),
        [tile] * 3 + [whole(BLOCK, BLOCK)],
        [shape(SIDE, step, BLOCK)] * 3 + [shape(BLOCK, BLOCK)],
        scalars=1,
        flops=2 * 3 * SIDE * step * 4 * BLOCK * PAIR,
        nbytes=4 * 7 * SIDE * step * BLOCK,
    )(info, own, other, *blocks)


def rotate_ahead(info, lower, cross, up0, blocks, rows, step):
    starting = len(blocks) == 1
    kernel = functools.partial(start_ahead_kernel, step, rows) if starting else functools.partial(ahead_kernel, rows)
    tile = group_tile(step)
    return call(
        kernel,
        (SIDE,),
        [whole(PAIR, BLOCK)] * 2 + [whole(BLOCK, BLOCK), tile] + ([arrived(blocks[0])] if starting else [tile] * 2),
        [tile] + [whole(BLOCK, BLOCK)] * 2,
        [shape(SIDE, step, BLOCK)] + [shape(BLOCK, BLOCK)] * 2,
        scalars=1,
        scratch=[pltpu.VMEM((BLOCK, BLOCK), F32)],
        flops=2 * 3 * SIDE * step * 2 * BLOCK * PAIR,
        nbytes=4 * 4 * SIDE * step * BLOCK,
    )(info, *lower, cross, up0, *blocks)


def rotate_up(info, upper, before, low1, blocks, step):
    starting = len(blocks) == 1
    kernel = functools.partial(start_up_kernel, step) if starting else up_kernel
    tile = group_tile(step)
    return call(
        kernel,
        (SIDE,),
        [whole(PAIR, BLOCK)] * 2
        + [pl.BlockSpec(memory_space=pl.ANY), tile]
        + ([arrived(blocks[0])] if starting else [tile] * 2),
        [tile] * 2,
        [shape(SIDE, step, BLOCK)] * 2,
        scalars=1,
        flops=2 * 3 * SIDE * step * BLOCK * PAIR,
        nbytes=4 * 5 * SIDE * step * BLOCK,
    )(info, *upper, before, low1, *blocks)


def other_slot_kernel(info_ref, before_ref, up0_ref, low0_ref, up1_ref, low1_ref, up_ref, low_ref):
    first = info_ref[0] == 0
    up_ref[0] = jnp.where(first, up1_ref[0], up0_ref[0])
    low_ref[0] = jnp.where(first, low1_ref[0], low0_ref[0])


def other_slot(info, before, blocks, step):
    tile = group_tile(step)
    return call(
        other_slot_kernel,
        (SIDE,),
        [pl.BlockSpec(memory_space=pl.ANY)] + [tile] * 4,
        [tile] * 2,
        [shape(SIDE, step, BLOCK)] * 2,
        scalars=1,
        nbytes=4 * 6 * SIDE * step * BLOCK,
    )(info, before, *blocks)


def final_kernel(rows, total, info_ref, weights_ref, gram_ref, up0_ref, low0_ref, up1_ref, low1_ref, ru_ref, rl_ref,
                 out_ref, frame_ref, scale_ref):
    weights = weights_ref[...]
    first = info_ref[0] == 0
    mine = mm3(jnp.where(first, halves(up0_ref, low0_ref), halves(up1_ref, low1_ref)), weights)
    theirs = mm3(halves(ru_ref, rl_ref), weights)
    for k, turned in enumerate((jnp.where(first, mine, theirs), jnp.where(first, theirs, mine))):
        out_ref[k] = turned[:rows]
        frame_ref[k] = turned[rows:]

    @pl.when(pl.program_id(0) == 0)
    def _():
        squares = jnp.sum(weights * mm(gram_ref[...], weights), axis=0, keepdims=True)
        scale_ref[...] = jnp.sqrt(squares / total)


def rotate_final(info, weights, gram, blocks, rows, step):
    tile = group_tile(step)
    share = step - rows
    return call(
        functools.partial(final_kernel, rows, float(rows * COLS * ROWS)),
        (SIDE,),
        [whole(PAIR, PAIR)] * 2 + [tile] * 6,
        [
            pl.BlockSpec((2, rows, PAIR), lambda i, c: (i, 0, 0)),
            pl.BlockSpec((2, share, PAIR), lambda i, c: (0, i, 0)),
            whole(1, PAIR),
        ],
        [shape(COLS, rows, PAIR), shape(2, SIDE * share, PAIR), shape(1, PAIR)],
        scalars=1,
        flops=2 * 3 * 2 * SIDE * step * PAIR * PAIR,
        nbytes=4 * 4 * SIDE * step * PAIR,
    )(info, weights, gram, *blocks)


def swap_core(value):
    return lax.ppermute(value, "cols", TURN_CORE)


def sum_over_rows(value):
    value = value + sum(lax.ppermute(value, "rows", pairs) for pairs in ALONG_X)
    return [value] + [lax.ppermute(value, "rows", pairs) for pairs in ALONG_Z]


def spread_over_rows(share):
    copies = jnp.broadcast_to(share[None], (ROWS,) + share.shape)
    return lax.all_to_all(copies, "rows", 0, 0, tiled=True)


def to_next_chip(value):
    return [lax.ppermute(value, "cols", pairs) for pairs in (ODD_TO_EVEN, ODD_TO_ODD)]


def body(sensitivity):
    x = sensitivity[0]
    rows = x.shape[0]
    column = lax.axis_index("cols")
    parity = column % 2
    basis_rows = x.shape[1] // ROWS // 2
    basis_at = (lax.axis_index("rows") * 2 + parity) * basis_rows
    info = jnp.stack([parity, column // 2, basis_at]).astype(jnp.int32)
    step = rows + basis_rows // SIDE

    packed = pack_main(info, x)
    main = [packed[0]] + [lax.ppermute(packed[k], "cols", CHIPS_ON[k]) for k in range(1, SIDE)]

    parts = lax.all_to_all(row_grams(x, packed[0]), "rows", 0, 0, tiled=True)
    parts = lax.all_to_all(jnp.sum(parts, axis=0), "cols", 0, 0, tiled=True)
    share = jnp.sum(parts, axis=0)

    packed = pack_ahead(info, x, share)
    ahead = [packed[0]] + [lax.ppermute(packed[k], "cols", CHIPS_ON[k]) for k in range(1, SIDE)]
    weights, upper, lower, gram = first_cayley(spread_over_rows(share))

    own_blocks = [jnp.stack(main)]
    ahead_blocks = [jnp.stack(ahead)]
    for sweep_round in range(ROUNDS - 1):
        lower = to_next_chip(lower)
        other = swap_core(weights)
        up, low = project(gram, weights)
        low = lax.ppermute(low, "cols", NEXT_SLOT)
        up0, up1, low1, cross = rotate_own(info, weights, other, own_blocks, rows, step)
        low0, keep, send = rotate_ahead(info, lower, cross, up0, ahead_blocks, rows, step)
        parts = sum_over_rows(keep + swap_core(send))
        own_blocks = [up0, low0, up1, low1]
        if sweep_round < ROUNDS - 2:
            up_m, passed = rotate_up(info, to_next_chip(upper), low, low1, ahead_blocks, step)
            ahead_blocks = [up_m, lax.ppermute(passed, "cols", CHIPS_ON[1])]
        else:
            received = [swap_core(value) for value in other_slot(info, parts[0], own_blocks, step)]
        weights, upper, lower, gram = cayley(up, low, parts)

    rotated, frame, column_scale = rotate_final(info, weights, gram, own_blocks + received, rows, step)
    return rotated, frame.reshape(2 * basis_rows, PAIR), column_scale.reshape(PAIR)


def solution(mesh):
    in_specs = (P("cols", "rows", None),)
    out_specs = (P(None, "rows", "cols"), P("rows", "cols"), P("cols"))
    return jax.shard_map(body, mesh=mesh, in_specs=in_specs, out_specs=out_specs, check_vma=False)
```

time: 233 us -> 206 us (0.88); the launches traced: 233 us -> 203 us
  waiting for transfers between devices: 65.5 us -> 44.6 us
  Pallas kernels: 69.8 us -> 54.1 us
  starting transfers between devices: 71.6 us -> 78.3 us
  blocking collectives: 11.7 us -> 15.4 us
    pallas_call x14 -> x16, Pallas kernels: 62.6 us -> 48 us  [the longest x3 14 us: rotate_own(): call(kernel, (SIDE,), [whole(PAIR, PAIR)] * 2 + ([arrived(blocks[0])] if...]
    ppermute x9, waiting for transfers between devices: 24.8 us -> 13.4 us  [sum_over_rows(): return [value] + [lax.ppermute(value, 'rows', pairs) for pairs in ALONG_Z]]
    ppermute x8 -> x12, starting transfers between devices: 18 us -> 22.6 us  [the longest x10 21.6 us: to_next_chip(): lax.ppermute(value, 'cols', pairs)]
    ppermute x8 -> x12, waiting for transfers between devices: 4.59 us -> 0.03 us  [the longest x10 0.03 us: to_next_chip(): lax.ppermute(value, 'cols', pairs)]
    all_to_all x2, waiting for transfers between devices: 23.7 us -> 19.2 us  [the longest x1 17.9 us: body(): parts = lax.all_to_all(row_grams(x, packed[0]), 'rows', 0, 0, tiled=True)]
    ppermute x9, starting transfers between devices: 10.4 us -> 6.53 us  [sum_over_rows(): return [value] + [lax.ppermute(value, 'rows', pairs) for pairs in ALONG_Z]]
    all_to_all x1, blocking collectives: 11.7 us -> 15.4 us  [body(): parts = lax.all_to_all(jnp.sum(parts, axis=0), 'cols', 0, 0, tiled=True)]
    ppermute x3, starting transfers between devices: 0.33 us -> 3.32 us  [body(): low = lax.ppermute(low, 'cols', NEXT_SLOT)]
  transfers between devices with their start and end apart: 45 -> 49, of which waited for: 19 -> 20; matrix products, arithmetic and copies ran while one was open for 3% -> 2% of each run, Pallas kernels for 23% -> 20%
where the time goes in v3:
time: 206 us; the launch traced here: 203 us
  starting transfers between devices  78.3 us (38%)
  Pallas kernels  54.1 us (26%)
  waiting for transfers between devices  44.6 us (22%)
  blocking collectives  15.4 us (7%)
  local copies, waits for them, and re-layouts  5.4 us (3%)
  other arithmetic  3.75 us (2%)
    ppermute x10, starting transfers between devices, to_next_chip(): lax.ppermute(value, 'cols', pairs)  21.6 us
    all_to_all x1, waiting for transfers between devices, body(): parts = lax.all_to_all(row_grams(x, packed[0]), 'rows', 0, 0, tiled=True)  17.9 us
    all_to_all x1, blocking collectives, body(): parts = lax.all_to_all(jnp.sum(parts, axis=0), 'cols', 0, 0, tiled=True)  15.4 us
    pallas_call x3, Pallas kernels, rotate_own(): call(kernel, (SIDE,), [whole(PAIR, PAIR)] * 2 + ([arrived(blocks[0])] if...  14 us
    ppermute x9, waiting for transfers between devices, sum_over_rows(): return [value] + [lax.ppermute(value, 'rows', pairs) for pairs in ALONG_Z]  13.4 us
    pallas_call x4, Pallas kernels, cayley_call(): call(lambda *refs: cayley_kernel(fill, *refs), (1,), [whole(*arg.shape) f...  12.8 us
    ppermute x8, starting transfers between devices, swap_core(): return lax.ppermute(value, 'cols', TURN_CORE)  11 us
    ppermute x9, starting transfers between devices, sum_over_rows(): lax.ppermute(value, 'rows', pairs)  10.4 us
  transfers between devices with their start and end apart: 49, of which 20 were waited for; matrix products, arithmetic and copies ran while one was open for 2% of the time, Pallas kernels for 20%

profile of v3, /device:TPU:1, one launch (start us, length us, event | category | flops | bytes accessed | tf_op | source)
XLA Modules:
  0.0 202.7 jit_solution(2477670253789268649)
XLA Ops:
  0.7 2.8 %shard_map.38 = (f32[2,2,384,128]{3,2,1,0:T(8,128)S(1)}, f32[2,2,384,128]{3,2,1,0:T(8,128)S(1)}, f32[2,2,384,128]{3,2,1,0:T(8,128)S(1)}, f32[2,2,384,128]{3,2,1,0:T(8,128)S(1)}) custom-call(s32[3]{0:T(128)S(1)} %pad_add_fusion.info_ref, f32[384,2048]{1,0:T(8,128)} %bitcast.14, f32[384,2048]{1,0:T(8,128)} %bitcast.15, f32[384,2048]{1,0:T(8,128)} %bitcast.16, ...), custom_call_target="tpu_custom_call" | custom-call | bytes 6291456 | tf_op jit(solution)/shard_map/pallas_call | solution.py:94
  6.2 3.5 %shard_map.39 = f32[16,8,3,8,128]{4,3,2,1,0:T(8,128)S(1)} custom-call(f32[384,2048]{1,0:T(8,128)S(1)} %bitcast.18, f32[2,2,384,128]{3,2,1,0:T(8,128)S(1)} %get-tuple-element.60.before_ref), custom_call_target="tpu_custom_call" | custom-call | flops 805306368 | bytes 5242880 | tf_op jit(solution)/shard_map/pallas_call | solution.py:138
  11.8 8.5 %all-to-all-start = ((f32[16,8,3,8,128]{4,3,2,1,0:T(8,128)}), f32[16,8,3,8,128]{4,3,2,1,0:T(8,128)}, u32[]{:S(2)}, u32[]{:S(2)}) async-start(f32[16,8,3,8,128]{4,3,2,1,0:T(8,128)} %copy-done.1), calls=%async_computation | async-start | bytes 3145728 | tf_op jit(solution)/shard_map/all_to_all | solution.py:460
  21.6 2.6 %collective-permute-start.5 = (f32[2,2,384,128]{3,2,1,0:T(8,128)}, f32[2,2,384,128]{3,2,1,0:T(8,128)}, u32[]{:S(2)}, u32[]{:S(2)}) collective-permute-start(f32[2,2,384,128]{3,2,1,0:T(8,128)} %copy-done.7), channel_id=1, source_target_pairs={{0,64},{16,80},{32,96},{48,112},{64,0},{80,16},{96,32},{112,48},{1... | collective-permute-start | bytes 2359304 | tf_op jit(solution)/shard_map/ppermute | solution.py:458
  25.3 17.9 %all-to-all-done = f32[16,8,3,8,128]{4,3,2,1,0:T(8,128)} async-done(((f32[16,8,3,8,128]{4,3,2,1,0:T(8,128)}), f32[16,8,3,8,128]{4,3,2,1,0:T(8,128)}, u32[]{:S(2)}, u32[]{:S(2)}) %all-to-all-start) | async-done | bytes 1572896 | tf_op jit(solution)/shard_map/all_to_all | solution.py:460
  44.7 15.4 %all_to_all.15 = f32[8,3,8,128]{3,2,1,0:T(8,128)S(1)} all-to-all(f32[8,3,8,128]{3,2,1,0:T(8,128)S(1)} %reduce_sum.18), channel_id=1, replica_groups=mesh['cols'=8,'rows'=16] {'cols'}, dimensions={0} | all-to-all | bytes 196608 | tf_op jit(solution)/shard_map/all_to_all | solution.py:461
  60.8 6.6 %all-to-all-start.2 = ((f32[16,3,8,128]{3,2,1,0:T(8,128)}), f32[16,3,8,128]{3,2,1,0:T(8,128)}, u32[]{:S(2)}, u32[]{:S(2)}) async-start(f32[16,3,8,128]{3,2,1,0:T(8,128)} %broadcast_in_dim.2), calls=%async_computation.2 | async-start | bytes 393216 | tf_op jit(solution)/shard_map/all_to_all | solution.py:440
  74.7 3.9 %shard_map.40 = (f32[256,256]{1,0:T(8,128)S(1)}, f32[256,128]{1,0:T(8,128)S(1)}, f32[256,128]{1,0:T(8,128)S(1)}, f32[256,256]{1,0:T(8,128)S(1)}) custom-call(f32[16,3,8,128]{3,2,1,0:T(8,128)} %all-to-all-done.2.refs_0_), custom_call_target="tpu_custom_call" | custom-call | flops 1610612736 | bytes 1310720 | tf_op jit(solution)/shard_map/pallas_call | solution.py:192
  78.7 2.3 %collective-permute-start.3 = (f32[256,256]{1,0:T(8,128)S(1)}, f32[256,256]{1,0:T(8,128)S(1)}, u32[]{:S(2)}, u32[]{:S(2)}) collective-permute-start(f32[256,256]{1,0:T(8,128)S(1)} %get-tuple-element.62.weights_ref.own_ref), channel_id=1, source_target_pairs={{0,16},{16,0},{32,48},{48,32},{64,80},{80,64},{96,112},{112,96},{1... | collective-permute-start | bytes 786440 | tf_op jit(solution)/shard_map/ppermute | solution.py:430
  80.9 2.0 pad_maximum_fusion.main_ref
  82.9 3.5 %collective-permute-start.2 = (f32[256,128]{1,0:T(8,128)S(1)}, f32[256,128]{1,0:T(8,128)S(1)}, u32[]{:S(2)}, u32[]{:S(2)}) collective-permute-start(f32[256,128]{1,0:T(8,128)S(1)} %get-tuple-element.65), channel_id=1, source_target_pairs={{16,48},{48,80},{80,112},{112,16},{17,49},{49,81},{81,113},{113,17... | collective-permute-start | bytes 393224 | tf_op jit(solution)/shard_map/ppermute | solution.py:444
  90.7 3.6 %collective-permute-start.21 = (f32[256,128]{1,0:T(8,128)S(1)}, f32[256,128]{1,0:T(8,128)S(1)}, u32[]{:S(2)}, u32[]{:S(2)}) collective-permute-start(f32[256,128]{1,0:T(8,128)S(1)} %get-tuple-element.87), channel_id=1, source_target_pairs={{16,32},{48,64},{80,96},{112,0},{17,33},{49,65},{81,97},{113,1},{1... | collective-permute-start | bytes 393224 | tf_op jit(solution)/shard_map/ppermute | solution.py:444
  94.4 4.0 %shard_map.42 = (f32[4,400,128]{2,1,0:T(8,128)S(1)}, f32[4,400,128]{2,1,0:T(8,128)S(1)}, f32[4,400,128]{2,1,0:T(8,128)S(1)}, f32[128,128]{1,0:T(8,128)S(1)}) custom-call(s32[3]{0:T(128)S(1)} %pad_add_fusion.info_ref, f32[256,256]{1,0:T(8,128)S(1)} %get-tuple-element.62.weights_ref.own_ref, f32[256,256]{1,0:T(8,128)S(1)} %collective-permute-done.3.other_ref, ...), custom_call_target="tpu_custom_call" | custom-call | flops 1258291200 | bytes 5734400 | tf_op jit(solution)/shard_map/pallas_call | solution.py:328
  98.4 2.6 %shard_map.44 = (f32[4,400,128]{2,1,0:T(8,128)S(1)}, f32[128,128]{1,0:T(8,128)S(1)}, f32[128,128]{1,0:T(8,128)S(1)}) custom-call(s32[3]{0:T(128)S(1)} %pad_add_fusion.info_ref, f32[256,128]{1,0:T(8,128)S(1)} %collective-permute-done.1.even_ref, f32[256,128]{1,0:T(8,128)S(1)} %collective-permute-done.2.odd_ref, f32[128,128]{1,0:T(8,128)S(1)} %get-tuple-element.69.cross_ref, ...), custom_call_target="tpu_custom_call" | custom-call | flops 629145600 | bytes 3276800 | tf_op jit(solution)/shard_map/pallas_call | solution.py:344
  104.1 3.3 %collective-permute-start.13 = (f32[128,128]{1,0:T(8,128)S(1)}, f32[128,128]{1,0:T(8,128)S(1)}, u32[]{:S(2)}, u32[]{:S(2)}) collective-permute-start(f32[128,128]{1,0:T(8,128)S(1)} %add.46), channel_id=1, source_target_pairs={{0,3},{1,0},{2,1},{3,2},{4,7},{5,4},{6,5},{7,6},{8,11},{9,8},{10,9... | collective-permute-start | bytes 196616 | tf_op jit(solution)/shard_map/ppermute | solution.py:434
  113.7 2.1 %collective-permute-start.16 = (f32[128,128]{1,0:T(8,128)S(1)}, f32[128,128]{1,0:T(8,128)S(1)}, u32[]{:S(2)}, u32[]{:S(2)}) collective-permute-start(f32[128,128]{1,0:T(8,128)S(1)} %add_add_fusion.2.refs_2_), channel_id=1, source_target_pairs={{0,12},{1,13},{2,14},{3,15},{4,0},{5,1},{6,2},{7,3},{8,4},{9,5},{1... | collective-permute-start | bytes 196616 | tf_op jit(solution)/shard_map/ppermute | solution.py:435
  117.2 3.3 %collective-permute-done.15.refs_4_ = f32[128,128]{1,0:T(8,128)S(1)} collective-permute-done((f32[128,128]{1,0:T(8,128)S(1)}, f32[128,128]{1,0:T(8,128)S(1)}, u32[]{:S(2)}, u32[]{:S(2)}) %collective-permute-start.15) | collective-permute-done | bytes 65568 | tf_op jit(solution)/shard_map/ppermute | solution.py:435
  121.5 2.6 %shard_map.45 = (f32[256,256]{1,0:T(8,128)S(1)}, f32[256,128]{1,0:T(8,128)S(1)}, f32[256,128]{1,0:T(8,128)S(1)}, f32[256,256]{1,0:T(8,128)S(1)}) custom-call(f32[128,128]{1,0:T(8,128)S(1)} %get-tuple-element.63.refs_0_, f32[128,128]{1,0:T(8,128)S(1)} %collective-permute-done.refs_1_.before_ref, f32[128,128]{1,0:T(8,128)S(1)} %add_add_fusion.2.refs_2_, ...), custom_call_target="tpu_custom_call" | custom-call | flops 1610612736 | bytes 1310720 | tf_op jit(solution)/shard_map/pallas_call | solution.py:192
  124.1 1.9 collective-permute-start.20
  126.1 2.4 %collective-permute-start.19 = (f32[256,128]{1,0:T(8,128)S(1)}, f32[256,128]{1,0:T(8,128)S(1)}, u32[]{:S(2)}, u32[]{:S(2)}) collective-permute-start(f32[256,128]{1,0:T(8,128)S(1)} %get-tuple-element.81), channel_id=1, source_target_pairs={{16,48},{48,80},{80,112},{112,16},{17,49},{49,81},{81,113},{113,17... | collective-permute-start | bytes 393224 | tf_op jit(solution)/shard_map/ppermute | solution.py:444
  129.7 3.1 %collective-permute-start.36 = (f32[256,128]{1,0:T(8,128)S(1)}, f32[256,128]{1,0:T(8,128)S(1)}, u32[]{:S(2)}, u32[]{:S(2)}) collective-permute-start(f32[256,128]{1,0:T(8,128)S(1)} %get-tuple-element.102), channel_id=1, source_target_pairs={{16,48},{48,80},{80,112},{112,16},{17,49},{49,81},{81,113},{113,17... | collective-permute-start | bytes 393224 | tf_op jit(solution)/shard_map/ppermute | solution.py:444
  134.2 5.0 %shard_map.47 = (f32[4,400,128]{2,1,0:T(8,128)S(1)}, f32[4,400,128]{2,1,0:T(8,128)S(1)}, f32[4,400,128]{2,1,0:T(8,128)S(1)}, f32[128,128]{1,0:T(8,128)S(1)}) custom-call(s32[3]{0:T(128)S(1)} %pad_add_fusion.info_ref, f32[256,256]{1,0:T(8,128)S(1)} %get-tuple-element.78.weights_ref.own_ref, f32[256,256]{1,0:T(8,128)S(1)} %collective-permute-done.20.other_ref, ...), custom_call_target="tpu_custom_call" | custom-call | flops 1258291200 | bytes 5734400 | tf_op jit(solution)/shard_map/pallas_call | solution.py:328
  139.2 2.5 %shard_map.49 = (f32[4,400,128]{2,1,0:T(8,128)S(1)}, f32[128,128]{1,0:T(8,128)S(1)}, f32[128,128]{1,0:T(8,128)S(1)}) custom-call(s32[3]{0:T(128)S(1)} %pad_add_fusion.info_ref, f32[256,128]{1,0:T(8,128)S(1)} %collective-permute-done.18.even_ref, f32[256,128]{1,0:T(8,128)S(1)} %collective-permute-done.19.odd_ref, f32[128,128]{1,0:T(8,128)S(1)} %get-tuple-element.85.cross_ref, ...), custom_call_target="tpu_custom_call" | custom-call | flops 629145600 | bytes 3276800 | tf_op jit(solution)/shard_map/pallas_call | solution.py:344
  156.9 3.1 %shard_map.50 = (f32[256,256]{1,0:T(8,128)S(1)}, f32[256,128]{1,0:T(8,128)}, f32[256,128]{1,0:T(8,128)S(1)}, f32[256,256]{1,0:T(8,128)S(1)}) custom-call(f32[128,128]{1,0:T(8,128)S(1)} %get-tuple-element.79.refs_0_, f32[128,128]{1,0:T(8,128)S(1)} %collective-permute-done.17.refs_1_.before_ref, f32[128,128]{1,0:T(8,128)S(1)} %add_add_fusion.1.refs_2_, ...), custom_call_target="tpu_custom_call" | custom-call | flops 1610612736 | bytes 1310720 | tf_op jit(solution)/shard_map/pallas_call | solution.py:192
  160.0 4.0 %collective-permute-start.34 = (f32[256,256]{1,0:T(8,128)S(1)}, f32[256,256]{1,0:T(8,128)S(1)}, u32[]{:S(2)}, u32[]{:S(2)}) collective-permute-start(f32[256,256]{1,0:T(8,128)S(1)} %get-tuple-element.93.weights_ref.own_ref), channel_id=1, source_target_pairs={{0,16},{16,0},{32,48},{48,32},{64,80},{80,64},{96,112},{112,96},{1... | collective-permute-start | bytes 786440 | tf_op jit(solution)/shard_map/ppermute | solution.py:430
  164.0 2.0 collective-permute-start.33
  167.3 5.0 %shard_map.52 = (f32[4,400,128]{2,1,0:T(8,128)S(1)}, f32[4,400,128]{2,1,0:T(8,128)S(1)}, f32[4,400,128]{2,1,0:T(8,128)S(1)}, f32[128,128]{1,0:T(8,128)S(1)}) custom-call(s32[3]{0:T(128)S(1)} %pad_add_fusion.info_ref, f32[256,256]{1,0:T(8,128)S(1)} %get-tuple-element.93.weights_ref.own_ref, f32[256,256]{1,0:T(8,128)S(1)} %collective-permute-done.34.other_ref, ...), custom_call_target="tpu_custom_call" | custom-call | flops 1258291200 | bytes 5734400 | tf_op jit(solution)/shard_map/pallas_call | solution.py:328
  172.4 2.5 %shard_map.54 = (f32[4,400,128]{2,1,0:T(8,128)S(1)}, f32[128,128]{1,0:T(8,128)S(1)}, f32[128,128]{1,0:T(8,128)S(1)}) custom-call(s32[3]{0:T(128)S(1)} %pad_add_fusion.info_ref, f32[256,128]{1,0:T(8,128)S(1)} %collective-permute-done.32.even_ref, f32[256,128]{1,0:T(8,128)S(1)} %collective-permute-done.33.odd_ref, ...), custom_call_target="tpu_custom_call" | custom-call | flops 629145600 | bytes 3276800 | tf_op jit(solution)/shard_map/pallas_call | solution.py:344
  176.6 2.2 %collective-permute-start.41 = (f32[128,128]{1,0:T(8,128)S(1)}, f32[128,128]{1,0:T(8,128)S(1)}, u32[]{:S(2)}, u32[]{:S(2)}) collective-permute-start(f32[128,128]{1,0:T(8,128)S(1)} %add.54), channel_id=1, source_target_pairs={{0,3},{1,0},{2,1},{3,2},{4,7},{5,4},{6,5},{7,6},{8,11},{9,8},{10,9... | collective-permute-start | bytes 196616 | tf_op jit(solution)/shard_map/ppermute | solution.py:434
  180.5 2.9 %collective-permute-done.40 = f32[128,128]{1,0:T(8,128)S(1)} collective-permute-done((f32[128,128]{1,0:T(8,128)S(1)}, f32[128,128]{1,0:T(8,128)S(1)}, u32[]{:S(2)}, u32[]{:S(2)}) %collective-permute-start.40) | collective-permute-done | bytes 65568 | tf_op jit(solution)/shard_map/ppermute | solution.py:434
  195.3 3.1 %shard_map.55 = (f32[256,256]{1,0:T(8,128)S(1)}, f32[256,128]{1,0:T(8,128)}, f32[256,128]{1,0:T(8,128)}, f32[256,256]{1,0:T(8,128)S(1)}) custom-call(f32[128,128]{1,0:T(8,128)S(1)} %get-tuple-element.94.refs_0_, f32[128,128]{1,0:T(8,128)S(1)} %collective-permute-done.31.refs_1_, f32[128,128]{1,0:T(8,128)S(1)} %add_add_fusion.refs_2_.before_ref, ...), custom_call_target="tpu_custom_call" | custom-call | flops 1610612736 | bytes 1310720 | tf_op jit(solution)/shard_map/pallas_call | solution.py:192
  198.4 4.3 %shard_map.57 = (f32[8,384,256]{2,1,0:T(8,128)}, f32[2,64,256]{2,1,0:T(8,128)}, f32[1,256]{1,0:T(1,128)}) custom-call(s32[3]{0:T(128)S(1)} %pad_add_fusion.info_ref, f32[256,256]{1,0:T(8,128)S(1)} %get-tuple-element.107.weights_ref, f32[256,256]{1,0:T(8,128)S(1)} %get-tuple-element.108.gram_ref, f32[4,400,128]{2,1,0:T(8,128)S(1)} %get-tuple-element.101.up0_ref, ...), custom_call_target="tpu_custom_call" | custom-call | flops 1258291200 | bytes 6553600 | tf_op jit(solution)/shard_map/pallas_call | solution.py:413
  (117 shorter events, 66.9 us)
Async XLA Ops:
  11.8 31.4 %all-to-all-start = ((f32[16,8,3,8,128]{4,3,2,1,0:T(8,128)}), f32[16,8,3,8,128]{4,3,2,1,0:T(8,128)}, u32[]{:S(2)}, u32[]{:S(2)}) async-start(f32[16,8,3,8,128]{4,3,2,1,0:T(8,128)} %copy-done.1), calls=%async_computation | async-start | bytes 3145728 | tf_op jit(solution)/shard_map/all_to_all | solution.py:460
  20.3 51.9 %collective-permute-start.4 = (f32[2,2,384,128]{3,2,1,0:T(8,128)}, f32[2,2,384,128]{3,2,1,0:T(8,128)}, u32[]{:S(2)}, u32[]{:S(2)}) collective-permute-start(f32[2,2,384,128]{3,2,1,0:T(8,128)} %copy-done.8), channel_id=1, source_target_pairs={{0,32},{16,48},{32,64},{48,80},{64,96},{80,112},{96,0},{112,16},{1... | collective-permute-start | bytes 2359304 | tf_op jit(solution)/shard_map/ppermute | solution.py:458
  21.6 57.0 %collective-permute-start.5 = (f32[2,2,384,128]{3,2,1,0:T(8,128)}, f32[2,2,384,128]{3,2,1,0:T(8,128)}, u32[]{:S(2)}, u32[]{:S(2)}) collective-permute-start(f32[2,2,384,128]{3,2,1,0:T(8,128)} %copy-done.7), channel_id=1, source_target_pairs={{0,64},{16,80},{32,96},{48,112},{64,0},{80,16},{96,32},{112,48},{1... | collective-permute-start | bytes 2359304 | tf_op jit(solution)/shard_map/ppermute | solution.py:458
  24.3 56.7 %collective-permute-start.6 = (f32[2,2,384,128]{3,2,1,0:T(8,128)}, f32[2,2,384,128]{3,2,1,0:T(8,128)}, u32[]{:S(2)}, u32[]{:S(2)}) collective-permute-start(f32[2,2,384,128]{3,2,1,0:T(8,128)} %copy-done.6), channel_id=1, source_target_pairs={{0,96},{16,112},{32,0},{48,16},{64,32},{80,48},{96,64},{112,80},{1... | collective-permute-start | bytes 2359304 | tf_op jit(solution)/shard_map/ppermute | solution.py:458
  60.8 13.9 %all-to-all-start.2 = ((f32[16,3,8,128]{3,2,1,0:T(8,128)}), f32[16,3,8,128]{3,2,1,0:T(8,128)}, u32[]{:S(2)}, u32[]{:S(2)}) async-start(f32[16,3,8,128]{3,2,1,0:T(8,128)} %broadcast_in_dim.2), calls=%async_computation.2 | async-start | bytes 393216 | tf_op jit(solution)/shard_map/all_to_all | solution.py:440
  69.1 17.4 %collective-permute-start.7 = (f32[2,384,128]{2,1,0:T(8,128)}, f32[2,384,128]{2,1,0:T(8,128)S(1)}, u32[]{:S(2)}, u32[]{:S(2)}) collective-permute-start(f32[2,384,128]{2,1,0:T(8,128)} %get-tuple-element.72), channel_id=1, source_target_pairs={{0,32},{16,48},{32,64},{48,80},{64,96},{80,112},{96,0},{112,16},{1... | collective-permute-start | bytes 1179656 | tf_op jit(solution)/shard_map/ppermute | solution.py:465
  70.7 18.1 %collective-permute-start.8 = (f32[2,384,128]{2,1,0:T(8,128)}, f32[2,384,128]{2,1,0:T(8,128)S(1)}, u32[]{:S(2)}, u32[]{:S(2)}) collective-permute-start(f32[2,384,128]{2,1,0:T(8,128)} %get-tuple-element.73), channel_id=1, source_target_pairs={{0,64},{16,80},{32,96},{48,112},{64,0},{80,16},{96,32},{112,48},{1... | collective-permute-start | bytes 1179656 | tf_op jit(solution)/shard_map/ppermute | solution.py:465
  72.1 18.6 %collective-permute-start.9 = (f32[2,384,128]{2,1,0:T(8,128)}, f32[2,384,128]{2,1,0:T(8,128)S(1)}, u32[]{:S(2)}, u32[]{:S(2)}) collective-permute-start(f32[2,384,128]{2,1,0:T(8,128)} %get-tuple-element.74), channel_id=1, source_target_pairs={{0,96},{16,112},{32,0},{48,16},{64,32},{80,48},{96,64},{112,80},{1... | collective-permute-start | bytes 1179656 | tf_op jit(solution)/shard_map/ppermute | solution.py:465
  78.7 15.7 %collective-permute-start.3 = (f32[256,256]{1,0:T(8,128)S(1)}, f32[256,256]{1,0:T(8,128)S(1)}, u32[]{:S(2)}, u32[]{:S(2)}) collective-permute-start(f32[256,256]{1,0:T(8,128)S(1)} %get-tuple-element.62.weights_ref.own_ref), channel_id=1, source_target_pairs={{0,16},{16,0},{32,48},{48,32},{64,80},{80,64},{96,112},{112,96},{1... | collective-permute-start | bytes 786440 | tf_op jit(solution)/shard_map/ppermute | solution.py:430
  82.9 15.5 %collective-permute-start.2 = (f32[256,128]{1,0:T(8,128)S(1)}, f32[256,128]{1,0:T(8,128)S(1)}, u32[]{:S(2)}, u32[]{:S(2)}) collective-permute-start(f32[256,128]{1,0:T(8,128)S(1)} %get-tuple-element.65), channel_id=1, source_target_pairs={{16,48},{48,80},{80,112},{112,16},{17,49},{49,81},{81,113},{113,17... | collective-permute-start | bytes 393224 | tf_op jit(solution)/shard_map/ppermute | solution.py:444
  86.5 11.9 %collective-permute-start.1 = (f32[256,128]{1,0:T(8,128)S(1)}, f32[256,128]{1,0:T(8,128)S(1)}, u32[]{:S(2)}, u32[]{:S(2)}) collective-permute-start(f32[256,128]{1,0:T(8,128)S(1)} %get-tuple-element.65), channel_id=1, source_target_pairs={{16,32},{48,64},{80,96},{112,0},{17,33},{49,65},{81,97},{113,1},{1... | collective-permute-start | bytes 393224 | tf_op jit(solution)/shard_map/ppermute | solution.py:444
  88.8 19.8 %collective-permute-start.22 = (f32[256,128]{1,0:T(8,128)S(1)}, f32[256,128]{1,0:T(8,128)S(1)}, u32[]{:S(2)}, u32[]{:S(2)}) collective-permute-start(f32[256,128]{1,0:T(8,128)S(1)} %get-tuple-element.87), channel_id=1, source_target_pairs={{16,48},{48,80},{80,112},{112,16},{17,49},{49,81},{81,113},{113,17... | collective-permute-start | bytes 393224 | tf_op jit(solution)/shard_map/ppermute | solution.py:444
  90.7 17.8 %collective-permute-start.21 = (f32[256,128]{1,0:T(8,128)S(1)}, f32[256,128]{1,0:T(8,128)S(1)}, u32[]{:S(2)}, u32[]{:S(2)}) collective-permute-start(f32[256,128]{1,0:T(8,128)S(1)} %get-tuple-element.87), channel_id=1, source_target_pairs={{16,32},{48,64},{80,96},{112,0},{17,33},{49,65},{81,97},{113,1},{1... | collective-permute-start | bytes 393224 | tf_op jit(solution)/shard_map/ppermute | solution.py:444
  102.2 5.7 %collective-permute-start = (f32[128,128]{1,0:T(8,128)S(1)}, f32[128,128]{1,0:T(8,128)S(1)}, u32[]{:S(2)}, u32[]{:S(2)}) collective-permute-start(f32[128,128]{1,0:T(8,128)S(1)} %get-tuple-element.64), channel_id=1, source_target_pairs={{0,16},{16,32},{32,48},{48,64},{64,80},{80,96},{96,112},{112,0},{1... | collective-permute-start | bytes 196616 | tf_op jit(solution)/shard_map/ppermute | solution.py:474
  104.1 6.3 %collective-permute-start.13 = (f32[128,128]{1,0:T(8,128)S(1)}, f32[128,128]{1,0:T(8,128)S(1)}, u32[]{:S(2)}, u32[]{:S(2)}) collective-permute-start(f32[128,128]{1,0:T(8,128)S(1)} %add.46), channel_id=1, source_target_pairs={{0,3},{1,0},{2,1},{3,2},{4,7},{5,4},{6,5},{7,6},{8,11},{9,8},{10,9... | collective-permute-start | bytes 196616 | tf_op jit(solution)/shard_map/ppermute | solution.py:434
  107.9 5.8 %collective-permute-start.11 = (f32[128,128]{1,0:T(8,128)S(1)}, f32[128,128]{1,0:T(8,128)S(1)}, u32[]{:S(2)}, u32[]{:S(2)}) collective-permute-start(f32[128,128]{1,0:T(8,128)S(1)} %add.46), channel_id=1, source_target_pairs={{0,1},{1,2},{2,3},{3,0},{4,5},{5,6},{6,7},{7,4},{8,9},{9,10},{10,1... | collective-permute-start | bytes 196616 | tf_op jit(solution)/shard_map/ppermute | solution.py:434
  110.3 28.9 %collective-permute-start.23 = (f32[4,400,128]{2,1,0:T(8,128)S(1)}, f32[4,400,128]{2,1,0:T(8,128)S(1)}, u32[]{:S(2)}, u32[]{:S(2)}) collective-permute-start(f32[4,400,128]{2,1,0:T(8,128)S(1)} %get-tuple-element.89), channel_id=1, source_target_pairs={{0,32},{16,48},{32,64},{48,80},{64,96},{80,112},{96,0},{112,16},{1... | collective-permute-start | bytes 2457608 | tf_op jit(solution)/shard_map/ppermute | solution.py:481
  116.4 5.0 %collective-permute-start.14 = (f32[128,128]{1,0:T(8,128)S(1)}, f32[128,128]{1,0:T(8,128)S(1)}, u32[]{:S(2)}, u32[]{:S(2)}) collective-permute-start(f32[128,128]{1,0:T(8,128)S(1)} %add_add_fusion.2.refs_2_), channel_id=1, source_target_pairs={{0,4},{1,5},{2,6},{3,7},{4,8},{5,9},{6,10},{7,11},{8,12},{9,13},{1... | collective-permute-start | bytes 196616 | tf_op jit(solution)/shard_map/ppermute | solution.py:435
  124.1 8.7 %collective-permute-start.20 = (f32[256,256]{1,0:T(8,128)S(1)}, f32[256,256]{1,0:T(8,128)S(1)}, u32[]{:S(2)}, u32[]{:S(2)}) collective-permute-start(f32[256,256]{1,0:T(8,128)S(1)} %get-tuple-element.78.weights_ref.own_ref), channel_id=1, source_target_pairs={{0,16},{16,0},{32,48},{48,32},{64,80},{80,64},{96,112},{112,96},{1... | collective-permute-start | bytes 786440 | tf_op jit(solution)/shard_map/ppermute | solution.py:430
  126.1 13.1 %collective-permute-start.19 = (f32[256,128]{1,0:T(8,128)S(1)}, f32[256,128]{1,0:T(8,128)S(1)}, u32[]{:S(2)}, u32[]{:S(2)}) collective-permute-start(f32[256,128]{1,0:T(8,128)S(1)} %get-tuple-element.81), channel_id=1, source_target_pairs={{16,48},{48,80},{80,112},{112,16},{17,49},{49,81},{81,113},{113,17... | collective-permute-start | bytes 393224 | tf_op jit(solution)/shard_map/ppermute | solution.py:444
  128.4 10.8 %collective-permute-start.18 = (f32[256,128]{1,0:T(8,128)S(1)}, f32[256,128]{1,0:T(8,128)S(1)}, u32[]{:S(2)}, u32[]{:S(2)}) collective-permute-start(f32[256,128]{1,0:T(8,128)S(1)} %get-tuple-element.81), channel_id=1, source_target_pairs={{16,32},{48,64},{80,96},{112,0},{17,33},{49,65},{81,97},{113,1},{1... | collective-permute-start | bytes 393224 | tf_op jit(solution)/shard_map/ppermute | solution.py:444
  129.7 16.7 %collective-permute-start.36 = (f32[256,128]{1,0:T(8,128)S(1)}, f32[256,128]{1,0:T(8,128)S(1)}, u32[]{:S(2)}, u32[]{:S(2)}) collective-permute-start(f32[256,128]{1,0:T(8,128)S(1)} %get-tuple-element.102), channel_id=1, source_target_pairs={{16,48},{48,80},{80,112},{112,16},{17,49},{49,81},{81,113},{113,17... | collective-permute-start | bytes 393224 | tf_op jit(solution)/shard_map/ppermute | solution.py:444
  132.9 13.6 %collective-permute-start.35 = (f32[256,128]{1,0:T(8,128)S(1)}, f32[256,128]{1,0:T(8,128)S(1)}, u32[]{:S(2)}, u32[]{:S(2)}) collective-permute-start(f32[256,128]{1,0:T(8,128)S(1)} %get-tuple-element.102), channel_id=1, source_target_pairs={{16,32},{48,64},{80,96},{112,0},{17,33},{49,65},{81,97},{113,1},{1... | collective-permute-start | bytes 393224 | tf_op jit(solution)/shard_map/ppermute | solution.py:444
  145.3 5.0 %collective-permute-start.26 = (f32[128,128]{1,0:T(8,128)S(1)}, f32[128,128]{1,0:T(8,128)S(1)}, u32[]{:S(2)}, u32[]{:S(2)}) collective-permute-start(f32[128,128]{1,0:T(8,128)S(1)} %add.50), channel_id=1, source_target_pairs={{0,2},{1,3},{2,0},{3,1},{4,6},{5,7},{6,4},{7,5},{8,10},{9,11},{10,... | collective-permute-start | bytes 196616 | tf_op jit(solution)/shard_map/ppermute | solution.py:434
  148.2 24.2 %collective-permute-start.37 = (f32[4,400,128]{2,1,0:T(8,128)S(1)}, f32[4,400,128]{2,1,0:T(8,128)S(1)}, u32[]{:S(2)}, u32[]{:S(2)}) collective-permute-start(f32[4,400,128]{2,1,0:T(8,128)S(1)} %get-tuple-element.104), channel_id=1, source_target_pairs={{0,32},{16,48},{32,64},{48,80},{64,96},{80,112},{96,0},{112,16},{1... | collective-permute-start | bytes 2457608 | tf_op jit(solution)/shard_map/ppermute | solution.py:481
  151.9 5.0 %collective-permute-start.28 = (f32[128,128]{1,0:T(8,128)S(1)}, f32[128,128]{1,0:T(8,128)S(1)}, u32[]{:S(2)}, u32[]{:S(2)}) collective-permute-start(f32[128,128]{1,0:T(8,128)S(1)} %add_add_fusion.1.refs_2_), channel_id=1, source_target_pairs={{0,4},{1,5},{2,6},{3,7},{4,8},{5,9},{6,10},{7,11},{8,12},{9,13},{1... | collective-permute-start | bytes 196616 | tf_op jit(solution)/shard_map/ppermute | solution.py:435
  160.0 7.3 %collective-permute-start.34 = (f32[256,256]{1,0:T(8,128)S(1)}, f32[256,256]{1,0:T(8,128)S(1)}, u32[]{:S(2)}, u32[]{:S(2)}) collective-permute-start(f32[256,256]{1,0:T(8,128)S(1)} %get-tuple-element.93.weights_ref.own_ref), channel_id=1, source_target_pairs={{0,16},{16,0},{32,48},{48,32},{64,80},{80,64},{96,112},{112,96},{1... | collective-permute-start | bytes 786440 | tf_op jit(solution)/shard_map/ppermute | solution.py:430
  164.0 8.3 %collective-permute-start.33 = (f32[256,128]{1,0:T(8,128)S(1)}, f32[256,128]{1,0:T(8,128)S(1)}, u32[]{:S(2)}, u32[]{:S(2)}) collective-permute-start(f32[256,128]{1,0:T(8,128)S(1)} %get-tuple-element.96), channel_id=1, source_target_pairs={{16,48},{48,80},{80,112},{112,16},{17,49},{49,81},{81,113},{113,17... | collective-permute-start | bytes 393224 | tf_op jit(solution)/shard_map/ppermute | solution.py:444
  166.0 6.4 %collective-permute-start.32 = (f32[256,128]{1,0:T(8,128)S(1)}, f32[256,128]{1,0:T(8,128)S(1)}, u32[]{:S(2)}, u32[]{:S(2)}) collective-permute-start(f32[256,128]{1,0:T(8,128)S(1)} %get-tuple-element.96), channel_id=1, source_target_pairs={{16,32},{48,64},{80,96},{112,0},{17,33},{49,65},{81,97},{113,1},{1... | collective-permute-start | bytes 393224 | tf_op jit(solution)/shard_map/ppermute | solution.py:444
  185.6 12.8 %collective-permute-start.45 = (f32[4,400,128]{2,1,0:T(8,128)S(1)}, f32[4,400,128]{2,1,0:T(8,128)S(1)}, u32[]{:S(2)}, u32[]{:S(2)}) collective-permute-start(f32[4,400,128]{2,1,0:T(8,128)S(1)} %get-tuple-element.112), channel_id=1, source_target_pairs={{0,16},{16,0},{32,48},{48,32},{64,80},{80,64},{96,112},{112,96},{1... | collective-permute-start | bytes 2457608 | tf_op jit(solution)/shard_map/ppermute | solution.py:430
  187.1 11.3 %collective-permute-start.46 = (f32[4,400,128]{2,1,0:T(8,128)S(1)}, f32[4,400,128]{2,1,0:T(8,128)S(1)}, u32[]{:S(2)}, u32[]{:S(2)}) collective-permute-start(f32[4,400,128]{2,1,0:T(8,128)S(1)} %get-tuple-element.113), channel_id=1, source_target_pairs={{0,16},{16,0},{32,48},{48,32},{64,80},{80,64},{96,112},{112,96},{1... | collective-permute-start | bytes 2457608 | tf_op jit(solution)/shard_map/ppermute | solution.py:430
  190.2 5.0 %collective-permute-start.42 = (f32[128,128]{1,0:T(8,128)S(1)}, f32[128,128]{1,0:T(8,128)S(1)}, u32[]{:S(2)}, u32[]{:S(2)}) collective-permute-start(f32[128,128]{1,0:T(8,128)S(1)} %add_add_fusion.refs_2_.before_ref), channel_id=1, source_target_pairs={{0,4},{1,5},{2,6},{3,7},{4,8},{5,9},{6,10},{7,11},{8,12},{9,13},{1... | collective-permute-start | bytes 196616 | tf_op jit(solution)/shard_map/ppermute | solution.py:435
  (26 other events, 106.5 us)

commit v4 on v3

v4 whole, which is shorter than its diff:
```python
import functools

import jax
import jax.numpy as jnp
from jax import lax
from jax.experimental import pallas as pl
from jax.experimental.pallas import tpu as pltpu
from jax.sharding import PartitionSpec as P

ROUNDS = 4
BLOCK = 128
PAIR = 256
SIDE = 4
ROWS = 16
COLS = 8
F32 = jnp.float32
BF16 = jnp.bfloat16
VMEM_LIMIT = 16 * 1024 * 1024

TURN_CORE = [(c, c ^ 1) for c in range(COLS)]
NEXT_SLOT = [(c, (c + 1) % COLS) for c in range(COLS)]
CHIPS_ON = [[(c, (c + 2 * k) % COLS) for c in range(COLS)] for k in range(SIDE)]
ODD_TO_EVEN = [(c, (c + 1) % COLS) for c in range(1, COLS, 2)]
ODD_TO_ODD = [(c, (c + 2) % COLS) for c in range(1, COLS, 2)]
ALONG_X = [[(r, r - r % SIDE + (r + k) % SIDE) for r in range(ROWS)] for k in range(1, SIDE)]
ALONG_Z = [[(r, (r + SIDE * k) % ROWS) for r in range(ROWS)] for k in range(1, SIDE)]


def mm(left, right):
    return jnp.dot(left, right, precision=lax.Precision.HIGHEST, preferred_element_type=F32)


def mm_t(left, right):
    return lax.dot_general(
        left, right, (((0,), (0,)), ((), ())), precision=lax.Precision.HIGHEST, preferred_element_type=F32
    )


def parts_of(value):
    high = value.astype(BF16)
    return high, (value - high.astype(F32)).astype(BF16)


def dot(left, right, axis):
    return lax.dot_general(left, right, (((axis,), (0,)), ((), ())), preferred_element_type=F32)


def mm3(left, right, axis=1):
    high, low = parts_of(left)
    right_high, right_low = parts_of(right)
    width = right.shape[1]
    if width < PAIR:
        both = dot(high, jnp.concatenate([right_high, right_low], axis=1), axis)
        return both[:, :width] + (both[:, width:] + dot(low, right_high, axis))
    return dot(high, right_high, axis) + (dot(high, right_low, axis) + dot(low, right_high, axis))


def call(kernel, grid, in_specs, out_specs, out_shape, scalars=0, scratch=(), flops=0, nbytes=0):
    return pl.pallas_call(
        kernel,
        grid_spec=pltpu.PrefetchScalarGridSpec(
            num_scalar_prefetch=scalars,
            grid=grid,
            in_specs=in_specs,
            out_specs=out_specs,
            scratch_shapes=list(scratch),
        ),
        out_shape=out_shape,
        compiler_params=pltpu.CompilerParams(vmem_limit_bytes=VMEM_LIMIT),
        cost_estimate=pl.CostEstimate(flops=flops, bytes_accessed=nbytes, transcendentals=0),
    )


def call_whole(kernel, args, out_shape, before=(), scratch=(), flops=0, nbytes=0):
    inner = kernel
    if before:
        inner = lambda *refs: kernel(*refs[: len(args)], *refs[len(args) + len(before):])
    return pl.pallas_call(
        inner,
        in_specs=[pl.BlockSpec(memory_space=pltpu.SMEM)]
        + [pl.BlockSpec(memory_space=pltpu.VMEM)] * (len(args) - 1)
        + [pl.BlockSpec(memory_space=pl.ANY)] * len(before),
        out_specs=[pl.BlockSpec(memory_space=pltpu.VMEM)] * len(out_shape),
        out_shape=out_shape,
        scratch_shapes=list(scratch),
        compiler_params=pltpu.CompilerParams(vmem_limit_bytes=VMEM_LIMIT),
        cost_estimate=pl.CostEstimate(flops=flops, bytes_accessed=nbytes, transcendentals=0),
    )(*args, *before)


def shape(*dims):
    return jax.ShapeDtypeStruct(dims, F32)


def whole(*dims):
    return pl.BlockSpec(dims, lambda *_: (0,) * len(dims))


def pack_main_kernel(info_ref, *refs):
    for x_ref, out_ref in zip(refs[:SIDE], refs[SIDE:]):
        out_ref[0, 0] = x_ref[:, :BLOCK]
        out_ref[0, 1] = x_ref[:, BLOCK:]


def pack_main(info, x):
    rows = x.shape[0]

    def columns(k):
        return pl.BlockSpec((rows, PAIR), lambda j, c: (0, 2 * ((c[1] + k) % SIDE) + j))

    return call(
        pack_main_kernel,
        (2,),
        [columns(k) for k in range(SIDE)],
        [pl.BlockSpec((1, 2, rows, BLOCK), lambda j, c: (j, 0, 0, 0))] * SIDE,
        [shape(2, 2, rows, BLOCK)] * SIDE,
        scalars=1,
        nbytes=8 * SIDE * rows * 2 * PAIR,
    )(info, *[x] * SIDE)


def pack_ahead_kernel(info_ref, *refs):
    parts_ref, shares_ref = refs[SIDE], refs[-1]
    shares_ref[...] = jnp.broadcast_to(jnp.sum(parts_ref[...], axis=0)[None], shares_ref.shape)
    for x_ref, out_ref in zip(refs[:SIDE], refs[SIDE + 1:]):
        out_ref[0] = x_ref[:, :BLOCK]
        out_ref[1] = x_ref[:, BLOCK:]


def pack_ahead(info, x, parts):
    rows = x.shape[0]
    shares = (ROWS,) + parts.shape[1:]

    def columns(k):
        return pl.BlockSpec((rows, PAIR), lambda i, c: (0, (2 * ((c[1] + k) % SIDE) + COLS - 1) % COLS))

    return call(
        pack_ahead_kernel,
        (1,),
        [columns(k) for k in range(SIDE)] + [whole(*parts.shape)],
        [whole(2, rows, BLOCK)] * SIDE + [whole(*shares)],
        [shape(2, rows, BLOCK)] * SIDE + [shape(*shares)],
        scalars=1,
        nbytes=8 * SIDE * rows * PAIR,
    )(info, *[x] * SIDE, parts)


def gram_kernel(x_ref, before_ref, out_ref):
    high, low = parts_of(x_ref[...])
    mixed = dot(high, low, 0)
    gram = dot(high, high, 0) + (mixed + mixed.T)
    for k, block in enumerate((gram[:BLOCK, :BLOCK], gram[:BLOCK, BLOCK:], gram[BLOCK:, BLOCK:])):
        out_ref[:, 0, k] = block.reshape(ROWS, BLOCK // ROWS, BLOCK)


def row_grams(x, before):
    rows = x.shape[0]
    return call(
        gram_kernel,
        (COLS,),
        [pl.BlockSpec((rows, PAIR), lambda s: (0, s)), pl.BlockSpec(memory_space=pl.ANY)],
        pl.BlockSpec((ROWS, 1, 3, BLOCK // ROWS, BLOCK), lambda s: (0, s, 0, 0, 0)),
        shape(ROWS, COLS, 3, BLOCK // ROWS, BLOCK),
        flops=2 * 2 * COLS * rows * PAIR * PAIR,
        nbytes=4 * COLS * (rows * PAIR + PAIR * PAIR),
    )(x, before)


def sum_kernel(info_ref, parts_ref, out_ref):
    out_ref[...] = jnp.sum(parts_ref[...], axis=0)


def sum_parts(info, parts, before):
    return call_whole(sum_kernel, (info, parts), [shape(*parts.shape[1:])], before, nbytes=4 * parts.size)[0]


def rotation_of(gram, x_ref, r_ref):
    rows = lax.broadcasted_iota(jnp.int32, (PAIR, PAIR), 0)
    columns = lax.broadcasted_iota(jnp.int32, (PAIR, PAIR), 1)
    eye = (rows == columns).astype(F32)
    on_diagonal = gram * eye
    across = jnp.sum(on_diagonal, axis=0, keepdims=True)
    down = jnp.sum(on_diagonal, axis=1, keepdims=True)
    spread = across - down
    totals = across + down
    skew = gram * spread / (2.0 * spread * spread + 0.5 * totals * totals)
    square = mm3(skew, skew)
    bound = jnp.max(jnp.sum(jnp.abs(square), axis=0))
    scale = 2.0 / (2.0 + bound)
    x_ref[...] = scale * (eye + skew)
    r_ref[...] = (1.0 - scale) * eye + scale * square

    def step(size):
        left = r_ref[...]
        x = x_ref[...]
        x_ref[...] = x + mm3(x, left)
        r_ref[...] = mm3(left, left)
        return size * size

    lax.while_loop(lambda size: size > 3e-4, step, bound / (2.0 + bound))
    x = x_ref[...]
    x = x + mm3(x, eye - x + mm3(skew, x))
    return 2.0 * x - eye


def cayley_kernel(fill, info_ref, *refs):
    weights_ref, up_ref, low_ref, gram_ref, x_ref, r_ref = refs[-6:]
    up, cross, low = fill(*refs[:-6])
    gram_ref[:BLOCK, :BLOCK] = up
    gram_ref[:BLOCK, BLOCK:] = cross
    gram_ref[BLOCK:, :BLOCK] = cross.T
    gram_ref[BLOCK:, BLOCK:] = low
    weights = rotation_of(gram_ref[...], x_ref, r_ref)
    weights_ref[...] = weights
    up_ref[...] = weights[:, :BLOCK]
    low_ref[...] = weights[:, BLOCK:]


def cayley_call(fill, args):
    return call_whole(
        functools.partial(cayley_kernel, fill),
        args,
        [shape(PAIR, PAIR), shape(PAIR, BLOCK), shape(PAIR, BLOCK), shape(PAIR, PAIR)],
        scratch=[pltpu.VMEM((PAIR, PAIR), F32)] * 2,
        flops=2 * 3 * 8 * PAIR**3,
        nbytes=20 * PAIR * PAIR,
    )


def first_cayley(info, blocks):
    return cayley_call(lambda ref: [ref[:, k].reshape(BLOCK, BLOCK) for k in range(3)], (info, blocks))


def cayley(info, up, low, parts):
    def fill(up_ref, low_ref, *part_refs):
        first, second, third, fourth = (ref[...] for ref in part_refs)
        return up_ref[...], (first + second) + (third + fourth), low_ref[...]

    return cayley_call(fill, (info, up, low, *parts))


def project_kernel(info_ref, gram_ref, weights_ref, up_ref, low_ref):
    weights = weights_ref[...]
    turned = mm3(gram_ref[...], weights)
    up_ref[...] = mm3(weights[:, :BLOCK], turned[:, :BLOCK], 0)
    low_ref[...] = mm3(weights[:, BLOCK:], turned[:, BLOCK:], 0)


def project(info, gram, weights):
    out = [shape(BLOCK, BLOCK)] * 2
    return call_whole(project_kernel, (info, gram, weights), out, flops=2 * 3 * 2 * PAIR**3, nbytes=12 * PAIR * PAIR)


def start_pair(info_ref, step, group, slot, up, low):
    share = step - up.shape[0]
    column = slot * PAIR - info_ref[2] - share * group
    rows = lax.broadcasted_iota(jnp.int32, (share, PAIR), 0)
    columns = lax.broadcasted_iota(jnp.int32, (share, PAIR), 1)
    basis = (rows == columns + column).astype(F32)
    return jnp.concatenate([jnp.concatenate([up, low], axis=1), basis], axis=0)


def groups_of(info_ref, step, refs, slots):
    if refs[0].shape[0] == SIDE:
        for group in range(SIDE):
            pairs = [(refs[2 * j][group], refs[2 * j + 1][group]) for j in range(len(slots))]
            yield group, [jnp.concatenate(pair, axis=1) for pair in pairs]
    else:
        for k, ref in enumerate(refs):
            group = lax.rem(info_ref[1] + SIDE - k, SIDE)
            yield group, [start_pair(info_ref, step, group, slot, ref[j, 0], ref[j, 1]) for j, slot in enumerate(slots)]


def own_kernel(rows, step, info_ref, own_ref, other_ref, *refs):
    up0_ref, up1_ref, low1_ref, cross_ref = refs[-4:]
    first = info_ref[0] == 0
    weights0 = jnp.where(first, own_ref[...], other_ref[...])
    weights1 = jnp.where(first, other_ref[:, :BLOCK], own_ref[:, :BLOCK])
    slot = 2 * info_ref[1]
    cross = jnp.zeros((BLOCK, BLOCK), F32)
    for group, (pair0, pair1) in groups_of(info_ref, step, refs[:-4], (slot, slot + 1)):
        turned = mm3(pair0, weights0)
        up1 = mm3(pair1, weights1)
        up0_ref[group] = turned[:, :BLOCK]
        low1_ref[group] = turned[:, BLOCK:]
        up1_ref[group] = up1
        cross = cross + mm3(up1[:rows], turned[:rows, BLOCK:], 0)
    cross_ref[...] = cross


def rotate_own(info, own, other, blocks, before, rows, step):
    return call_whole(
        functools.partial(own_kernel, rows, step),
        (info, own, other, *blocks),
        [shape(SIDE, step, BLOCK)] * 3 + [shape(BLOCK, BLOCK)],
        before,
        flops=2 * 3 * SIDE * step * 4 * BLOCK * PAIR,
        nbytes=4 * 7 * SIDE * step * BLOCK,
    )


def ahead_kernel(rows, step, info_ref, even_ref, odd_ref, upper_ref, cross_ref, up0_ref, *refs):
    low0_ref, keep_ref, send_ref, upper_out_ref = refs[-4:]
    upper_out_ref[...] = upper_ref[...]
    weights = even_ref[...] + odd_ref[...]
    slot = (2 * info_ref[1] + COLS - 1) % COLS
    total = jnp.zeros((BLOCK, BLOCK), F32)
    for group, (pair,) in groups_of(info_ref, step, refs[:-4], (slot,)):
        low0 = mm3(pair, weights)
        low0_ref[group] = low0
        total = total + mm3(up0_ref[group, :rows], low0[:rows], 0)
    first = info_ref[0] == 0
    keep_ref[...] = jnp.where(first, total, cross_ref[...])
    send_ref[...] = jnp.where(first, cross_ref[...], total)


def rotate_ahead(info, lower, upper, cross, up0, blocks, rows, step):
    return call_whole(
        functools.partial(ahead_kernel, rows, step),
        (info, *lower, upper, cross, up0, *blocks),
        [shape(SIDE, step, BLOCK)] + [shape(BLOCK, BLOCK)] * 2 + [shape(PAIR, BLOCK)],
        flops=2 * 3 * SIDE * step * 2 * BLOCK * PAIR,
        nbytes=4 * 4 * SIDE * step * BLOCK,
    )


def up_kernel(step, info_ref, even_ref, odd_ref, low1_ref, *refs):
    up_ref, pass_ref = refs[-2:]
    weights = even_ref[...] + odd_ref[...]
    slot = (2 * info_ref[1] + COLS - 1) % COLS
    for group, (pair,) in groups_of(info_ref, step, refs[:-2], (slot,)):
        up_ref[group] = mm3(pair, weights)
    pass_ref[...] = low1_ref[...]


def rotate_up(info, upper, low1, blocks, before, step):
    return call_whole(
        functools.partial(up_kernel, step),
        (info, *upper, low1, *blocks),
        [shape(SIDE, step, BLOCK)] * 2,
        before,
        flops=2 * 3 * SIDE * step * BLOCK * PAIR,
        nbytes=4 * 5 * SIDE * step * BLOCK,
    )


def other_slot_kernel(info_ref, up0_ref, low0_ref, up1_ref, low1_ref, up_ref, low_ref):
    first = info_ref[0] == 0
    up_ref[...] = jnp.where(first, up1_ref[...], up0_ref[...])
    low_ref[...] = jnp.where(first, low1_ref[...], low0_ref[...])


def other_slot(info, blocks, before):
    return call_whole(other_slot_kernel, (info, *blocks), [shape(*blocks[0].shape)] * 2, before, nbytes=24 * blocks[0].size)


def final_kernel(rows, total, info_ref, weights_ref, gram_ref, up0_ref, low0_ref, up1_ref, low1_ref, ru_ref, rl_ref,
                 out_ref, frame_ref, scale_ref):
    weights = weights_ref[...]
    first = info_ref[0] == 0
    i = pl.program_id(0)
    up = jnp.where(first, up0_ref[i], up1_ref[i])
    low = jnp.where(first, low0_ref[i], low1_ref[i])
    mine = mm3(jnp.concatenate([up, low], axis=1), weights)
    theirs = mm3(jnp.concatenate([ru_ref[i], rl_ref[i]], axis=1), weights)
    for k, turned in enumerate((jnp.where(first, mine, theirs), jnp.where(first, theirs, mine))):
        out_ref[k] = turned[:rows]
        frame_ref[k] = turned[rows:]

    @pl.when(i == 0)
    def _():
        squares = jnp.sum(weights * mm3(gram_ref[...], weights), axis=0, keepdims=True)
        scale_ref[...] = jnp.sqrt(squares / total)


def rotate_final(info, weights, gram, blocks, rows, step):
    share = step - rows
    return call(
        functools.partial(final_kernel, rows, float(rows * COLS * ROWS)),
        (SIDE,),
        [pl.BlockSpec(memory_space=pltpu.VMEM)] * 8,
        [
            pl.BlockSpec((2, rows, PAIR), lambda i, c: (i, 0, 0)),
            pl.BlockSpec((2, share, PAIR), lambda i, c: (0, i, 0)),
            whole(1, PAIR),
        ],
        [shape(COLS, rows, PAIR), shape(2, SIDE * share, PAIR), shape(1, PAIR)],
        scalars=1,
        flops=2 * 3 * 2 * SIDE * step * PAIR * PAIR,
        nbytes=4 * 4 * SIDE * step * PAIR,
    )(info, weights, gram, *blocks)


def swap_core(value):
    return lax.ppermute(value, "cols", TURN_CORE)


def sum_over_rows(value):
    value = value + sum(lax.ppermute(value, "rows", pairs) for pairs in ALONG_X)
    return [value] + [lax.ppermute(value, "rows", pairs) for pairs in ALONG_Z]


def to_next_chip(value):
    return [lax.ppermute(value, "cols", pairs) for pairs in (ODD_TO_EVEN, ODD_TO_ODD)]


def body(sensitivity):
    x = sensitivity[0]
    rows = x.shape[0]
    column = lax.axis_index("cols")
    parity = column % 2
    basis_rows = x.shape[1] // ROWS // 2
    basis_at = (lax.axis_index("rows") * 2 + parity) * basis_rows
    info = jnp.stack([parity, column // 2, basis_at]).astype(jnp.int32)
    step = rows + basis_rows // SIDE

    packed = pack_main(info, x)
    main = [packed[0]] + [lax.ppermute(packed[k], "cols", CHIPS_ON[k]) for k in range(1, SIDE)]

    parts = lax.all_to_all(row_grams(x, packed[0]), "rows", 0, 0, tiled=True)
    parts = lax.all_to_all(sum_parts(info, parts, main[1:]), "cols", 0, 0, tiled=True)
    *packed, shares = pack_ahead(info, x, parts)
    ahead = [packed[0]] + [lax.ppermute(packed[k], "cols", CHIPS_ON[k]) for k in range(1, SIDE)]
    weights, upper, lower, gram = first_cayley(info, lax.all_to_all(shares, "rows", 0, 0, tiled=True))

    own_blocks = main
    ahead_blocks = [value[None] for value in ahead]
    for sweep_round in range(ROUNDS - 1):
        lower = to_next_chip(lower)
        other = swap_core(weights)
        up, low = project(info, gram, weights)
        up0, up1, low1, cross = rotate_own(info, weights, other, own_blocks, [up], rows, step)
        low = lax.ppermute(low, "cols", NEXT_SLOT)
        low0, keep, send, upper = rotate_ahead(info, lower, upper, cross, up0, ahead_blocks, rows, step)
        parts = sum_over_rows(keep + swap_core(send))
        own_blocks = [up0, low0, up1, low1]
        if sweep_round < ROUNDS - 2:
            up_m, passed = rotate_up(info, to_next_chip(upper), low1, ahead_blocks, [low], step)
            ahead_blocks = [up_m, lax.ppermute(passed, "cols", CHIPS_ON[1])]
        else:
            received = [swap_core(value) for value in other_slot(info, own_blocks, [parts[0]])]
        weights, upper, lower, gram = cayley(info, up, low, parts)

    rotated, frame, column_scale = rotate_final(info, weights, gram, own_blocks + received, rows, step)
    return rotated, frame.reshape(2 * basis_rows, PAIR), column_scale.reshape(PAIR)


def solution(mesh):
    in_specs = (P("cols", "rows", None),)
    out_specs = (P(None, "rows", "cols"), P("rows", "cols"), P("cols"))
    return jax.shard_map(body, mesh=mesh, in_specs=in_specs, out_specs=out_specs, check_vma=False)
```

time: 206 us -> 218 us (1.058)
  waiting for transfers between devices: 44.6 us -> 69.6 us
  Pallas kernels: 54.1 us -> 41.8 us
  starting transfers between devices: 78.3 us -> 67.2 us
  blocking collectives: 15.4 us -> 23.5 us
  local copies, waits for them, and re-layouts: 5.4 us -> 12.7 us
  other arithmetic: 3.75 us -> 0.15 us
    ppermute x6, waiting for transfers between devices: 1 us -> 31.7 us  [body(): lax.ppermute(packed[k], 'cols', CHIPS_ON[k])]
    all_to_all x1, waiting for transfers between devices: 17.9 us -> 0.01 us  [body(): parts = lax.all_to_all(row_grams(x, packed[0]), 'rows', 0, 0, tiled=True)]
    ppermute x10, waiting for transfers between devices: 0.03 us -> 11 us  [to_next_chip(): lax.ppermute(value, 'cols', pairs)]
    pallas_call x17 -> x18, Pallas kernels: 43.5 us -> 32.9 us  [the longest x17 32.2 us: call_whole(): pl.pallas_call(inner, in_specs=[pl.BlockSpec(memory_space=pltpu.SMEM)] +...]
    all_to_all x1 -> x2, blocking collectives: 15.4 us -> 23.5 us  [the longest x1 13.9 us: body(): lax.all_to_all(shares, 'rows', 0, 0, tiled=True)]
    unnamed x18 -> x34, local copies, waits for them, and re-layouts: 4.7 us -> 12.7 us
    all_to_all x1 -> x0, starting transfers between devices: 6.59 us -> none  [spread_over_rows(): return lax.all_to_all(copies, 'rows', 0, 0, tiled=True)]
    ppermute x8, starting transfers between devices: 11 us -> 17.5 us  [swap_core(): return lax.ppermute(value, 'cols', TURN_CORE)]
  transfers between devices with their start and end apart: 49 -> 48, of which waited for: 20 -> 22; matrix products, arithmetic and copies ran while one was open for 2% -> 0% of each run, Pallas kernels for 20% -> 10%
where the time goes in v4:
time: 218 us; the launch traced here: 216 us
  waiting for transfers between devices  69.6 us (32%)
  starting transfers between devices  67.2 us (31%)
  Pallas kernels  41.8 us (19%)
  blocking collectives  23.5 us (11%)
  local copies, waits for them, and re-layouts  12.7 us (6%)
    pallas_call x17, Pallas kernels, call_whole(): pl.pallas_call(inner, in_specs=[pl.BlockSpec(memory_space=pltpu.SMEM)] +...  32.2 us
    ppermute x6, waiting for transfers between devices, body(): lax.ppermute(packed[k], 'cols', CHIPS_ON[k])  31.7 us
    ppermute x10, starting transfers between devices, to_next_chip(): lax.ppermute(value, 'cols', pairs)  17.7 us
    ppermute x8, starting transfers between devices, swap_core(): return lax.ppermute(value, 'cols', TURN_CORE)  17.5 us
    ppermute x9, waiting for transfers between devices, sum_over_rows(): return [value] + [lax.ppermute(value, 'rows', pairs) for pairs in ALONG_Z]  14.2 us
    all_to_all x1, blocking collectives, body(): lax.all_to_all(shares, 'rows', 0, 0, tiled=True)  13.9 us
    unnamed x34, local copies, waits for them, and re-layouts  12.7 us
    ppermute x10, waiting for transfers between devices, to_next_chip(): lax.ppermute(value, 'cols', pairs)  11 us
  transfers between devices with their start and end apart: 48, of which 22 were waited for; matrix products, arithmetic and copies ran while one was open for 0% of the time, Pallas kernels for 10%

profile of v4, /device:TPU:1, one launch (start us, length us, event | category | flops | bytes accessed | tf_op | source)
XLA Modules:
  0.0 216.0 jit_solution(13892218190600357660)
XLA Ops:
  0.7 1.9 copy-done
  6.5 3.5 %shard_map.39 = f32[16,8,3,8,128]{4,3,2,1,0:T(8,128)S(1)} custom-call(f32[384,2048]{1,0:T(8,128)S(1)} %bitcast.14, f32[2,2,384,128]{3,2,1,0:T(8,128)S(1)} %get-tuple-element.64.before_ref.refs_3_), custom_call_target="tpu_custom_call" | custom-call | flops 805306368 | bytes 5242880 | tf_op jit(solution)/shard_map/pallas_call | solution.py:158
  12.1 8.5 %all-to-all-start = ((f32[16,8,3,8,128]{4,3,2,1,0:T(8,128)}), f32[16,8,3,8,128]{4,3,2,1,0:T(8,128)}, u32[]{:S(2)}, u32[]{:S(2)}) async-start(f32[16,8,3,8,128]{4,3,2,1,0:T(8,128)} %copy-done.2), calls=%async_computation | async-start | bytes 3145728 | tf_op jit(solution)/shard_map/all_to_all | solution.py:420
  21.9 2.6 %collective-permute-start.1 = (f32[2,2,384,128]{3,2,1,0:T(8,128)}, f32[2,2,384,128]{3,2,1,0:T(8,128)S(1)}, u32[]{:S(2)}, u32[]{:S(2)}) collective-permute-start(f32[2,2,384,128]{3,2,1,0:T(8,128)} %copy-done.15), channel_id=1, source_target_pairs={{0,64},{16,80},{32,96},{48,112},{64,0},{80,16},{96,32},{112,48},{1... | collective-permute-start | bytes 2359304 | tf_op jit(solution)/shard_map/ppermute | solution.py:418
  25.6 14.7 %collective-permute-done.refs_2_.refs_4_ = f32[2,2,384,128]{3,2,1,0:T(8,128)S(1)} collective-permute-done((f32[2,2,384,128]{3,2,1,0:T(8,128)}, f32[2,2,384,128]{3,2,1,0:T(8,128)S(1)}, u32[]{:S(2)}, u32[]{:S(2)}) %collective-permute-start) | collective-permute-done | bytes 786464 | tf_op jit(solution)/shard_map/ppermute | solution.py:418
  41.1 17.1 %collective-permute-done.1.refs_3_.refs_5_ = f32[2,2,384,128]{3,2,1,0:T(8,128)S(1)} collective-permute-done((f32[2,2,384,128]{3,2,1,0:T(8,128)}, f32[2,2,384,128]{3,2,1,0:T(8,128)S(1)}, u32[]{:S(2)}, u32[]{:S(2)}) %collective-permute-start.1) | collective-permute-done | bytes 786464 | tf_op jit(solution)/shard_map/ppermute | solution.py:418
  64.9 9.6 %all_to_all.15.refs_4_ = f32[8,3,8,128]{3,2,1,0:T(8,128)S(1)} all-to-all(f32[8,3,8,128]{3,2,1,0:T(8,128)S(1)} %shard_map.40), channel_id=1, replica_groups=mesh['cols'=8,'rows'=16] {'cols'}, dimensions={0} | all-to-all | bytes 196608 | tf_op jit(solution)/shard_map/all_to_all | solution.py:421
  75.2 13.9 %all_to_all.16.refs_0_ = f32[16,3,8,128]{3,2,1,0:T(8,128)S(1)} all-to-all(f32[16,3,8,128]{3,2,1,0:T(8,128)S(1)} %get-tuple-element.68), channel_id=1, replica_groups=mesh['cols'=8,'rows'=16] {'rows'}, dimensions={0} | all-to-all | bytes 393216 | tf_op jit(solution)/shard_map/all_to_all | solution.py:424
  89.1 2.6 %shard_map.42 = (f32[256,256]{1,0:T(8,128)S(1)}, f32[256,128]{1,0:T(8,128)S(1)}, f32[256,128]{1,0:T(8,128)S(1)}, f32[256,256]{1,0:T(8,128)S(1)}) custom-call(s32[3]{0:T(128)S(1)} %pad_add_fusion.info_ref.refs_0_, f32[16,3,8,128]{3,2,1,0:T(8,128)S(1)} %all_to_all.16.refs_0_), custom_call_target="tpu_custom_call" | custom-call | flops 805306368 | bytes 1310720 | tf_op jit(solution)/shard_map/pallas_call | solution.py:78
  91.7 2.2 %collective-permute-start.6 = (f32[256,256]{1,0:T(8,128)S(1)}, f32[256,256]{1,0:T(8,128)S(1)}, u32[]{:S(2)}, u32[]{:S(2)}) collective-permute-start(f32[256,256]{1,0:T(8,128)S(1)} %get-tuple-element.70.weights_ref.refs_1_), channel_id=1, source_target_pairs={{0,16},{16,0},{32,48},{48,32},{64,80},{80,64},{96,112},{112,96},{1... | collective-permute-start | bytes 786440 | tf_op jit(solution)/shard_map/ppermute | solution.py:395
  96.7 2.7 %collective-permute-start.5 = (f32[256,128]{1,0:T(8,128)S(1)}, f32[256,128]{1,0:T(8,128)S(1)}, u32[]{:S(2)}, u32[]{:S(2)}) collective-permute-start(f32[256,128]{1,0:T(8,128)S(1)} %get-tuple-element.73), channel_id=1, source_target_pairs={{16,48},{48,80},{80,112},{112,16},{17,49},{49,81},{81,113},{113,17... | collective-permute-start | bytes 393224 | tf_op jit(solution)/shard_map/ppermute | solution.py:404
  102.1 2.8 %shard_map.44 = (f32[4,400,128]{2,1,0:T(8,128)S(1)}, f32[4,400,128]{2,1,0:T(8,128)S(1)}, f32[4,400,128]{2,1,0:T(8,128)S(1)}, f32[128,128]{1,0:T(8,128)S(1)}) custom-call(s32[3]{0:T(128)S(1)} %pad_add_fusion.info_ref.refs_0_, f32[256,256]{1,0:T(8,128)S(1)} %get-tuple-element.70.weights_ref.refs_1_, f32[256,256]{1,0:T(8,128)S(1)} %collective-permute-done.6.refs_2_, ...), custom_call_target="tpu_custom_call" | custom-call | flops 1258291200 | bytes 5734400 | tf_op jit(solution)/shard_map/pallas_call | solution.py:78
  104.8 11.0 %collective-permute-done.5.odd_ref = f32[256,128]{1,0:T(8,128)S(1)} collective-permute-done((f32[256,128]{1,0:T(8,128)S(1)}, f32[256,128]{1,0:T(8,128)S(1)}, u32[]{:S(2)}, u32[]{:S(2)}) %collective-permute-start.5) | collective-permute-done | bytes 131104 | tf_op jit(solution)/shard_map/ppermute | solution.py:404
  117.7 1.9 collective-permute-start.22
  133.4 2.2 %collective-permute-done.15.refs_4_ = f32[128,128]{1,0:T(8,128)S(1)} collective-permute-done((f32[128,128]{1,0:T(8,128)S(1)}, f32[128,128]{1,0:T(8,128)S(1)}, u32[]{:S(2)}, u32[]{:S(2)}) %collective-permute-start.15) | collective-permute-done | bytes 65568 | tf_op jit(solution)/shard_map/ppermute | solution.py:400
  136.5 2.2 %shard_map.46 = (f32[256,256]{1,0:T(8,128)S(1)}, f32[256,128]{1,0:T(8,128)S(1)}, f32[256,128]{1,0:T(8,128)S(1)}, f32[256,256]{1,0:T(8,128)S(1)}) custom-call(s32[3]{0:T(128)S(1)} %pad_add_fusion.info_ref.refs_0_, f32[128,128]{1,0:T(8,128)S(1)} %get-tuple-element.71.refs_7_.refs_0_, f32[128,128]{1,0:T(8,128)S(1)} %collective-permute-done.3.refs_1_.refs_8_, ...), custom_call_target="tpu_custom_call" | custom-call | flops 805306368 | bytes 1310720 | tf_op jit(solution)/shard_map/pallas_call | solution.py:78
  138.8 5.7 %collective-permute-start.20 = (f32[256,256]{1,0:T(8,128)S(1)}, f32[256,256]{1,0:T(8,128)S(1)}, u32[]{:S(2)}, u32[]{:S(2)}) collective-permute-start(f32[256,256]{1,0:T(8,128)S(1)} %get-tuple-element.84.weights_ref.refs_1_), channel_id=1, source_target_pairs={{0,16},{16,0},{32,48},{48,32},{64,80},{80,64},{96,112},{112,96},{1... | collective-permute-start | bytes 786440 | tf_op jit(solution)/shard_map/ppermute | solution.py:395
  144.5 1.9 collective-permute-start.19
  148.8 2.8 %shard_map.48 = (f32[4,400,128]{2,1,0:T(8,128)S(1)}, f32[4,400,128]{2,1,0:T(8,128)S(1)}, f32[4,400,128]{2,1,0:T(8,128)S(1)}, f32[128,128]{1,0:T(8,128)S(1)}) custom-call(s32[3]{0:T(128)S(1)} %pad_add_fusion.info_ref.refs_0_, f32[256,256]{1,0:T(8,128)S(1)} %get-tuple-element.84.weights_ref.refs_1_, f32[256,256]{1,0:T(8,128)S(1)} %collective-permute-done.20.refs_2_, ...), custom_call_target="tpu_custom_call" | custom-call | flops 1258291200 | bytes 5734400 | tf_op jit(solution)/shard_map/pallas_call | solution.py:78
  151.6 1.8 shard_map.50
  153.5 1.9 collective-permute-start.36
  158.4 1.9 collective-permute-start.27
  164.0 1.9 collective-permute-done.26
  169.6 2.1 collective-permute-done.29.refs_4_
  172.6 2.2 %shard_map.51 = (f32[256,256]{1,0:T(8,128)S(1)}, f32[256,128]{1,0:T(8,128)S(1)}, f32[256,128]{1,0:T(8,128)S(1)}, f32[256,256]{1,0:T(8,128)S(1)}) custom-call(s32[3]{0:T(128)S(1)} %pad_add_fusion.info_ref.refs_0_, f32[128,128]{1,0:T(8,128)S(1)} %get-tuple-element.85.refs_7_.refs_0_, f32[128,128]{1,0:T(8,128)S(1)} %collective-permute-done.17.refs_1_.refs_6_, ...), custom_call_target="tpu_custom_call" | custom-call | flops 805306368 | bytes 1310720 | tf_op jit(solution)/shard_map/pallas_call | solution.py:78
  174.9 5.2 %collective-permute-start.34 = (f32[256,256]{1,0:T(8,128)S(1)}, f32[256,256]{1,0:T(8,128)S(1)}, u32[]{:S(2)}, u32[]{:S(2)}) collective-permute-start(f32[256,256]{1,0:T(8,128)S(1)} %get-tuple-element.100.weights_ref.refs_1_), channel_id=1, source_target_pairs={{0,16},{16,0},{32,48},{48,32},{64,80},{80,64},{96,112},{112,96},{1... | collective-permute-start | bytes 786440 | tf_op jit(solution)/shard_map/ppermute | solution.py:395
  180.0 1.9 collective-permute-start.33
  184.6 2.8 %shard_map.53 = (f32[4,400,128]{2,1,0:T(8,128)S(1)}, f32[4,400,128]{2,1,0:T(8,128)S(1)}, f32[4,400,128]{2,1,0:T(8,128)S(1)}, f32[128,128]{1,0:T(8,128)S(1)}) custom-call(s32[3]{0:T(128)S(1)} %pad_add_fusion.info_ref.refs_0_, f32[256,256]{1,0:T(8,128)S(1)} %get-tuple-element.100.weights_ref.refs_1_, f32[256,256]{1,0:T(8,128)S(1)} %collective-permute-done.34.refs_2_, ...), custom_call_target="tpu_custom_call" | custom-call | flops 1258291200 | bytes 5734400 | tf_op jit(solution)/shard_map/pallas_call | solution.py:78
  187.4 2.4 %shard_map.55 = (f32[4,400,128]{2,1,0:T(8,128)S(1)}, f32[128,128]{1,0:T(8,128)S(1)}, f32[128,128]{1,0:T(8,128)S(1)}, f32[256,128]{1,0:T(8,128)}) custom-call(s32[3]{0:T(128)S(1)} %pad_add_fusion.info_ref.refs_0_, f32[256,128]{1,0:T(8,128)S(1)} %collective-permute-done.32.even_ref, f32[256,128]{1,0:T(8,128)S(1)} %collective-permute-done.33.odd_ref, ...), custom_call_target="tpu_custom_call" | custom-call | flops 629145600 | bytes 3276800 | tf_op jit(solution)/shard_map/pallas_call | solution.py:78
  205.4 2.4 %collective-permute-done.43.refs_4_ = f32[128,128]{1,0:T(8,128)S(1)} collective-permute-done((f32[128,128]{1,0:T(8,128)S(1)}, f32[128,128]{1,0:T(8,128)S(1)}, u32[]{:S(2)}, u32[]{:S(2)}) %collective-permute-start.43) | collective-permute-done | bytes 65568 | tf_op jit(solution)/shard_map/ppermute | solution.py:400
  208.9 2.9 %shard_map.56 = (f32[256,256]{1,0:T(8,128)S(1)}, f32[256,128]{1,0:T(8,128)}, f32[256,128]{1,0:T(8,128)}, f32[256,256]{1,0:T(8,128)S(1)}) custom-call(s32[3]{0:T(128)S(1)} %pad_add_fusion.info_ref.refs_0_, f32[128,128]{1,0:T(8,128)S(1)} %get-tuple-element.101.refs_7_.refs_0_, f32[128,128]{1,0:T(8,128)S(1)} %collective-permute-done.31.refs_1_, ...), custom_call_target="tpu_custom_call" | custom-call | flops 805306368 | bytes 1310720 | tf_op jit(solution)/shard_map/pallas_call | solution.py:78
  211.9 4.2 %shard_map.58 = (f32[8,384,256]{2,1,0:T(8,128)}, f32[2,64,256]{2,1,0:T(8,128)}, f32[1,256]{1,0:T(1,128)}) custom-call(s32[3]{0:T(128)S(1)} %pad_add_fusion.info_ref.refs_0_, f32[256,256]{1,0:T(8,128)S(1)} %get-tuple-element.115.weights_ref, f32[256,256]{1,0:T(8,128)S(1)} %get-tuple-element.116.gram_ref, ...), custom_call_target="tpu_custom_call" | custom-call | flops 1258291200 | bytes 6553600 | tf_op jit(solution)/shard_map/pallas_call | solution.py:378
  (128 shorter events, 71.5 us)
Async XLA Ops:
  12.1 48.0 %all-to-all-start = ((f32[16,8,3,8,128]{4,3,2,1,0:T(8,128)}), f32[16,8,3,8,128]{4,3,2,1,0:T(8,128)}, u32[]{:S(2)}, u32[]{:S(2)}) async-start(f32[16,8,3,8,128]{4,3,2,1,0:T(8,128)} %copy-done.2), calls=%async_computation | async-start | bytes 3145728 | tf_op jit(solution)/shard_map/all_to_all | solution.py:420
  20.5 19.7 %collective-permute-start = (f32[2,2,384,128]{3,2,1,0:T(8,128)}, f32[2,2,384,128]{3,2,1,0:T(8,128)S(1)}, u32[]{:S(2)}, u32[]{:S(2)}) collective-permute-start(f32[2,2,384,128]{3,2,1,0:T(8,128)} %copy-done.16), channel_id=1, source_target_pairs={{0,32},{16,48},{32,64},{48,80},{64,96},{80,112},{96,0},{112,16},{1... | collective-permute-start | bytes 2359304 | tf_op jit(solution)/shard_map/ppermute | solution.py:418
  21.9 36.3 %collective-permute-start.1 = (f32[2,2,384,128]{3,2,1,0:T(8,128)}, f32[2,2,384,128]{3,2,1,0:T(8,128)S(1)}, u32[]{:S(2)}, u32[]{:S(2)}) collective-permute-start(f32[2,2,384,128]{3,2,1,0:T(8,128)} %copy-done.15), channel_id=1, source_target_pairs={{0,64},{16,80},{32,96},{48,112},{64,0},{80,16},{96,32},{112,48},{1... | collective-permute-start | bytes 2359304 | tf_op jit(solution)/shard_map/ppermute | solution.py:418
  24.5 34.6 %collective-permute-start.2 = (f32[2,2,384,128]{3,2,1,0:T(8,128)}, f32[2,2,384,128]{3,2,1,0:T(8,128)S(1)}, u32[]{:S(2)}, u32[]{:S(2)}) collective-permute-start(f32[2,2,384,128]{3,2,1,0:T(8,128)} %copy-done.14), channel_id=1, source_target_pairs={{0,96},{16,112},{32,0},{48,16},{64,32},{80,48},{96,64},{112,80},{1... | collective-permute-start | bytes 2359304 | tf_op jit(solution)/shard_map/ppermute | solution.py:418
  91.7 7.7 %collective-permute-start.6 = (f32[256,256]{1,0:T(8,128)S(1)}, f32[256,256]{1,0:T(8,128)S(1)}, u32[]{:S(2)}, u32[]{:S(2)}) collective-permute-start(f32[256,256]{1,0:T(8,128)S(1)} %get-tuple-element.70.weights_ref.refs_1_), channel_id=1, source_target_pairs={{0,16},{16,0},{32,48},{48,32},{64,80},{80,64},{96,112},{112,96},{1... | collective-permute-start | bytes 786440 | tf_op jit(solution)/shard_map/ppermute | solution.py:395
  94.0 21.9 %collective-permute-start.7 = (f32[2,384,128]{2,1,0:T(8,128)S(1)}, f32[2,384,128]{2,1,0:T(8,128)S(1)}, u32[]{:S(2)}, u32[]{:S(2)}) collective-permute-start(f32[2,384,128]{2,1,0:T(8,128)S(1)} %get-tuple-element.78), channel_id=1, source_target_pairs={{0,32},{16,48},{32,64},{48,80},{64,96},{80,112},{96,0},{112,16},{1... | collective-permute-start | bytes 1179656 | tf_op jit(solution)/shard_map/ppermute | solution.py:423
  94.3 21.6 %collective-permute-start.8 = (f32[2,384,128]{2,1,0:T(8,128)S(1)}, f32[2,384,128]{2,1,0:T(8,128)S(1)}, u32[]{:S(2)}, u32[]{:S(2)}) collective-permute-start(f32[2,384,128]{2,1,0:T(8,128)S(1)} %get-tuple-element.79), channel_id=1, source_target_pairs={{0,64},{16,80},{32,96},{48,112},{64,0},{80,16},{96,32},{112,48},{1... | collective-permute-start | bytes 1179656 | tf_op jit(solution)/shard_map/ppermute | solution.py:423
  96.1 19.8 %collective-permute-start.9 = (f32[2,384,128]{2,1,0:T(8,128)S(1)}, f32[2,384,128]{2,1,0:T(8,128)S(1)}, u32[]{:S(2)}, u32[]{:S(2)}) collective-permute-start(f32[2,384,128]{2,1,0:T(8,128)S(1)} %get-tuple-element.80), channel_id=1, source_target_pairs={{0,96},{16,112},{32,0},{48,16},{64,32},{80,48},{96,64},{112,80},{1... | collective-permute-start | bytes 1179656 | tf_op jit(solution)/shard_map/ppermute | solution.py:423
  96.7 19.2 %collective-permute-start.5 = (f32[256,128]{1,0:T(8,128)S(1)}, f32[256,128]{1,0:T(8,128)S(1)}, u32[]{:S(2)}, u32[]{:S(2)}) collective-permute-start(f32[256,128]{1,0:T(8,128)S(1)} %get-tuple-element.73), channel_id=1, source_target_pairs={{16,48},{48,80},{80,112},{112,16},{17,49},{49,81},{81,113},{113,17... | collective-permute-start | bytes 393224 | tf_op jit(solution)/shard_map/ppermute | solution.py:404
  99.4 16.4 %collective-permute-start.4 = (f32[256,128]{1,0:T(8,128)S(1)}, f32[256,128]{1,0:T(8,128)S(1)}, u32[]{:S(2)}, u32[]{:S(2)}) collective-permute-start(f32[256,128]{1,0:T(8,128)S(1)} %get-tuple-element.73), channel_id=1, source_target_pairs={{16,32},{48,64},{80,96},{112,0},{17,33},{49,65},{81,97},{113,1},{1... | collective-permute-start | bytes 393224 | tf_op jit(solution)/shard_map/ppermute | solution.py:404
  117.7 7.2 %collective-permute-start.22 = (f32[256,128]{1,0:T(8,128)S(1)}, f32[256,128]{1,0:T(8,128)S(1)}, u32[]{:S(2)}, u32[]{:S(2)}) collective-permute-start(f32[256,128]{1,0:T(8,128)S(1)} %get-tuple-element.94), channel_id=1, source_target_pairs={{16,48},{48,80},{80,112},{112,16},{17,49},{49,81},{81,113},{113,17... | collective-permute-start | bytes 393224 | tf_op jit(solution)/shard_map/ppermute | solution.py:404
  119.7 5.3 %collective-permute-start.21 = (f32[256,128]{1,0:T(8,128)S(1)}, f32[256,128]{1,0:T(8,128)S(1)}, u32[]{:S(2)}, u32[]{:S(2)}) collective-permute-start(f32[256,128]{1,0:T(8,128)S(1)} %get-tuple-element.94), channel_id=1, source_target_pairs={{16,32},{48,64},{80,96},{112,0},{17,33},{49,65},{81,97},{113,1},{1... | collective-permute-start | bytes 393224 | tf_op jit(solution)/shard_map/ppermute | solution.py:404
  124.9 4.9 %collective-permute-start.11 = (f32[128,128]{1,0:T(8,128)S(1)}, f32[128,128]{1,0:T(8,128)S(1)}, u32[]{:S(2)}, u32[]{:S(2)}) collective-permute-start(f32[128,128]{1,0:T(8,128)S(1)} %add.46), channel_id=1, source_target_pairs={{0,1},{1,2},{2,3},{3,0},{4,5},{5,6},{6,7},{7,4},{8,9},{9,10},{10,1... | collective-permute-start | bytes 196616 | tf_op jit(solution)/shard_map/ppermute | solution.py:399
  126.1 25.5 %collective-permute-start.23 = (f32[4,400,128]{2,1,0:T(8,128)S(1)}, f32[4,400,128]{2,1,0:T(8,128)S(1)}, u32[]{:S(2)}, u32[]{:S(2)}) collective-permute-start(f32[4,400,128]{2,1,0:T(8,128)S(1)} %get-tuple-element.96), channel_id=1, source_target_pairs={{0,32},{16,48},{32,64},{48,80},{64,96},{80,112},{96,0},{112,16},{1... | collective-permute-start | bytes 2457608 | tf_op jit(solution)/shard_map/ppermute | solution.py:439
  131.5 5.1 %collective-permute-start.14 = (f32[128,128]{1,0:T(8,128)S(1)}, f32[128,128]{1,0:T(8,128)S(1)}, u32[]{:S(2)}, u32[]{:S(2)}) collective-permute-start(f32[128,128]{1,0:T(8,128)S(1)} %add_add_fusion.2.refs_2_), channel_id=1, source_target_pairs={{0,4},{1,5},{2,6},{3,7},{4,8},{5,9},{6,10},{7,11},{8,12},{9,13},{1... | collective-permute-start | bytes 196616 | tf_op jit(solution)/shard_map/ppermute | solution.py:400
  138.8 10.0 %collective-permute-start.20 = (f32[256,256]{1,0:T(8,128)S(1)}, f32[256,256]{1,0:T(8,128)S(1)}, u32[]{:S(2)}, u32[]{:S(2)}) collective-permute-start(f32[256,256]{1,0:T(8,128)S(1)} %get-tuple-element.84.weights_ref.refs_1_), channel_id=1, source_target_pairs={{0,16},{16,0},{32,48},{48,32},{64,80},{80,64},{96,112},{112,96},{1... | collective-permute-start | bytes 786440 | tf_op jit(solution)/shard_map/ppermute | solution.py:395
  144.5 7.1 %collective-permute-start.19 = (f32[256,128]{1,0:T(8,128)S(1)}, f32[256,128]{1,0:T(8,128)S(1)}, u32[]{:S(2)}, u32[]{:S(2)}) collective-permute-start(f32[256,128]{1,0:T(8,128)S(1)} %get-tuple-element.87), channel_id=1, source_target_pairs={{16,48},{48,80},{80,112},{112,16},{17,49},{49,81},{81,113},{113,17... | collective-permute-start | bytes 393224 | tf_op jit(solution)/shard_map/ppermute | solution.py:404
  146.4 5.2 %collective-permute-start.18 = (f32[256,128]{1,0:T(8,128)S(1)}, f32[256,128]{1,0:T(8,128)S(1)}, u32[]{:S(2)}, u32[]{:S(2)}) collective-permute-start(f32[256,128]{1,0:T(8,128)S(1)} %get-tuple-element.87), channel_id=1, source_target_pairs={{16,32},{48,64},{80,96},{112,0},{17,33},{49,65},{81,97},{113,1},{1... | collective-permute-start | bytes 393224 | tf_op jit(solution)/shard_map/ppermute | solution.py:404
  153.5 7.9 %collective-permute-start.36 = (f32[256,128]{1,0:T(8,128)S(1)}, f32[256,128]{1,0:T(8,128)S(1)}, u32[]{:S(2)}, u32[]{:S(2)}) collective-permute-start(f32[256,128]{1,0:T(8,128)S(1)} %get-tuple-element.110), channel_id=1, source_target_pairs={{16,48},{48,80},{80,112},{112,16},{17,49},{49,81},{81,113},{113,17... | collective-permute-start | bytes 393224 | tf_op jit(solution)/shard_map/ppermute | solution.py:404
  155.4 6.0 %collective-permute-start.35 = (f32[256,128]{1,0:T(8,128)S(1)}, f32[256,128]{1,0:T(8,128)S(1)}, u32[]{:S(2)}, u32[]{:S(2)}) collective-permute-start(f32[256,128]{1,0:T(8,128)S(1)} %get-tuple-element.110), channel_id=1, source_target_pairs={{16,32},{48,64},{80,96},{112,0},{17,33},{49,65},{81,97},{113,1},{1... | collective-permute-start | bytes 393224 | tf_op jit(solution)/shard_map/ppermute | solution.py:404
  158.4 5.6 %collective-permute-start.27 = (f32[128,128]{1,0:T(8,128)S(1)}, f32[128,128]{1,0:T(8,128)S(1)}, u32[]{:S(2)}, u32[]{:S(2)}) collective-permute-start(f32[128,128]{1,0:T(8,128)S(1)} %add.50), channel_id=1, source_target_pairs={{0,3},{1,0},{2,1},{3,2},{4,7},{5,4},{6,5},{7,6},{8,11},{9,8},{10,9... | collective-permute-start | bytes 196616 | tf_op jit(solution)/shard_map/ppermute | solution.py:399
  160.3 5.6 %collective-permute-start.26 = (f32[128,128]{1,0:T(8,128)S(1)}, f32[128,128]{1,0:T(8,128)S(1)}, u32[]{:S(2)}, u32[]{:S(2)}) collective-permute-start(f32[128,128]{1,0:T(8,128)S(1)} %add.50), channel_id=1, source_target_pairs={{0,2},{1,3},{2,0},{3,1},{4,6},{5,7},{6,4},{7,5},{8,10},{9,11},{10,... | collective-permute-start | bytes 196616 | tf_op jit(solution)/shard_map/ppermute | solution.py:399
  160.6 5.7 %collective-permute-start.25 = (f32[128,128]{1,0:T(8,128)S(1)}, f32[128,128]{1,0:T(8,128)S(1)}, u32[]{:S(2)}, u32[]{:S(2)}) collective-permute-start(f32[128,128]{1,0:T(8,128)S(1)} %add.50), channel_id=1, source_target_pairs={{0,1},{1,2},{2,3},{3,0},{4,5},{5,6},{6,7},{7,4},{8,9},{9,10},{10,1... | collective-permute-start | bytes 196616 | tf_op jit(solution)/shard_map/ppermute | solution.py:399
  162.6 24.8 %collective-permute-start.37 = (f32[4,400,128]{2,1,0:T(8,128)S(1)}, f32[4,400,128]{2,1,0:T(8,128)S(1)}, u32[]{:S(2)}, u32[]{:S(2)}) collective-permute-start(f32[4,400,128]{2,1,0:T(8,128)S(1)} %get-tuple-element.112), channel_id=1, source_target_pairs={{0,32},{16,48},{32,64},{48,80},{64,96},{80,112},{96,0},{112,16},{1... | collective-permute-start | bytes 2457608 | tf_op jit(solution)/shard_map/ppermute | solution.py:439
  167.9 4.7 %collective-permute-start.28 = (f32[128,128]{1,0:T(8,128)S(1)}, f32[128,128]{1,0:T(8,128)S(1)}, u32[]{:S(2)}, u32[]{:S(2)}) collective-permute-start(f32[128,128]{1,0:T(8,128)S(1)} %add_add_fusion.1.refs_2_), channel_id=1, source_target_pairs={{0,4},{1,5},{2,6},{3,7},{4,8},{5,9},{6,10},{7,11},{8,12},{9,13},{1... | collective-permute-start | bytes 196616 | tf_op jit(solution)/shard_map/ppermute | solution.py:400
  174.9 9.7 %collective-permute-start.34 = (f32[256,256]{1,0:T(8,128)S(1)}, f32[256,256]{1,0:T(8,128)S(1)}, u32[]{:S(2)}, u32[]{:S(2)}) collective-permute-start(f32[256,256]{1,0:T(8,128)S(1)} %get-tuple-element.100.weights_ref.refs_1_), channel_id=1, source_target_pairs={{0,16},{16,0},{32,48},{48,32},{64,80},{80,64},{96,112},{112,96},{1... | collective-permute-start | bytes 786440 | tf_op jit(solution)/shard_map/ppermute | solution.py:395
  180.0 7.3 %collective-permute-start.33 = (f32[256,128]{1,0:T(8,128)S(1)}, f32[256,128]{1,0:T(8,128)S(1)}, u32[]{:S(2)}, u32[]{:S(2)}) collective-permute-start(f32[256,128]{1,0:T(8,128)S(1)} %get-tuple-element.103), channel_id=1, source_target_pairs={{16,48},{48,80},{80,112},{112,16},{17,49},{49,81},{81,113},{113,17... | collective-permute-start | bytes 393224 | tf_op jit(solution)/shard_map/ppermute | solution.py:404
  182.0 5.4 %collective-permute-start.32 = (f32[256,128]{1,0:T(8,128)S(1)}, f32[256,128]{1,0:T(8,128)S(1)}, u32[]{:S(2)}, u32[]{:S(2)}) collective-permute-start(f32[256,128]{1,0:T(8,128)S(1)} %get-tuple-element.103), channel_id=1, source_target_pairs={{16,32},{48,64},{80,96},{112,0},{17,33},{49,65},{81,97},{113,1},{1... | collective-permute-start | bytes 393224 | tf_op jit(solution)/shard_map/ppermute | solution.py:404
  194.0 5.0 %collective-permute-start.39 = (f32[128,128]{1,0:T(8,128)S(1)}, f32[128,128]{1,0:T(8,128)S(1)}, u32[]{:S(2)}, u32[]{:S(2)}) collective-permute-start(f32[128,128]{1,0:T(8,128)S(1)} %add.54), channel_id=1, source_target_pairs={{0,1},{1,2},{2,3},{3,0},{4,5},{5,6},{6,7},{7,4},{8,9},{9,10},{10,1... | collective-permute-start | bytes 196616 | tf_op jit(solution)/shard_map/ppermute | solution.py:399
  199.8 12.1 %collective-permute-start.45 = (f32[4,400,128]{2,1,0:T(8,128)S(1)}, f32[4,400,128]{2,1,0:T(8,128)S(1)}, u32[]{:S(2)}, u32[]{:S(2)}) collective-permute-start(f32[4,400,128]{2,1,0:T(8,128)S(1)} %get-tuple-element.120), channel_id=1, source_target_pairs={{0,16},{16,0},{32,48},{48,32},{64,80},{80,64},{96,112},{112,96},{1... | collective-permute-start | bytes 2457608 | tf_op jit(solution)/shard_map/ppermute | solution.py:395
  201.3 10.6 %collective-permute-start.46 = (f32[4,400,128]{2,1,0:T(8,128)S(1)}, f32[4,400,128]{2,1,0:T(8,128)S(1)}, u32[]{:S(2)}, u32[]{:S(2)}) collective-permute-start(f32[4,400,128]{2,1,0:T(8,128)S(1)} %get-tuple-element.121), channel_id=1, source_target_pairs={{0,16},{16,0},{32,48},{48,32},{64,80},{80,64},{96,112},{112,96},{1... | collective-permute-start | bytes 2457608 | tf_op jit(solution)/shard_map/ppermute | solution.py:395
  202.8 5.0 %collective-permute-start.43 = (f32[128,128]{1,0:T(8,128)S(1)}, f32[128,128]{1,0:T(8,128)S(1)}, u32[]{:S(2)}, u32[]{:S(2)}) collective-permute-start(f32[128,128]{1,0:T(8,128)S(1)} %add_add_fusion.refs_2_.refs_5_), channel_id=1, source_target_pairs={{0,8},{1,9},{2,10},{3,11},{4,12},{5,13},{6,14},{7,15},{8,0},{9,1},... | collective-permute-start | bytes 196616 | tf_op jit(solution)/shard_map/ppermute | solution.py:400
  (33 other events, 179.7 us)

commit v5 on v4

--- a/solution.py
+++ b/solution.py
@@ -120,16 +120,13 @@
 
 
 def pack_ahead_kernel(info_ref, *refs):
-    parts_ref, shares_ref = refs[SIDE], refs[-1]
-    shares_ref[...] = jnp.broadcast_to(jnp.sum(parts_ref[...], axis=0)[None], shares_ref.shape)
-    for x_ref, out_ref in zip(refs[:SIDE], refs[SIDE + 1:]):
+    for x_ref, out_ref in zip(refs[:SIDE], refs[-SIDE:]):
         out_ref[0] = x_ref[:, :BLOCK]
         out_ref[1] = x_ref[:, BLOCK:]
 
 
-def pack_ahead(info, x, parts):
+def pack_ahead(info, x, before):
     rows = x.shape[0]
-    shares = (ROWS,) + parts.shape[1:]
 
     def columns(k):
         return pl.BlockSpec((rows, PAIR), lambda i, c: (0, (2 * ((c[1] + k) % SIDE) + COLS - 1) % COLS))
@@ -137,41 +134,44 @@
     return call(
         pack_ahead_kernel,
         (1,),
-        [columns(k) for k in range(SIDE)] + [whole(*parts.shape)],
-        [whole(2, rows, BLOCK)] * SIDE + [whole(*shares)],
-        [shape(2, rows, BLOCK)] * SIDE + [shape(*shares)],
+        [columns(k) for k in range(SIDE)] + [pl.BlockSpec(memory_space=pl.ANY)] * len(before),
+        [whole(2, rows, BLOCK)] * SIDE,
+        [shape(2, rows, BLOCK)] * SIDE,
         scalars=1,
         nbytes=8 * SIDE * rows * PAIR,
-    )(info, *[x] * SIDE, parts)
-
-
-def gram_kernel(x_ref, before_ref, out_ref):
-    high, low = parts_of(x_ref[...])
-    mixed = dot(high, low, 0)
-    gram = dot(high, high, 0) + (mixed + mixed.T)
-    for k, block in enumerate((gram[:BLOCK, :BLOCK], gram[:BLOCK, BLOCK:], gram[BLOCK:, BLOCK:])):
-        out_ref[:, 0, k] = block.reshape(ROWS, BLOCK // ROWS, BLOCK)
-
-
-def row_grams(x, before):
-    rows = x.shape[0]
-    return call(
-        gram_kernel,
-        (COLS,),
-        [pl.BlockSpec((rows, PAIR), lambda s: (0, s)), pl.BlockSpec(memory_space=pl.ANY)],
-        pl.BlockSpec((ROWS, 1, 3, BLOCK // ROWS, BLOCK), lambda s: (0, s, 0, 0, 0)),
-        shape(ROWS, COLS, 3, BLOCK // ROWS, BLOCK),
-        flops=2 * 2 * COLS * rows * PAIR * PAIR,
-        nbytes=4 * COLS * (rows * PAIR + PAIR * PAIR),
-    )(x, before)
-
-
-def sum_kernel(info_ref, parts_ref, out_ref):
-    out_ref[...] = jnp.sum(parts_ref[...], axis=0)
-
-
-def sum_parts(info, parts, before):
-    return call_whole(sum_kernel, (info, parts), [shape(*parts.shape[1:])], before, nbytes=4 * parts.size)[0]
+    )(info, *[x] * SIDE, *before)
+
+
+def gram_kernel(info_ref, *refs):
+    keep_ref, send_ref = refs[-2:]
+    first = info_ref[0] == 0
+    grams = []
+    for slot in range(2):
+        squares = jnp.zeros((PAIR, PAIR), F32)
+        mixed = jnp.zeros((PAIR, PAIR), F32)
+        for ref in refs[:-2]:
+            high, low = parts_of(jnp.concatenate([ref[slot, 0], ref[slot, 1]], axis=1))
+            squares = squares + dot(high, high, 0)
+            mixed = mixed + dot(high, low, 0)
+        grams.append(squares + (mixed + mixed.T))
+    for ref, gram in ((keep_ref, jnp.where(first, grams[0], grams[1])), (send_ref, jnp.where(first, grams[1], grams[0]))):
+        for k, block in enumerate((gram[:BLOCK, :BLOCK], gram[:BLOCK, BLOCK:], gram[BLOCK:, BLOCK:])):
+            ref[:, k] = block.reshape(ROWS, BLOCK // ROWS, BLOCK)
+
+
+def first_grams(info, main):
+    out = shape(ROWS, 3, BLOCK // ROWS, BLOCK)
+    return call_whole(
+        gram_kernel, (info, *main), [out, out], flops=2 * 2 * 4 * main[0].size * PAIR, nbytes=16 * main[0].size
+    )
+
+
+def spread_kernel(info_ref, parts_ref, out_ref):
+    out_ref[...] = jnp.broadcast_to(jnp.sum(parts_ref[...], axis=0)[None], out_ref.shape)
+
+
+def spread_parts(info, parts, before):
+    return call_whole(spread_kernel, (info, parts), [shape(*parts.shape)], before, nbytes=8 * parts.size)[0]
 
 
 def rotation_of(gram, x_ref, r_ref):
@@ -205,7 +205,7 @@
 
 def cayley_kernel(fill, info_ref, *refs):
     weights_ref, up_ref, low_ref, gram_ref, x_ref, r_ref = refs[-6:]
-    up, cross, low = fill(*refs[:-6])
+    up, cross, low = fill(info_ref, *refs[:-6])
     gram_ref[:BLOCK, :BLOCK] = up
     gram_ref[:BLOCK, BLOCK:] = cross
     gram_ref[BLOCK:, :BLOCK] = cross.T
@@ -216,27 +216,29 @@
     low_ref[...] = weights[:, BLOCK:]
 
 
-def cayley_call(fill, args):
+def cayley_call(fill, args, before=()):
     return call_whole(
         functools.partial(cayley_kernel, fill),
         args,
         [shape(PAIR, PAIR), shape(PAIR, BLOCK), shape(PAIR, BLOCK), shape(PAIR, PAIR)],
+        before,
         scratch=[pltpu.VMEM((PAIR, PAIR), F32)] * 2,
         flops=2 * 3 * 8 * PAIR**3,
         nbytes=20 * PAIR * PAIR,
     )
 
 
-def first_cayley(info, blocks):
-    return cayley_call(lambda ref: [ref[:, k].reshape(BLOCK, BLOCK) for k in range(3)], (info, blocks))
-
-
-def cayley(info, up, low, parts):
-    def fill(up_ref, low_ref, *part_refs):
+def first_cayley(info, blocks, before):
+    return cayley_call(lambda _, ref: [ref[:, k].reshape(BLOCK, BLOCK) for k in range(3)], (info, blocks), before)
+
+
+def cayley(info, up, across_chips, across_cores, parts):
+    def fill(info_ref, up_ref, chips_ref, cores_ref, *part_refs):
         first, second, third, fourth = (ref[...] for ref in part_refs)
-        return up_ref[...], (first + second) + (third + fourth), low_ref[...]
-
-    return cayley_call(fill, (info, up, low, *parts))
+        low = jnp.where(info_ref[0] == 0, chips_ref[-BLOCK:], cores_ref[-BLOCK:])
+        return up_ref[...], (first + second) + (third + fourth), low
+
+    return cayley_call(fill, (info, up, across_chips, across_cores, *parts))
 
 
 def project_kernel(info_ref, gram_ref, weights_ref, up_ref, low_ref):
@@ -288,20 +290,23 @@
     cross_ref[...] = cross
 
 
-def rotate_own(info, own, other, blocks, before, rows, step):
+def rotate_own(info, own, other, blocks, rows, step):
     return call_whole(
         functools.partial(own_kernel, rows, step),
         (info, own, other, *blocks),
         [shape(SIDE, step, BLOCK)] * 3 + [shape(BLOCK, BLOCK)],
-        before,
         flops=2 * 3 * SIDE * step * 4 * BLOCK * PAIR,
         nbytes=4 * 7 * SIDE * step * BLOCK,
     )
 
 
-def ahead_kernel(rows, step, info_ref, even_ref, odd_ref, upper_ref, cross_ref, up0_ref, *refs):
-    low0_ref, keep_ref, send_ref, upper_out_ref = refs[-4:]
-    upper_out_ref[...] = upper_ref[...]
+def ahead_kernel(rows, step, info_ref, even_ref, odd_ref, upper_ref, low_ref, cross_ref, up0_ref, *refs):
+    low0_ref, keep_ref, send_ref, bundle_ref = refs[-4:]
+    low = low_ref[...]
+    if bundle_ref.shape[0] > BLOCK:
+        bundle_ref[:PAIR] = upper_ref[...]
+    bundle_ref[-BLOCK:] = low
+    send_ref[BLOCK:] = low
     weights = even_ref[...] + odd_ref[...]
     slot = (2 * info_ref[1] + COLS - 1) % COLS
     total = jnp.zeros((BLOCK, BLOCK), F32)
@@ -311,14 +316,14 @@
         total = total + mm3(up0_ref[group, :rows], low0[:rows], 0)
     first = info_ref[0] == 0
     keep_ref[...] = jnp.where(first, total, cross_ref[...])
-    send_ref[...] = jnp.where(first, cross_ref[...], total)
-
-
-def rotate_ahead(info, lower, upper, cross, up0, blocks, rows, step):
+    send_ref[:BLOCK] = jnp.where(first, cross_ref[...], total)
+
+
+def rotate_ahead(info, lower, upper, low, cross, up0, blocks, last, rows, step):
     return call_whole(
         functools.partial(ahead_kernel, rows, step),
-        (info, *lower, upper, cross, up0, *blocks),
-        [shape(SIDE, step, BLOCK)] + [shape(BLOCK, BLOCK)] * 2 + [shape(PAIR, BLOCK)],
+        (info, *lower, upper, low, cross, up0, *blocks),
+        [shape(SIDE, step, BLOCK), shape(BLOCK, BLOCK), shape(2 * BLOCK, BLOCK), shape(BLOCK if last else 3 * BLOCK, BLOCK)],
         flops=2 * 3 * SIDE * step * 2 * BLOCK * PAIR,
         nbytes=4 * 4 * SIDE * step * BLOCK,
     )
@@ -326,19 +331,18 @@
 
 def up_kernel(step, info_ref, even_ref, odd_ref, low1_ref, *refs):
     up_ref, pass_ref = refs[-2:]
-    weights = even_ref[...] + odd_ref[...]
+    weights = even_ref[:PAIR] + odd_ref[:PAIR]
     slot = (2 * info_ref[1] + COLS - 1) % COLS
     for group, (pair,) in groups_of(info_ref, step, refs[:-2], (slot,)):
         up_ref[group] = mm3(pair, weights)
     pass_ref[...] = low1_ref[...]
 
 
-def rotate_up(info, upper, low1, blocks, before, step):
+def rotate_up(info, upper, low1, blocks, step):
     return call_whole(
         functools.partial(up_kernel, step),
         (info, *upper, low1, *blocks),
         [shape(SIDE, step, BLOCK)] * 2,
-        before,
         flops=2 * 3 * SIDE * step * BLOCK * PAIR,
         nbytes=4 * 5 * SIDE * step * BLOCK,
     )
@@ -417,31 +421,33 @@
     packed = pack_main(info, x)
     main = [packed[0]] + [lax.ppermute(packed[k], "cols", CHIPS_ON[k]) for k in range(1, SIDE)]
 
-    parts = lax.all_to_all(row_grams(x, packed[0]), "rows", 0, 0, tiled=True)
-    parts = lax.all_to_all(sum_parts(info, parts, main[1:]), "cols", 0, 0, tiled=True)
-    *packed, shares = pack_ahead(info, x, parts)
+    keep, send = first_grams(info, main)
+    packed = pack_ahead(info, x, main[1:])
     ahead = [packed[0]] + [lax.ppermute(packed[k], "cols", CHIPS_ON[k]) for k in range(1, SIDE)]
-    weights, upper, lower, gram = first_cayley(info, lax.all_to_all(shares, "rows", 0, 0, tiled=True))
+    parts = lax.all_to_all(keep + swap_core(send), "rows", 0, 0, tiled=True)
+    parts = lax.all_to_all(spread_parts(info, parts, [ahead[1], ahead[3]]), "rows", 0, 0, tiled=True)
+    weights, upper, lower, gram = first_cayley(info, parts, [ahead[2]])
 
     own_blocks = main
     ahead_blocks = [value[None] for value in ahead]
     for sweep_round in range(ROUNDS - 1):
+        last = sweep_round == ROUNDS - 2
         lower = to_next_chip(lower)
-        other = swap_core(weights)
         up, low = project(info, gram, weights)
-        up0, up1, low1, cross = rotate_own(info, weights, other, own_blocks, [up], rows, step)
-        low = lax.ppermute(low, "cols", NEXT_SLOT)
-        low0, keep, send, upper = rotate_ahead(info, lower, upper, cross, up0, ahead_blocks, rows, step)
-        parts = sum_over_rows(keep + swap_core(send))
+        up0, up1, low1, cross = rotate_own(info, weights, swap_core(weights), own_blocks, rows, step)
+        low0, keep, send, bundle = rotate_ahead(info, lower, upper, low, cross, up0, ahead_blocks, last, rows, step)
+        received = swap_core(send)
+        parts = sum_over_rows(keep + received[:BLOCK])
         own_blocks = [up0, low0, up1, low1]
-        if sweep_round < ROUNDS - 2:
-            up_m, passed = rotate_up(info, to_next_chip(upper), low1, ahead_blocks, [low], step)
+        bundles = to_next_chip(bundle)
+        if last:
+            other_blocks = [swap_core(value) for value in other_slot(info, own_blocks, [parts[0]])]
+        else:
+            up_m, passed = rotate_up(info, bundles, low1, ahead_blocks, step)
             ahead_blocks = [up_m, lax.ppermute(passed, "cols", CHIPS_ON[1])]
-        else:
-            received = [swap_core(value) for value in other_slot(info, own_blocks, [parts[0]])]
-        weights, upper, lower, gram = cayley(info, up, low, parts)
-
-    rotated, frame, column_scale = rotate_final(info, weights, gram, own_blocks + received, rows, step)
+        weights, upper, lower, gram = cayley(info, up, bundles[0], received, parts)
+
+    rotated, frame, column_scale = rotate_final(info, weights, gram, own_blocks + other_blocks, rows, step)
     return rotated, frame.reshape(2 * basis_rows, PAIR), column_scale.reshape(PAIR)
 
 

time: 218 us -> 198 us (0.908)
  local copies, waits for them, and re-layouts: 12.7 us -> 2.58 us
  blocking collectives: 23.5 us -> 14.6 us
    unnamed x34 -> x8, local copies, waits for them, and re-layouts: 12.7 us -> 2.58 us
    all_to_all x2 -> x1, blocking collectives: 23.5 us -> 14.6 us  [body(): parts = lax.all_to_all(keep + swap_core(send), 'rows', 0, 0, tiled=True)]
    all_to_all x1, waiting for transfers between devices: 0.01 us -> 7.19 us  [body(): lax.all_to_all(spread_parts(info, parts, [ahead[1], ahead[3]]), 'rows', 0...]
    all_to_all x1, starting transfers between devices: 8.47 us -> 4.17 us  [body(): lax.all_to_all(spread_parts(info, parts, [ahead[1], ahead[3]]), 'rows', 0...]
    ppermute x9, waiting for transfers between devices: 9.89 us -> 6.71 us  [sum_over_rows(): lax.ppermute(value, 'rows', pairs)]
    ppermute x8 -> x9, starting transfers between devices: 17.5 us -> 20.6 us  [swap_core(): return lax.ppermute(value, 'cols', TURN_CORE)]
    pallas_call x2 -> x1, Pallas kernels: 4.19 us -> 1.42 us  [pack_ahead(): call(pack_ahead_kernel, (1,), [columns(k) for k in range(SIDE)] + [pl.Blo...]
    ppermute x10 -> x11, waiting for transfers between devices: 11 us -> 8.46 us  [to_next_chip(): lax.ppermute(value, 'cols', pairs)]
  transfers between devices with their start and end apart: 48 -> 47, of which waited for: 22 -> 23; matrix products, arithmetic and copies ran while one was open for 0% -> 0% of each run, Pallas kernels for 10% -> 12%
where the time goes in v5:
time: 198 us; the launch traced here: 195 us
  waiting for transfers between devices  70.5 us (36%)
  starting transfers between devices  65.5 us (33%)
  Pallas kernels  40.7 us (21%)
  blocking collectives  14.6 us (7%)
  local copies, waits for them, and re-layouts  2.58 us (1%)
    pallas_call x18, Pallas kernels, call_whole(): pl.pallas_call(inner, in_specs=[pl.BlockSpec(memory_space=pltpu.SMEM)] +...  33.9 us
    ppermute x6, waiting for transfers between devices, body(): lax.ppermute(packed[k], 'cols', CHIPS_ON[k])  32.7 us
    ppermute x9, starting transfers between devices, swap_core(): return lax.ppermute(value, 'cols', TURN_CORE)  20.6 us
    ppermute x11, starting transfers between devices, to_next_chip(): lax.ppermute(value, 'cols', pairs)  18.2 us
    all_to_all x1, blocking collectives, body(): parts = lax.all_to_all(keep + swap_core(send), 'rows', 0, 0, tiled=True)  14.6 us
    ppermute x9, waiting for transfers between devices, sum_over_rows(): return [value] + [lax.ppermute(value, 'rows', pairs) for pairs in ALONG_Z]  14.4 us
    ppermute x6, starting transfers between devices, body(): lax.ppermute(packed[k], 'cols', CHIPS_ON[k])  9.91 us
    ppermute x11, waiting for transfers between devices, to_next_chip(): lax.ppermute(value, 'cols', pairs)  8.46 us
  transfers between devices with their start and end apart: 47, of which 23 were waited for; matrix products, arithmetic and copies ran while one was open for 0% of the time, Pallas kernels for 12%

profile of v5, /device:TPU:1, one launch (start us, length us, event | category | flops | bytes accessed | tf_op | source)
XLA Modules:
  0.0 195.1 jit_solution(12439596169008346550)
XLA Ops:
  3.8 2.2 %collective-permute-start = (f32[2,2,384,128]{3,2,1,0:T(8,128)S(1)}, f32[2,2,384,128]{3,2,1,0:T(8,128)S(1)}, u32[]{:S(2)}, u32[]{:S(2)}) collective-permute-start(f32[2,2,384,128]{3,2,1,0:T(8,128)S(1)} %get-tuple-element.67), channel_id=1, source_target_pairs={{0,32},{16,48},{32,64},{48,80},{64,96},{80,112},{96,0},{112,16},{1... | collective-permute-start | bytes 2359304 | tf_op jit(solution)/shard_map/ppermute | solution.py:422
  6.0 2.6 %collective-permute-start.1 = (f32[2,2,384,128]{3,2,1,0:T(8,128)S(1)}, f32[2,2,384,128]{3,2,1,0:T(8,128)S(1)}, u32[]{:S(2)}, u32[]{:S(2)}) collective-permute-start(f32[2,2,384,128]{3,2,1,0:T(8,128)S(1)} %get-tuple-element.68), channel_id=1, source_target_pairs={{0,64},{16,80},{32,96},{48,112},{64,0},{80,16},{96,32},{112,48},{1... | collective-permute-start | bytes 2359304 | tf_op jit(solution)/shard_map/ppermute | solution.py:422
  9.7 14.9 %collective-permute-done.refs_1_.refs_4_ = f32[2,2,384,128]{3,2,1,0:T(8,128)S(1)} collective-permute-done((f32[2,2,384,128]{3,2,1,0:T(8,128)S(1)}, f32[2,2,384,128]{3,2,1,0:T(8,128)S(1)}, u32[]{:S(2)}, u32[]{:S(2)}) %collective-permute-start) | collective-permute-done | bytes 786464 | tf_op jit(solution)/shard_map/ppermute | solution.py:422
  24.6 17.9 %collective-permute-done.1.refs_2_.refs_5_ = f32[2,2,384,128]{3,2,1,0:T(8,128)S(1)} collective-permute-done((f32[2,2,384,128]{3,2,1,0:T(8,128)S(1)}, f32[2,2,384,128]{3,2,1,0:T(8,128)S(1)}, u32[]{:S(2)}, u32[]{:S(2)}) %collective-permute-start.1) | collective-permute-done | bytes 786464 | tf_op jit(solution)/shard_map/ppermute | solution.py:422
  48.7 1.9 collective-permute-start.3
  51.8 14.6 %all_to_all.10.refs_1_ = f32[16,3,8,128]{3,2,1,0:T(8,128)S(1)} all-to-all(f32[16,3,8,128]{3,2,1,0:T(8,128)S(1)} %add.49), channel_id=1, replica_groups=mesh['cols'=8,'rows'=16] {'rows'}, dimensions={0} | all-to-all | bytes 393216 | tf_op jit(solution)/shard_map/all_to_all | solution.py:427
  67.6 4.2 %all-to-all-start.1 = ((f32[16,3,8,128]{3,2,1,0:T(8,128)}), f32[16,3,8,128]{3,2,1,0:T(8,128)}, u32[]{:S(2)}, u32[]{:S(2)}) async-start(f32[16,3,8,128]{3,2,1,0:T(8,128)} %copy-done.1), calls=%async_computation.1 | async-start | bytes 393216 | tf_op jit(solution)/shard_map/all_to_all | solution.py:428
  71.8 7.2 %all-to-all-done.1.refs_1_ = f32[16,3,8,128]{3,2,1,0:T(8,128)} async-done(((f32[16,3,8,128]{3,2,1,0:T(8,128)}), f32[16,3,8,128]{3,2,1,0:T(8,128)}, u32[]{:S(2)}, u32[]{:S(2)}) %all-to-all-start.1) | async-done | bytes 196640 | tf_op jit(solution)/shard_map/all_to_all | solution.py:428
  79.0 3.1 %shard_map.42 = (f32[256,256]{1,0:T(8,128)S(1)}, f32[256,128]{1,0:T(8,128)S(1)}, f32[256,128]{1,0:T(8,128)S(1)}, f32[256,256]{1,0:T(8,128)S(1)}) custom-call(s32[3]{0:T(128)S(1)} %pad_add_fusion.info_ref.refs_0_, f32[16,3,8,128]{3,2,1,0:T(8,128)} %all-to-all-done.1.refs_1_, f32[2,384,128]{2,1,0:T(8,128)} %collective-permute-done.6.refs_2_), custom_call_target="tpu_custom_call" | custom-call | flops 805306368 | bytes 1310720 | tf_op jit(solution)/shard_map/pallas_call | solution.py:78
  82.1 3.2 %collective-permute-start.9 = (f32[256,256]{1,0:T(8,128)S(1)}, f32[256,256]{1,0:T(8,128)S(1)}, u32[]{:S(2)}, u32[]{:S(2)}) collective-permute-start(f32[256,256]{1,0:T(8,128)S(1)} %get-tuple-element.76.weights_ref.own_ref), channel_id=1, source_target_pairs={{0,16},{16,0},{32,48},{48,32},{64,80},{80,64},{96,112},{112,96},{1... | collective-permute-start | bytes 786440 | tf_op jit(solution)/shard_map/ppermute | solution.py:399
  85.3 1.9 collective-permute-start.8
  89.7 2.7 %shard_map.44 = (f32[4,400,128]{2,1,0:T(8,128)S(1)}, f32[4,400,128]{2,1,0:T(8,128)S(1)}, f32[4,400,128]{2,1,0:T(8,128)S(1)}, f32[128,128]{1,0:T(8,128)S(1)}) custom-call(s32[3]{0:T(128)S(1)} %pad_add_fusion.info_ref.refs_0_, f32[256,256]{1,0:T(8,128)S(1)} %get-tuple-element.76.weights_ref.own_ref, f32[256,256]{1,0:T(8,128)S(1)} %collective-permute-done.9.other_ref, ...), custom_call_target="tpu_custom_call" | custom-call | flops 1258291200 | bytes 5734400 | tf_op jit(solution)/shard_map/pallas_call | solution.py:78
  93.0 2.3 %shard_map.45 = (f32[4,400,128]{2,1,0:T(8,128)S(1)}, f32[128,128]{1,0:T(8,128)S(1)}, f32[256,128]{1,0:T(8,128)S(1)}, f32[384,128]{1,0:T(8,128)S(1)}) custom-call(s32[3]{0:T(128)S(1)} %pad_add_fusion.info_ref.refs_0_, f32[256,128]{1,0:T(8,128)S(1)} %collective-permute-done.7.even_ref, f32[256,128]{1,0:T(8,128)S(1)} %collective-permute-done.8.odd_ref, ...), custom_call_target="tpu_custom_call" | custom-call | flops 629145600 | bytes 3276800 | tf_op jit(solution)/shard_map/pallas_call | solution.py:78
  95.3 2.2 %collective-permute-start.11 = (f32[256,128]{1,0:T(8,128)S(1)}, f32[256,128]{1,0:T(8,128)S(1)}, u32[]{:S(2)}, u32[]{:S(2)}) collective-permute-start(f32[256,128]{1,0:T(8,128)S(1)} %get-tuple-element.85), channel_id=1, source_target_pairs={{0,16},{16,0},{32,48},{48,32},{64,80},{80,64},{96,112},{112,96},{1... | collective-permute-start | bytes 393224 | tf_op jit(solution)/shard_map/ppermute | solution.py:399
  97.4 1.9 collective-permute-start.21
  102.8 2.5 %collective-permute-done.21.odd_ref = f32[384,128]{1,0:T(8,128)S(1)} collective-permute-done((f32[384,128]{1,0:T(8,128)S(1)}, f32[384,128]{1,0:T(8,128)S(1)}, u32[]{:S(2)}, u32[]{:S(2)}) %collective-permute-start.21) | collective-permute-done | bytes 196640 | tf_op jit(solution)/shard_map/ppermute | solution.py:408
  110.9 2.4 %collective-permute-done.16.refs_5_ = f32[128,128]{1,0:T(8,128)S(1)} collective-permute-done((f32[128,128]{1,0:T(8,128)S(1)}, f32[128,128]{1,0:T(8,128)S(1)}, u32[]{:S(2)}, u32[]{:S(2)}) %collective-permute-start.16) | collective-permute-done | bytes 65568 | tf_op jit(solution)/shard_map/ppermute | solution.py:404
  114.6 2.2 %shard_map.46 = (f32[256,256]{1,0:T(8,128)S(1)}, f32[256,128]{1,0:T(8,128)S(1)}, f32[256,128]{1,0:T(8,128)S(1)}, f32[256,256]{1,0:T(8,128)S(1)}) custom-call(s32[3]{0:T(128)S(1)} %pad_add_fusion.info_ref.refs_0_, f32[128,128]{1,0:T(8,128)S(1)} %get-tuple-element.77.refs_0_, f32[384,128]{1,0:T(8,128)S(1)} %collective-permute-done.10.refs_1_.even_ref, ...), custom_call_target="tpu_custom_call" | custom-call | flops 805306368 | bytes 1310720 | tf_op jit(solution)/shard_map/pallas_call | solution.py:78
  116.8 2.9 %collective-permute-start.20 = (f32[256,256]{1,0:T(8,128)S(1)}, f32[256,256]{1,0:T(8,128)S(1)}, u32[]{:S(2)}, u32[]{:S(2)}) collective-permute-start(f32[256,256]{1,0:T(8,128)S(1)} %get-tuple-element.88.weights_ref.own_ref), channel_id=1, source_target_pairs={{0,16},{16,0},{32,48},{48,32},{64,80},{80,64},{96,112},{112,96},{1... | collective-permute-start | bytes 786440 | tf_op jit(solution)/shard_map/ppermute | solution.py:399
  119.8 2.6 %collective-permute-start.19 = (f32[256,128]{1,0:T(8,128)S(1)}, f32[256,128]{1,0:T(8,128)S(1)}, u32[]{:S(2)}, u32[]{:S(2)}) collective-permute-start(f32[256,128]{1,0:T(8,128)S(1)} %get-tuple-element.90), channel_id=1, source_target_pairs={{16,48},{48,80},{80,112},{112,16},{17,49},{49,81},{81,113},{113,17... | collective-permute-start | bytes 393224 | tf_op jit(solution)/shard_map/ppermute | solution.py:408
  124.8 2.7 %shard_map.48 = (f32[4,400,128]{2,1,0:T(8,128)S(1)}, f32[4,400,128]{2,1,0:T(8,128)S(1)}, f32[4,400,128]{2,1,0:T(8,128)S(1)}, f32[128,128]{1,0:T(8,128)S(1)}) custom-call(s32[3]{0:T(128)S(1)} %pad_add_fusion.info_ref.refs_0_, f32[256,256]{1,0:T(8,128)S(1)} %get-tuple-element.88.weights_ref.own_ref, f32[256,256]{1,0:T(8,128)S(1)} %collective-permute-done.20.other_ref, ...), custom_call_target="tpu_custom_call" | custom-call | flops 1258291200 | bytes 5734400 | tf_op jit(solution)/shard_map/pallas_call | solution.py:78
  130.5 3.3 %collective-permute-start.24 = (f32[256,128]{1,0:T(8,128)S(1)}, f32[256,128]{1,0:T(8,128)S(1)}, u32[]{:S(2)}, u32[]{:S(2)}) collective-permute-start(f32[256,128]{1,0:T(8,128)S(1)} %get-tuple-element.101), channel_id=1, source_target_pairs={{0,16},{16,0},{32,48},{48,32},{64,80},{80,64},{96,112},{112,96},{1... | collective-permute-start | bytes 393224 | tf_op jit(solution)/shard_map/ppermute | solution.py:399
  138.9 2.8 %collective-permute-done.34.odd_ref = f32[384,128]{1,0:T(8,128)S(1)} collective-permute-done((f32[384,128]{1,0:T(8,128)S(1)}, f32[384,128]{1,0:T(8,128)S(1)}, u32[]{:S(2)}, u32[]{:S(2)}) %collective-permute-start.34) | collective-permute-done | bytes 196640 | tf_op jit(solution)/shard_map/ppermute | solution.py:408
  147.4 2.3 %collective-permute-done.29.refs_5_ = f32[128,128]{1,0:T(8,128)S(1)} collective-permute-done((f32[128,128]{1,0:T(8,128)S(1)}, f32[128,128]{1,0:T(8,128)S(1)}, u32[]{:S(2)}, u32[]{:S(2)}) %collective-permute-start.29) | collective-permute-done | bytes 65568 | tf_op jit(solution)/shard_map/ppermute | solution.py:404
  150.9 2.2 %shard_map.51 = (f32[256,256]{1,0:T(8,128)S(1)}, f32[256,128]{1,0:T(8,128)S(1)}, f32[256,128]{1,0:T(8,128)S(1)}, f32[256,256]{1,0:T(8,128)S(1)}) custom-call(s32[3]{0:T(128)S(1)} %pad_add_fusion.info_ref.refs_0_, f32[128,128]{1,0:T(8,128)S(1)} %get-tuple-element.89.refs_0_, f32[384,128]{1,0:T(8,128)S(1)} %collective-permute-done.23.refs_1_.even_ref, ...), custom_call_target="tpu_custom_call" | custom-call | flops 805306368 | bytes 1310720 | tf_op jit(solution)/shard_map/pallas_call | solution.py:78
  153.2 2.2 %collective-permute-start.33 = (f32[256,256]{1,0:T(8,128)S(1)}, f32[256,256]{1,0:T(8,128)S(1)}, u32[]{:S(2)}, u32[]{:S(2)}) collective-permute-start(f32[256,256]{1,0:T(8,128)S(1)} %get-tuple-element.104.weights_ref.own_ref), channel_id=1, source_target_pairs={{0,16},{16,0},{32,48},{48,32},{64,80},{80,64},{96,112},{112,96},{1... | collective-permute-start | bytes 786440 | tf_op jit(solution)/shard_map/ppermute | solution.py:399
  160.0 2.7 %shard_map.53 = (f32[4,400,128]{2,1,0:T(8,128)S(1)}, f32[4,400,128]{2,1,0:T(8,128)S(1)}, f32[4,400,128]{2,1,0:T(8,128)S(1)}, f32[128,128]{1,0:T(8,128)S(1)}) custom-call(s32[3]{0:T(128)S(1)} %pad_add_fusion.info_ref.refs_0_, f32[256,256]{1,0:T(8,128)S(1)} %get-tuple-element.104.weights_ref.own_ref, f32[256,256]{1,0:T(8,128)S(1)} %collective-permute-done.33.other_ref, ...), custom_call_target="tpu_custom_call" | custom-call | flops 1258291200 | bytes 5734400 | tf_op jit(solution)/shard_map/pallas_call | solution.py:78
  166.0 3.5 %collective-permute-start.37 = (f32[256,128]{1,0:T(8,128)S(1)}, f32[256,128]{1,0:T(8,128)S(1)}, u32[]{:S(2)}, u32[]{:S(2)}) collective-permute-start(f32[256,128]{1,0:T(8,128)S(1)} %get-tuple-element.117), channel_id=1, source_target_pairs={{0,16},{16,0},{32,48},{48,32},{64,80},{80,64},{96,112},{112,96},{1... | collective-permute-start | bytes 393224 | tf_op jit(solution)/shard_map/ppermute | solution.py:399
  173.7 2.1 %collective-permute-done.39 = f32[128,128]{1,0:T(8,128)S(1)} collective-permute-done((f32[128,128]{1,0:T(8,128)S(1)}, f32[128,128]{1,0:T(8,128)S(1)}, u32[]{:S(2)}, u32[]{:S(2)}) %collective-permute-start.39) | collective-permute-done | bytes 65568 | tf_op jit(solution)/shard_map/ppermute | solution.py:403
  184.0 2.3 %collective-permute-done.42.refs_5_ = f32[128,128]{1,0:T(8,128)S(1)} collective-permute-done((f32[128,128]{1,0:T(8,128)S(1)}, f32[128,128]{1,0:T(8,128)S(1)}, u32[]{:S(2)}, u32[]{:S(2)}) %collective-permute-start.42) | collective-permute-done | bytes 65568 | tf_op jit(solution)/shard_map/ppermute | solution.py:404
  188.0 2.9 %shard_map.56 = (f32[256,256]{1,0:T(8,128)S(1)}, f32[256,128]{1,0:T(8,128)}, f32[256,128]{1,0:T(8,128)}, f32[256,256]{1,0:T(8,128)S(1)}) custom-call(s32[3]{0:T(128)S(1)} %pad_add_fusion.info_ref.refs_0_, f32[128,128]{1,0:T(8,128)S(1)} %get-tuple-element.105.refs_0_, f32[128,128]{1,0:T(8,128)S(1)} %collective-permute-done.36.refs_1_, ...), custom_call_target="tpu_custom_call" | custom-call | flops 805306368 | bytes 1310720 | tf_op jit(solution)/shard_map/pallas_call | solution.py:78
  191.0 4.2 %shard_map.58 = (f32[8,384,256]{2,1,0:T(8,128)}, f32[2,64,256]{2,1,0:T(8,128)}, f32[1,256]{1,0:T(1,128)}) custom-call(s32[3]{0:T(128)S(1)} %pad_add_fusion.info_ref.refs_0_, f32[256,256]{1,0:T(8,128)S(1)} %get-tuple-element.119.weights_ref, f32[256,256]{1,0:T(8,128)S(1)} %get-tuple-element.120.gram_ref, ...), custom_call_target="tpu_custom_call" | custom-call | flops 1258291200 | bytes 6553600 | tf_op jit(solution)/shard_map/pallas_call | solution.py:382
  (100 shorter events, 65.2 us)
Async XLA Ops:
  3.8 20.7 %collective-permute-start = (f32[2,2,384,128]{3,2,1,0:T(8,128)S(1)}, f32[2,2,384,128]{3,2,1,0:T(8,128)S(1)}, u32[]{:S(2)}, u32[]{:S(2)}) collective-permute-start(f32[2,2,384,128]{3,2,1,0:T(8,128)S(1)} %get-tuple-element.67), channel_id=1, source_target_pairs={{0,32},{16,48},{32,64},{48,80},{64,96},{80,112},{96,0},{112,16},{1... | collective-permute-start | bytes 2359304 | tf_op jit(solution)/shard_map/ppermute | solution.py:422
  6.0 36.4 %collective-permute-start.1 = (f32[2,2,384,128]{3,2,1,0:T(8,128)S(1)}, f32[2,2,384,128]{3,2,1,0:T(8,128)S(1)}, u32[]{:S(2)}, u32[]{:S(2)}) collective-permute-start(f32[2,2,384,128]{3,2,1,0:T(8,128)S(1)} %get-tuple-element.68), channel_id=1, source_target_pairs={{0,64},{16,80},{32,96},{48,112},{64,0},{80,16},{96,32},{112,48},{1... | collective-permute-start | bytes 2359304 | tf_op jit(solution)/shard_map/ppermute | solution.py:422
  8.6 33.8 %collective-permute-start.2 = (f32[2,2,384,128]{3,2,1,0:T(8,128)S(1)}, f32[2,2,384,128]{3,2,1,0:T(8,128)S(1)}, u32[]{:S(2)}, u32[]{:S(2)}) collective-permute-start(f32[2,2,384,128]{3,2,1,0:T(8,128)S(1)} %get-tuple-element.69), channel_id=1, source_target_pairs={{0,96},{16,112},{32,0},{48,16},{64,32},{80,48},{96,64},{112,80},{1... | collective-permute-start | bytes 2359304 | tf_op jit(solution)/shard_map/ppermute | solution.py:422
  43.9 22.5 %collective-permute-start.4 = (f32[2,384,128]{2,1,0:T(8,128)S(1)}, f32[2,384,128]{2,1,0:T(8,128)S(1)}, u32[]{:S(2)}, u32[]{:S(2)}) collective-permute-start(f32[2,384,128]{2,1,0:T(8,128)S(1)} %get-tuple-element.72), channel_id=1, source_target_pairs={{0,32},{16,48},{32,64},{48,80},{64,96},{80,112},{96,0},{112,16},{1... | collective-permute-start | bytes 1179656 | tf_op jit(solution)/shard_map/ppermute | solution.py:426
  45.1 21.3 %collective-permute-start.5 = (f32[2,384,128]{2,1,0:T(8,128)S(1)}, f32[2,384,128]{2,1,0:T(8,128)S(1)}, u32[]{:S(2)}, u32[]{:S(2)}) collective-permute-start(f32[2,384,128]{2,1,0:T(8,128)S(1)} %get-tuple-element.73), channel_id=1, source_target_pairs={{0,96},{16,112},{32,0},{48,16},{64,32},{80,48},{96,64},{112,80},{1... | collective-permute-start | bytes 1179656 | tf_op jit(solution)/shard_map/ppermute | solution.py:426
  50.6 21.2 %collective-permute-start.6 = (f32[2,384,128]{2,1,0:T(8,128)}, f32[2,384,128]{2,1,0:T(8,128)}, u32[]{:S(2)}, u32[]{:S(2)}) collective-permute-start(f32[2,384,128]{2,1,0:T(8,128)} %get-tuple-element.74), channel_id=1, source_target_pairs={{0,64},{16,80},{32,96},{48,112},{64,0},{80,16},{96,32},{112,48},{1... | collective-permute-start | bytes 1179656 | tf_op jit(solution)/shard_map/ppermute | solution.py:426
  67.6 11.4 %all-to-all-start.1 = ((f32[16,3,8,128]{3,2,1,0:T(8,128)}), f32[16,3,8,128]{3,2,1,0:T(8,128)}, u32[]{:S(2)}, u32[]{:S(2)}) async-start(f32[16,3,8,128]{3,2,1,0:T(8,128)} %copy-done.1), calls=%async_computation.1 | async-start | bytes 393216 | tf_op jit(solution)/shard_map/all_to_all | solution.py:428
  82.1 7.6 %collective-permute-start.9 = (f32[256,256]{1,0:T(8,128)S(1)}, f32[256,256]{1,0:T(8,128)S(1)}, u32[]{:S(2)}, u32[]{:S(2)}) collective-permute-start(f32[256,256]{1,0:T(8,128)S(1)} %get-tuple-element.76.weights_ref.own_ref), channel_id=1, source_target_pairs={{0,16},{16,0},{32,48},{48,32},{64,80},{80,64},{96,112},{112,96},{1... | collective-permute-start | bytes 786440 | tf_op jit(solution)/shard_map/ppermute | solution.py:399
  85.3 7.6 %collective-permute-start.8 = (f32[256,128]{1,0:T(8,128)S(1)}, f32[256,128]{1,0:T(8,128)S(1)}, u32[]{:S(2)}, u32[]{:S(2)}) collective-permute-start(f32[256,128]{1,0:T(8,128)S(1)} %get-tuple-element.78), channel_id=1, source_target_pairs={{16,48},{48,80},{80,112},{112,16},{17,49},{49,81},{81,113},{113,17... | collective-permute-start | bytes 393224 | tf_op jit(solution)/shard_map/ppermute | solution.py:408
  87.3 5.7 %collective-permute-start.7 = (f32[256,128]{1,0:T(8,128)S(1)}, f32[256,128]{1,0:T(8,128)S(1)}, u32[]{:S(2)}, u32[]{:S(2)}) collective-permute-start(f32[256,128]{1,0:T(8,128)S(1)} %get-tuple-element.78), channel_id=1, source_target_pairs={{16,32},{48,64},{80,96},{112,0},{17,33},{49,65},{81,97},{113,1},{1... | collective-permute-start | bytes 393224 | tf_op jit(solution)/shard_map/ppermute | solution.py:408
  95.3 5.4 %collective-permute-start.11 = (f32[256,128]{1,0:T(8,128)S(1)}, f32[256,128]{1,0:T(8,128)S(1)}, u32[]{:S(2)}, u32[]{:S(2)}) collective-permute-start(f32[256,128]{1,0:T(8,128)S(1)} %get-tuple-element.85), channel_id=1, source_target_pairs={{0,16},{16,0},{32,48},{48,32},{64,80},{80,64},{96,112},{112,96},{1... | collective-permute-start | bytes 393224 | tf_op jit(solution)/shard_map/ppermute | solution.py:399
  97.4 7.9 %collective-permute-start.21 = (f32[384,128]{1,0:T(8,128)S(1)}, f32[384,128]{1,0:T(8,128)S(1)}, u32[]{:S(2)}, u32[]{:S(2)}) collective-permute-start(f32[384,128]{1,0:T(8,128)S(1)} %get-tuple-element.84), channel_id=1, source_target_pairs={{16,48},{48,80},{80,112},{112,16},{17,49},{49,81},{81,113},{113,17... | collective-permute-start | bytes 589832 | tf_op jit(solution)/shard_map/ppermute | solution.py:408
  99.4 6.0 %collective-permute-start.10 = (f32[384,128]{1,0:T(8,128)S(1)}, f32[384,128]{1,0:T(8,128)S(1)}, u32[]{:S(2)}, u32[]{:S(2)}) collective-permute-start(f32[384,128]{1,0:T(8,128)S(1)} %get-tuple-element.84), channel_id=1, source_target_pairs={{16,32},{48,64},{80,96},{112,0},{17,33},{49,65},{81,97},{113,1},{1... | collective-permute-start | bytes 589832 | tf_op jit(solution)/shard_map/ppermute | solution.py:408
  100.7 6.9 %collective-permute-start.14 = (f32[128,128]{1,0:T(8,128)S(1)}, f32[128,128]{1,0:T(8,128)S(1)}, u32[]{:S(2)}, u32[]{:S(2)}) collective-permute-start(f32[128,128]{1,0:T(8,128)S(1)} %slice_add_fusion.2), channel_id=1, source_target_pairs={{0,3},{1,0},{2,1},{3,2},{4,7},{5,4},{6,5},{7,6},{8,11},{9,8},{10,9... | collective-permute-start | bytes 196616 | tf_op jit(solution)/shard_map/ppermute | solution.py:403
  101.3 6.2 %collective-permute-start.13 = (f32[128,128]{1,0:T(8,128)S(1)}, f32[128,128]{1,0:T(8,128)S(1)}, u32[]{:S(2)}, u32[]{:S(2)}) collective-permute-start(f32[128,128]{1,0:T(8,128)S(1)} %slice_add_fusion.2), channel_id=1, source_target_pairs={{0,2},{1,3},{2,0},{3,1},{4,6},{5,7},{6,4},{7,5},{8,10},{9,11},{10,... | collective-permute-start | bytes 196616 | tf_op jit(solution)/shard_map/ppermute | solution.py:403
  107.0 21.7 %collective-permute-start.22 = (f32[4,400,128]{2,1,0:T(8,128)S(1)}, f32[4,400,128]{2,1,0:T(8,128)S(1)}, u32[]{:S(2)}, u32[]{:S(2)}) collective-permute-start(f32[4,400,128]{2,1,0:T(8,128)S(1)} %get-tuple-element.99), channel_id=1, source_target_pairs={{0,32},{16,48},{32,64},{48,80},{64,96},{80,112},{96,0},{112,16},{1... | collective-permute-start | bytes 2457608 | tf_op jit(solution)/shard_map/ppermute | solution.py:447
  116.8 8.0 %collective-permute-start.20 = (f32[256,256]{1,0:T(8,128)S(1)}, f32[256,256]{1,0:T(8,128)S(1)}, u32[]{:S(2)}, u32[]{:S(2)}) collective-permute-start(f32[256,256]{1,0:T(8,128)S(1)} %get-tuple-element.88.weights_ref.own_ref), channel_id=1, source_target_pairs={{0,16},{16,0},{32,48},{48,32},{64,80},{80,64},{96,112},{112,96},{1... | collective-permute-start | bytes 786440 | tf_op jit(solution)/shard_map/ppermute | solution.py:399
  119.8 8.9 %collective-permute-start.19 = (f32[256,128]{1,0:T(8,128)S(1)}, f32[256,128]{1,0:T(8,128)S(1)}, u32[]{:S(2)}, u32[]{:S(2)}) collective-permute-start(f32[256,128]{1,0:T(8,128)S(1)} %get-tuple-element.90), channel_id=1, source_target_pairs={{16,48},{48,80},{80,112},{112,16},{17,49},{49,81},{81,113},{113,17... | collective-permute-start | bytes 393224 | tf_op jit(solution)/shard_map/ppermute | solution.py:408
  122.4 6.3 %collective-permute-start.18 = (f32[256,128]{1,0:T(8,128)S(1)}, f32[256,128]{1,0:T(8,128)S(1)}, u32[]{:S(2)}, u32[]{:S(2)}) collective-permute-start(f32[256,128]{1,0:T(8,128)S(1)} %get-tuple-element.90), channel_id=1, source_target_pairs={{16,32},{48,64},{80,96},{112,0},{17,33},{49,65},{81,97},{113,1},{1... | collective-permute-start | bytes 393224 | tf_op jit(solution)/shard_map/ppermute | solution.py:408
  130.5 6.5 %collective-permute-start.24 = (f32[256,128]{1,0:T(8,128)S(1)}, f32[256,128]{1,0:T(8,128)S(1)}, u32[]{:S(2)}, u32[]{:S(2)}) collective-permute-start(f32[256,128]{1,0:T(8,128)S(1)} %get-tuple-element.101), channel_id=1, source_target_pairs={{0,16},{16,0},{32,48},{48,32},{64,80},{80,64},{96,112},{112,96},{1... | collective-permute-start | bytes 393224 | tf_op jit(solution)/shard_map/ppermute | solution.py:399
  133.8 7.9 %collective-permute-start.34 = (f32[384,128]{1,0:T(8,128)S(1)}, f32[384,128]{1,0:T(8,128)S(1)}, u32[]{:S(2)}, u32[]{:S(2)}) collective-permute-start(f32[384,128]{1,0:T(8,128)S(1)} %get-tuple-element.100), channel_id=1, source_target_pairs={{16,48},{48,80},{80,112},{112,16},{17,49},{49,81},{81,113},{113,17... | collective-permute-start | bytes 589832 | tf_op jit(solution)/shard_map/ppermute | solution.py:408
  135.7 6.0 %collective-permute-start.23 = (f32[384,128]{1,0:T(8,128)S(1)}, f32[384,128]{1,0:T(8,128)S(1)}, u32[]{:S(2)}, u32[]{:S(2)}) collective-permute-start(f32[384,128]{1,0:T(8,128)S(1)} %get-tuple-element.100), channel_id=1, source_target_pairs={{16,32},{48,64},{80,96},{112,0},{17,33},{49,65},{81,97},{113,1},{1... | collective-permute-start | bytes 589832 | tf_op jit(solution)/shard_map/ppermute | solution.py:408
  137.1 5.9 %collective-permute-start.27 = (f32[128,128]{1,0:T(8,128)S(1)}, f32[128,128]{1,0:T(8,128)S(1)}, u32[]{:S(2)}, u32[]{:S(2)}) collective-permute-start(f32[128,128]{1,0:T(8,128)S(1)} %slice_add_fusion.1), channel_id=1, source_target_pairs={{0,3},{1,0},{2,1},{3,2},{4,7},{5,4},{6,5},{7,6},{8,11},{9,8},{10,9... | collective-permute-start | bytes 196616 | tf_op jit(solution)/shard_map/ppermute | solution.py:403
  137.7 5.2 %collective-permute-start.26 = (f32[128,128]{1,0:T(8,128)S(1)}, f32[128,128]{1,0:T(8,128)S(1)}, u32[]{:S(2)}, u32[]{:S(2)}) collective-permute-start(f32[128,128]{1,0:T(8,128)S(1)} %slice_add_fusion.1), channel_id=1, source_target_pairs={{0,2},{1,3},{2,0},{3,1},{4,6},{5,7},{6,4},{7,5},{8,10},{9,11},{10,... | collective-permute-start | bytes 196616 | tf_op jit(solution)/shard_map/ppermute | solution.py:403
  138.9 5.3 %collective-permute-start.25 = (f32[128,128]{1,0:T(8,128)S(1)}, f32[128,128]{1,0:T(8,128)S(1)}, u32[]{:S(2)}, u32[]{:S(2)}) collective-permute-start(f32[128,128]{1,0:T(8,128)S(1)} %slice_add_fusion.1), channel_id=1, source_target_pairs={{0,1},{1,2},{2,3},{3,0},{4,5},{5,6},{6,7},{7,4},{8,9},{9,10},{10,1... | collective-permute-start | bytes 196616 | tf_op jit(solution)/shard_map/ppermute | solution.py:403
  142.9 21.3 %collective-permute-start.35 = (f32[4,400,128]{2,1,0:T(8,128)S(1)}, f32[4,400,128]{2,1,0:T(8,128)S(1)}, u32[]{:S(2)}, u32[]{:S(2)}) collective-permute-start(f32[4,400,128]{2,1,0:T(8,128)S(1)} %get-tuple-element.115), channel_id=1, source_target_pairs={{0,32},{16,48},{32,64},{48,80},{64,96},{80,112},{96,0},{112,16},{1... | collective-permute-start | bytes 2457608 | tf_op jit(solution)/shard_map/ppermute | solution.py:447
  153.2 6.8 %collective-permute-start.33 = (f32[256,256]{1,0:T(8,128)S(1)}, f32[256,256]{1,0:T(8,128)S(1)}, u32[]{:S(2)}, u32[]{:S(2)}) collective-permute-start(f32[256,256]{1,0:T(8,128)S(1)} %get-tuple-element.104.weights_ref.own_ref), channel_id=1, source_target_pairs={{0,16},{16,0},{32,48},{48,32},{64,80},{80,64},{96,112},{112,96},{1... | collective-permute-start | bytes 786440 | tf_op jit(solution)/shard_map/ppermute | solution.py:399
  155.4 8.8 %collective-permute-start.32 = (f32[256,128]{1,0:T(8,128)S(1)}, f32[256,128]{1,0:T(8,128)S(1)}, u32[]{:S(2)}, u32[]{:S(2)}) collective-permute-start(f32[256,128]{1,0:T(8,128)S(1)} %get-tuple-element.106), channel_id=1, source_target_pairs={{16,48},{48,80},{80,112},{112,16},{17,49},{49,81},{81,113},{113,17... | collective-permute-start | bytes 393224 | tf_op jit(solution)/shard_map/ppermute | solution.py:408
  157.3 6.9 %collective-permute-start.31 = (f32[256,128]{1,0:T(8,128)S(1)}, f32[256,128]{1,0:T(8,128)S(1)}, u32[]{:S(2)}, u32[]{:S(2)}) collective-permute-start(f32[256,128]{1,0:T(8,128)S(1)} %get-tuple-element.106), channel_id=1, source_target_pairs={{16,32},{48,64},{80,96},{112,0},{17,33},{49,65},{81,97},{113,1},{1... | collective-permute-start | bytes 393224 | tf_op jit(solution)/shard_map/ppermute | solution.py:408
  172.1 5.3 %collective-permute-start.38 = (f32[128,128]{1,0:T(8,128)S(1)}, f32[128,128]{1,0:T(8,128)S(1)}, u32[]{:S(2)}, u32[]{:S(2)}) collective-permute-start(f32[128,128]{1,0:T(8,128)S(1)} %slice_add_fusion), channel_id=1, source_target_pairs={{0,1},{1,2},{2,3},{3,0},{4,5},{5,6},{6,7},{7,4},{8,9},{9,10},{10,1... | collective-permute-start | bytes 196616 | tf_op jit(solution)/shard_map/ppermute | solution.py:403
  178.1 12.8 %collective-permute-start.44 = (f32[4,400,128]{2,1,0:T(8,128)S(1)}, f32[4,400,128]{2,1,0:T(8,128)S(1)}, u32[]{:S(2)}, u32[]{:S(2)}) collective-permute-start(f32[4,400,128]{2,1,0:T(8,128)S(1)} %get-tuple-element.124), channel_id=1, source_target_pairs={{0,16},{16,0},{32,48},{48,32},{64,80},{80,64},{96,112},{112,96},{1... | collective-permute-start | bytes 2457608 | tf_op jit(solution)/shard_map/ppermute | solution.py:399
  179.4 11.5 %collective-permute-start.45 = (f32[4,400,128]{2,1,0:T(8,128)S(1)}, f32[4,400,128]{2,1,0:T(8,128)S(1)}, u32[]{:S(2)}, u32[]{:S(2)}) collective-permute-start(f32[4,400,128]{2,1,0:T(8,128)S(1)} %get-tuple-element.125), channel_id=1, source_target_pairs={{0,16},{16,0},{32,48},{48,32},{64,80},{80,64},{96,112},{112,96},{1... | collective-permute-start | bytes 2457608 | tf_op jit(solution)/shard_map/ppermute | solution.py:399
  (19 other events, 117.6 us)

commit v6 on v5

--- a/solution.py
+++ b/solution.py
@@ -21,7 +21,7 @@
 NEXT_SLOT = [(c, (c + 1) % COLS) for c in range(COLS)]
 CHIPS_ON = [[(c, (c + 2 * k) % COLS) for c in range(COLS)] for k in range(SIDE)]
 ODD_TO_EVEN = [(c, (c + 1) % COLS) for c in range(1, COLS, 2)]
-ODD_TO_ODD = [(c, (c + 2) % COLS) for c in range(1, COLS, 2)]
+EVEN_TO_ODD = [(c, c + 1) for c in range(0, COLS, 2)]
 ALONG_X = [[(r, r - r % SIDE + (r + k) % SIDE) for r in range(ROWS)] for k in range(1, SIDE)]
 ALONG_Z = [[(r, (r + SIDE * k) % ROWS) for r in range(ROWS)] for k in range(1, SIDE)]
 
@@ -154,24 +154,39 @@
             squares = squares + dot(high, high, 0)
             mixed = mixed + dot(high, low, 0)
         grams.append(squares + (mixed + mixed.T))
+    rows = lax.broadcasted_iota(jnp.int32, (BLOCK, BLOCK), 0)
+    columns = lax.broadcasted_iota(jnp.int32, (BLOCK, BLOCK), 1)
     for ref, gram in ((keep_ref, jnp.where(first, grams[0], grams[1])), (send_ref, jnp.where(first, grams[1], grams[0]))):
-        for k, block in enumerate((gram[:BLOCK, :BLOCK], gram[:BLOCK, BLOCK:], gram[BLOCK:, BLOCK:])):
-            ref[:, k] = block.reshape(ROWS, BLOCK // ROWS, BLOCK)
+        low = gram[BLOCK:, BLOCK:]
+        diagonal = jnp.sum(jnp.where(rows == columns, low, 0.0), axis=0, keepdims=True)
+        ref[:BLOCK] = gram[:BLOCK, BLOCK:]
+        ref[BLOCK:PAIR] = jnp.where(rows <= columns, gram[:BLOCK, :BLOCK], low)
+        ref[PAIR:] = jnp.broadcast_to(diagonal, (8, BLOCK))
+
+
+def unpacked(packed):
+    rows = lax.broadcasted_iota(jnp.int32, (BLOCK, BLOCK), 0)
+    columns = lax.broadcasted_iota(jnp.int32, (BLOCK, BLOCK), 1)
+    triangles = packed[BLOCK:PAIR]
+    turned = triangles.T
+    up = jnp.where(rows <= columns, triangles, turned)
+    low = jnp.where(rows > columns, triangles, jnp.where(rows < columns, turned, packed[PAIR : PAIR + 1]))
+    return up, packed[:BLOCK], low
 
 
 def first_grams(info, main):
-    out = shape(ROWS, 3, BLOCK // ROWS, BLOCK)
+    out = shape(PAIR + 8, BLOCK)
     return call_whole(
         gram_kernel, (info, *main), [out, out], flops=2 * 2 * 4 * main[0].size * PAIR, nbytes=16 * main[0].size
     )
 
 
-def spread_kernel(info_ref, parts_ref, out_ref):
-    out_ref[...] = jnp.broadcast_to(jnp.sum(parts_ref[...], axis=0)[None], out_ref.shape)
-
-
-def spread_parts(info, parts, before):
-    return call_whole(spread_kernel, (info, parts), [shape(*parts.shape)], before, nbytes=8 * parts.size)[0]
+def sum_kernel(info_ref, *refs):
+    refs[-1][...] = (refs[0][...] + refs[1][...]) + (refs[2][...] + refs[3][...])
+
+
+def sum_parts(info, parts, before):
+    return call_whole(sum_kernel, (info, *parts), [shape(*parts[0].shape)], before, nbytes=20 * parts[0].size)[0]
 
 
 def rotation_of(gram, x_ref, r_ref):
@@ -204,53 +219,58 @@
 
 
 def cayley_kernel(fill, info_ref, *refs):
-    weights_ref, up_ref, low_ref, gram_ref, x_ref, r_ref = refs[-6:]
-    up, cross, low = fill(info_ref, *refs[:-6])
+    weights_ref, gram_ref, x_ref, r_ref = refs[-4:]
+    up, cross, low = fill(info_ref, *refs[:-4])
     gram_ref[:BLOCK, :BLOCK] = up
     gram_ref[:BLOCK, BLOCK:] = cross
     gram_ref[BLOCK:, :BLOCK] = cross.T
     gram_ref[BLOCK:, BLOCK:] = low
     weights = rotation_of(gram_ref[...], x_ref, r_ref)
-    weights_ref[...] = weights
-    up_ref[...] = weights[:, :BLOCK]
-    low_ref[...] = weights[:, BLOCK:]
-
-
-def cayley_call(fill, args, before=()):
+    weights_ref[:PAIR] = weights
+    if weights_ref.shape[0] > PAIR:
+        turned = mm3(weights[:, BLOCK:], mm3(gram_ref[...], weights[:, BLOCK:]), 0)
+        weights_ref[PAIR:, :BLOCK] = turned[: BLOCK // 2]
+        weights_ref[PAIR:, BLOCK:] = turned[BLOCK // 2 :]
+
+
+def cayley_call(fill, args, before=(), last=False):
     return call_whole(
         functools.partial(cayley_kernel, fill),
         args,
-        [shape(PAIR, PAIR), shape(PAIR, BLOCK), shape(PAIR, BLOCK), shape(PAIR, PAIR)],
+        [shape(PAIR if last else PAIR + BLOCK // 2, PAIR), shape(PAIR, PAIR)],
         before,
         scratch=[pltpu.VMEM((PAIR, PAIR), F32)] * 2,
         flops=2 * 3 * 8 * PAIR**3,
-        nbytes=20 * PAIR * PAIR,
-    )
-
-
-def first_cayley(info, blocks, before):
-    return cayley_call(lambda _, ref: [ref[:, k].reshape(BLOCK, BLOCK) for k in range(3)], (info, blocks), before)
-
-
-def cayley(info, up, across_chips, across_cores, parts):
-    def fill(info_ref, up_ref, chips_ref, cores_ref, *part_refs):
-        first, second, third, fourth = (ref[...] for ref in part_refs)
-        low = jnp.where(info_ref[0] == 0, chips_ref[-BLOCK:], cores_ref[-BLOCK:])
-        return up_ref[...], (first + second) + (third + fourth), low
-
-    return cayley_call(fill, (info, up, across_chips, across_cores, *parts))
-
-
-def project_kernel(info_ref, gram_ref, weights_ref, up_ref, low_ref):
-    weights = weights_ref[...]
-    turned = mm3(gram_ref[...], weights)
-    up_ref[...] = mm3(weights[:, :BLOCK], turned[:, :BLOCK], 0)
-    low_ref[...] = mm3(weights[:, BLOCK:], turned[:, BLOCK:], 0)
+        nbytes=16 * PAIR * PAIR,
+    )
+
+
+def total_of(part_refs):
+    first, second, third, fourth = (ref[...] for ref in part_refs)
+    return (first + second) + (third + fourth)
+
+
+def first_cayley(info, parts, before):
+    return cayley_call(lambda _, *part_refs: unpacked(total_of(part_refs)), (info, *parts), before)
+
+
+def cayley(info, up, even, other, parts, before, last):
+    def fill(info_ref, up_ref, even_ref, other_ref, *part_refs):
+        folded = jnp.where(info_ref[0] == 0, even_ref[PAIR:], other_ref[PAIR:])
+        low = jnp.concatenate([folded[:, :BLOCK], folded[:, BLOCK:]], axis=0)
+        return up_ref[...], total_of(part_refs), low
+
+    return cayley_call(fill, (info, up, even, other, *parts), before, last)
+
+
+def project_kernel(info_ref, gram_ref, weights_ref, up_ref):
+    weights = weights_ref[:PAIR, :BLOCK]
+    up_ref[...] = mm3(weights, mm3(gram_ref[...], weights), 0)
 
 
 def project(info, gram, weights):
-    out = [shape(BLOCK, BLOCK)] * 2
-    return call_whole(project_kernel, (info, gram, weights), out, flops=2 * 3 * 2 * PAIR**3, nbytes=12 * PAIR * PAIR)
+    out = [shape(BLOCK, BLOCK)]
+    return call_whole(project_kernel, (info, gram, weights), out, flops=2 * 3 * PAIR**3, nbytes=12 * PAIR * PAIR)[0]
 
 
 def start_pair(info_ref, step, group, slot, up, low):
@@ -276,8 +296,8 @@
 def own_kernel(rows, step, info_ref, own_ref, other_ref, *refs):
     up0_ref, up1_ref, low1_ref, cross_ref = refs[-4:]
     first = info_ref[0] == 0
-    weights0 = jnp.where(first, own_ref[...], other_ref[...])
-    weights1 = jnp.where(first, other_ref[:, :BLOCK], own_ref[:, :BLOCK])
+    weights0 = jnp.where(first, own_ref[:PAIR], other_ref[:PAIR])
+    weights1 = jnp.where(first, other_ref[:PAIR, :BLOCK], own_ref[:PAIR, :BLOCK])
     slot = 2 * info_ref[1]
     cross = jnp.zeros((BLOCK, BLOCK), F32)
     for group, (pair0, pair1) in groups_of(info_ref, step, refs[:-4], (slot, slot + 1)):
@@ -290,62 +310,57 @@
     cross_ref[...] = cross
 
 
-def rotate_own(info, own, other, blocks, rows, step):
+def rotate_own(info, own, other, blocks, before, rows, step):
     return call_whole(
         functools.partial(own_kernel, rows, step),
         (info, own, other, *blocks),
         [shape(SIDE, step, BLOCK)] * 3 + [shape(BLOCK, BLOCK)],
+        before,
         flops=2 * 3 * SIDE * step * 4 * BLOCK * PAIR,
         nbytes=4 * 7 * SIDE * step * BLOCK,
     )
 
 
-def ahead_kernel(rows, step, info_ref, even_ref, odd_ref, upper_ref, low_ref, cross_ref, up0_ref, *refs):
-    low0_ref, keep_ref, send_ref, bundle_ref = refs[-4:]
-    low = low_ref[...]
-    if bundle_ref.shape[0] > BLOCK:
-        bundle_ref[:PAIR] = upper_ref[...]
-    bundle_ref[-BLOCK:] = low
-    send_ref[BLOCK:] = low
-    weights = even_ref[...] + odd_ref[...]
+def ahead_kernel(rows, step, info_ref, even_ref, odd_ref, cross_ref, up0_ref, *refs):
+    low0_ref, keep_ref, send_ref = refs[-3:]
+    weights = even_ref[:PAIR, BLOCK:] + odd_ref[:, BLOCK:]
     slot = (2 * info_ref[1] + COLS - 1) % COLS
     total = jnp.zeros((BLOCK, BLOCK), F32)
-    for group, (pair,) in groups_of(info_ref, step, refs[:-4], (slot,)):
+    for group, (pair,) in groups_of(info_ref, step, refs[:-3], (slot,)):
         low0 = mm3(pair, weights)
         low0_ref[group] = low0
         total = total + mm3(up0_ref[group, :rows], low0[:rows], 0)
     first = info_ref[0] == 0
     keep_ref[...] = jnp.where(first, total, cross_ref[...])
-    send_ref[:BLOCK] = jnp.where(first, cross_ref[...], total)
-
-
-def rotate_ahead(info, lower, upper, low, cross, up0, blocks, last, rows, step):
+    send_ref[...] = jnp.where(first, cross_ref[...], total)
+
+
+def rotate_ahead(info, ahead, cross, up0, blocks, rows, step):
     return call_whole(
         functools.partial(ahead_kernel, rows, step),
-        (info, *lower, upper, low, cross, up0, *blocks),
-        [shape(SIDE, step, BLOCK), shape(BLOCK, BLOCK), shape(2 * BLOCK, BLOCK), shape(BLOCK if last else 3 * BLOCK, BLOCK)],
+        (info, *ahead, cross, up0, *blocks),
+        [shape(SIDE, step, BLOCK), shape(BLOCK, BLOCK), shape(BLOCK, BLOCK)],
         flops=2 * 3 * SIDE * step * 2 * BLOCK * PAIR,
         nbytes=4 * 4 * SIDE * step * BLOCK,
     )
 
 
-def up_kernel(step, info_ref, even_ref, odd_ref, low1_ref, *refs):
-    up_ref, pass_ref = refs[-2:]
-    weights = even_ref[:PAIR] + odd_ref[:PAIR]
+def up_kernel(step, info_ref, even_ref, odd_ref, *refs):
+    up_ref = refs[-1]
+    weights = even_ref[:PAIR, :BLOCK] + odd_ref[:, :BLOCK]
     slot = (2 * info_ref[1] + COLS - 1) % COLS
-    for group, (pair,) in groups_of(info_ref, step, refs[:-2], (slot,)):
+    for group, (pair,) in groups_of(info_ref, step, refs[:-1], (slot,)):
         up_ref[group] = mm3(pair, weights)
-    pass_ref[...] = low1_ref[...]
-
-
-def rotate_up(info, upper, low1, blocks, step):
+
+
+def rotate_up(info, ahead, blocks, step):
     return call_whole(
         functools.partial(up_kernel, step),
-        (info, *upper, low1, *blocks),
-        [shape(SIDE, step, BLOCK)] * 2,
+        (info, *ahead, *blocks),
+        [shape(SIDE, step, BLOCK)],
         flops=2 * 3 * SIDE * step * BLOCK * PAIR,
-        nbytes=4 * 5 * SIDE * step * BLOCK,
-    )
+        nbytes=4 * 3 * SIDE * step * BLOCK,
+    )[0]
 
 
 def other_slot_kernel(info_ref, up0_ref, low0_ref, up1_ref, low1_ref, up_ref, low_ref):
@@ -399,13 +414,18 @@
     return lax.ppermute(value, "cols", TURN_CORE)
 
 
-def sum_over_rows(value):
-    value = value + sum(lax.ppermute(value, "rows", pairs) for pairs in ALONG_X)
-    return [value] + [lax.ppermute(value, "rows", pairs) for pairs in ALONG_Z]
-
-
-def to_next_chip(value):
-    return [lax.ppermute(value, "cols", pairs) for pairs in (ODD_TO_EVEN, ODD_TO_ODD)]
+def along(value, shifts):
+    return [lax.ppermute(value, "rows", pairs) for pairs in shifts]
+
+
+def same_kernel(info_ref, value_ref, out_ref):
+    out_ref[...] = value_ref[: out_ref.shape[0]]
+
+
+def odd_slot_before(info, weights, before):
+    even = lax.ppermute(weights, "cols", ODD_TO_EVEN)
+    copy = call_whole(same_kernel, (info, even), [shape(PAIR, PAIR)], before, nbytes=8 * PAIR * PAIR)[0]
+    return [even, lax.ppermute(copy, "cols", EVEN_TO_ODD)]
 
 
 def body(sensitivity):
@@ -424,28 +444,30 @@
     keep, send = first_grams(info, main)
     packed = pack_ahead(info, x, main[1:])
     ahead = [packed[0]] + [lax.ppermute(packed[k], "cols", CHIPS_ON[k]) for k in range(1, SIDE)]
-    parts = lax.all_to_all(keep + swap_core(send), "rows", 0, 0, tiled=True)
-    parts = lax.all_to_all(spread_parts(info, parts, [ahead[1], ahead[3]]), "rows", 0, 0, tiled=True)
-    weights, upper, lower, gram = first_cayley(info, parts, [ahead[2]])
+    value = keep + swap_core(send)
+    value = sum_parts(info, [value] + along(value, ALONG_X), [ahead[1], ahead[3]])
+    weights, gram = first_cayley(info, [value] + along(value, ALONG_Z), [ahead[2]])
 
     own_blocks = main
     ahead_blocks = [value[None] for value in ahead]
     for sweep_round in range(ROUNDS - 1):
         last = sweep_round == ROUNDS - 2
-        lower = to_next_chip(lower)
-        up, low = project(info, gram, weights)
-        up0, up1, low1, cross = rotate_own(info, weights, swap_core(weights), own_blocks, rows, step)
-        low0, keep, send, bundle = rotate_ahead(info, lower, upper, low, cross, up0, ahead_blocks, last, rows, step)
-        received = swap_core(send)
-        parts = sum_over_rows(keep + received[:BLOCK])
+        other = swap_core(weights)
+        up = project(info, gram, weights)
+        before = [up] + ([ahead_blocks[0]] if sweep_round else [])
+        up0, up1, low1, cross = rotate_own(info, weights, other, own_blocks, before, rows, step)
+        weights_m = odd_slot_before(info, weights, [cross])
+        low0, keep, send = rotate_ahead(info, weights_m, cross, up0, ahead_blocks, rows, step)
+        value = keep + swap_core(send)
+        value = value + sum(along(value, ALONG_X))
         own_blocks = [up0, low0, up1, low1]
-        bundles = to_next_chip(bundle)
         if last:
-            other_blocks = [swap_core(value) for value in other_slot(info, own_blocks, [parts[0]])]
+            other_blocks = [swap_core(block) for block in other_slot(info, own_blocks, [value])]
         else:
-            up_m, passed = rotate_up(info, bundles, low1, ahead_blocks, step)
-            ahead_blocks = [up_m, lax.ppermute(passed, "cols", CHIPS_ON[1])]
-        weights, upper, lower, gram = cayley(info, up, bundles[0], received, parts)
+            up_m = rotate_up(info, weights_m, ahead_blocks, step)
+            ahead_blocks = [up_m, lax.ppermute(low1, "cols", CHIPS_ON[1])]
+        before = [] if last else [ahead_blocks[1]]
+        weights, gram = cayley(info, up, weights_m[0], other, [value] + along(value, ALONG_Z), before, last)
 
     rotated, frame, column_scale = rotate_final(info, weights, gram, own_blocks + other_blocks, rows, step)
     return rotated, frame.reshape(2 * basis_rows, PAIR), column_scale.reshape(PAIR)

time: 198 us -> 192 us (0.970); the launches traced: 195 us -> 192 us
  waiting for transfers between devices: 70.5 us -> 91.4 us
  blocking collectives: 14.6 us -> 0 us
  starting transfers between devices: 65.5 us -> 57.2 us
    ppermute x31 -> x32, waiting for transfers between devices: 29.5 us -> 54.7 us  [the longest x24 43.6 us: along(): return [lax.ppermute(value, 'rows', pairs) for pairs in shifts]]
    all_to_all x1 -> x0, blocking collectives: 14.6 us -> none  [body(): parts = lax.all_to_all(keep + swap_core(send), 'rows', 0, 0, tiled=True)]
    all_to_all x1 -> x0, waiting for transfers between devices: 7.19 us -> none  [body(): lax.all_to_all(spread_parts(info, parts, [ahead[1], ahead[3]]), 'rows', 0...]
    ppermute x9, starting transfers between devices: 20.6 us -> 15 us  [swap_core(): return lax.ppermute(value, 'cols', TURN_CORE)]
    all_to_all x1 -> x0, starting transfers between devices: 4.17 us -> none  [body(): lax.all_to_all(spread_parts(info, parts, [ahead[1], ahead[3]]), 'rows', 0...]
    ppermute x9, waiting for transfers between devices: 1.01 us -> 3.37 us  [swap_core(): return lax.ppermute(value, 'cols', TURN_CORE)]
    ppermute x31 -> x32, starting transfers between devices: 30.8 us -> 32.5 us  [the longest x24 21.2 us: along(): return [lax.ppermute(value, 'rows', pairs) for pairs in shifts]]
    pallas_call x18 -> x21, Pallas kernels: 33.9 us -> 34.3 us  [call_whole(): pl.pallas_call(inner, in_specs=[pl.BlockSpec(memory_space=pltpu.SMEM)] +...]
  transfers between devices with their start and end apart: 47 -> 47, of which waited for: 23 -> 34; matrix products, arithmetic and copies ran while one was open for 0% -> 0% of each run, Pallas kernels for 12% -> 11%
where the time goes in v6:
time: 192 us
  waiting for transfers between devices  91.4 us (48%)
  starting transfers between devices  57.2 us (30%)
  Pallas kernels  40.3 us (21%)
    ppermute x24, waiting for transfers between devices, along(): return [lax.ppermute(value, 'rows', pairs) for pairs in shifts]  43.6 us
    pallas_call x21, Pallas kernels, call_whole(): pl.pallas_call(inner, in_specs=[pl.BlockSpec(memory_space=pltpu.SMEM)] +...  34.3 us
    ppermute x6, waiting for transfers between devices, body(): lax.ppermute(packed[k], 'cols', CHIPS_ON[k])  33.3 us
    ppermute x24, starting transfers between devices, along(): return [lax.ppermute(value, 'rows', pairs) for pairs in shifts]  21.2 us
    ppermute x9, starting transfers between devices, swap_core(): return lax.ppermute(value, 'cols', TURN_CORE)  15 us
    ppermute x3, waiting for transfers between devices, odd_slot_before(): return [even, lax.ppermute(copy, 'cols', EVEN_TO_ODD)]  10.9 us
    ppermute x6, starting transfers between devices, body(): lax.ppermute(packed[k], 'cols', CHIPS_ON[k])  9.72 us
    ppermute x3, starting transfers between devices, odd_slot_before(): even = lax.ppermute(weights, 'cols', ODD_TO_EVEN)  7.12 us
  transfers between devices with their start and end apart: 47, of which 34 were waited for; matrix products, arithmetic and copies ran while one was open for 0% of the time, Pallas kernels for 11%

profile of v6, /device:TPU:1, one launch (start us, length us, event | category | flops | bytes accessed | tf_op | source)
XLA Modules:
  0.0 192.0 jit_solution(11418687518452956189)
XLA Ops:
  3.8 2.2 %collective-permute-start = (f32[2,2,384,128]{3,2,1,0:T(8,128)S(1)}, f32[2,2,384,128]{3,2,1,0:T(8,128)S(1)}, u32[]{:S(2)}, u32[]{:S(2)}) collective-permute-start(f32[2,2,384,128]{3,2,1,0:T(8,128)S(1)} %get-tuple-element.48), channel_id=1, source_target_pairs={{0,32},{16,48},{32,64},{48,80},{64,96},{80,112},{96,0},{112,16},{1... | collective-permute-start | bytes 2359304 | tf_op jit(solution)/shard_map/ppermute | solution.py:442
  6.0 2.6 %collective-permute-start.1 = (f32[2,2,384,128]{3,2,1,0:T(8,128)S(1)}, f32[2,2,384,128]{3,2,1,0:T(8,128)S(1)}, u32[]{:S(2)}, u32[]{:S(2)}) collective-permute-start(f32[2,2,384,128]{3,2,1,0:T(8,128)S(1)} %get-tuple-element.49), channel_id=1, source_target_pairs={{0,64},{16,80},{32,96},{48,112},{64,0},{80,16},{96,32},{112,48},{1... | collective-permute-start | bytes 2359304 | tf_op jit(solution)/shard_map/ppermute | solution.py:442
  9.7 14.9 %collective-permute-done.refs_1_.refs_4_ = f32[2,2,384,128]{3,2,1,0:T(8,128)S(1)} collective-permute-done((f32[2,2,384,128]{3,2,1,0:T(8,128)S(1)}, f32[2,2,384,128]{3,2,1,0:T(8,128)S(1)}, u32[]{:S(2)}, u32[]{:S(2)}) %collective-permute-start) | collective-permute-done | bytes 786464 | tf_op jit(solution)/shard_map/ppermute | solution.py:442
  24.6 17.9 %collective-permute-done.1.refs_2_.refs_5_ = f32[2,2,384,128]{3,2,1,0:T(8,128)S(1)} collective-permute-done((f32[2,2,384,128]{3,2,1,0:T(8,128)S(1)}, f32[2,2,384,128]{3,2,1,0:T(8,128)S(1)}, u32[]{:S(2)}, u32[]{:S(2)}) %collective-permute-start.1) | collective-permute-done | bytes 786464 | tf_op jit(solution)/shard_map/ppermute | solution.py:442
  49.5 2.5 %collective-permute-start.6 = (f32[264,128]{1,0:T(8,128)S(1)}, f32[264,128]{1,0:T(8,128)S(1)}, u32[]{:S(2)}, u32[]{:S(2)}) collective-permute-start(f32[264,128]{1,0:T(8,128)S(1)} %add.49.refs_1_), channel_id=1, source_target_pairs={{0,3},{1,0},{2,1},{3,2},{4,7},{5,4},{6,5},{7,6},{8,11},{9,8},{10,9... | collective-permute-start | bytes 405512 | tf_op jit(solution)/shard_map/ppermute | solution.py:418
  55.3 3.2 %collective-permute-done.5.refs_3_ = f32[264,128]{1,0:T(8,128)S(1)} collective-permute-done((f32[264,128]{1,0:T(8,128)S(1)}, f32[264,128]{1,0:T(8,128)S(1)}, u32[]{:S(2)}, u32[]{:S(2)}) %collective-permute-start.5) | collective-permute-done | bytes 135200 | tf_op jit(solution)/shard_map/ppermute | solution.py:418
  58.5 3.3 %collective-permute-done.4.refs_2_ = f32[264,128]{1,0:T(8,128)S(1)} collective-permute-done((f32[264,128]{1,0:T(8,128)S(1)}, f32[264,128]{1,0:T(8,128)S(1)}, u32[]{:S(2)}, u32[]{:S(2)}) %collective-permute-start.4) | collective-permute-done | bytes 135200 | tf_op jit(solution)/shard_map/ppermute | solution.py:418
  62.4 3.8 %collective-permute-start.11 = (f32[264,128]{1,0:T(8,128)S(1)}, f32[264,128]{1,0:T(8,128)S(1)}, u32[]{:S(2)}, u32[]{:S(2)}) collective-permute-start(f32[264,128]{1,0:T(8,128)S(1)} %shard_map.41.refs_1_), channel_id=1, source_target_pairs={{0,12},{1,13},{2,14},{3,15},{4,0},{5,1},{6,2},{7,3},{8,4},{9,5},{1... | collective-permute-start | bytes 405512 | tf_op jit(solution)/shard_map/ppermute | solution.py:418
  67.5 2.1 %collective-permute-done.11.refs_4_ = f32[264,128]{1,0:T(8,128)S(1)} collective-permute-done((f32[264,128]{1,0:T(8,128)S(1)}, f32[264,128]{1,0:T(8,128)S(1)}, u32[]{:S(2)}, u32[]{:S(2)}) %collective-permute-start.11) | collective-permute-done | bytes 135200 | tf_op jit(solution)/shard_map/ppermute | solution.py:418
  72.7 3.1 %shard_map.42 = (f32[320,256]{1,0:T(8,128)S(1)}, f32[256,256]{1,0:T(8,128)S(1)}) custom-call(s32[3]{0:T(128)S(1)} %pad_add_fusion.info_ref.refs_0_, f32[264,128]{1,0:T(8,128)S(1)} %shard_map.41.refs_1_, f32[264,128]{1,0:T(8,128)S(1)} %collective-permute-done.9.refs_2_, f32[264,128]{1,0:T(8,128)S(1)} %collective-permute-done.10.refs_3_, ...), custom_call_target="tpu_custom_call" | custom-call | flops 805306368 | bytes 1048576 | tf_op jit(solution)/shard_map/pallas_call | solution.py:78
  75.8 6.9 %collective-permute-start.14 = (f32[320,256]{1,0:T(8,128)S(1)}, f32[320,256]{1,0:T(8,128)S(1)}, u32[]{:S(2)}, u32[]{:S(2)}) collective-permute-start(f32[320,256]{1,0:T(8,128)S(1)} %get-tuple-element.57.weights_ref.refs_1_), channel_id=1, source_target_pairs={{0,16},{16,0},{32,48},{48,32},{64,80},{80,64},{96,112},{112,96},{1... | collective-permute-start | bytes 983048 | tf_op jit(solution)/shard_map/ppermute | solution.py:414
  85.0 2.8 %shard_map.44 = (f32[4,400,128]{2,1,0:T(8,128)S(1)}, f32[4,400,128]{2,1,0:T(8,128)S(1)}, f32[4,400,128]{2,1,0:T(8,128)S(1)}, f32[128,128]{1,0:T(8,128)S(1)}) custom-call(s32[3]{0:T(128)S(1)} %pad_add_fusion.info_ref.refs_0_, f32[320,256]{1,0:T(8,128)S(1)} %get-tuple-element.57.weights_ref.refs_1_, f32[320,256]{1,0:T(8,128)S(1)} %collective-permute-done.14.refs_2_.refs_3_, ...), custom_call_target="tpu_custom_call" | custom-call | flops 1258291200 | bytes 5734400 | tf_op jit(solution)/shard_map/pallas_call | solution.py:78
  89.9 5.5 %collective-permute-done.15.odd_ref = f32[256,256]{1,0:T(8,128)S(1)} collective-permute-done((f32[256,256]{1,0:T(8,128)S(1)}, f32[256,256]{1,0:T(8,128)S(1)}, u32[]{:S(2)}, u32[]{:S(2)}) %collective-permute-start.15) | collective-permute-done | bytes 262176 | tf_op jit(solution)/shard_map/ppermute | solution.py:428
  98.6 2.7 %collective-permute-start.19 = (f32[128,128]{1,0:T(8,128)S(1)}, f32[128,128]{1,0:T(8,128)S(1)}, u32[]{:S(2)}, u32[]{:S(2)}) collective-permute-start(f32[128,128]{1,0:T(8,128)S(1)} %add.50), channel_id=1, source_target_pairs={{0,3},{1,0},{2,1},{3,2},{4,7},{5,4},{6,5},{7,6},{8,11},{9,8},{10,9... | collective-permute-start | bytes 196616 | tf_op jit(solution)/shard_map/ppermute | solution.py:418
  102.6 3.3 %collective-permute-done.18 = f32[128,128]{1,0:T(8,128)S(1)} collective-permute-done((f32[128,128]{1,0:T(8,128)S(1)}, f32[128,128]{1,0:T(8,128)S(1)}, u32[]{:S(2)}, u32[]{:S(2)}) %collective-permute-start.18) | collective-permute-done | bytes 65568 | tf_op jit(solution)/shard_map/ppermute | solution.py:418
  111.1 2.2 %collective-permute-done.21.refs_6_ = f32[128,128]{1,0:T(8,128)S(1)} collective-permute-done((f32[128,128]{1,0:T(8,128)S(1)}, f32[128,128]{1,0:T(8,128)S(1)}, u32[]{:S(2)}, u32[]{:S(2)}) %collective-permute-start.21) | collective-permute-done | bytes 65568 | tf_op jit(solution)/shard_map/ppermute | solution.py:418
  113.9 2.6 %shard_map.47 = (f32[320,256]{1,0:T(8,128)S(1)}, f32[256,256]{1,0:T(8,128)S(1)}) custom-call(s32[3]{0:T(128)S(1)} %pad_add_fusion.info_ref.refs_0_, f32[128,128]{1,0:T(8,128)S(1)} %shard_map.43.refs_7_.refs_1_, f32[320,256]{1,0:T(8,128)S(1)} %collective-permute-done.13.refs_1_.even_ref.refs_2_, f32[320,256]{1,0:T(8,128)S(1)} %collective-permute-done.14.refs_2_.refs_3_, ...), custom_call_target="tpu_custom_call" | custom-call | flops 805306368 | bytes 1048576 | tf_op jit(solution)/shard_map/pallas_call | solution.py:78
  116.5 2.5 %collective-permute-start.25 = (f32[320,256]{1,0:T(8,128)S(1)}, f32[320,256]{1,0:T(8,128)S(1)}, u32[]{:S(2)}, u32[]{:S(2)}) collective-permute-start(f32[320,256]{1,0:T(8,128)S(1)} %get-tuple-element.65.weights_ref.refs_1_), channel_id=1, source_target_pairs={{0,16},{16,0},{32,48},{48,32},{64,80},{80,64},{96,112},{112,96},{1... | collective-permute-start | bytes 983048 | tf_op jit(solution)/shard_map/ppermute | solution.py:414
  119.0 3.0 %collective-permute-start.24 = (f32[320,256]{1,0:T(8,128)S(1)}, f32[320,256]{1,0:T(8,128)S(1)}, u32[]{:S(2)}, u32[]{:S(2)}) collective-permute-start(f32[320,256]{1,0:T(8,128)S(1)} %get-tuple-element.65.weights_ref.refs_1_), channel_id=1, source_target_pairs={{16,32},{48,64},{80,96},{112,0},{17,33},{49,65},{81,97},{113,1},{1... | collective-permute-start | bytes 983048 | tf_op jit(solution)/shard_map/ppermute | solution.py:426
  124.1 2.8 %shard_map.50 = (f32[4,400,128]{2,1,0:T(8,128)S(1)}, f32[4,400,128]{2,1,0:T(8,128)S(1)}, f32[4,400,128]{2,1,0:T(8,128)S(1)}, f32[128,128]{1,0:T(8,128)S(1)}) custom-call(s32[3]{0:T(128)S(1)} %pad_add_fusion.info_ref.refs_0_, f32[320,256]{1,0:T(8,128)S(1)} %get-tuple-element.65.weights_ref.refs_1_, f32[320,256]{1,0:T(8,128)S(1)} %collective-permute-done.25.refs_2_.refs_3_, ...), custom_call_target="tpu_custom_call" | custom-call | flops 1258291200 | bytes 5734400 | tf_op jit(solution)/shard_map/pallas_call | solution.py:78
  129.0 2.5 %collective-permute-done.26.odd_ref = f32[256,256]{1,0:T(8,128)S(1)} collective-permute-done((f32[256,256]{1,0:T(8,128)S(1)}, f32[256,256]{1,0:T(8,128)S(1)}, u32[]{:S(2)}, u32[]{:S(2)}) %collective-permute-start.26) | collective-permute-done | bytes 262176 | tf_op jit(solution)/shard_map/ppermute | solution.py:428
  139.6 2.2 %collective-permute-done.28 = f32[128,128]{1,0:T(8,128)S(1)} collective-permute-done((f32[128,128]{1,0:T(8,128)S(1)}, f32[128,128]{1,0:T(8,128)S(1)}, u32[]{:S(2)}, u32[]{:S(2)}) %collective-permute-start.28) | collective-permute-done | bytes 65568 | tf_op jit(solution)/shard_map/ppermute | solution.py:418
  145.3 2.5 %collective-permute-done.32.refs_6_ = f32[128,128]{1,0:T(8,128)S(1)} collective-permute-done((f32[128,128]{1,0:T(8,128)S(1)}, f32[128,128]{1,0:T(8,128)S(1)}, u32[]{:S(2)}, u32[]{:S(2)}) %collective-permute-start.32) | collective-permute-done | bytes 65568 | tf_op jit(solution)/shard_map/ppermute | solution.py:418
  148.8 2.6 %shard_map.53 = (f32[320,256]{1,0:T(8,128)S(1)}, f32[256,256]{1,0:T(8,128)S(1)}) custom-call(s32[3]{0:T(128)S(1)} %pad_add_fusion.info_ref.refs_0_, f32[128,128]{1,0:T(8,128)S(1)} %shard_map.48.refs_7_.refs_1_, f32[320,256]{1,0:T(8,128)S(1)} %collective-permute-done.24.refs_1_.even_ref.refs_2_, f32[320,256]{1,0:T(8,128)S(1)} %collective-permute-done.25.refs_2_.refs_3_, ...), custom_call_target="tpu_custom_call" | custom-call | flops 805306368 | bytes 1048576 | tf_op jit(solution)/shard_map/pallas_call | solution.py:78
  151.4 2.3 %collective-permute-start.36 = (f32[320,256]{1,0:T(8,128)S(1)}, f32[320,256]{1,0:T(8,128)S(1)}, u32[]{:S(2)}, u32[]{:S(2)}) collective-permute-start(f32[320,256]{1,0:T(8,128)S(1)} %get-tuple-element.74.weights_ref.refs_1_), channel_id=1, source_target_pairs={{0,16},{16,0},{32,48},{48,32},{64,80},{80,64},{96,112},{112,96},{1... | collective-permute-start | bytes 983048 | tf_op jit(solution)/shard_map/ppermute | solution.py:414
  153.7 2.8 %collective-permute-start.35 = (f32[320,256]{1,0:T(8,128)S(1)}, f32[320,256]{1,0:T(8,128)S(1)}, u32[]{:S(2)}, u32[]{:S(2)}) collective-permute-start(f32[320,256]{1,0:T(8,128)S(1)} %get-tuple-element.74.weights_ref.refs_1_), channel_id=1, source_target_pairs={{16,32},{48,64},{80,96},{112,0},{17,33},{49,65},{81,97},{113,1},{1... | collective-permute-start | bytes 983048 | tf_op jit(solution)/shard_map/ppermute | solution.py:426
  158.7 2.8 %shard_map.56 = (f32[4,400,128]{2,1,0:T(8,128)S(1)}, f32[4,400,128]{2,1,0:T(8,128)S(1)}, f32[4,400,128]{2,1,0:T(8,128)S(1)}, f32[128,128]{1,0:T(8,128)S(1)}) custom-call(s32[3]{0:T(128)S(1)} %pad_add_fusion.info_ref.refs_0_, f32[320,256]{1,0:T(8,128)S(1)} %get-tuple-element.74.weights_ref.refs_1_, f32[320,256]{1,0:T(8,128)S(1)} %collective-permute-done.36.refs_2_, ...), custom_call_target="tpu_custom_call" | custom-call | flops 1258291200 | bytes 5734400 | tf_op jit(solution)/shard_map/pallas_call | solution.py:78
  163.3 2.9 %collective-permute-done.37.odd_ref = f32[256,256]{1,0:T(8,128)S(1)} collective-permute-done((f32[256,256]{1,0:T(8,128)S(1)}, f32[256,256]{1,0:T(8,128)S(1)}, u32[]{:S(2)}, u32[]{:S(2)}) %collective-permute-start.37) | collective-permute-done | bytes 262176 | tf_op jit(solution)/shard_map/ppermute | solution.py:428
  173.0 2.1 %collective-permute-done.40 = f32[128,128]{1,0:T(8,128)S(1)} collective-permute-done((f32[128,128]{1,0:T(8,128)S(1)}, f32[128,128]{1,0:T(8,128)S(1)}, u32[]{:S(2)}, u32[]{:S(2)}) %collective-permute-start.40) | collective-permute-done | bytes 65568 | tf_op jit(solution)/shard_map/ppermute | solution.py:418
  181.9 2.3 %collective-permute-done.43.refs_5_ = f32[128,128]{1,0:T(8,128)S(1)} collective-permute-done((f32[128,128]{1,0:T(8,128)S(1)}, f32[128,128]{1,0:T(8,128)S(1)}, u32[]{:S(2)}, u32[]{:S(2)}) %collective-permute-start.43) | collective-permute-done | bytes 65568 | tf_op jit(solution)/shard_map/ppermute | solution.py:418
  185.5 2.2 %shard_map.59 = (f32[256,256]{1,0:T(8,128)S(1)}, f32[256,256]{1,0:T(8,128)S(1)}) custom-call(s32[3]{0:T(128)S(1)} %pad_add_fusion.info_ref.refs_0_, f32[128,128]{1,0:T(8,128)S(1)} %shard_map.54.refs_7_.refs_0_, f32[320,256]{1,0:T(8,128)S(1)} %collective-permute-done.35.refs_1_.even_ref, f32[320,256]{1,0:T(8,128)S(1)} %collective-permute-done.36.refs_2_, ...), custom_call_target="tpu_custom_call" | custom-call | flops 805306368 | bytes 1048576 | tf_op jit(solution)/shard_map/pallas_call | solution.py:78
  187.8 4.2 %shard_map.61 = (f32[8,384,256]{2,1,0:T(8,128)}, f32[2,64,256]{2,1,0:T(8,128)}, f32[1,256]{1,0:T(1,128)}) custom-call(s32[3]{0:T(128)S(1)} %pad_add_fusion.info_ref.refs_0_, f32[256,256]{1,0:T(8,128)S(1)} %get-tuple-element.81.weights_ref, f32[256,256]{1,0:T(8,128)S(1)} %get-tuple-element.82.gram_ref, f32[4,400,128]{2,1,0:T(8,128)S(1)} %get-tuple-element.78.up0_ref.refs_1_, ...), custom_call_target="tpu_custom_call" | custom-call | flops 1258291200 | bytes 6553600 | tf_op jit(solution)/shard_map/pallas_call | solution.py:397
  (98 shorter events, 69.8 us)
Async XLA Ops:
  3.8 20.7 %collective-permute-start = (f32[2,2,384,128]{3,2,1,0:T(8,128)S(1)}, f32[2,2,384,128]{3,2,1,0:T(8,128)S(1)}, u32[]{:S(2)}, u32[]{:S(2)}) collective-permute-start(f32[2,2,384,128]{3,2,1,0:T(8,128)S(1)} %get-tuple-element.48), channel_id=1, source_target_pairs={{0,32},{16,48},{32,64},{48,80},{64,96},{80,112},{96,0},{112,16},{1... | collective-permute-start | bytes 2359304 | tf_op jit(solution)/shard_map/ppermute | solution.py:442
  6.0 36.4 %collective-permute-start.1 = (f32[2,2,384,128]{3,2,1,0:T(8,128)S(1)}, f32[2,2,384,128]{3,2,1,0:T(8,128)S(1)}, u32[]{:S(2)}, u32[]{:S(2)}) collective-permute-start(f32[2,2,384,128]{3,2,1,0:T(8,128)S(1)} %get-tuple-element.49), channel_id=1, source_target_pairs={{0,64},{16,80},{32,96},{48,112},{64,0},{80,16},{96,32},{112,48},{1... | collective-permute-start | bytes 2359304 | tf_op jit(solution)/shard_map/ppermute | solution.py:442
  8.6 33.8 %collective-permute-start.2 = (f32[2,2,384,128]{3,2,1,0:T(8,128)S(1)}, f32[2,2,384,128]{3,2,1,0:T(8,128)S(1)}, u32[]{:S(2)}, u32[]{:S(2)}) collective-permute-start(f32[2,2,384,128]{3,2,1,0:T(8,128)S(1)} %get-tuple-element.50), channel_id=1, source_target_pairs={{0,96},{16,112},{32,0},{48,16},{64,32},{80,48},{96,64},{112,80},{1... | collective-permute-start | bytes 2359304 | tf_op jit(solution)/shard_map/ppermute | solution.py:442
  44.4 5.0 %collective-permute-start.3 = (f32[264,128]{1,0:T(8,128)S(1)}, f32[264,128]{1,0:T(8,128)S(1)}, u32[]{:S(2)}, u32[]{:S(2)}) collective-permute-start(f32[264,128]{1,0:T(8,128)S(1)} %get-tuple-element.52), channel_id=1, source_target_pairs={{0,16},{16,0},{32,48},{48,32},{64,80},{80,64},{96,112},{112,96},{1... | collective-permute-start | bytes 405512 | tf_op jit(solution)/shard_map/ppermute | solution.py:414
  46.7 15.1 %collective-permute-start.7 = (f32[2,384,128]{2,1,0:T(8,128)S(1)}, f32[2,384,128]{2,1,0:T(8,128)S(1)}, u32[]{:S(2)}, u32[]{:S(2)}) collective-permute-start(f32[2,384,128]{2,1,0:T(8,128)S(1)} %get-tuple-element.53), channel_id=1, source_target_pairs={{0,32},{16,48},{32,64},{48,80},{64,96},{80,112},{96,0},{112,16},{1... | collective-permute-start | bytes 1179656 | tf_op jit(solution)/shard_map/ppermute | solution.py:446
  47.7 14.1 %collective-permute-start.8 = (f32[2,384,128]{2,1,0:T(8,128)S(1)}, f32[2,384,128]{2,1,0:T(8,128)S(1)}, u32[]{:S(2)}, u32[]{:S(2)}) collective-permute-start(f32[2,384,128]{2,1,0:T(8,128)S(1)} %get-tuple-element.54), channel_id=1, source_target_pairs={{0,96},{16,112},{32,0},{48,16},{64,32},{80,48},{96,64},{112,80},{1... | collective-permute-start | bytes 1179656 | tf_op jit(solution)/shard_map/ppermute | solution.py:446
  49.5 4.9 %collective-permute-start.6 = (f32[264,128]{1,0:T(8,128)S(1)}, f32[264,128]{1,0:T(8,128)S(1)}, u32[]{:S(2)}, u32[]{:S(2)}) collective-permute-start(f32[264,128]{1,0:T(8,128)S(1)} %add.49.refs_1_), channel_id=1, source_target_pairs={{0,3},{1,0},{2,1},{3,2},{4,7},{5,4},{6,5},{7,6},{8,11},{9,8},{10,9... | collective-permute-start | bytes 405512 | tf_op jit(solution)/shard_map/ppermute | solution.py:418
  52.0 15.5 %collective-permute-start.12 = (f32[2,384,128]{2,1,0:T(8,128)S(1)}, f32[2,384,128]{2,1,0:T(8,128)S(1)}, u32[]{:S(2)}, u32[]{:S(2)}) collective-permute-start(f32[2,384,128]{2,1,0:T(8,128)S(1)} %get-tuple-element.55), channel_id=1, source_target_pairs={{0,64},{16,80},{32,96},{48,112},{64,0},{80,16},{96,32},{112,48},{1... | collective-permute-start | bytes 1179656 | tf_op jit(solution)/shard_map/ppermute | solution.py:446
  53.1 5.4 %collective-permute-start.5 = (f32[264,128]{1,0:T(8,128)S(1)}, f32[264,128]{1,0:T(8,128)S(1)}, u32[]{:S(2)}, u32[]{:S(2)}) collective-permute-start(f32[264,128]{1,0:T(8,128)S(1)} %add.49.refs_1_), channel_id=1, source_target_pairs={{0,2},{1,3},{2,0},{3,1},{4,6},{5,7},{6,4},{7,5},{8,10},{9,11},{10,... | collective-permute-start | bytes 405512 | tf_op jit(solution)/shard_map/ppermute | solution.py:418
  54.4 7.5 %collective-permute-start.4 = (f32[264,128]{1,0:T(8,128)S(1)}, f32[264,128]{1,0:T(8,128)S(1)}, u32[]{:S(2)}, u32[]{:S(2)}) collective-permute-start(f32[264,128]{1,0:T(8,128)S(1)} %add.49.refs_1_), channel_id=1, source_target_pairs={{0,1},{1,2},{2,3},{3,0},{4,5},{5,6},{6,7},{7,4},{8,9},{9,10},{10,1... | collective-permute-start | bytes 405512 | tf_op jit(solution)/shard_map/ppermute | solution.py:418
  62.4 7.2 %collective-permute-start.11 = (f32[264,128]{1,0:T(8,128)S(1)}, f32[264,128]{1,0:T(8,128)S(1)}, u32[]{:S(2)}, u32[]{:S(2)}) collective-permute-start(f32[264,128]{1,0:T(8,128)S(1)} %shard_map.41.refs_1_), channel_id=1, source_target_pairs={{0,12},{1,13},{2,14},{3,15},{4,0},{5,1},{6,2},{7,3},{8,4},{9,5},{1... | collective-permute-start | bytes 405512 | tf_op jit(solution)/shard_map/ppermute | solution.py:418
  66.2 5.5 %collective-permute-start.10 = (f32[264,128]{1,0:T(8,128)S(1)}, f32[264,128]{1,0:T(8,128)S(1)}, u32[]{:S(2)}, u32[]{:S(2)}) collective-permute-start(f32[264,128]{1,0:T(8,128)S(1)} %shard_map.41.refs_1_), channel_id=1, source_target_pairs={{0,8},{1,9},{2,10},{3,11},{4,12},{5,13},{6,14},{7,15},{8,0},{9,1},... | collective-permute-start | bytes 405512 | tf_op jit(solution)/shard_map/ppermute | solution.py:418
  66.2 6.5 %collective-permute-start.9 = (f32[264,128]{1,0:T(8,128)S(1)}, f32[264,128]{1,0:T(8,128)S(1)}, u32[]{:S(2)}, u32[]{:S(2)}) collective-permute-start(f32[264,128]{1,0:T(8,128)S(1)} %shard_map.41.refs_1_), channel_id=1, source_target_pairs={{0,4},{1,5},{2,6},{3,7},{4,8},{5,9},{6,10},{7,11},{8,12},{9,13},{1... | collective-permute-start | bytes 405512 | tf_op jit(solution)/shard_map/ppermute | solution.py:418
  75.8 9.2 %collective-permute-start.14 = (f32[320,256]{1,0:T(8,128)S(1)}, f32[320,256]{1,0:T(8,128)S(1)}, u32[]{:S(2)}, u32[]{:S(2)}) collective-permute-start(f32[320,256]{1,0:T(8,128)S(1)} %get-tuple-element.57.weights_ref.refs_1_), channel_id=1, source_target_pairs={{0,16},{16,0},{32,48},{48,32},{64,80},{80,64},{96,112},{112,96},{1... | collective-permute-start | bytes 983048 | tf_op jit(solution)/shard_map/ppermute | solution.py:414
  82.7 5.3 %collective-permute-start.13 = (f32[320,256]{1,0:T(8,128)S(1)}, f32[320,256]{1,0:T(8,128)S(1)}, u32[]{:S(2)}, u32[]{:S(2)}) collective-permute-start(f32[320,256]{1,0:T(8,128)S(1)} %get-tuple-element.57.weights_ref.refs_1_), channel_id=1, source_target_pairs={{16,32},{48,64},{80,96},{112,0},{17,33},{49,65},{81,97},{113,1},{1... | collective-permute-start | bytes 983048 | tf_op jit(solution)/shard_map/ppermute | solution.py:426
  87.7 26.1 %collective-permute-start.23 = (f32[4,400,128]{2,1,0:T(8,128)S(1)}, f32[4,400,128]{2,1,0:T(8,128)S(1)}, u32[]{:S(2)}, u32[]{:S(2)}) collective-permute-start(f32[4,400,128]{2,1,0:T(8,128)S(1)} %get-tuple-element.63.refs_6_), channel_id=1, source_target_pairs={{0,32},{16,48},{32,64},{48,80},{64,96},{80,112},{96,0},{112,16},{1... | collective-permute-start | bytes 2457608 | tf_op jit(solution)/shard_map/ppermute | solution.py:468
  88.6 6.8 %collective-permute-start.15 = (f32[256,256]{1,0:T(8,128)S(1)}, f32[256,256]{1,0:T(8,128)S(1)}, u32[]{:S(2)}, u32[]{:S(2)}) collective-permute-start(f32[256,256]{1,0:T(8,128)S(1)} %shard_map.45), channel_id=1, source_target_pairs={{0,16},{32,48},{64,80},{96,112},{1,17},{33,49},{65,81},{97,113},{2... | collective-permute-start | bytes 786440 | tf_op jit(solution)/shard_map/ppermute | solution.py:428
  101.3 4.7 %collective-permute-start.18 = (f32[128,128]{1,0:T(8,128)S(1)}, f32[128,128]{1,0:T(8,128)S(1)}, u32[]{:S(2)}, u32[]{:S(2)}) collective-permute-start(f32[128,128]{1,0:T(8,128)S(1)} %add.50), channel_id=1, source_target_pairs={{0,2},{1,3},{2,0},{3,1},{4,6},{5,7},{6,4},{7,5},{8,10},{9,11},{10,... | collective-permute-start | bytes 196616 | tf_op jit(solution)/shard_map/ppermute | solution.py:418
  101.8 6.0 %collective-permute-start.17 = (f32[128,128]{1,0:T(8,128)S(1)}, f32[128,128]{1,0:T(8,128)S(1)}, u32[]{:S(2)}, u32[]{:S(2)}) collective-permute-start(f32[128,128]{1,0:T(8,128)S(1)} %add.50), channel_id=1, source_target_pairs={{0,1},{1,2},{2,3},{3,0},{4,5},{5,6},{6,7},{7,4},{8,9},{9,10},{10,1... | collective-permute-start | bytes 196616 | tf_op jit(solution)/shard_map/ppermute | solution.py:418
  108.6 4.7 %collective-permute-start.21 = (f32[128,128]{1,0:T(8,128)S(1)}, f32[128,128]{1,0:T(8,128)S(1)}, u32[]{:S(2)}, u32[]{:S(2)}) collective-permute-start(f32[128,128]{1,0:T(8,128)S(1)} %add_add_fusion.2.refs_4_), channel_id=1, source_target_pairs={{0,8},{1,9},{2,10},{3,11},{4,12},{5,13},{6,14},{7,15},{8,0},{9,1},... | collective-permute-start | bytes 196616 | tf_op jit(solution)/shard_map/ppermute | solution.py:418
  108.6 5.2 %collective-permute-start.20 = (f32[128,128]{1,0:T(8,128)S(1)}, f32[128,128]{1,0:T(8,128)S(1)}, u32[]{:S(2)}, u32[]{:S(2)}) collective-permute-start(f32[128,128]{1,0:T(8,128)S(1)} %add_add_fusion.2.refs_4_), channel_id=1, source_target_pairs={{0,4},{1,5},{2,6},{3,7},{4,8},{5,9},{6,10},{7,11},{8,12},{9,13},{1... | collective-permute-start | bytes 196616 | tf_op jit(solution)/shard_map/ppermute | solution.py:418
  116.5 7.6 %collective-permute-start.25 = (f32[320,256]{1,0:T(8,128)S(1)}, f32[320,256]{1,0:T(8,128)S(1)}, u32[]{:S(2)}, u32[]{:S(2)}) collective-permute-start(f32[320,256]{1,0:T(8,128)S(1)} %get-tuple-element.65.weights_ref.refs_1_), channel_id=1, source_target_pairs={{0,16},{16,0},{32,48},{48,32},{64,80},{80,64},{96,112},{112,96},{1... | collective-permute-start | bytes 983048 | tf_op jit(solution)/shard_map/ppermute | solution.py:414
  119.0 8.2 %collective-permute-start.24 = (f32[320,256]{1,0:T(8,128)S(1)}, f32[320,256]{1,0:T(8,128)S(1)}, u32[]{:S(2)}, u32[]{:S(2)}) collective-permute-start(f32[320,256]{1,0:T(8,128)S(1)} %get-tuple-element.65.weights_ref.refs_1_), channel_id=1, source_target_pairs={{16,32},{48,64},{80,96},{112,0},{17,33},{49,65},{81,97},{113,1},{1... | collective-permute-start | bytes 983048 | tf_op jit(solution)/shard_map/ppermute | solution.py:426
  126.9 21.9 %collective-permute-start.34 = (f32[4,400,128]{2,1,0:T(8,128)S(1)}, f32[4,400,128]{2,1,0:T(8,128)S(1)}, u32[]{:S(2)}, u32[]{:S(2)}) collective-permute-start(f32[4,400,128]{2,1,0:T(8,128)S(1)} %get-tuple-element.72.refs_6_), channel_id=1, source_target_pairs={{0,32},{16,48},{32,64},{48,80},{64,96},{80,112},{96,0},{112,16},{1... | collective-permute-start | bytes 2457608 | tf_op jit(solution)/shard_map/ppermute | solution.py:468
  135.6 6.2 %collective-permute-start.28 = (f32[128,128]{1,0:T(8,128)S(1)}, f32[128,128]{1,0:T(8,128)S(1)}, u32[]{:S(2)}, u32[]{:S(2)}) collective-permute-start(f32[128,128]{1,0:T(8,128)S(1)} %add.54), channel_id=1, source_target_pairs={{0,1},{1,2},{2,3},{3,0},{4,5},{5,6},{6,7},{7,4},{8,9},{9,10},{10,1... | collective-permute-start | bytes 196616 | tf_op jit(solution)/shard_map/ppermute | solution.py:418
  143.7 5.1 %collective-permute-start.31 = (f32[128,128]{1,0:T(8,128)S(1)}, f32[128,128]{1,0:T(8,128)S(1)}, u32[]{:S(2)}, u32[]{:S(2)}) collective-permute-start(f32[128,128]{1,0:T(8,128)S(1)} %add_add_fusion.1.refs_4_), channel_id=1, source_target_pairs={{0,4},{1,5},{2,6},{3,7},{4,8},{5,9},{6,10},{7,11},{8,12},{9,13},{1... | collective-permute-start | bytes 196616 | tf_op jit(solution)/shard_map/ppermute | solution.py:418
  151.4 7.2 %collective-permute-start.36 = (f32[320,256]{1,0:T(8,128)S(1)}, f32[320,256]{1,0:T(8,128)S(1)}, u32[]{:S(2)}, u32[]{:S(2)}) collective-permute-start(f32[320,256]{1,0:T(8,128)S(1)} %get-tuple-element.74.weights_ref.refs_1_), channel_id=1, source_target_pairs={{0,16},{16,0},{32,48},{48,32},{64,80},{80,64},{96,112},{112,96},{1... | collective-permute-start | bytes 983048 | tf_op jit(solution)/shard_map/ppermute | solution.py:414
  153.7 7.7 %collective-permute-start.35 = (f32[320,256]{1,0:T(8,128)S(1)}, f32[320,256]{1,0:T(8,128)S(1)}, u32[]{:S(2)}, u32[]{:S(2)}) collective-permute-start(f32[320,256]{1,0:T(8,128)S(1)} %get-tuple-element.74.weights_ref.refs_1_), channel_id=1, source_target_pairs={{16,32},{48,64},{80,96},{112,0},{17,33},{49,65},{81,97},{113,1},{1... | collective-permute-start | bytes 983048 | tf_op jit(solution)/shard_map/ppermute | solution.py:426
  171.1 6.0 %collective-permute-start.39 = (f32[128,128]{1,0:T(8,128)S(1)}, f32[128,128]{1,0:T(8,128)S(1)}, u32[]{:S(2)}, u32[]{:S(2)}) collective-permute-start(f32[128,128]{1,0:T(8,128)S(1)} %add.58), channel_id=1, source_target_pairs={{0,1},{1,2},{2,3},{3,0},{4,5},{5,6},{6,7},{7,4},{8,9},{9,10},{10,1... | collective-permute-start | bytes 196616 | tf_op jit(solution)/shard_map/ppermute | solution.py:418
  177.8 10.0 %collective-permute-start.45 = (f32[4,400,128]{2,1,0:T(8,128)S(1)}, f32[4,400,128]{2,1,0:T(8,128)S(1)}, u32[]{:S(2)}, u32[]{:S(2)}) collective-permute-start(f32[4,400,128]{2,1,0:T(8,128)S(1)} %get-tuple-element.86), channel_id=1, source_target_pairs={{0,16},{16,0},{32,48},{48,32},{64,80},{80,64},{96,112},{112,96},{1... | collective-permute-start | bytes 2457608 | tf_op jit(solution)/shard_map/ppermute | solution.py:414
  178.7 9.1 %collective-permute-start.46 = (f32[4,400,128]{2,1,0:T(8,128)S(1)}, f32[4,400,128]{2,1,0:T(8,128)S(1)}, u32[]{:S(2)}, u32[]{:S(2)}) collective-permute-start(f32[4,400,128]{2,1,0:T(8,128)S(1)} %get-tuple-element.87), channel_id=1, source_target_pairs={{0,16},{16,0},{32,48},{48,32},{64,80},{80,64},{96,112},{112,96},{1... | collective-permute-start | bytes 2457608 | tf_op jit(solution)/shard_map/ppermute | solution.py:414
  180.1 5.4 %collective-permute-start.42 = (f32[128,128]{1,0:T(8,128)S(1)}, f32[128,128]{1,0:T(8,128)S(1)}, u32[]{:S(2)}, u32[]{:S(2)}) collective-permute-start(f32[128,128]{1,0:T(8,128)S(1)} %add_add_fusion.refs_3_.refs_5_), channel_id=1, source_target_pairs={{0,4},{1,5},{2,6},{3,7},{4,8},{5,9},{6,10},{7,11},{8,12},{9,13},{1... | collective-permute-start | bytes 196616 | tf_op jit(solution)/shard_map/ppermute | solution.py:418
  (17 other events, 95.8 us)

commit v7 on v6

--- a/solution.py
+++ b/solution.py
@@ -21,6 +21,7 @@
 NEXT_SLOT = [(c, (c + 1) % COLS) for c in range(COLS)]
 CHIPS_ON = [[(c, (c + 2 * k) % COLS) for c in range(COLS)] for k in range(SIDE)]
 ODD_TO_EVEN = [(c, (c + 1) % COLS) for c in range(1, COLS, 2)]
+ODD_TO_ODD = [(c, (c + 2) % COLS) for c in range(1, COLS, 2)]
 EVEN_TO_ODD = [(c, c + 1) for c in range(0, COLS, 2)]
 ALONG_X = [[(r, r - r % SIDE + (r + k) % SIDE) for r in range(ROWS)] for k in range(1, SIDE)]
 ALONG_Z = [[(r, (r + SIDE * k) % ROWS) for r in range(ROWS)] for k in range(1, SIDE)]
@@ -219,14 +220,15 @@
 
 
 def cayley_kernel(fill, info_ref, *refs):
-    weights_ref, gram_ref, x_ref, r_ref = refs[-4:]
-    up, cross, low = fill(info_ref, *refs[:-4])
+    weights_ref, lower_ref, gram_ref, x_ref, r_ref = refs[-5:]
+    up, cross, low = fill(info_ref, *refs[:-5])
     gram_ref[:BLOCK, :BLOCK] = up
     gram_ref[:BLOCK, BLOCK:] = cross
     gram_ref[BLOCK:, :BLOCK] = cross.T
     gram_ref[BLOCK:, BLOCK:] = low
     weights = rotation_of(gram_ref[...], x_ref, r_ref)
     weights_ref[:PAIR] = weights
+    lower_ref[...] = weights[:, BLOCK:]
     if weights_ref.shape[0] > PAIR:
         turned = mm3(weights[:, BLOCK:], mm3(gram_ref[...], weights[:, BLOCK:]), 0)
         weights_ref[PAIR:, :BLOCK] = turned[: BLOCK // 2]
@@ -237,7 +239,7 @@
     return call_whole(
         functools.partial(cayley_kernel, fill),
         args,
-        [shape(PAIR if last else PAIR + BLOCK // 2, PAIR), shape(PAIR, PAIR)],
+        [shape(PAIR if last else PAIR + BLOCK // 2, PAIR), shape(PAIR, BLOCK), shape(PAIR, PAIR)],
         before,
         scratch=[pltpu.VMEM((PAIR, PAIR), F32)] * 2,
         flops=2 * 3 * 8 * PAIR**3,
@@ -321,9 +323,9 @@
     )
 
 
-def ahead_kernel(rows, step, info_ref, even_ref, odd_ref, cross_ref, up0_ref, *refs):
+def ahead_kernel(rows, step, info_ref, lower_ref, cross_ref, up0_ref, *refs):
     low0_ref, keep_ref, send_ref = refs[-3:]
-    weights = even_ref[:PAIR, BLOCK:] + odd_ref[:, BLOCK:]
+    weights = lower_ref[...]
     slot = (2 * info_ref[1] + COLS - 1) % COLS
     total = jnp.zeros((BLOCK, BLOCK), F32)
     for group, (pair,) in groups_of(info_ref, step, refs[:-3], (slot,)):
@@ -335,10 +337,10 @@
     send_ref[...] = jnp.where(first, cross_ref[...], total)
 
 
-def rotate_ahead(info, ahead, cross, up0, blocks, rows, step):
+def rotate_ahead(info, lower, cross, up0, blocks, rows, step):
     return call_whole(
         functools.partial(ahead_kernel, rows, step),
-        (info, *ahead, cross, up0, *blocks),
+        (info, lower, cross, up0, *blocks),
         [shape(SIDE, step, BLOCK), shape(BLOCK, BLOCK), shape(BLOCK, BLOCK)],
         flops=2 * 3 * SIDE * step * 2 * BLOCK * PAIR,
         nbytes=4 * 4 * SIDE * step * BLOCK,
@@ -347,7 +349,7 @@
 
 def up_kernel(step, info_ref, even_ref, odd_ref, *refs):
     up_ref = refs[-1]
-    weights = even_ref[:PAIR, :BLOCK] + odd_ref[:, :BLOCK]
+    weights = even_ref[:PAIR, :BLOCK] + odd_ref[...]
     slot = (2 * info_ref[1] + COLS - 1) % COLS
     for group, (pair,) in groups_of(info_ref, step, refs[:-1], (slot,)):
         up_ref[group] = mm3(pair, weights)
@@ -418,14 +420,23 @@
     return [lax.ppermute(value, "rows", pairs) for pairs in shifts]
 
 
-def same_kernel(info_ref, value_ref, out_ref):
-    out_ref[...] = value_ref[: out_ref.shape[0]]
-
-
-def odd_slot_before(info, weights, before):
-    even = lax.ppermute(weights, "cols", ODD_TO_EVEN)
-    copy = call_whole(same_kernel, (info, even), [shape(PAIR, PAIR)], before, nbytes=8 * PAIR * PAIR)[0]
-    return [even, lax.ppermute(copy, "cols", EVEN_TO_ODD)]
+def lower_kernel(info_ref, even_ref, odd_ref, low1_ref, lower_ref, pass_ref):
+    lower_ref[...] = even_ref[:PAIR, BLOCK:] + odd_ref[...]
+    pass_ref[...] = low1_ref[...]
+
+
+def lower_before(info, even, odd, low1):
+    out = [shape(PAIR, BLOCK), shape(*low1.shape)]
+    return call_whole(lower_kernel, (info, even, odd, low1), out, nbytes=8 * (low1.size + PAIR * BLOCK))
+
+
+def upper_kernel(info_ref, value_ref, out_ref):
+    out_ref[...] = value_ref[:PAIR, :BLOCK]
+
+
+def relayed_upper(info, even, before):
+    upper = call_whole(upper_kernel, (info, even), [shape(PAIR, BLOCK)], before, nbytes=8 * PAIR * BLOCK)[0]
+    return lax.ppermute(upper, "cols", EVEN_TO_ODD)
 
 
 def body(sensitivity):
@@ -445,29 +456,31 @@
     packed = pack_ahead(info, x, main[1:])
     ahead = [packed[0]] + [lax.ppermute(packed[k], "cols", CHIPS_ON[k]) for k in range(1, SIDE)]
     value = keep + swap_core(send)
-    value = sum_parts(info, [value] + along(value, ALONG_X), [ahead[1], ahead[3]])
-    weights, gram = first_cayley(info, [value] + along(value, ALONG_Z), [ahead[2]])
+    value = sum_parts(info, [value] + along(value, ALONG_X), [])
+    weights, lower, gram = first_cayley(info, [value] + along(value, ALONG_Z), ahead[1:])
 
     own_blocks = main
     ahead_blocks = [value[None] for value in ahead]
     for sweep_round in range(ROUNDS - 1):
         last = sweep_round == ROUNDS - 2
+        odd = lax.ppermute(lower, "cols", ODD_TO_ODD)
+        even = lax.ppermute(weights, "cols", ODD_TO_EVEN)
         other = swap_core(weights)
         up = project(info, gram, weights)
         before = [up] + ([ahead_blocks[0]] if sweep_round else [])
         up0, up1, low1, cross = rotate_own(info, weights, other, own_blocks, before, rows, step)
-        weights_m = odd_slot_before(info, weights, [cross])
-        low0, keep, send = rotate_ahead(info, weights_m, cross, up0, ahead_blocks, rows, step)
+        lower, passed = lower_before(info, even, odd, low1)
+        low0, keep, send = rotate_ahead(info, lower, cross, up0, ahead_blocks, rows, step)
         value = keep + swap_core(send)
         value = value + sum(along(value, ALONG_X))
         own_blocks = [up0, low0, up1, low1]
         if last:
             other_blocks = [swap_core(block) for block in other_slot(info, own_blocks, [value])]
         else:
-            up_m = rotate_up(info, weights_m, ahead_blocks, step)
-            ahead_blocks = [up_m, lax.ppermute(low1, "cols", CHIPS_ON[1])]
+            up_m = rotate_up(info, [even, relayed_upper(info, even, [keep])], ahead_blocks, step)
+            ahead_blocks = [up_m, lax.ppermute(passed, "cols", CHIPS_ON[1])]
         before = [] if last else [ahead_blocks[1]]
-        weights, gram = cayley(info, up, weights_m[0], other, [value] + along(value, ALONG_Z), before, last)
+        weights, lower, gram = cayley(info, up, even, other, [value] + along(value, ALONG_Z), before, last)
 
     rotated, frame, column_scale = rotate_final(info, weights, gram, own_blocks + other_blocks, rows, step)
     return rotated, frame.reshape(2 * basis_rows, PAIR), column_scale.reshape(PAIR)

time: 192 us -> 192 us (level)
  starting transfers between devices: 57.2 us -> 48.9 us
  waiting for transfers between devices: 91.4 us -> 96.3 us
  Pallas kernels: 40.3 us -> 43.5 us
    ppermute x9, starting transfers between devices: 15 us -> 4.69 us  [swap_core(): return lax.ppermute(value, 'cols', TURN_CORE)]
    ppermute x24, waiting for transfers between devices: 43.6 us -> 47.6 us  [along(): return [lax.ppermute(value, 'rows', pairs) for pairs in shifts]]
    pallas_call x21 -> x23, Pallas kernels: 34.3 us -> 37.5 us  [call_whole(): pl.pallas_call(inner, in_specs=[pl.BlockSpec(memory_space=pltpu.SMEM)] +...]
    ppermute x8 -> x10, starting transfers between devices: 11.3 us -> 14.5 us  [the longest x3 6.45 us: body(): odd = lax.ppermute(lower, 'cols', ODD_TO_ODD)]
    ppermute x8 -> x10, waiting for transfers between devices: 11.1 us -> 10.9 us  [the longest x2 7.49 us: body(): ahead_blocks = [up_m, lax.ppermute(passed, 'cols', CHIPS_ON[1])]]
  transfers between devices with their start and end apart: 47 -> 49, of which waited for: 34 -> 32; matrix products, arithmetic and copies ran while one was open for 0% -> 0% of each run, Pallas kernels for 11% -> 12%
where the time goes in v7:
time: 192 us
  waiting for transfers between devices  96.3 us (50%)
  starting transfers between devices  48.9 us (25%)
  Pallas kernels  43.5 us (23%)
    ppermute x24, waiting for transfers between devices, along(): return [lax.ppermute(value, 'rows', pairs) for pairs in shifts]  47.6 us
    pallas_call x23, Pallas kernels, call_whole(): pl.pallas_call(inner, in_specs=[pl.BlockSpec(memory_space=pltpu.SMEM)] +...  37.5 us
    ppermute x6, waiting for transfers between devices, body(): lax.ppermute(packed[k], 'cols', CHIPS_ON[k])  34.1 us
    ppermute x24, starting transfers between devices, along(): return [lax.ppermute(value, 'rows', pairs) for pairs in shifts]  19.4 us
    ppermute x6, starting transfers between devices, body(): lax.ppermute(packed[k], 'cols', CHIPS_ON[k])  10.3 us
    ppermute x2, waiting for transfers between devices, body(): ahead_blocks = [up_m, lax.ppermute(passed, 'cols', CHIPS_ON[1])]  7.49 us
    ppermute x3, starting transfers between devices, body(): odd = lax.ppermute(lower, 'cols', ODD_TO_ODD)  6.45 us
    ppermute x3, starting transfers between devices, body(): even = lax.ppermute(weights, 'cols', ODD_TO_EVEN)  5.16 us
  transfers between devices with their start and end apart: 49, of which 32 were waited for; matrix products, arithmetic and copies ran while one was open for 0% of the time, Pallas kernels for 12%

profile of v7, /device:TPU:1, one launch (start us, length us, event | category | flops | bytes accessed | tf_op | source)
XLA Modules:
  0.0 191.8 jit_solution(12032565377087437620)
XLA Ops:
  3.8 2.2 %collective-permute-start = (f32[2,2,384,128]{3,2,1,0:T(8,128)S(1)}, f32[2,2,384,128]{3,2,1,0:T(8,128)S(1)}, u32[]{:S(2)}, u32[]{:S(2)}) collective-permute-start(f32[2,2,384,128]{3,2,1,0:T(8,128)S(1)} %get-tuple-element.56), channel_id=1, source_target_pairs={{0,32},{16,48},{32,64},{48,80},{64,96},{80,112},{96,0},{112,16},{1... | collective-permute-start | bytes 2359304 | tf_op jit(solution)/shard_map/ppermute | solution.py:453
  6.0 2.6 %collective-permute-start.1 = (f32[2,2,384,128]{3,2,1,0:T(8,128)S(1)}, f32[2,2,384,128]{3,2,1,0:T(8,128)S(1)}, u32[]{:S(2)}, u32[]{:S(2)}) collective-permute-start(f32[2,2,384,128]{3,2,1,0:T(8,128)S(1)} %get-tuple-element.57), channel_id=1, source_target_pairs={{0,64},{16,80},{32,96},{48,112},{64,0},{80,16},{96,32},{112,48},{1... | collective-permute-start | bytes 2359304 | tf_op jit(solution)/shard_map/ppermute | solution.py:453
  9.7 14.9 %collective-permute-done.refs_1_.refs_4_ = f32[2,2,384,128]{3,2,1,0:T(8,128)S(1)} collective-permute-done((f32[2,2,384,128]{3,2,1,0:T(8,128)S(1)}, f32[2,2,384,128]{3,2,1,0:T(8,128)S(1)}, u32[]{:S(2)}, u32[]{:S(2)}) %collective-permute-start) | collective-permute-done | bytes 786464 | tf_op jit(solution)/shard_map/ppermute | solution.py:453
  24.6 17.9 %collective-permute-done.1.refs_2_.refs_5_ = f32[2,2,384,128]{3,2,1,0:T(8,128)S(1)} collective-permute-done((f32[2,2,384,128]{3,2,1,0:T(8,128)S(1)}, f32[2,2,384,128]{3,2,1,0:T(8,128)S(1)}, u32[]{:S(2)}, u32[]{:S(2)}) %collective-permute-start.1) | collective-permute-done | bytes 786464 | tf_op jit(solution)/shard_map/ppermute | solution.py:453
  42.4 1.9 %shard_map.39 = (f32[264,128]{1,0:T(8,128)S(1)}, f32[264,128]{1,0:T(8,128)S(1)}) custom-call(s32[3]{0:T(128)S(1)} %pad_add_fusion.info_ref.refs_0_, f32[2,2,384,128]{3,2,1,0:T(8,128)S(1)} %get-tuple-element.55.refs_0_.refs_3_, f32[2,2,384,128]{3,2,1,0:T(8,128)S(1)} %collective-permute-done.refs_1_.refs_4_, ...), custom_call_target="tpu_custom_call" | custom-call | flops 805306368 | bytes 3145728 | tf_op jit(solution)/shard_map/pallas_call | solution.py:79
  47.7 2.6 %collective-permute-start.6 = (f32[264,128]{1,0:T(8,128)S(1)}, f32[264,128]{1,0:T(8,128)S(1)}, u32[]{:S(2)}, u32[]{:S(2)}) collective-permute-start(f32[264,128]{1,0:T(8,128)S(1)} %add.49.refs_0_), channel_id=1, source_target_pairs={{0,3},{1,0},{2,1},{3,2},{4,7},{5,4},{6,5},{7,6},{8,11},{9,8},{10,9... | collective-permute-start | bytes 405512 | tf_op jit(solution)/shard_map/ppermute | solution.py:420
  50.3 2.1 %collective-permute-start.11 = (f32[2,384,128]{2,1,0:T(8,128)S(1)}, f32[2,384,128]{2,1,0:T(8,128)S(1)}, u32[]{:S(2)}, u32[]{:S(2)}) collective-permute-start(f32[2,384,128]{2,1,0:T(8,128)S(1)} %get-tuple-element.62), channel_id=1, source_target_pairs={{0,64},{16,80},{32,96},{48,112},{64,0},{80,16},{96,32},{112,48},{1... | collective-permute-start | bytes 1179656 | tf_op jit(solution)/shard_map/ppermute | solution.py:457
  54.8 4.3 %collective-permute-done.5.refs_2_ = f32[264,128]{1,0:T(8,128)S(1)} collective-permute-done((f32[264,128]{1,0:T(8,128)S(1)}, f32[264,128]{1,0:T(8,128)S(1)}, u32[]{:S(2)}, u32[]{:S(2)}) %collective-permute-start.5) | collective-permute-done | bytes 135200 | tf_op jit(solution)/shard_map/ppermute | solution.py:420
  59.2 4.0 %collective-permute-done.4.refs_1_ = f32[264,128]{1,0:T(8,128)S(1)} collective-permute-done((f32[264,128]{1,0:T(8,128)S(1)}, f32[264,128]{1,0:T(8,128)S(1)}, u32[]{:S(2)}, u32[]{:S(2)}) %collective-permute-start.4) | collective-permute-done | bytes 135200 | tf_op jit(solution)/shard_map/ppermute | solution.py:420
  63.8 3.8 %collective-permute-start.9 = (f32[264,128]{1,0:T(8,128)S(1)}, f32[264,128]{1,0:T(8,128)S(1)}, u32[]{:S(2)}, u32[]{:S(2)}) collective-permute-start(f32[264,128]{1,0:T(8,128)S(1)} %shard_map.40.refs_1_), channel_id=1, source_target_pairs={{0,12},{1,13},{2,14},{3,15},{4,0},{5,1},{6,2},{7,3},{8,4},{9,5},{1... | collective-permute-start | bytes 405512 | tf_op jit(solution)/shard_map/ppermute | solution.py:420
  69.7 3.6 %collective-permute-done.9.refs_4_ = f32[264,128]{1,0:T(8,128)S(1)} collective-permute-done((f32[264,128]{1,0:T(8,128)S(1)}, f32[264,128]{1,0:T(8,128)S(1)}, u32[]{:S(2)}, u32[]{:S(2)}) %collective-permute-start.9) | collective-permute-done | bytes 135200 | tf_op jit(solution)/shard_map/ppermute | solution.py:420
  73.3 3.6 %collective-permute-done.7.refs_2_ = f32[264,128]{1,0:T(8,128)S(1)} collective-permute-done((f32[264,128]{1,0:T(8,128)S(1)}, f32[264,128]{1,0:T(8,128)S(1)}, u32[]{:S(2)}, u32[]{:S(2)}) %collective-permute-start.7) | collective-permute-done | bytes 135200 | tf_op jit(solution)/shard_map/ppermute | solution.py:420
  76.9 3.1 %shard_map.42 = (f32[320,256]{1,0:T(8,128)S(1)}, f32[256,128]{1,0:T(8,128)S(1)}, f32[256,256]{1,0:T(8,128)S(1)}) custom-call(s32[3]{0:T(128)S(1)} %pad_add_fusion.info_ref.refs_0_, f32[264,128]{1,0:T(8,128)S(1)} %shard_map.40.refs_1_, f32[264,128]{1,0:T(8,128)S(1)} %collective-permute-done.7.refs_2_, f32[264,128]{1,0:T(8,128)S(1)} %collective-permute-done.8.refs_3_, ...), custom_call_target="tpu_custom_call" | custom-call | flops 805306368 | bytes 1048576 | tf_op jit(solution)/shard_map/pallas_call | solution.py:79
  80.9 2.1 %collective-permute-start.13 = (f32[320,256]{1,0:T(8,128)S(1)}, f32[320,256]{1,0:T(8,128)S(1)}, u32[]{:S(2)}, u32[]{:S(2)}) collective-permute-start(f32[320,256]{1,0:T(8,128)S(1)} %get-tuple-element.65.weights_ref.refs_1_), channel_id=1, source_target_pairs={{16,32},{48,64},{80,96},{112,0},{17,33},{49,65},{81,97},{113,1},{1... | collective-permute-start | bytes 983048 | tf_op jit(solution)/shard_map/ppermute | solution.py:467
  83.0 2.2 %collective-permute-start.15 = (f32[256,128]{1,0:T(8,128)S(1)}, f32[256,128]{1,0:T(8,128)S(1)}, u32[]{:S(2)}, u32[]{:S(2)}) collective-permute-start(f32[256,128]{1,0:T(8,128)S(1)} %get-tuple-element.66), channel_id=1, source_target_pairs={{16,48},{48,80},{80,112},{112,16},{17,49},{49,81},{81,113},{113,17... | collective-permute-start | bytes 393224 | tf_op jit(solution)/shard_map/ppermute | solution.py:466
  86.2 2.8 %shard_map.44 = (f32[4,400,128]{2,1,0:T(8,128)S(1)}, f32[4,400,128]{2,1,0:T(8,128)S(1)}, f32[4,400,128]{2,1,0:T(8,128)S(1)}, f32[128,128]{1,0:T(8,128)S(1)}) custom-call(s32[3]{0:T(128)S(1)} %pad_add_fusion.info_ref.refs_0_, f32[320,256]{1,0:T(8,128)S(1)} %get-tuple-element.65.weights_ref.refs_1_, f32[320,256]{1,0:T(8,128)S(1)} %collective-permute-done.14.refs_2_.refs_3_, ...), custom_call_target="tpu_custom_call" | custom-call | flops 1258291200 | bytes 5734400 | tf_op jit(solution)/shard_map/pallas_call | solution.py:79
  88.9 2.3 %collective-permute-done.15.odd_ref = f32[256,128]{1,0:T(8,128)S(1)} collective-permute-done((f32[256,128]{1,0:T(8,128)S(1)}, f32[256,128]{1,0:T(8,128)S(1)}, u32[]{:S(2)}, u32[]{:S(2)}) %collective-permute-start.15) | collective-permute-done | bytes 131104 | tf_op jit(solution)/shard_map/ppermute | solution.py:466
  96.8 2.1 %collective-permute-done.19 = f32[128,128]{1,0:T(8,128)S(1)} collective-permute-done((f32[128,128]{1,0:T(8,128)S(1)}, f32[128,128]{1,0:T(8,128)S(1)}, u32[]{:S(2)}, u32[]{:S(2)}) %collective-permute-start.19) | collective-permute-done | bytes 65568 | tf_op jit(solution)/shard_map/ppermute | solution.py:420
  103.7 1.9 %collective-permute-done.22.refs_7_ = f32[128,128]{1,0:T(8,128)S(1)} collective-permute-done((f32[128,128]{1,0:T(8,128)S(1)}, f32[128,128]{1,0:T(8,128)S(1)}, u32[]{:S(2)}, u32[]{:S(2)}) %collective-permute-start.22) | collective-permute-done | bytes 65568 | tf_op jit(solution)/shard_map/ppermute | solution.py:420
  108.5 4.4 %collective-permute-done.23.refs_8_.refs_1_ = f32[4,400,128]{2,1,0:T(8,128)S(1)} collective-permute-done((f32[4,400,128]{2,1,0:T(8,128)S(1)}, f32[4,400,128]{2,1,0:T(8,128)S(1)}, u32[]{:S(2)}, u32[]{:S(2)}) %collective-permute-start.23) | collective-permute-done | bytes 819232 | tf_op jit(solution)/shard_map/ppermute | solution.py:481
  112.8 3.0 %shard_map.47 = (f32[320,256]{1,0:T(8,128)S(1)}, f32[256,128]{1,0:T(8,128)S(1)}, f32[256,256]{1,0:T(8,128)S(1)}) custom-call(s32[3]{0:T(128)S(1)} %pad_add_fusion.info_ref.refs_0_, f32[128,128]{1,0:T(8,128)S(1)} %shard_map.43.refs_7_.refs_1_, f32[320,256]{1,0:T(8,128)S(1)} %collective-permute-done.13.even_ref.refs_2_.refs_1_, ...), custom_call_target="tpu_custom_call" | custom-call | flops 805306368 | bytes 1048576 | tf_op jit(solution)/shard_map/pallas_call | solution.py:79
  123.1 2.8 %shard_map.51 = (f32[4,400,128]{2,1,0:T(8,128)S(1)}, f32[4,400,128]{2,1,0:T(8,128)S(1)}, f32[4,400,128]{2,1,0:T(8,128)S(1)}, f32[128,128]{1,0:T(8,128)S(1)}) custom-call(s32[3]{0:T(128)S(1)} %pad_add_fusion.info_ref.refs_0_, f32[320,256]{1,0:T(8,128)S(1)} %get-tuple-element.76.weights_ref.refs_1_, f32[320,256]{1,0:T(8,128)S(1)} %collective-permute-done.25.refs_2_.refs_3_, ...), custom_call_target="tpu_custom_call" | custom-call | flops 1258291200 | bytes 5734400 | tf_op jit(solution)/shard_map/pallas_call | solution.py:79
  134.6 2.3 %collective-permute-done.30 = f32[128,128]{1,0:T(8,128)S(1)} collective-permute-done((f32[128,128]{1,0:T(8,128)S(1)}, f32[128,128]{1,0:T(8,128)S(1)}, u32[]{:S(2)}, u32[]{:S(2)}) %collective-permute-start.30) | collective-permute-done | bytes 65568 | tf_op jit(solution)/shard_map/ppermute | solution.py:420
  142.3 2.6 %collective-permute-done.33.refs_6_ = f32[128,128]{1,0:T(8,128)S(1)} collective-permute-done((f32[128,128]{1,0:T(8,128)S(1)}, f32[128,128]{1,0:T(8,128)S(1)}, u32[]{:S(2)}, u32[]{:S(2)}) %collective-permute-start.33) | collective-permute-done | bytes 65568 | tf_op jit(solution)/shard_map/ppermute | solution.py:420
  145.8 3.1 %collective-permute-done.35.refs_8_.refs_1_ = f32[4,400,128]{2,1,0:T(8,128)S(1)} collective-permute-done((f32[4,400,128]{2,1,0:T(8,128)S(1)}, f32[4,400,128]{2,1,0:T(8,128)S(1)}, u32[]{:S(2)}, u32[]{:S(2)}) %collective-permute-start.35) | collective-permute-done | bytes 819232 | tf_op jit(solution)/shard_map/ppermute | solution.py:481
  148.9 2.6 %shard_map.54 = (f32[320,256]{1,0:T(8,128)S(1)}, f32[256,128]{1,0:T(8,128)S(1)}, f32[256,256]{1,0:T(8,128)S(1)}) custom-call(s32[3]{0:T(128)S(1)} %pad_add_fusion.info_ref.refs_0_, f32[128,128]{1,0:T(8,128)S(1)} %shard_map.48.refs_7_.refs_1_, f32[320,256]{1,0:T(8,128)S(1)} %collective-permute-done.24.even_ref.refs_2_.refs_1_, ...), custom_call_target="tpu_custom_call" | custom-call | flops 805306368 | bytes 1048576 | tf_op jit(solution)/shard_map/pallas_call | solution.py:79
  155.8 2.3 %collective-permute-start.38 = (f32[256,128]{1,0:T(8,128)S(1)}, f32[256,128]{1,0:T(8,128)S(1)}, u32[]{:S(2)}, u32[]{:S(2)}) collective-permute-start(f32[256,128]{1,0:T(8,128)S(1)} %get-tuple-element.89), channel_id=1, source_target_pairs={{16,48},{48,80},{80,112},{112,16},{17,49},{49,81},{81,113},{113,17... | collective-permute-start | bytes 393224 | tf_op jit(solution)/shard_map/ppermute | solution.py:466
  160.3 2.8 %shard_map.58 = (f32[4,400,128]{2,1,0:T(8,128)S(1)}, f32[4,400,128]{2,1,0:T(8,128)S(1)}, f32[4,400,128]{2,1,0:T(8,128)S(1)}, f32[128,128]{1,0:T(8,128)S(1)}) custom-call(s32[3]{0:T(128)S(1)} %pad_add_fusion.info_ref.refs_0_, f32[320,256]{1,0:T(8,128)S(1)} %get-tuple-element.88.weights_ref.refs_1_, f32[320,256]{1,0:T(8,128)S(1)} %collective-permute-done.37.refs_2_, ...), custom_call_target="tpu_custom_call" | custom-call | flops 1258291200 | bytes 5734400 | tf_op jit(solution)/shard_map/pallas_call | solution.py:79
  171.4 2.4 %collective-permute-done.42 = f32[128,128]{1,0:T(8,128)S(1)} collective-permute-done((f32[128,128]{1,0:T(8,128)S(1)}, f32[128,128]{1,0:T(8,128)S(1)}, u32[]{:S(2)}, u32[]{:S(2)}) %collective-permute-start.42) | collective-permute-done | bytes 65568 | tf_op jit(solution)/shard_map/ppermute | solution.py:420
  180.6 2.9 %collective-permute-done.45.refs_5_ = f32[128,128]{1,0:T(8,128)S(1)} collective-permute-done((f32[128,128]{1,0:T(8,128)S(1)}, f32[128,128]{1,0:T(8,128)S(1)}, u32[]{:S(2)}, u32[]{:S(2)}) %collective-permute-start.45) | collective-permute-done | bytes 65568 | tf_op jit(solution)/shard_map/ppermute | solution.py:420
  184.7 2.9 %shard_map.61 = (f32[256,256]{1,0:T(8,128)S(1)}, f32[256,128]{1,0:T(8,128)}, f32[256,256]{1,0:T(8,128)S(1)}) custom-call(s32[3]{0:T(128)S(1)} %pad_add_fusion.info_ref.refs_0_, f32[128,128]{1,0:T(8,128)S(1)} %shard_map.55.refs_7_.refs_0_, f32[320,256]{1,0:T(8,128)S(1)} %collective-permute-done.36.even_ref.refs_1_, ...), custom_call_target="tpu_custom_call" | custom-call | flops 805306368 | bytes 1048576 | tf_op jit(solution)/shard_map/pallas_call | solution.py:79
  187.6 4.2 %shard_map.63 = (f32[8,384,256]{2,1,0:T(8,128)}, f32[2,64,256]{2,1,0:T(8,128)}, f32[1,256]{1,0:T(1,128)}) custom-call(s32[3]{0:T(128)S(1)} %pad_add_fusion.info_ref.refs_0_, f32[256,256]{1,0:T(8,128)S(1)} %get-tuple-element.98.weights_ref, f32[256,256]{1,0:T(8,128)S(1)} %get-tuple-element.99.gram_ref, f32[4,400,128]{2,1,0:T(8,128)S(1)} %get-tuple-element.95.up0_ref.refs_1_, ...), custom_call_target="tpu_custom_call" | custom-call | flops 1258291200 | bytes 6553600 | tf_op jit(solution)/shard_map/pallas_call | solution.py:399
  (104 shorter events, 72.7 us)
Async XLA Ops:
  3.8 20.7 %collective-permute-start = (f32[2,2,384,128]{3,2,1,0:T(8,128)S(1)}, f32[2,2,384,128]{3,2,1,0:T(8,128)S(1)}, u32[]{:S(2)}, u32[]{:S(2)}) collective-permute-start(f32[2,2,384,128]{3,2,1,0:T(8,128)S(1)} %get-tuple-element.56), channel_id=1, source_target_pairs={{0,32},{16,48},{32,64},{48,80},{64,96},{80,112},{96,0},{112,16},{1... | collective-permute-start | bytes 2359304 | tf_op jit(solution)/shard_map/ppermute | solution.py:453
  6.0 36.4 %collective-permute-start.1 = (f32[2,2,384,128]{3,2,1,0:T(8,128)S(1)}, f32[2,2,384,128]{3,2,1,0:T(8,128)S(1)}, u32[]{:S(2)}, u32[]{:S(2)}) collective-permute-start(f32[2,2,384,128]{3,2,1,0:T(8,128)S(1)} %get-tuple-element.57), channel_id=1, source_target_pairs={{0,64},{16,80},{32,96},{48,112},{64,0},{80,16},{96,32},{112,48},{1... | collective-permute-start | bytes 2359304 | tf_op jit(solution)/shard_map/ppermute | solution.py:453
  8.6 33.8 %collective-permute-start.2 = (f32[2,2,384,128]{3,2,1,0:T(8,128)S(1)}, f32[2,2,384,128]{3,2,1,0:T(8,128)S(1)}, u32[]{:S(2)}, u32[]{:S(2)}) collective-permute-start(f32[2,2,384,128]{3,2,1,0:T(8,128)S(1)} %get-tuple-element.58), channel_id=1, source_target_pairs={{0,96},{16,112},{32,0},{48,16},{64,32},{80,48},{96,64},{112,80},{1... | collective-permute-start | bytes 2359304 | tf_op jit(solution)/shard_map/ppermute | solution.py:453
  46.7 20.9 %collective-permute-start.10 = (f32[2,384,128]{2,1,0:T(8,128)S(1)}, f32[2,384,128]{2,1,0:T(8,128)S(1)}, u32[]{:S(2)}, u32[]{:S(2)}) collective-permute-start(f32[2,384,128]{2,1,0:T(8,128)S(1)} %get-tuple-element.61), channel_id=1, source_target_pairs={{0,32},{16,48},{32,64},{48,80},{64,96},{80,112},{96,0},{112,16},{1... | collective-permute-start | bytes 1179656 | tf_op jit(solution)/shard_map/ppermute | solution.py:457
  47.7 6.5 %collective-permute-start.6 = (f32[264,128]{1,0:T(8,128)S(1)}, f32[264,128]{1,0:T(8,128)S(1)}, u32[]{:S(2)}, u32[]{:S(2)}) collective-permute-start(f32[264,128]{1,0:T(8,128)S(1)} %add.49.refs_0_), channel_id=1, source_target_pairs={{0,3},{1,0},{2,1},{3,2},{4,7},{5,4},{6,5},{7,6},{8,11},{9,8},{10,9... | collective-permute-start | bytes 405512 | tf_op jit(solution)/shard_map/ppermute | solution.py:420
  50.3 18.0 %collective-permute-start.11 = (f32[2,384,128]{2,1,0:T(8,128)S(1)}, f32[2,384,128]{2,1,0:T(8,128)S(1)}, u32[]{:S(2)}, u32[]{:S(2)}) collective-permute-start(f32[2,384,128]{2,1,0:T(8,128)S(1)} %get-tuple-element.62), channel_id=1, source_target_pairs={{0,64},{16,80},{32,96},{48,112},{64,0},{80,16},{96,32},{112,48},{1... | collective-permute-start | bytes 1179656 | tf_op jit(solution)/shard_map/ppermute | solution.py:457
  52.4 17.3 %collective-permute-start.12 = (f32[2,384,128]{2,1,0:T(8,128)S(1)}, f32[2,384,128]{2,1,0:T(8,128)S(1)}, u32[]{:S(2)}, u32[]{:S(2)}) collective-permute-start(f32[2,384,128]{2,1,0:T(8,128)S(1)} %get-tuple-element.63), channel_id=1, source_target_pairs={{0,96},{16,112},{32,0},{48,16},{64,32},{80,48},{96,64},{112,80},{1... | collective-permute-start | bytes 1179656 | tf_op jit(solution)/shard_map/ppermute | solution.py:457
  53.7 5.5 %collective-permute-start.5 = (f32[264,128]{1,0:T(8,128)S(1)}, f32[264,128]{1,0:T(8,128)S(1)}, u32[]{:S(2)}, u32[]{:S(2)}) collective-permute-start(f32[264,128]{1,0:T(8,128)S(1)} %add.49.refs_0_), channel_id=1, source_target_pairs={{0,2},{1,3},{2,0},{3,1},{4,6},{5,7},{6,4},{7,5},{8,10},{9,11},{10,... | collective-permute-start | bytes 405512 | tf_op jit(solution)/shard_map/ppermute | solution.py:420
  54.2 9.0 %collective-permute-start.4 = (f32[264,128]{1,0:T(8,128)S(1)}, f32[264,128]{1,0:T(8,128)S(1)}, u32[]{:S(2)}, u32[]{:S(2)}) collective-permute-start(f32[264,128]{1,0:T(8,128)S(1)} %add.49.refs_0_), channel_id=1, source_target_pairs={{0,1},{1,2},{2,3},{3,0},{4,5},{5,6},{6,7},{7,4},{8,9},{9,10},{10,1... | collective-permute-start | bytes 405512 | tf_op jit(solution)/shard_map/ppermute | solution.py:420
  63.8 9.5 %collective-permute-start.9 = (f32[264,128]{1,0:T(8,128)S(1)}, f32[264,128]{1,0:T(8,128)S(1)}, u32[]{:S(2)}, u32[]{:S(2)}) collective-permute-start(f32[264,128]{1,0:T(8,128)S(1)} %shard_map.40.refs_1_), channel_id=1, source_target_pairs={{0,12},{1,13},{2,14},{3,15},{4,0},{5,1},{6,2},{7,3},{8,4},{9,5},{1... | collective-permute-start | bytes 405512 | tf_op jit(solution)/shard_map/ppermute | solution.py:420
  67.6 5.7 %collective-permute-start.8 = (f32[264,128]{1,0:T(8,128)S(1)}, f32[264,128]{1,0:T(8,128)S(1)}, u32[]{:S(2)}, u32[]{:S(2)}) collective-permute-start(f32[264,128]{1,0:T(8,128)S(1)} %shard_map.40.refs_1_), channel_id=1, source_target_pairs={{0,8},{1,9},{2,10},{3,11},{4,12},{5,13},{6,14},{7,15},{8,0},{9,1},... | collective-permute-start | bytes 405512 | tf_op jit(solution)/shard_map/ppermute | solution.py:420
  67.6 9.3 %collective-permute-start.7 = (f32[264,128]{1,0:T(8,128)S(1)}, f32[264,128]{1,0:T(8,128)S(1)}, u32[]{:S(2)}, u32[]{:S(2)}) collective-permute-start(f32[264,128]{1,0:T(8,128)S(1)} %shard_map.40.refs_1_), channel_id=1, source_target_pairs={{0,4},{1,5},{2,6},{3,7},{4,8},{5,9},{6,10},{7,11},{8,12},{9,13},{1... | collective-permute-start | bytes 405512 | tf_op jit(solution)/shard_map/ppermute | solution.py:420
  79.9 6.2 %collective-permute-start.14 = (f32[320,256]{1,0:T(8,128)S(1)}, f32[320,256]{1,0:T(8,128)S(1)}, u32[]{:S(2)}, u32[]{:S(2)}) collective-permute-start(f32[320,256]{1,0:T(8,128)S(1)} %get-tuple-element.65.weights_ref.refs_1_), channel_id=1, source_target_pairs={{0,16},{16,0},{32,48},{48,32},{64,80},{80,64},{96,112},{112,96},{1... | collective-permute-start | bytes 983048 | tf_op jit(solution)/shard_map/ppermute | solution.py:416
  80.9 10.3 %collective-permute-start.13 = (f32[320,256]{1,0:T(8,128)S(1)}, f32[320,256]{1,0:T(8,128)S(1)}, u32[]{:S(2)}, u32[]{:S(2)}) collective-permute-start(f32[320,256]{1,0:T(8,128)S(1)} %get-tuple-element.65.weights_ref.refs_1_), channel_id=1, source_target_pairs={{16,32},{48,64},{80,96},{112,0},{17,33},{49,65},{81,97},{113,1},{1... | collective-permute-start | bytes 983048 | tf_op jit(solution)/shard_map/ppermute | solution.py:467
  83.0 8.2 %collective-permute-start.15 = (f32[256,128]{1,0:T(8,128)S(1)}, f32[256,128]{1,0:T(8,128)S(1)}, u32[]{:S(2)}, u32[]{:S(2)}) collective-permute-start(f32[256,128]{1,0:T(8,128)S(1)} %get-tuple-element.66), channel_id=1, source_target_pairs={{16,48},{48,80},{80,112},{112,16},{17,49},{49,81},{81,113},{113,17... | collective-permute-start | bytes 393224 | tf_op jit(solution)/shard_map/ppermute | solution.py:466
  91.8 21.0 %collective-permute-start.23 = (f32[4,400,128]{2,1,0:T(8,128)S(1)}, f32[4,400,128]{2,1,0:T(8,128)S(1)}, u32[]{:S(2)}, u32[]{:S(2)}) collective-permute-start(f32[4,400,128]{2,1,0:T(8,128)S(1)} %get-tuple-element.74), channel_id=1, source_target_pairs={{0,32},{16,48},{32,64},{48,80},{64,96},{80,112},{96,0},{112,16},{1... | collective-permute-start | bytes 2457608 | tf_op jit(solution)/shard_map/ppermute | solution.py:481
  95.3 5.1 %collective-permute-start.18 = (f32[128,128]{1,0:T(8,128)S(1)}, f32[128,128]{1,0:T(8,128)S(1)}, u32[]{:S(2)}, u32[]{:S(2)}) collective-permute-start(f32[128,128]{1,0:T(8,128)S(1)} %add.50), channel_id=1, source_target_pairs={{0,2},{1,3},{2,0},{3,1},{4,6},{5,7},{6,4},{7,5},{8,10},{9,11},{10,... | collective-permute-start | bytes 196616 | tf_op jit(solution)/shard_map/ppermute | solution.py:420
  95.6 6.6 %collective-permute-start.17 = (f32[128,128]{1,0:T(8,128)S(1)}, f32[128,128]{1,0:T(8,128)S(1)}, u32[]{:S(2)}, u32[]{:S(2)}) collective-permute-start(f32[128,128]{1,0:T(8,128)S(1)} %add.50), channel_id=1, source_target_pairs={{0,1},{1,2},{2,3},{3,0},{4,5},{5,6},{6,7},{7,4},{8,9},{9,10},{10,1... | collective-permute-start | bytes 196616 | tf_op jit(solution)/shard_map/ppermute | solution.py:420
  102.9 5.6 %collective-permute-start.20 = (f32[128,128]{1,0:T(8,128)S(1)}, f32[128,128]{1,0:T(8,128)S(1)}, u32[]{:S(2)}, u32[]{:S(2)}) collective-permute-start(f32[128,128]{1,0:T(8,128)S(1)} %add_add_fusion.2.refs_4_), channel_id=1, source_target_pairs={{0,4},{1,5},{2,6},{3,7},{4,8},{5,9},{6,10},{7,11},{8,12},{9,13},{1... | collective-permute-start | bytes 196616 | tf_op jit(solution)/shard_map/ppermute | solution.py:420
  115.8 7.3 %collective-permute-start.25 = (f32[320,256]{1,0:T(8,128)S(1)}, f32[320,256]{1,0:T(8,128)S(1)}, u32[]{:S(2)}, u32[]{:S(2)}) collective-permute-start(f32[320,256]{1,0:T(8,128)S(1)} %get-tuple-element.76.weights_ref.refs_1_), channel_id=1, source_target_pairs={{0,16},{16,0},{32,48},{48,32},{64,80},{80,64},{96,112},{112,96},{1... | collective-permute-start | bytes 983048 | tf_op jit(solution)/shard_map/ppermute | solution.py:416
  115.9 11.1 %collective-permute-start.24 = (f32[320,256]{1,0:T(8,128)S(1)}, f32[320,256]{1,0:T(8,128)S(1)}, u32[]{:S(2)}, u32[]{:S(2)}) collective-permute-start(f32[320,256]{1,0:T(8,128)S(1)} %get-tuple-element.76.weights_ref.refs_1_), channel_id=1, source_target_pairs={{16,32},{48,64},{80,96},{112,0},{17,33},{49,65},{81,97},{113,1},{1... | collective-permute-start | bytes 983048 | tf_op jit(solution)/shard_map/ppermute | solution.py:467
  119.1 7.9 %collective-permute-start.26 = (f32[256,128]{1,0:T(8,128)S(1)}, f32[256,128]{1,0:T(8,128)S(1)}, u32[]{:S(2)}, u32[]{:S(2)}) collective-permute-start(f32[256,128]{1,0:T(8,128)S(1)} %get-tuple-element.77), channel_id=1, source_target_pairs={{16,48},{48,80},{80,112},{112,16},{17,49},{49,81},{81,113},{113,17... | collective-permute-start | bytes 393224 | tf_op jit(solution)/shard_map/ppermute | solution.py:466
  127.6 21.3 %collective-permute-start.35 = (f32[4,400,128]{2,1,0:T(8,128)S(1)}, f32[4,400,128]{2,1,0:T(8,128)S(1)}, u32[]{:S(2)}, u32[]{:S(2)}) collective-permute-start(f32[4,400,128]{2,1,0:T(8,128)S(1)} %get-tuple-element.86), channel_id=1, source_target_pairs={{0,32},{16,48},{32,64},{48,80},{64,96},{80,112},{96,0},{112,16},{1... | collective-permute-start | bytes 2457608 | tf_op jit(solution)/shard_map/ppermute | solution.py:481
  132.9 5.9 %collective-permute-start.29 = (f32[128,128]{1,0:T(8,128)S(1)}, f32[128,128]{1,0:T(8,128)S(1)}, u32[]{:S(2)}, u32[]{:S(2)}) collective-permute-start(f32[128,128]{1,0:T(8,128)S(1)} %add.54), channel_id=1, source_target_pairs={{0,1},{1,2},{2,3},{3,0},{4,5},{5,6},{6,7},{7,4},{8,9},{9,10},{10,1... | collective-permute-start | bytes 196616 | tf_op jit(solution)/shard_map/ppermute | solution.py:420
  140.8 5.0 %collective-permute-start.32 = (f32[128,128]{1,0:T(8,128)S(1)}, f32[128,128]{1,0:T(8,128)S(1)}, u32[]{:S(2)}, u32[]{:S(2)}) collective-permute-start(f32[128,128]{1,0:T(8,128)S(1)} %add_add_fusion.1.refs_4_), channel_id=1, source_target_pairs={{0,4},{1,5},{2,6},{3,7},{4,8},{5,9},{6,10},{7,11},{8,12},{9,13},{1... | collective-permute-start | bytes 196616 | tf_op jit(solution)/shard_map/ppermute | solution.py:420
  151.6 8.7 %collective-permute-start.37 = (f32[320,256]{1,0:T(8,128)S(1)}, f32[320,256]{1,0:T(8,128)S(1)}, u32[]{:S(2)}, u32[]{:S(2)}) collective-permute-start(f32[320,256]{1,0:T(8,128)S(1)} %get-tuple-element.88.weights_ref.refs_1_), channel_id=1, source_target_pairs={{0,16},{16,0},{32,48},{48,32},{64,80},{80,64},{96,112},{112,96},{1... | collective-permute-start | bytes 983048 | tf_op jit(solution)/shard_map/ppermute | solution.py:416
  152.3 10.8 %collective-permute-start.36 = (f32[320,256]{1,0:T(8,128)S(1)}, f32[320,256]{1,0:T(8,128)S(1)}, u32[]{:S(2)}, u32[]{:S(2)}) collective-permute-start(f32[320,256]{1,0:T(8,128)S(1)} %get-tuple-element.88.weights_ref.refs_1_), channel_id=1, source_target_pairs={{16,32},{48,64},{80,96},{112,0},{17,33},{49,65},{81,97},{113,1},{1... | collective-permute-start | bytes 983048 | tf_op jit(solution)/shard_map/ppermute | solution.py:467
  155.8 7.2 %collective-permute-start.38 = (f32[256,128]{1,0:T(8,128)S(1)}, f32[256,128]{1,0:T(8,128)S(1)}, u32[]{:S(2)}, u32[]{:S(2)}) collective-permute-start(f32[256,128]{1,0:T(8,128)S(1)} %get-tuple-element.89), channel_id=1, source_target_pairs={{16,48},{48,80},{80,112},{112,16},{17,49},{49,81},{81,113},{113,17... | collective-permute-start | bytes 393224 | tf_op jit(solution)/shard_map/ppermute | solution.py:466
  169.7 5.9 %collective-permute-start.41 = (f32[128,128]{1,0:T(8,128)S(1)}, f32[128,128]{1,0:T(8,128)S(1)}, u32[]{:S(2)}, u32[]{:S(2)}) collective-permute-start(f32[128,128]{1,0:T(8,128)S(1)} %add.58), channel_id=1, source_target_pairs={{0,1},{1,2},{2,3},{3,0},{4,5},{5,6},{6,7},{7,4},{8,9},{9,10},{10,1... | collective-permute-start | bytes 196616 | tf_op jit(solution)/shard_map/ppermute | solution.py:420
  176.4 11.3 %collective-permute-start.47 = (f32[4,400,128]{2,1,0:T(8,128)S(1)}, f32[4,400,128]{2,1,0:T(8,128)S(1)}, u32[]{:S(2)}, u32[]{:S(2)}) collective-permute-start(f32[4,400,128]{2,1,0:T(8,128)S(1)} %get-tuple-element.102), channel_id=1, source_target_pairs={{0,16},{16,0},{32,48},{48,32},{64,80},{80,64},{96,112},{112,96},{1... | collective-permute-start | bytes 2457608 | tf_op jit(solution)/shard_map/ppermute | solution.py:416
  177.4 10.3 %collective-permute-start.48 = (f32[4,400,128]{2,1,0:T(8,128)S(1)}, f32[4,400,128]{2,1,0:T(8,128)S(1)}, u32[]{:S(2)}, u32[]{:S(2)}) collective-permute-start(f32[4,400,128]{2,1,0:T(8,128)S(1)} %get-tuple-element.103), channel_id=1, source_target_pairs={{0,16},{16,0},{32,48},{48,32},{64,80},{80,64},{96,112},{112,96},{1... | collective-permute-start | bytes 2457608 | tf_op jit(solution)/shard_map/ppermute | solution.py:416
  179.4 5.3 %collective-permute-start.44 = (f32[128,128]{1,0:T(8,128)S(1)}, f32[128,128]{1,0:T(8,128)S(1)}, u32[]{:S(2)}, u32[]{:S(2)}) collective-permute-start(f32[128,128]{1,0:T(8,128)S(1)} %add_add_fusion.refs_3_.refs_5_), channel_id=1, source_target_pairs={{0,4},{1,5},{2,6},{3,7},{4,8},{5,9},{6,10},{7,11},{8,12},{9,13},{1... | collective-permute-start | bytes 196616 | tf_op jit(solution)/shard_map/ppermute | solution.py:420
  (19 other events, 102.7 us)

commit v8 on v7

--- a/solution.py
+++ b/solution.py
@@ -312,12 +312,11 @@
     cross_ref[...] = cross
 
 
-def rotate_own(info, own, other, blocks, before, rows, step):
+def rotate_own(info, own, other, blocks, rows, step):
     return call_whole(
         functools.partial(own_kernel, rows, step),
         (info, own, other, *blocks),
         [shape(SIDE, step, BLOCK)] * 3 + [shape(BLOCK, BLOCK)],
-        before,
         flops=2 * 3 * SIDE * step * 4 * BLOCK * PAIR,
         nbytes=4 * 7 * SIDE * step * BLOCK,
     )
@@ -467,8 +466,7 @@
         even = lax.ppermute(weights, "cols", ODD_TO_EVEN)
         other = swap_core(weights)
         up = project(info, gram, weights)
-        before = [up] + ([ahead_blocks[0]] if sweep_round else [])
-        up0, up1, low1, cross = rotate_own(info, weights, other, own_blocks, before, rows, step)
+        up0, up1, low1, cross = rotate_own(info, weights, other, own_blocks, rows, step)
         lower, passed = lower_before(info, even, odd, low1)
         low0, keep, send = rotate_ahead(info, lower, cross, up0, ahead_blocks, rows, step)
         value = keep + swap_core(send)
@@ -479,7 +477,7 @@
         else:
             up_m = rotate_up(info, [even, relayed_upper(info, even, [keep])], ahead_blocks, step)
             ahead_blocks = [up_m, lax.ppermute(passed, "cols", CHIPS_ON[1])]
-        before = [] if last else [ahead_blocks[1]]
+        before = [] if last else ahead_blocks
         weights, lower, gram = cayley(info, up, even, other, [value] + along(value, ALONG_Z), before, last)
 
     rotated, frame, column_scale = rotate_final(info, weights, gram, own_blocks + other_blocks, rows, step)

time: 192 us -> 190 us (0.990)
  starting transfers between devices: 48.9 us -> 46 us
    ppermute x24, waiting for transfers between devices: 47.6 us -> 37.9 us  [along(): return [lax.ppermute(value, 'rows', pairs) for pairs in shifts]]
    ppermute x3, waiting for transfers between devices: 3.37 us -> 12 us  [body(): odd = lax.ppermute(lower, 'cols', ODD_TO_ODD)]
  transfers between devices with their start and end apart: 49 -> 49, of which waited for: 32 -> 31; matrix products, arithmetic and copies ran while one was open for 0% -> 0% of each run, Pallas kernels for 12% -> 12%
where the time goes in v8:
time: 190 us; the launch traced here: 189 us
  waiting for transfers between devices  96.7 us (51%)
  starting transfers between devices  46 us (24%)
  Pallas kernels  43.3 us (23%)
    ppermute x24, waiting for transfers between devices, along(): return [lax.ppermute(value, 'rows', pairs) for pairs in shifts]  37.9 us
    pallas_call x23, Pallas kernels, call_whole(): pl.pallas_call(inner, in_specs=[pl.BlockSpec(memory_space=pltpu.SMEM)] +...  37.3 us
    ppermute x6, waiting for transfers between devices, body(): lax.ppermute(packed[k], 'cols', CHIPS_ON[k])  34.1 us
    ppermute x24, starting transfers between devices, along(): return [lax.ppermute(value, 'rows', pairs) for pairs in shifts]  17.5 us
    ppermute x3, waiting for transfers between devices, body(): odd = lax.ppermute(lower, 'cols', ODD_TO_ODD)  12 us
    ppermute x6, starting transfers between devices, body(): lax.ppermute(packed[k], 'cols', CHIPS_ON[k])  10.3 us
    ppermute x2, waiting for transfers between devices, body(): ahead_blocks = [up_m, lax.ppermute(passed, 'cols', CHIPS_ON[1])]  8.89 us
    ppermute x3, starting transfers between devices, body(): odd = lax.ppermute(lower, 'cols', ODD_TO_ODD)  6.04 us
  transfers between devices with their start and end apart: 49, of which 31 were waited for; matrix products, arithmetic and copies ran while one was open for 0% of the time, Pallas kernels for 12%

profile of v8, /device:TPU:1, one launch (start us, length us, event | category | flops | bytes accessed | tf_op | source)
XLA Modules:
  0.0 189.1 jit_solution(3845088202159920880)
XLA Ops:
  0.7 1.9 copy-done
  3.8 2.2 %collective-permute-start = (f32[2,2,384,128]{3,2,1,0:T(8,128)S(1)}, f32[2,2,384,128]{3,2,1,0:T(8,128)S(1)}, u32[]{:S(2)}, u32[]{:S(2)}) collective-permute-start(f32[2,2,384,128]{3,2,1,0:T(8,128)S(1)} %get-tuple-element.56), channel_id=1, source_target_pairs={{0,32},{16,48},{32,64},{48,80},{64,96},{80,112},{96,0},{112,16},{1... | collective-permute-start | bytes 2359304 | tf_op jit(solution)/shard_map/ppermute | solution.py:452
  6.0 2.6 %collective-permute-start.1 = (f32[2,2,384,128]{3,2,1,0:T(8,128)S(1)}, f32[2,2,384,128]{3,2,1,0:T(8,128)S(1)}, u32[]{:S(2)}, u32[]{:S(2)}) collective-permute-start(f32[2,2,384,128]{3,2,1,0:T(8,128)S(1)} %get-tuple-element.57), channel_id=1, source_target_pairs={{0,64},{16,80},{32,96},{48,112},{64,0},{80,16},{96,32},{112,48},{1... | collective-permute-start | bytes 2359304 | tf_op jit(solution)/shard_map/ppermute | solution.py:452
  9.7 14.9 %collective-permute-done.refs_1_.refs_4_ = f32[2,2,384,128]{3,2,1,0:T(8,128)S(1)} collective-permute-done((f32[2,2,384,128]{3,2,1,0:T(8,128)S(1)}, f32[2,2,384,128]{3,2,1,0:T(8,128)S(1)}, u32[]{:S(2)}, u32[]{:S(2)}) %collective-permute-start) | collective-permute-done | bytes 786464 | tf_op jit(solution)/shard_map/ppermute | solution.py:452
  24.6 17.9 %collective-permute-done.1.refs_2_.refs_5_ = f32[2,2,384,128]{3,2,1,0:T(8,128)S(1)} collective-permute-done((f32[2,2,384,128]{3,2,1,0:T(8,128)S(1)}, f32[2,2,384,128]{3,2,1,0:T(8,128)S(1)}, u32[]{:S(2)}, u32[]{:S(2)}) %collective-permute-start.1) | collective-permute-done | bytes 786464 | tf_op jit(solution)/shard_map/ppermute | solution.py:452
  42.4 1.9 %shard_map.39 = (f32[264,128]{1,0:T(8,128)S(1)}, f32[264,128]{1,0:T(8,128)S(1)}) custom-call(s32[3]{0:T(128)S(1)} %pad_add_fusion.info_ref.refs_0_, f32[2,2,384,128]{3,2,1,0:T(8,128)S(1)} %get-tuple-element.55.refs_0_, f32[2,2,384,128]{3,2,1,0:T(8,128)S(1)} %collective-permute-done.refs_1_.refs_4_, ...), custom_call_target="tpu_custom_call" | custom-call | flops 805306368 | bytes 3145728 | tf_op jit(solution)/shard_map/pallas_call | solution.py:79
  47.7 2.6 %collective-permute-start.6 = (f32[264,128]{1,0:T(8,128)S(1)}, f32[264,128]{1,0:T(8,128)S(1)}, u32[]{:S(2)}, u32[]{:S(2)}) collective-permute-start(f32[264,128]{1,0:T(8,128)S(1)} %add.49.refs_0_), channel_id=1, source_target_pairs={{0,3},{1,0},{2,1},{3,2},{4,7},{5,4},{6,5},{7,6},{8,11},{9,8},{10,9... | collective-permute-start | bytes 405512 | tf_op jit(solution)/shard_map/ppermute | solution.py:419
  50.3 2.1 %collective-permute-start.11 = (f32[2,384,128]{2,1,0:T(8,128)S(1)}, f32[2,384,128]{2,1,0:T(8,128)S(1)}, u32[]{:S(2)}, u32[]{:S(2)}) collective-permute-start(f32[2,384,128]{2,1,0:T(8,128)S(1)} %get-tuple-element.62), channel_id=1, source_target_pairs={{0,64},{16,80},{32,96},{48,112},{64,0},{80,16},{96,32},{112,48},{1... | collective-permute-start | bytes 1179656 | tf_op jit(solution)/shard_map/ppermute | solution.py:456
  54.8 4.3 %collective-permute-done.5.refs_2_ = f32[264,128]{1,0:T(8,128)S(1)} collective-permute-done((f32[264,128]{1,0:T(8,128)S(1)}, f32[264,128]{1,0:T(8,128)S(1)}, u32[]{:S(2)}, u32[]{:S(2)}) %collective-permute-start.5) | collective-permute-done | bytes 135200 | tf_op jit(solution)/shard_map/ppermute | solution.py:419
  59.2 4.0 %collective-permute-done.4.refs_1_ = f32[264,128]{1,0:T(8,128)S(1)} collective-permute-done((f32[264,128]{1,0:T(8,128)S(1)}, f32[264,128]{1,0:T(8,128)S(1)}, u32[]{:S(2)}, u32[]{:S(2)}) %collective-permute-start.4) | collective-permute-done | bytes 135200 | tf_op jit(solution)/shard_map/ppermute | solution.py:419
  63.8 3.8 %collective-permute-start.9 = (f32[264,128]{1,0:T(8,128)S(1)}, f32[264,128]{1,0:T(8,128)S(1)}, u32[]{:S(2)}, u32[]{:S(2)}) collective-permute-start(f32[264,128]{1,0:T(8,128)S(1)} %shard_map.40.refs_1_), channel_id=1, source_target_pairs={{0,12},{1,13},{2,14},{3,15},{4,0},{5,1},{6,2},{7,3},{8,4},{9,5},{1... | collective-permute-start | bytes 405512 | tf_op jit(solution)/shard_map/ppermute | solution.py:419
  69.7 3.6 %collective-permute-done.9.refs_4_ = f32[264,128]{1,0:T(8,128)S(1)} collective-permute-done((f32[264,128]{1,0:T(8,128)S(1)}, f32[264,128]{1,0:T(8,128)S(1)}, u32[]{:S(2)}, u32[]{:S(2)}) %collective-permute-start.9) | collective-permute-done | bytes 135200 | tf_op jit(solution)/shard_map/ppermute | solution.py:419
  73.3 3.6 %collective-permute-done.7.refs_2_ = f32[264,128]{1,0:T(8,128)S(1)} collective-permute-done((f32[264,128]{1,0:T(8,128)S(1)}, f32[264,128]{1,0:T(8,128)S(1)}, u32[]{:S(2)}, u32[]{:S(2)}) %collective-permute-start.7) | collective-permute-done | bytes 135200 | tf_op jit(solution)/shard_map/ppermute | solution.py:419
  76.9 3.0 %shard_map.42 = (f32[320,256]{1,0:T(8,128)S(1)}, f32[256,128]{1,0:T(8,128)S(1)}, f32[256,256]{1,0:T(8,128)S(1)}) custom-call(s32[3]{0:T(128)S(1)} %pad_add_fusion.info_ref.refs_0_, f32[264,128]{1,0:T(8,128)S(1)} %shard_map.40.refs_1_, f32[264,128]{1,0:T(8,128)S(1)} %collective-permute-done.7.refs_2_, f32[264,128]{1,0:T(8,128)S(1)} %collective-permute-done.8.refs_3_, ...), custom_call_target="tpu_custom_call" | custom-call | flops 805306368 | bytes 1048576 | tf_op jit(solution)/shard_map/pallas_call | solution.py:79
  80.9 2.1 %collective-permute-start.13 = (f32[320,256]{1,0:T(8,128)S(1)}, f32[320,256]{1,0:T(8,128)S(1)}, u32[]{:S(2)}, u32[]{:S(2)}) collective-permute-start(f32[320,256]{1,0:T(8,128)S(1)} %get-tuple-element.65.weights_ref.own_ref), channel_id=1, source_target_pairs={{16,32},{48,64},{80,96},{112,0},{17,33},{49,65},{81,97},{113,1},{1... | collective-permute-start | bytes 983048 | tf_op jit(solution)/shard_map/ppermute | solution.py:466
  83.0 2.2 %collective-permute-start.15 = (f32[256,128]{1,0:T(8,128)S(1)}, f32[256,128]{1,0:T(8,128)S(1)}, u32[]{:S(2)}, u32[]{:S(2)}) collective-permute-start(f32[256,128]{1,0:T(8,128)S(1)} %get-tuple-element.66), channel_id=1, source_target_pairs={{16,48},{48,80},{80,112},{112,16},{17,49},{49,81},{81,113},{113,17... | collective-permute-start | bytes 393224 | tf_op jit(solution)/shard_map/ppermute | solution.py:465
  85.2 2.8 %shard_map.44 = (f32[4,400,128]{2,1,0:T(8,128)S(1)}, f32[4,400,128]{2,1,0:T(8,128)S(1)}, f32[4,400,128]{2,1,0:T(8,128)S(1)}, f32[128,128]{1,0:T(8,128)S(1)}) custom-call(s32[3]{0:T(128)S(1)} %pad_add_fusion.info_ref.refs_0_, f32[320,256]{1,0:T(8,128)S(1)} %get-tuple-element.65.weights_ref.own_ref, f32[320,256]{1,0:T(8,128)S(1)} %collective-permute-done.14.other_ref.refs_3_, ...), custom_call_target="tpu_custom_call" | custom-call | flops 1258291200 | bytes 5734400 | tf_op jit(solution)/shard_map/pallas_call | solution.py:79
  88.0 3.2 %collective-permute-done.15.odd_ref = f32[256,128]{1,0:T(8,128)S(1)} collective-permute-done((f32[256,128]{1,0:T(8,128)S(1)}, f32[256,128]{1,0:T(8,128)S(1)}, u32[]{:S(2)}, u32[]{:S(2)}) %collective-permute-start.15) | collective-permute-done | bytes 131104 | tf_op jit(solution)/shard_map/ppermute | solution.py:465
  108.5 4.4 %collective-permute-done.24.refs_9_.refs_1_ = f32[4,400,128]{2,1,0:T(8,128)S(1)} collective-permute-done((f32[4,400,128]{2,1,0:T(8,128)S(1)}, f32[4,400,128]{2,1,0:T(8,128)S(1)}, u32[]{:S(2)}, u32[]{:S(2)}) %collective-permute-start.24) | collective-permute-done | bytes 819232 | tf_op jit(solution)/shard_map/ppermute | solution.py:479
  112.8 2.6 %shard_map.49 = (f32[320,256]{1,0:T(8,128)S(1)}, f32[256,128]{1,0:T(8,128)S(1)}, f32[256,256]{1,0:T(8,128)S(1)}) custom-call(s32[3]{0:T(128)S(1)} %pad_add_fusion.info_ref.refs_0_, f32[128,128]{1,0:T(8,128)S(1)} %shard_map.43.refs_1_, f32[320,256]{1,0:T(8,128)S(1)} %collective-permute-done.13.even_ref.refs_1_.refs_2_, ...), custom_call_target="tpu_custom_call" | custom-call | flops 805306368 | bytes 1048576 | tf_op jit(solution)/shard_map/pallas_call | solution.py:79
  117.2 1.9 %collective-permute-start.27 = (f32[256,128]{1,0:T(8,128)S(1)}, f32[256,128]{1,0:T(8,128)S(1)}, u32[]{:S(2)}, u32[]{:S(2)}) collective-permute-start(f32[256,128]{1,0:T(8,128)S(1)} %get-tuple-element.77), channel_id=1, source_target_pairs={{16,48},{48,80},{80,112},{112,16},{17,49},{49,81},{81,113},{113,17... | collective-permute-start | bytes 393224 | tf_op jit(solution)/shard_map/ppermute | solution.py:465
  119.2 2.8 %shard_map.51 = (f32[4,400,128]{2,1,0:T(8,128)S(1)}, f32[4,400,128]{2,1,0:T(8,128)S(1)}, f32[4,400,128]{2,1,0:T(8,128)S(1)}, f32[128,128]{1,0:T(8,128)S(1)}) custom-call(s32[3]{0:T(128)S(1)} %pad_add_fusion.info_ref.refs_0_, f32[320,256]{1,0:T(8,128)S(1)} %get-tuple-element.76.weights_ref.own_ref, f32[320,256]{1,0:T(8,128)S(1)} %collective-permute-done.26.other_ref.refs_3_, ...), custom_call_target="tpu_custom_call" | custom-call | flops 1258291200 | bytes 5734400 | tf_op jit(solution)/shard_map/pallas_call | solution.py:79
  121.9 4.4 %collective-permute-done.27.odd_ref = f32[256,128]{1,0:T(8,128)S(1)} collective-permute-done((f32[256,128]{1,0:T(8,128)S(1)}, f32[256,128]{1,0:T(8,128)S(1)}, u32[]{:S(2)}, u32[]{:S(2)}) %collective-permute-start.27) | collective-permute-done | bytes 131104 | tf_op jit(solution)/shard_map/ppermute | solution.py:465
  143.4 4.5 %collective-permute-done.36.refs_9_.refs_1_ = f32[4,400,128]{2,1,0:T(8,128)S(1)} collective-permute-done((f32[4,400,128]{2,1,0:T(8,128)S(1)}, f32[4,400,128]{2,1,0:T(8,128)S(1)}, u32[]{:S(2)}, u32[]{:S(2)}) %collective-permute-start.36) | collective-permute-done | bytes 819232 | tf_op jit(solution)/shard_map/ppermute | solution.py:479
  148.0 2.8 %shard_map.56 = (f32[320,256]{1,0:T(8,128)S(1)}, f32[256,128]{1,0:T(8,128)S(1)}, f32[256,256]{1,0:T(8,128)S(1)}) custom-call(s32[3]{0:T(128)S(1)} %pad_add_fusion.info_ref.refs_0_, f32[128,128]{1,0:T(8,128)S(1)} %shard_map.50.refs_1_, f32[320,256]{1,0:T(8,128)S(1)} %collective-permute-done.25.even_ref.refs_1_.refs_2_, ...), custom_call_target="tpu_custom_call" | custom-call | flops 805306368 | bytes 1048576 | tf_op jit(solution)/shard_map/pallas_call | solution.py:79
  152.6 1.9 %collective-permute-start.39 = (f32[256,128]{1,0:T(8,128)S(1)}, f32[256,128]{1,0:T(8,128)S(1)}, u32[]{:S(2)}, u32[]{:S(2)}) collective-permute-start(f32[256,128]{1,0:T(8,128)S(1)} %get-tuple-element.89), channel_id=1, source_target_pairs={{16,48},{48,80},{80,112},{112,16},{17,49},{49,81},{81,113},{113,17... | collective-permute-start | bytes 393224 | tf_op jit(solution)/shard_map/ppermute | solution.py:465
  154.5 2.8 %shard_map.58 = (f32[4,400,128]{2,1,0:T(8,128)S(1)}, f32[4,400,128]{2,1,0:T(8,128)S(1)}, f32[4,400,128]{2,1,0:T(8,128)S(1)}, f32[128,128]{1,0:T(8,128)S(1)}) custom-call(s32[3]{0:T(128)S(1)} %pad_add_fusion.info_ref.refs_0_, f32[320,256]{1,0:T(8,128)S(1)} %get-tuple-element.88.weights_ref.own_ref, f32[320,256]{1,0:T(8,128)S(1)} %collective-permute-done.38.other_ref.refs_2_, ...), custom_call_target="tpu_custom_call" | custom-call | flops 1258291200 | bytes 5734400 | tf_op jit(solution)/shard_map/pallas_call | solution.py:79
  157.3 4.4 %collective-permute-done.39.odd_ref = f32[256,128]{1,0:T(8,128)S(1)} collective-permute-done((f32[256,128]{1,0:T(8,128)S(1)}, f32[256,128]{1,0:T(8,128)S(1)}, u32[]{:S(2)}, u32[]{:S(2)}) %collective-permute-start.39) | collective-permute-done | bytes 131104 | tf_op jit(solution)/shard_map/ppermute | solution.py:465
  167.9 2.1 %collective-permute-done.43 = f32[128,128]{1,0:T(8,128)S(1)} collective-permute-done((f32[128,128]{1,0:T(8,128)S(1)}, f32[128,128]{1,0:T(8,128)S(1)}, u32[]{:S(2)}, u32[]{:S(2)}) %collective-permute-start.43) | collective-permute-done | bytes 65568 | tf_op jit(solution)/shard_map/ppermute | solution.py:419
  178.0 2.2 %collective-permute-done.45.refs_5_ = f32[128,128]{1,0:T(8,128)S(1)} collective-permute-done((f32[128,128]{1,0:T(8,128)S(1)}, f32[128,128]{1,0:T(8,128)S(1)}, u32[]{:S(2)}, u32[]{:S(2)}) %collective-permute-start.45) | collective-permute-done | bytes 65568 | tf_op jit(solution)/shard_map/ppermute | solution.py:419
  182.0 2.9 %shard_map.61 = (f32[256,256]{1,0:T(8,128)S(1)}, f32[256,128]{1,0:T(8,128)}, f32[256,256]{1,0:T(8,128)S(1)}) custom-call(s32[3]{0:T(128)S(1)} %pad_add_fusion.info_ref.refs_0_, f32[128,128]{1,0:T(8,128)S(1)} %shard_map.57.refs_0_, f32[320,256]{1,0:T(8,128)S(1)} %collective-permute-done.37.even_ref.refs_1_, ...), custom_call_target="tpu_custom_call" | custom-call | flops 805306368 | bytes 1048576 | tf_op jit(solution)/shard_map/pallas_call | solution.py:79
  184.9 4.1 %shard_map.63 = (f32[8,384,256]{2,1,0:T(8,128)}, f32[2,64,256]{2,1,0:T(8,128)}, f32[1,256]{1,0:T(1,128)}) custom-call(s32[3]{0:T(128)S(1)} %pad_add_fusion.info_ref.refs_0_, f32[256,256]{1,0:T(8,128)S(1)} %get-tuple-element.98.weights_ref, f32[256,256]{1,0:T(8,128)S(1)} %get-tuple-element.99.gram_ref, f32[4,400,128]{2,1,0:T(8,128)S(1)} %get-tuple-element.95.up0_ref.refs_1_, ...), custom_call_target="tpu_custom_call" | custom-call | flops 1258291200 | bytes 6553600 | tf_op jit(solution)/shard_map/pallas_call | solution.py:398
  (104 shorter events, 65.5 us)
Async XLA Ops:
  3.8 20.7 %collective-permute-start = (f32[2,2,384,128]{3,2,1,0:T(8,128)S(1)}, f32[2,2,384,128]{3,2,1,0:T(8,128)S(1)}, u32[]{:S(2)}, u32[]{:S(2)}) collective-permute-start(f32[2,2,384,128]{3,2,1,0:T(8,128)S(1)} %get-tuple-element.56), channel_id=1, source_target_pairs={{0,32},{16,48},{32,64},{48,80},{64,96},{80,112},{96,0},{112,16},{1... | collective-permute-start | bytes 2359304 | tf_op jit(solution)/shard_map/ppermute | solution.py:452
  6.0 36.4 %collective-permute-start.1 = (f32[2,2,384,128]{3,2,1,0:T(8,128)S(1)}, f32[2,2,384,128]{3,2,1,0:T(8,128)S(1)}, u32[]{:S(2)}, u32[]{:S(2)}) collective-permute-start(f32[2,2,384,128]{3,2,1,0:T(8,128)S(1)} %get-tuple-element.57), channel_id=1, source_target_pairs={{0,64},{16,80},{32,96},{48,112},{64,0},{80,16},{96,32},{112,48},{1... | collective-permute-start | bytes 2359304 | tf_op jit(solution)/shard_map/ppermute | solution.py:452
  8.6 33.8 %collective-permute-start.2 = (f32[2,2,384,128]{3,2,1,0:T(8,128)S(1)}, f32[2,2,384,128]{3,2,1,0:T(8,128)S(1)}, u32[]{:S(2)}, u32[]{:S(2)}) collective-permute-start(f32[2,2,384,128]{3,2,1,0:T(8,128)S(1)} %get-tuple-element.58), channel_id=1, source_target_pairs={{0,96},{16,112},{32,0},{48,16},{64,32},{80,48},{96,64},{112,80},{1... | collective-permute-start | bytes 2359304 | tf_op jit(solution)/shard_map/ppermute | solution.py:452
  46.7 20.9 %collective-permute-start.10 = (f32[2,384,128]{2,1,0:T(8,128)S(1)}, f32[2,384,128]{2,1,0:T(8,128)S(1)}, u32[]{:S(2)}, u32[]{:S(2)}) collective-permute-start(f32[2,384,128]{2,1,0:T(8,128)S(1)} %get-tuple-element.61), channel_id=1, source_target_pairs={{0,32},{16,48},{32,64},{48,80},{64,96},{80,112},{96,0},{112,16},{1... | collective-permute-start | bytes 1179656 | tf_op jit(solution)/shard_map/ppermute | solution.py:456
  47.7 6.5 %collective-permute-start.6 = (f32[264,128]{1,0:T(8,128)S(1)}, f32[264,128]{1,0:T(8,128)S(1)}, u32[]{:S(2)}, u32[]{:S(2)}) collective-permute-start(f32[264,128]{1,0:T(8,128)S(1)} %add.49.refs_0_), channel_id=1, source_target_pairs={{0,3},{1,0},{2,1},{3,2},{4,7},{5,4},{6,5},{7,6},{8,11},{9,8},{10,9... | collective-permute-start | bytes 405512 | tf_op jit(solution)/shard_map/ppermute | solution.py:419
  50.3 18.0 %collective-permute-start.11 = (f32[2,384,128]{2,1,0:T(8,128)S(1)}, f32[2,384,128]{2,1,0:T(8,128)S(1)}, u32[]{:S(2)}, u32[]{:S(2)}) collective-permute-start(f32[2,384,128]{2,1,0:T(8,128)S(1)} %get-tuple-element.62), channel_id=1, source_target_pairs={{0,64},{16,80},{32,96},{48,112},{64,0},{80,16},{96,32},{112,48},{1... | collective-permute-start | bytes 1179656 | tf_op jit(solution)/shard_map/ppermute | solution.py:456
  52.4 17.3 %collective-permute-start.12 = (f32[2,384,128]{2,1,0:T(8,128)S(1)}, f32[2,384,128]{2,1,0:T(8,128)S(1)}, u32[]{:S(2)}, u32[]{:S(2)}) collective-permute-start(f32[2,384,128]{2,1,0:T(8,128)S(1)} %get-tuple-element.63), channel_id=1, source_target_pairs={{0,96},{16,112},{32,0},{48,16},{64,32},{80,48},{96,64},{112,80},{1... | collective-permute-start | bytes 1179656 | tf_op jit(solution)/shard_map/ppermute | solution.py:456
  53.7 5.5 %collective-permute-start.5 = (f32[264,128]{1,0:T(8,128)S(1)}, f32[264,128]{1,0:T(8,128)S(1)}, u32[]{:S(2)}, u32[]{:S(2)}) collective-permute-start(f32[264,128]{1,0:T(8,128)S(1)} %add.49.refs_0_), channel_id=1, source_target_pairs={{0,2},{1,3},{2,0},{3,1},{4,6},{5,7},{6,4},{7,5},{8,10},{9,11},{10,... | collective-permute-start | bytes 405512 | tf_op jit(solution)/shard_map/ppermute | solution.py:419
  54.2 9.0 %collective-permute-start.4 = (f32[264,128]{1,0:T(8,128)S(1)}, f32[264,128]{1,0:T(8,128)S(1)}, u32[]{:S(2)}, u32[]{:S(2)}) collective-permute-start(f32[264,128]{1,0:T(8,128)S(1)} %add.49.refs_0_), channel_id=1, source_target_pairs={{0,1},{1,2},{2,3},{3,0},{4,5},{5,6},{6,7},{7,4},{8,9},{9,10},{10,1... | collective-permute-start | bytes 405512 | tf_op jit(solution)/shard_map/ppermute | solution.py:419
  63.8 9.5 %collective-permute-start.9 = (f32[264,128]{1,0:T(8,128)S(1)}, f32[264,128]{1,0:T(8,128)S(1)}, u32[]{:S(2)}, u32[]{:S(2)}) collective-permute-start(f32[264,128]{1,0:T(8,128)S(1)} %shard_map.40.refs_1_), channel_id=1, source_target_pairs={{0,12},{1,13},{2,14},{3,15},{4,0},{5,1},{6,2},{7,3},{8,4},{9,5},{1... | collective-permute-start | bytes 405512 | tf_op jit(solution)/shard_map/ppermute | solution.py:419
  67.6 5.7 %collective-permute-start.8 = (f32[264,128]{1,0:T(8,128)S(1)}, f32[264,128]{1,0:T(8,128)S(1)}, u32[]{:S(2)}, u32[]{:S(2)}) collective-permute-start(f32[264,128]{1,0:T(8,128)S(1)} %shard_map.40.refs_1_), channel_id=1, source_target_pairs={{0,8},{1,9},{2,10},{3,11},{4,12},{5,13},{6,14},{7,15},{8,0},{9,1},... | collective-permute-start | bytes 405512 | tf_op jit(solution)/shard_map/ppermute | solution.py:419
  67.6 9.3 %collective-permute-start.7 = (f32[264,128]{1,0:T(8,128)S(1)}, f32[264,128]{1,0:T(8,128)S(1)}, u32[]{:S(2)}, u32[]{:S(2)}) collective-permute-start(f32[264,128]{1,0:T(8,128)S(1)} %shard_map.40.refs_1_), channel_id=1, source_target_pairs={{0,4},{1,5},{2,6},{3,7},{4,8},{5,9},{6,10},{7,11},{8,12},{9,13},{1... | collective-permute-start | bytes 405512 | tf_op jit(solution)/shard_map/ppermute | solution.py:419
  79.9 5.3 %collective-permute-start.14 = (f32[320,256]{1,0:T(8,128)S(1)}, f32[320,256]{1,0:T(8,128)S(1)}, u32[]{:S(2)}, u32[]{:S(2)}) collective-permute-start(f32[320,256]{1,0:T(8,128)S(1)} %get-tuple-element.65.weights_ref.own_ref), channel_id=1, source_target_pairs={{0,16},{16,0},{32,48},{48,32},{64,80},{80,64},{96,112},{112,96},{1... | collective-permute-start | bytes 983048 | tf_op jit(solution)/shard_map/ppermute | solution.py:415
  80.9 10.3 %collective-permute-start.13 = (f32[320,256]{1,0:T(8,128)S(1)}, f32[320,256]{1,0:T(8,128)S(1)}, u32[]{:S(2)}, u32[]{:S(2)}) collective-permute-start(f32[320,256]{1,0:T(8,128)S(1)} %get-tuple-element.65.weights_ref.own_ref), channel_id=1, source_target_pairs={{16,32},{48,64},{80,96},{112,0},{17,33},{49,65},{81,97},{113,1},{1... | collective-permute-start | bytes 983048 | tf_op jit(solution)/shard_map/ppermute | solution.py:466
  83.0 8.2 %collective-permute-start.15 = (f32[256,128]{1,0:T(8,128)S(1)}, f32[256,128]{1,0:T(8,128)S(1)}, u32[]{:S(2)}, u32[]{:S(2)}) collective-permute-start(f32[256,128]{1,0:T(8,128)S(1)} %get-tuple-element.66), channel_id=1, source_target_pairs={{16,48},{48,80},{80,112},{112,16},{17,49},{49,81},{81,113},{113,17... | collective-permute-start | bytes 393224 | tf_op jit(solution)/shard_map/ppermute | solution.py:465
  91.8 21.0 %collective-permute-start.24 = (f32[4,400,128]{2,1,0:T(8,128)S(1)}, f32[4,400,128]{2,1,0:T(8,128)S(1)}, u32[]{:S(2)}, u32[]{:S(2)}) collective-permute-start(f32[4,400,128]{2,1,0:T(8,128)S(1)} %get-tuple-element.74), channel_id=1, source_target_pairs={{0,32},{16,48},{32,64},{48,80},{64,96},{80,112},{96,0},{112,16},{1... | collective-permute-start | bytes 2457608 | tf_op jit(solution)/shard_map/ppermute | solution.py:479
  95.3 5.1 %collective-permute-start.18 = (f32[128,128]{1,0:T(8,128)S(1)}, f32[128,128]{1,0:T(8,128)S(1)}, u32[]{:S(2)}, u32[]{:S(2)}) collective-permute-start(f32[128,128]{1,0:T(8,128)S(1)} %add.50), channel_id=1, source_target_pairs={{0,2},{1,3},{2,0},{3,1},{4,6},{5,7},{6,4},{7,5},{8,10},{9,11},{10,... | collective-permute-start | bytes 196616 | tf_op jit(solution)/shard_map/ppermute | solution.py:419
  95.6 6.5 %collective-permute-start.17 = (f32[128,128]{1,0:T(8,128)S(1)}, f32[128,128]{1,0:T(8,128)S(1)}, u32[]{:S(2)}, u32[]{:S(2)}) collective-permute-start(f32[128,128]{1,0:T(8,128)S(1)} %add.50), channel_id=1, source_target_pairs={{0,1},{1,2},{2,3},{3,0},{4,5},{5,6},{6,7},{7,4},{8,9},{9,10},{10,1... | collective-permute-start | bytes 196616 | tf_op jit(solution)/shard_map/ppermute | solution.py:419
  97.3 7.3 %collective-permute-start.23 = (f32[256,128]{1,0:T(8,128)S(1)}, f32[256,128]{1,0:T(8,128)S(1)}, u32[]{:S(2)}, u32[]{:S(2)}) collective-permute-start(f32[256,128]{1,0:T(8,128)S(1)} %shard_map.47), channel_id=1, source_target_pairs={{0,16},{32,48},{64,80},{96,112},{1,17},{33,49},{65,81},{97,113},{2... | collective-permute-start | bytes 393224 | tf_op jit(solution)/shard_map/ppermute | solution.py:438
  102.9 5.6 %collective-permute-start.20 = (f32[128,128]{1,0:T(8,128)S(1)}, f32[128,128]{1,0:T(8,128)S(1)}, u32[]{:S(2)}, u32[]{:S(2)}) collective-permute-start(f32[128,128]{1,0:T(8,128)S(1)} %add_add_fusion.2.refs_4_), channel_id=1, source_target_pairs={{0,4},{1,5},{2,6},{3,7},{4,8},{5,9},{6,10},{7,11},{8,12},{9,13},{1... | collective-permute-start | bytes 196616 | tf_op jit(solution)/shard_map/ppermute | solution.py:419
  115.9 10.4 %collective-permute-start.25 = (f32[320,256]{1,0:T(8,128)S(1)}, f32[320,256]{1,0:T(8,128)S(1)}, u32[]{:S(2)}, u32[]{:S(2)}) collective-permute-start(f32[320,256]{1,0:T(8,128)S(1)} %get-tuple-element.76.weights_ref.own_ref), channel_id=1, source_target_pairs={{16,32},{48,64},{80,96},{112,0},{17,33},{49,65},{81,97},{113,1},{1... | collective-permute-start | bytes 983048 | tf_op jit(solution)/shard_map/ppermute | solution.py:466
  117.2 9.1 %collective-permute-start.27 = (f32[256,128]{1,0:T(8,128)S(1)}, f32[256,128]{1,0:T(8,128)S(1)}, u32[]{:S(2)}, u32[]{:S(2)}) collective-permute-start(f32[256,128]{1,0:T(8,128)S(1)} %get-tuple-element.77), channel_id=1, source_target_pairs={{16,48},{48,80},{80,112},{112,16},{17,49},{49,81},{81,113},{113,17... | collective-permute-start | bytes 393224 | tf_op jit(solution)/shard_map/ppermute | solution.py:465
  127.0 21.0 %collective-permute-start.36 = (f32[4,400,128]{2,1,0:T(8,128)S(1)}, f32[4,400,128]{2,1,0:T(8,128)S(1)}, u32[]{:S(2)}, u32[]{:S(2)}) collective-permute-start(f32[4,400,128]{2,1,0:T(8,128)S(1)} %get-tuple-element.86), channel_id=1, source_target_pairs={{0,32},{16,48},{32,64},{48,80},{64,96},{80,112},{96,0},{112,16},{1... | collective-permute-start | bytes 2457608 | tf_op jit(solution)/shard_map/ppermute | solution.py:479
  130.6 6.5 %collective-permute-start.29 = (f32[128,128]{1,0:T(8,128)S(1)}, f32[128,128]{1,0:T(8,128)S(1)}, u32[]{:S(2)}, u32[]{:S(2)}) collective-permute-start(f32[128,128]{1,0:T(8,128)S(1)} %add.54), channel_id=1, source_target_pairs={{0,1},{1,2},{2,3},{3,0},{4,5},{5,6},{6,7},{7,4},{8,9},{9,10},{10,1... | collective-permute-start | bytes 196616 | tf_op jit(solution)/shard_map/ppermute | solution.py:419
  132.3 7.3 %collective-permute-start.35 = (f32[256,128]{1,0:T(8,128)S(1)}, f32[256,128]{1,0:T(8,128)S(1)}, u32[]{:S(2)}, u32[]{:S(2)}) collective-permute-start(f32[256,128]{1,0:T(8,128)S(1)} %shard_map.54), channel_id=1, source_target_pairs={{0,16},{32,48},{64,80},{96,112},{1,17},{33,49},{65,81},{97,113},{2... | collective-permute-start | bytes 393224 | tf_op jit(solution)/shard_map/ppermute | solution.py:438
  137.8 5.6 %collective-permute-start.32 = (f32[128,128]{1,0:T(8,128)S(1)}, f32[128,128]{1,0:T(8,128)S(1)}, u32[]{:S(2)}, u32[]{:S(2)}) collective-permute-start(f32[128,128]{1,0:T(8,128)S(1)} %add_add_fusion.1.refs_4_), channel_id=1, source_target_pairs={{0,4},{1,5},{2,6},{3,7},{4,8},{5,9},{6,10},{7,11},{8,12},{9,13},{1... | collective-permute-start | bytes 196616 | tf_op jit(solution)/shard_map/ppermute | solution.py:419
  151.3 10.4 %collective-permute-start.37 = (f32[320,256]{1,0:T(8,128)S(1)}, f32[320,256]{1,0:T(8,128)S(1)}, u32[]{:S(2)}, u32[]{:S(2)}) collective-permute-start(f32[320,256]{1,0:T(8,128)S(1)} %get-tuple-element.88.weights_ref.own_ref), channel_id=1, source_target_pairs={{16,32},{48,64},{80,96},{112,0},{17,33},{49,65},{81,97},{113,1},{1... | collective-permute-start | bytes 983048 | tf_op jit(solution)/shard_map/ppermute | solution.py:466
  152.6 9.1 %collective-permute-start.39 = (f32[256,128]{1,0:T(8,128)S(1)}, f32[256,128]{1,0:T(8,128)S(1)}, u32[]{:S(2)}, u32[]{:S(2)}) collective-permute-start(f32[256,128]{1,0:T(8,128)S(1)} %get-tuple-element.89), channel_id=1, source_target_pairs={{16,48},{48,80},{80,112},{112,16},{17,49},{49,81},{81,113},{113,17... | collective-permute-start | bytes 393224 | tf_op jit(solution)/shard_map/ppermute | solution.py:465
  166.7 6.5 %collective-permute-start.41 = (f32[128,128]{1,0:T(8,128)S(1)}, f32[128,128]{1,0:T(8,128)S(1)}, u32[]{:S(2)}, u32[]{:S(2)}) collective-permute-start(f32[128,128]{1,0:T(8,128)S(1)} %add.58), channel_id=1, source_target_pairs={{0,1},{1,2},{2,3},{3,0},{4,5},{5,6},{6,7},{7,4},{8,9},{9,10},{10,1... | collective-permute-start | bytes 196616 | tf_op jit(solution)/shard_map/ppermute | solution.py:419
  174.0 10.9 %collective-permute-start.47 = (f32[4,400,128]{2,1,0:T(8,128)S(1)}, f32[4,400,128]{2,1,0:T(8,128)S(1)}, u32[]{:S(2)}, u32[]{:S(2)}) collective-permute-start(f32[4,400,128]{2,1,0:T(8,128)S(1)} %get-tuple-element.102), channel_id=1, source_target_pairs={{0,16},{16,0},{32,48},{48,32},{64,80},{80,64},{96,112},{112,96},{1... | collective-permute-start | bytes 2457608 | tf_op jit(solution)/shard_map/ppermute | solution.py:415
  174.8 10.1 %collective-permute-start.48 = (f32[4,400,128]{2,1,0:T(8,128)S(1)}, f32[4,400,128]{2,1,0:T(8,128)S(1)}, u32[]{:S(2)}, u32[]{:S(2)}) collective-permute-start(f32[4,400,128]{2,1,0:T(8,128)S(1)} %get-tuple-element.103), channel_id=1, source_target_pairs={{0,16},{16,0},{32,48},{48,32},{64,80},{80,64},{96,112},{112,96},{1... | collective-permute-start | bytes 2457608 | tf_op jit(solution)/shard_map/ppermute | solution.py:415
  175.5 6.5 %collective-permute-start.44 = (f32[128,128]{1,0:T(8,128)S(1)}, f32[128,128]{1,0:T(8,128)S(1)}, u32[]{:S(2)}, u32[]{:S(2)}) collective-permute-start(f32[128,128]{1,0:T(8,128)S(1)} %add_add_fusion.refs_3_.refs_5_), channel_id=1, source_target_pairs={{0,4},{1,5},{2,6},{3,7},{4,8},{5,9},{6,10},{7,11},{8,12},{9,13},{1... | collective-permute-start | bytes 196616 | tf_op jit(solution)/shard_map/ppermute | solution.py:419
  (19 other events, 104.5 us)

commit v9 on v8

--- a/solution.py
+++ b/solution.py
@@ -15,6 +15,7 @@
 COLS = 8
 F32 = jnp.float32
 BF16 = jnp.bfloat16
+AHEAD_COST = 180
 VMEM_LIMIT = 16 * 1024 * 1024
 
 TURN_CORE = [(c, c ^ 1) for c in range(COLS)]
@@ -97,27 +98,32 @@
     return pl.BlockSpec(dims, lambda *_: (0,) * len(dims))
 
 
-def pack_main_kernel(info_ref, *refs):
-    for x_ref, out_ref in zip(refs[:SIDE], refs[SIDE:]):
-        out_ref[0, 0] = x_ref[:, :BLOCK]
-        out_ref[0, 1] = x_ref[:, BLOCK:]
+def pack_main_kernel(info_ref, x_ref, *refs):
+    outs, sems = refs[:SIDE], refs[SIDE]
+    copies = []
+    for k, out_ref in enumerate(outs):
+        first = lax.rem(info_ref[1] + k, SIDE) * 2 * PAIR
+        for j in range(4):
+            at = pl.multiple_of(first + j * BLOCK, BLOCK)
+            target = out_ref.at[j // 2, j % 2]
+            copies.append(pltpu.make_async_copy(x_ref.at[:, pl.ds(at, BLOCK)], target, sems.at[4 * k + j]))
+    for copy in copies:
+        copy.start()
+    for copy in copies:
+        copy.wait()
 
 
 def pack_main(info, x):
     rows = x.shape[0]
-
-    def columns(k):
-        return pl.BlockSpec((rows, PAIR), lambda j, c: (0, 2 * ((c[1] + k) % SIDE) + j))
-
-    return call(
+    return pl.pallas_call(
         pack_main_kernel,
-        (2,),
-        [columns(k) for k in range(SIDE)],
-        [pl.BlockSpec((1, 2, rows, BLOCK), lambda j, c: (j, 0, 0, 0))] * SIDE,
-        [shape(2, 2, rows, BLOCK)] * SIDE,
-        scalars=1,
-        nbytes=8 * SIDE * rows * 2 * PAIR,
-    )(info, *[x] * SIDE)
+        in_specs=[pl.BlockSpec(memory_space=pltpu.SMEM), pl.BlockSpec(memory_space=pl.ANY)],
+        out_specs=[pl.BlockSpec(memory_space=pltpu.VMEM)] * SIDE,
+        out_shape=[shape(2, 2, rows, BLOCK)] * SIDE,
+        scratch_shapes=[pltpu.SemaphoreType.DMA((4 * SIDE,))],
+        compiler_params=pltpu.CompilerParams(vmem_limit_bytes=VMEM_LIMIT),
+        cost_estimate=pl.CostEstimate(flops=0, bytes_accessed=8 * SIDE * rows * 2 * PAIR, transcendentals=0),
+    )(info, x)
 
 
 def pack_ahead_kernel(info_ref, *refs):
@@ -322,9 +328,9 @@
     )
 
 
-def ahead_kernel(rows, step, info_ref, lower_ref, cross_ref, up0_ref, *refs):
+def ahead_kernel(rows, step, info_ref, even_ref, odd_ref, cross_ref, up0_ref, *refs):
     low0_ref, keep_ref, send_ref = refs[-3:]
-    weights = lower_ref[...]
+    weights = even_ref[:PAIR, BLOCK:] + odd_ref[...]
     slot = (2 * info_ref[1] + COLS - 1) % COLS
     total = jnp.zeros((BLOCK, BLOCK), F32)
     for group, (pair,) in groups_of(info_ref, step, refs[:-3], (slot,)):
@@ -336,12 +342,12 @@
     send_ref[...] = jnp.where(first, cross_ref[...], total)
 
 
-def rotate_ahead(info, lower, cross, up0, blocks, rows, step):
+def rotate_ahead(info, even, odd, cross, up0, blocks, rows, step):
     return call_whole(
         functools.partial(ahead_kernel, rows, step),
-        (info, lower, cross, up0, *blocks),
+        (info, even, odd, cross, up0, *blocks),
         [shape(SIDE, step, BLOCK), shape(BLOCK, BLOCK), shape(BLOCK, BLOCK)],
-        flops=2 * 3 * SIDE * step * 2 * BLOCK * PAIR,
+        flops=AHEAD_COST * SIDE * step * BLOCK * PAIR,
         nbytes=4 * 4 * SIDE * step * BLOCK,
     )
 
@@ -419,16 +425,6 @@
     return [lax.ppermute(value, "rows", pairs) for pairs in shifts]
 
 
-def lower_kernel(info_ref, even_ref, odd_ref, low1_ref, lower_ref, pass_ref):
-    lower_ref[...] = even_ref[:PAIR, BLOCK:] + odd_ref[...]
-    pass_ref[...] = low1_ref[...]
-
-
-def lower_before(info, even, odd, low1):
-    out = [shape(PAIR, BLOCK), shape(*low1.shape)]
-    return call_whole(lower_kernel, (info, even, odd, low1), out, nbytes=8 * (low1.size + PAIR * BLOCK))
-
-
 def upper_kernel(info_ref, value_ref, out_ref):
     out_ref[...] = value_ref[:PAIR, :BLOCK]
 
@@ -467,8 +463,7 @@
         other = swap_core(weights)
         up = project(info, gram, weights)
         up0, up1, low1, cross = rotate_own(info, weights, other, own_blocks, rows, step)
-        lower, passed = lower_before(info, even, odd, low1)
-        low0, keep, send = rotate_ahead(info, lower, cross, up0, ahead_blocks, rows, step)
+        low0, keep, send = rotate_ahead(info, even, odd, cross, up0, ahead_blocks, rows, step)
         value = keep + swap_core(send)
         value = value + sum(along(value, ALONG_X))
         own_blocks = [up0, low0, up1, low1]
@@ -476,7 +471,7 @@
             other_blocks = [swap_core(block) for block in other_slot(info, own_blocks, [value])]
         else:
             up_m = rotate_up(info, [even, relayed_upper(info, even, [keep])], ahead_blocks, step)
-            ahead_blocks = [up_m, lax.ppermute(passed, "cols", CHIPS_ON[1])]
+            ahead_blocks = [up_m, lax.ppermute(low1, "cols", CHIPS_ON[1])]
         before = [] if last else ahead_blocks
         weights, lower, gram = cayley(info, up, even, other, [value] + along(value, ALONG_Z), before, last)
 

time: 190 us -> 185 us (0.974)
  waiting for transfers between devices: 96.7 us -> 87.8 us
  starting transfers between devices: 46 us -> 53.6 us
  Pallas kernels: 43.3 us -> 40.6 us
    ppermute x2, waiting for transfers between devices: 8.89 us -> 0.01 us  [body(): ahead_blocks = [up_m, lax.ppermute(low1, 'cols', CHIPS_ON[1])]]
    ppermute x9, starting transfers between devices: 4.62 us -> 8.38 us  [swap_core(): return lax.ppermute(value, 'cols', TURN_CORE)]
    pallas_call x23 -> x20, Pallas kernels: 37.3 us -> 34.6 us  [call_whole(): pl.pallas_call(inner, in_specs=[pl.BlockSpec(memory_space=pltpu.SMEM)] +...]
  transfers between devices with their start and end apart: 49 -> 49, of which waited for: 31 -> 28; matrix products, arithmetic and copies ran while one was open for 0% -> 0% of each run, Pallas kernels for 12% -> 12%
where the time goes in v9:
time: 185 us
  waiting for transfers between devices  87.8 us (47%)
  starting transfers between devices  53.6 us (29%)
  Pallas kernels  40.6 us (22%)
  local copies, waits for them, and re-layouts  1.89 us (1%)
    ppermute x24, waiting for transfers between devices, along(): return [lax.ppermute(value, 'rows', pairs) for pairs in shifts]  37.1 us
    pallas_call x20, Pallas kernels, call_whole(): pl.pallas_call(inner, in_specs=[pl.BlockSpec(memory_space=pltpu.SMEM)] +...  34.6 us
    ppermute x6, waiting for transfers between devices, body(): lax.ppermute(packed[k], 'cols', CHIPS_ON[k])  34.1 us
    ppermute x24, starting transfers between devices, along(): return [lax.ppermute(value, 'rows', pairs) for pairs in shifts]  19.2 us
    ppermute x3, waiting for transfers between devices, body(): odd = lax.ppermute(lower, 'cols', ODD_TO_ODD)  12.8 us
    ppermute x6, starting transfers between devices, body(): lax.ppermute(packed[k], 'cols', CHIPS_ON[k])  10.3 us
    ppermute x9, starting transfers between devices, swap_core(): return lax.ppermute(value, 'cols', TURN_CORE)  8.38 us
    ppermute x3, starting transfers between devices, body(): odd = lax.ppermute(lower, 'cols', ODD_TO_ODD)  6.37 us
  transfers between devices with their start and end apart: 49, of which 28 were waited for; matrix products, arithmetic and copies ran while one was open for 0% of the time, Pallas kernels for 12%

profile of v9, /device:TPU:1, one launch (start us, length us, event | category | flops | bytes accessed | tf_op | source)
XLA Modules:
  0.0 185.0 jit_solution(18430171338193984415)
XLA Ops:
  3.8 2.2 %collective-permute-start = (f32[2,2,384,128]{3,2,1,0:T(8,128)S(1)}, f32[2,2,384,128]{3,2,1,0:T(8,128)S(1)}, u32[]{:S(2)}, u32[]{:S(2)}) collective-permute-start(f32[2,2,384,128]{3,2,1,0:T(8,128)S(1)} %get-tuple-element.51), channel_id=1, source_target_pairs={{0,32},{16,48},{32,64},{48,80},{64,96},{80,112},{96,0},{112,16},{1... | collective-permute-start | bytes 2359304 | tf_op jit(solution)/shard_map/ppermute | solution.py:448
  6.0 2.6 %collective-permute-start.1 = (f32[2,2,384,128]{3,2,1,0:T(8,128)S(1)}, f32[2,2,384,128]{3,2,1,0:T(8,128)S(1)}, u32[]{:S(2)}, u32[]{:S(2)}) collective-permute-start(f32[2,2,384,128]{3,2,1,0:T(8,128)S(1)} %get-tuple-element.52), channel_id=1, source_target_pairs={{0,64},{16,80},{32,96},{48,112},{64,0},{80,16},{96,32},{112,48},{1... | collective-permute-start | bytes 2359304 | tf_op jit(solution)/shard_map/ppermute | solution.py:448
  9.7 14.9 %collective-permute-done.refs_1_.refs_4_ = f32[2,2,384,128]{3,2,1,0:T(8,128)S(1)} collective-permute-done((f32[2,2,384,128]{3,2,1,0:T(8,128)S(1)}, f32[2,2,384,128]{3,2,1,0:T(8,128)S(1)}, u32[]{:S(2)}, u32[]{:S(2)}) %collective-permute-start) | collective-permute-done | bytes 786464 | tf_op jit(solution)/shard_map/ppermute | solution.py:448
  24.5 17.9 %collective-permute-done.1.refs_2_.refs_5_ = f32[2,2,384,128]{3,2,1,0:T(8,128)S(1)} collective-permute-done((f32[2,2,384,128]{3,2,1,0:T(8,128)S(1)}, f32[2,2,384,128]{3,2,1,0:T(8,128)S(1)}, u32[]{:S(2)}, u32[]{:S(2)}) %collective-permute-start.1) | collective-permute-done | bytes 786464 | tf_op jit(solution)/shard_map/ppermute | solution.py:448
  42.4 1.9 %shard_map.39 = (f32[264,128]{1,0:T(8,128)S(1)}, f32[264,128]{1,0:T(8,128)S(1)}) custom-call(s32[3]{0:T(128)S(1)} %pad_add_fusion.info_ref.refs_0_, f32[2,2,384,128]{3,2,1,0:T(8,128)S(1)} %get-tuple-element.50.refs_0_, f32[2,2,384,128]{3,2,1,0:T(8,128)S(1)} %collective-permute-done.refs_1_.refs_4_, ...), custom_call_target="tpu_custom_call" | custom-call | flops 805306368 | bytes 3145728 | tf_op jit(solution)/shard_map/pallas_call | solution.py:80
  47.7 2.5 %collective-permute-start.6 = (f32[264,128]{1,0:T(8,128)S(1)}, f32[264,128]{1,0:T(8,128)S(1)}, u32[]{:S(2)}, u32[]{:S(2)}) collective-permute-start(f32[264,128]{1,0:T(8,128)S(1)} %add.49.refs_0_), channel_id=1, source_target_pairs={{0,3},{1,0},{2,1},{3,2},{4,7},{5,4},{6,5},{7,6},{8,11},{9,8},{10,9... | collective-permute-start | bytes 405512 | tf_op jit(solution)/shard_map/ppermute | solution.py:425
  50.3 2.1 %collective-permute-start.11 = (f32[2,384,128]{2,1,0:T(8,128)S(1)}, f32[2,384,128]{2,1,0:T(8,128)S(1)}, u32[]{:S(2)}, u32[]{:S(2)}) collective-permute-start(f32[2,384,128]{2,1,0:T(8,128)S(1)} %get-tuple-element.57), channel_id=1, source_target_pairs={{0,64},{16,80},{32,96},{48,112},{64,0},{80,16},{96,32},{112,48},{1... | collective-permute-start | bytes 1179656 | tf_op jit(solution)/shard_map/ppermute | solution.py:452
  54.8 4.3 %collective-permute-done.5.refs_2_ = f32[264,128]{1,0:T(8,128)S(1)} collective-permute-done((f32[264,128]{1,0:T(8,128)S(1)}, f32[264,128]{1,0:T(8,128)S(1)}, u32[]{:S(2)}, u32[]{:S(2)}) %collective-permute-start.5) | collective-permute-done | bytes 135200 | tf_op jit(solution)/shard_map/ppermute | solution.py:425
  59.2 4.0 %collective-permute-done.4.refs_1_ = f32[264,128]{1,0:T(8,128)S(1)} collective-permute-done((f32[264,128]{1,0:T(8,128)S(1)}, f32[264,128]{1,0:T(8,128)S(1)}, u32[]{:S(2)}, u32[]{:S(2)}) %collective-permute-start.4) | collective-permute-done | bytes 135200 | tf_op jit(solution)/shard_map/ppermute | solution.py:425
  63.8 3.8 %collective-permute-start.9 = (f32[264,128]{1,0:T(8,128)S(1)}, f32[264,128]{1,0:T(8,128)S(1)}, u32[]{:S(2)}, u32[]{:S(2)}) collective-permute-start(f32[264,128]{1,0:T(8,128)S(1)} %shard_map.40.refs_1_), channel_id=1, source_target_pairs={{0,12},{1,13},{2,14},{3,15},{4,0},{5,1},{6,2},{7,3},{8,4},{9,5},{1... | collective-permute-start | bytes 405512 | tf_op jit(solution)/shard_map/ppermute | solution.py:425
  69.7 3.6 %collective-permute-done.9.refs_4_ = f32[264,128]{1,0:T(8,128)S(1)} collective-permute-done((f32[264,128]{1,0:T(8,128)S(1)}, f32[264,128]{1,0:T(8,128)S(1)}, u32[]{:S(2)}, u32[]{:S(2)}) %collective-permute-start.9) | collective-permute-done | bytes 135200 | tf_op jit(solution)/shard_map/ppermute | solution.py:425
  73.2 3.6 %collective-permute-done.7.refs_2_ = f32[264,128]{1,0:T(8,128)S(1)} collective-permute-done((f32[264,128]{1,0:T(8,128)S(1)}, f32[264,128]{1,0:T(8,128)S(1)}, u32[]{:S(2)}, u32[]{:S(2)}) %collective-permute-start.7) | collective-permute-done | bytes 135200 | tf_op jit(solution)/shard_map/ppermute | solution.py:425
  76.8 3.1 %shard_map.42 = (f32[320,256]{1,0:T(8,128)S(1)}, f32[256,128]{1,0:T(8,128)S(1)}, f32[256,256]{1,0:T(8,128)S(1)}) custom-call(s32[3]{0:T(128)S(1)} %pad_add_fusion.info_ref.refs_0_, f32[264,128]{1,0:T(8,128)S(1)} %shard_map.40.refs_1_, f32[264,128]{1,0:T(8,128)S(1)} %collective-permute-done.7.refs_2_, f32[264,128]{1,0:T(8,128)S(1)} %collective-permute-done.8.refs_3_, ...), custom_call_target="tpu_custom_call" | custom-call | flops 805306368 | bytes 1048576 | tf_op jit(solution)/shard_map/pallas_call | solution.py:80
  80.8 2.1 %collective-permute-start.13 = (f32[320,256]{1,0:T(8,128)S(1)}, f32[320,256]{1,0:T(8,128)S(1)}, u32[]{:S(2)}, u32[]{:S(2)}) collective-permute-start(f32[320,256]{1,0:T(8,128)S(1)} %get-tuple-element.60.weights_ref.own_ref), channel_id=1, source_target_pairs={{16,32},{48,64},{80,96},{112,0},{17,33},{49,65},{81,97},{113,1},{1... | collective-permute-start | bytes 983048 | tf_op jit(solution)/shard_map/ppermute | solution.py:462
  82.9 2.3 %collective-permute-start.15 = (f32[256,128]{1,0:T(8,128)S(1)}, f32[256,128]{1,0:T(8,128)S(1)}, u32[]{:S(2)}, u32[]{:S(2)}) collective-permute-start(f32[256,128]{1,0:T(8,128)S(1)} %get-tuple-element.61), channel_id=1, source_target_pairs={{16,48},{48,80},{80,112},{112,16},{17,49},{49,81},{81,113},{113,17... | collective-permute-start | bytes 393224 | tf_op jit(solution)/shard_map/ppermute | solution.py:461
  85.2 2.8 %shard_map.44 = (f32[4,400,128]{2,1,0:T(8,128)S(1)}, f32[4,400,128]{2,1,0:T(8,128)S(1)}, f32[4,400,128]{2,1,0:T(8,128)S(1)}, f32[128,128]{1,0:T(8,128)S(1)}) custom-call(s32[3]{0:T(128)S(1)} %pad_add_fusion.info_ref.refs_0_, f32[320,256]{1,0:T(8,128)S(1)} %get-tuple-element.60.weights_ref.own_ref, f32[320,256]{1,0:T(8,128)S(1)} %collective-permute-done.14.other_ref.refs_3_, ...), custom_call_target="tpu_custom_call" | custom-call | flops 1258291200 | bytes 5734400 | tf_op jit(solution)/shard_map/pallas_call | solution.py:80
  88.3 4.5 %collective-permute-done.15.odd_ref = f32[256,128]{1,0:T(8,128)S(1)} collective-permute-done((f32[256,128]{1,0:T(8,128)S(1)}, f32[256,128]{1,0:T(8,128)S(1)}, u32[]{:S(2)}, u32[]{:S(2)}) %collective-permute-start.15) | collective-permute-done | bytes 131104 | tf_op jit(solution)/shard_map/ppermute | solution.py:461
  109.1 2.6 %shard_map.48 = (f32[320,256]{1,0:T(8,128)S(1)}, f32[256,128]{1,0:T(8,128)S(1)}, f32[256,256]{1,0:T(8,128)S(1)}) custom-call(s32[3]{0:T(128)S(1)} %pad_add_fusion.info_ref.refs_0_, f32[128,128]{1,0:T(8,128)S(1)} %shard_map.43.refs_1_, f32[320,256]{1,0:T(8,128)S(1)} %collective-permute-done.13.even_ref.refs_1_.refs_2_, ...), custom_call_target="tpu_custom_call" | custom-call | flops 805306368 | bytes 1048576 | tf_op jit(solution)/shard_map/pallas_call | solution.py:80
  111.7 2.3 %collective-permute-start.26 = (f32[320,256]{1,0:T(8,128)S(1)}, f32[320,256]{1,0:T(8,128)S(1)}, u32[]{:S(2)}, u32[]{:S(2)}) collective-permute-start(f32[320,256]{1,0:T(8,128)S(1)} %get-tuple-element.69.weights_ref.own_ref), channel_id=1, source_target_pairs={{0,16},{16,0},{32,48},{48,32},{64,80},{80,64},{96,112},{112,96},{1... | collective-permute-start | bytes 983048 | tf_op jit(solution)/shard_map/ppermute | solution.py:421
  115.4 2.2 %collective-permute-start.27 = (f32[256,128]{1,0:T(8,128)S(1)}, f32[256,128]{1,0:T(8,128)S(1)}, u32[]{:S(2)}, u32[]{:S(2)}) collective-permute-start(f32[256,128]{1,0:T(8,128)S(1)} %get-tuple-element.70), channel_id=1, source_target_pairs={{16,48},{48,80},{80,112},{112,16},{17,49},{49,81},{81,113},{113,17... | collective-permute-start | bytes 393224 | tf_op jit(solution)/shard_map/ppermute | solution.py:461
  117.6 2.8 %shard_map.50 = (f32[4,400,128]{2,1,0:T(8,128)S(1)}, f32[4,400,128]{2,1,0:T(8,128)S(1)}, f32[4,400,128]{2,1,0:T(8,128)S(1)}, f32[128,128]{1,0:T(8,128)S(1)}) custom-call(s32[3]{0:T(128)S(1)} %pad_add_fusion.info_ref.refs_0_, f32[320,256]{1,0:T(8,128)S(1)} %get-tuple-element.69.weights_ref.own_ref, f32[320,256]{1,0:T(8,128)S(1)} %collective-permute-done.26.other_ref.refs_3_, ...), custom_call_target="tpu_custom_call" | custom-call | flops 1258291200 | bytes 5734400 | tf_op jit(solution)/shard_map/pallas_call | solution.py:80
  122.0 4.1 %collective-permute-done.27.odd_ref = f32[256,128]{1,0:T(8,128)S(1)} collective-permute-done((f32[256,128]{1,0:T(8,128)S(1)}, f32[256,128]{1,0:T(8,128)S(1)}, u32[]{:S(2)}, u32[]{:S(2)}) %collective-permute-start.27) | collective-permute-done | bytes 131104 | tf_op jit(solution)/shard_map/ppermute | solution.py:461
  133.1 2.1 %collective-permute-done.30 = f32[128,128]{1,0:T(8,128)S(1)} collective-permute-done((f32[128,128]{1,0:T(8,128)S(1)}, f32[128,128]{1,0:T(8,128)S(1)}, u32[]{:S(2)}, u32[]{:S(2)}) %collective-permute-start.30) | collective-permute-done | bytes 65568 | tf_op jit(solution)/shard_map/ppermute | solution.py:425
  143.7 2.8 %shard_map.54 = (f32[320,256]{1,0:T(8,128)S(1)}, f32[256,128]{1,0:T(8,128)S(1)}, f32[256,256]{1,0:T(8,128)S(1)}) custom-call(s32[3]{0:T(128)S(1)} %pad_add_fusion.info_ref.refs_0_, f32[128,128]{1,0:T(8,128)S(1)} %shard_map.49.refs_1_, f32[320,256]{1,0:T(8,128)S(1)} %collective-permute-done.25.even_ref.refs_1_.refs_2_, ...), custom_call_target="tpu_custom_call" | custom-call | flops 805306368 | bytes 1048576 | tf_op jit(solution)/shard_map/pallas_call | solution.py:80
  146.5 2.4 %collective-permute-start.38 = (f32[320,256]{1,0:T(8,128)S(1)}, f32[320,256]{1,0:T(8,128)S(1)}, u32[]{:S(2)}, u32[]{:S(2)}) collective-permute-start(f32[320,256]{1,0:T(8,128)S(1)} %get-tuple-element.79.weights_ref.own_ref), channel_id=1, source_target_pairs={{0,16},{16,0},{32,48},{48,32},{64,80},{80,64},{96,112},{112,96},{1... | collective-permute-start | bytes 983048 | tf_op jit(solution)/shard_map/ppermute | solution.py:421
  152.2 2.8 %shard_map.56 = (f32[4,400,128]{2,1,0:T(8,128)S(1)}, f32[4,400,128]{2,1,0:T(8,128)S(1)}, f32[4,400,128]{2,1,0:T(8,128)S(1)}, f32[128,128]{1,0:T(8,128)S(1)}) custom-call(s32[3]{0:T(128)S(1)} %pad_add_fusion.info_ref.refs_0_, f32[320,256]{1,0:T(8,128)S(1)} %get-tuple-element.79.weights_ref.own_ref, f32[320,256]{1,0:T(8,128)S(1)} %collective-permute-done.38.other_ref.refs_2_, ...), custom_call_target="tpu_custom_call" | custom-call | flops 1258291200 | bytes 5734400 | tf_op jit(solution)/shard_map/pallas_call | solution.py:80
  155.0 4.3 %collective-permute-done.39.odd_ref = f32[256,128]{1,0:T(8,128)S(1)} collective-permute-done((f32[256,128]{1,0:T(8,128)S(1)}, f32[256,128]{1,0:T(8,128)S(1)}, u32[]{:S(2)}, u32[]{:S(2)}) %collective-permute-start.39) | collective-permute-done | bytes 131104 | tf_op jit(solution)/shard_map/ppermute | solution.py:461
  164.2 1.9 %collective-permute-done.43 = f32[128,128]{1,0:T(8,128)S(1)} collective-permute-done((f32[128,128]{1,0:T(8,128)S(1)}, f32[128,128]{1,0:T(8,128)S(1)}, u32[]{:S(2)}, u32[]{:S(2)}) %collective-permute-start.43) | collective-permute-done | bytes 65568 | tf_op jit(solution)/shard_map/ppermute | solution.py:425
  167.5 2.1 %collective-permute-done.41 = f32[128,128]{1,0:T(8,128)S(1)} collective-permute-done((f32[128,128]{1,0:T(8,128)S(1)}, f32[128,128]{1,0:T(8,128)S(1)}, u32[]{:S(2)}, u32[]{:S(2)}) %collective-permute-start.41) | collective-permute-done | bytes 65568 | tf_op jit(solution)/shard_map/ppermute | solution.py:425
  174.3 2.3 %collective-permute-done.45.refs_5_ = f32[128,128]{1,0:T(8,128)S(1)} collective-permute-done((f32[128,128]{1,0:T(8,128)S(1)}, f32[128,128]{1,0:T(8,128)S(1)}, u32[]{:S(2)}, u32[]{:S(2)}) %collective-permute-start.45) | collective-permute-done | bytes 65568 | tf_op jit(solution)/shard_map/ppermute | solution.py:425
  178.0 2.9 %shard_map.58 = (f32[256,256]{1,0:T(8,128)S(1)}, f32[256,128]{1,0:T(8,128)}, f32[256,256]{1,0:T(8,128)S(1)}) custom-call(s32[3]{0:T(128)S(1)} %pad_add_fusion.info_ref.refs_0_, f32[128,128]{1,0:T(8,128)S(1)} %shard_map.55.refs_0_, f32[320,256]{1,0:T(8,128)S(1)} %collective-permute-done.37.even_ref.refs_1_, ...), custom_call_target="tpu_custom_call" | custom-call | flops 805306368 | bytes 1048576 | tf_op jit(solution)/shard_map/pallas_call | solution.py:80
  180.9 4.1 %shard_map.60 = (f32[8,384,256]{2,1,0:T(8,128)}, f32[2,64,256]{2,1,0:T(8,128)}, f32[1,256]{1,0:T(1,128)}) custom-call(s32[3]{0:T(128)S(1)} %pad_add_fusion.info_ref.refs_0_, f32[256,256]{1,0:T(8,128)S(1)} %get-tuple-element.87.weights_ref, f32[256,256]{1,0:T(8,128)S(1)} %get-tuple-element.88.gram_ref, f32[4,400,128]{2,1,0:T(8,128)S(1)} %get-tuple-element.84.up0_ref.refs_1_, ...), custom_call_target="tpu_custom_call" | custom-call | flops 1258291200 | bytes 6553600 | tf_op jit(solution)/shard_map/pallas_call | solution.py:404
  (101 shorter events, 64.2 us)
Async XLA Ops:
  3.8 20.7 %collective-permute-start = (f32[2,2,384,128]{3,2,1,0:T(8,128)S(1)}, f32[2,2,384,128]{3,2,1,0:T(8,128)S(1)}, u32[]{:S(2)}, u32[]{:S(2)}) collective-permute-start(f32[2,2,384,128]{3,2,1,0:T(8,128)S(1)} %get-tuple-element.51), channel_id=1, source_target_pairs={{0,32},{16,48},{32,64},{48,80},{64,96},{80,112},{96,0},{112,16},{1... | collective-permute-start | bytes 2359304 | tf_op jit(solution)/shard_map/ppermute | solution.py:448
  6.0 36.4 %collective-permute-start.1 = (f32[2,2,384,128]{3,2,1,0:T(8,128)S(1)}, f32[2,2,384,128]{3,2,1,0:T(8,128)S(1)}, u32[]{:S(2)}, u32[]{:S(2)}) collective-permute-start(f32[2,2,384,128]{3,2,1,0:T(8,128)S(1)} %get-tuple-element.52), channel_id=1, source_target_pairs={{0,64},{16,80},{32,96},{48,112},{64,0},{80,16},{96,32},{112,48},{1... | collective-permute-start | bytes 2359304 | tf_op jit(solution)/shard_map/ppermute | solution.py:448
  8.6 33.8 %collective-permute-start.2 = (f32[2,2,384,128]{3,2,1,0:T(8,128)S(1)}, f32[2,2,384,128]{3,2,1,0:T(8,128)S(1)}, u32[]{:S(2)}, u32[]{:S(2)}) collective-permute-start(f32[2,2,384,128]{3,2,1,0:T(8,128)S(1)} %get-tuple-element.53), channel_id=1, source_target_pairs={{0,96},{16,112},{32,0},{48,16},{64,32},{80,48},{96,64},{112,80},{1... | collective-permute-start | bytes 2359304 | tf_op jit(solution)/shard_map/ppermute | solution.py:448
  46.7 20.9 %collective-permute-start.10 = (f32[2,384,128]{2,1,0:T(8,128)S(1)}, f32[2,384,128]{2,1,0:T(8,128)S(1)}, u32[]{:S(2)}, u32[]{:S(2)}) collective-permute-start(f32[2,384,128]{2,1,0:T(8,128)S(1)} %get-tuple-element.56), channel_id=1, source_target_pairs={{0,32},{16,48},{32,64},{48,80},{64,96},{80,112},{96,0},{112,16},{1... | collective-permute-start | bytes 1179656 | tf_op jit(solution)/shard_map/ppermute | solution.py:452
  47.7 6.5 %collective-permute-start.6 = (f32[264,128]{1,0:T(8,128)S(1)}, f32[264,128]{1,0:T(8,128)S(1)}, u32[]{:S(2)}, u32[]{:S(2)}) collective-permute-start(f32[264,128]{1,0:T(8,128)S(1)} %add.49.refs_0_), channel_id=1, source_target_pairs={{0,3},{1,0},{2,1},{3,2},{4,7},{5,4},{6,5},{7,6},{8,11},{9,8},{10,9... | collective-permute-start | bytes 405512 | tf_op jit(solution)/shard_map/ppermute | solution.py:425
  50.3 18.0 %collective-permute-start.11 = (f32[2,384,128]{2,1,0:T(8,128)S(1)}, f32[2,384,128]{2,1,0:T(8,128)S(1)}, u32[]{:S(2)}, u32[]{:S(2)}) collective-permute-start(f32[2,384,128]{2,1,0:T(8,128)S(1)} %get-tuple-element.57), channel_id=1, source_target_pairs={{0,64},{16,80},{32,96},{48,112},{64,0},{80,16},{96,32},{112,48},{1... | collective-permute-start | bytes 1179656 | tf_op jit(solution)/shard_map/ppermute | solution.py:452
  52.4 17.3 %collective-permute-start.12 = (f32[2,384,128]{2,1,0:T(8,128)S(1)}, f32[2,384,128]{2,1,0:T(8,128)S(1)}, u32[]{:S(2)}, u32[]{:S(2)}) collective-permute-start(f32[2,384,128]{2,1,0:T(8,128)S(1)} %get-tuple-element.58), channel_id=1, source_target_pairs={{0,96},{16,112},{32,0},{48,16},{64,32},{80,48},{96,64},{112,80},{1... | collective-permute-start | bytes 1179656 | tf_op jit(solution)/shard_map/ppermute | solution.py:452
  53.7 5.5 %collective-permute-start.5 = (f32[264,128]{1,0:T(8,128)S(1)}, f32[264,128]{1,0:T(8,128)S(1)}, u32[]{:S(2)}, u32[]{:S(2)}) collective-permute-start(f32[264,128]{1,0:T(8,128)S(1)} %add.49.refs_0_), channel_id=1, source_target_pairs={{0,2},{1,3},{2,0},{3,1},{4,6},{5,7},{6,4},{7,5},{8,10},{9,11},{10,... | collective-permute-start | bytes 405512 | tf_op jit(solution)/shard_map/ppermute | solution.py:425
  54.2 9.0 %collective-permute-start.4 = (f32[264,128]{1,0:T(8,128)S(1)}, f32[264,128]{1,0:T(8,128)S(1)}, u32[]{:S(2)}, u32[]{:S(2)}) collective-permute-start(f32[264,128]{1,0:T(8,128)S(1)} %add.49.refs_0_), channel_id=1, source_target_pairs={{0,1},{1,2},{2,3},{3,0},{4,5},{5,6},{6,7},{7,4},{8,9},{9,10},{10,1... | collective-permute-start | bytes 405512 | tf_op jit(solution)/shard_map/ppermute | solution.py:425
  63.8 9.4 %collective-permute-start.9 = (f32[264,128]{1,0:T(8,128)S(1)}, f32[264,128]{1,0:T(8,128)S(1)}, u32[]{:S(2)}, u32[]{:S(2)}) collective-permute-start(f32[264,128]{1,0:T(8,128)S(1)} %shard_map.40.refs_1_), channel_id=1, source_target_pairs={{0,12},{1,13},{2,14},{3,15},{4,0},{5,1},{6,2},{7,3},{8,4},{9,5},{1... | collective-permute-start | bytes 405512 | tf_op jit(solution)/shard_map/ppermute | solution.py:425
  67.6 5.6 %collective-permute-start.8 = (f32[264,128]{1,0:T(8,128)S(1)}, f32[264,128]{1,0:T(8,128)S(1)}, u32[]{:S(2)}, u32[]{:S(2)}) collective-permute-start(f32[264,128]{1,0:T(8,128)S(1)} %shard_map.40.refs_1_), channel_id=1, source_target_pairs={{0,8},{1,9},{2,10},{3,11},{4,12},{5,13},{6,14},{7,15},{8,0},{9,1},... | collective-permute-start | bytes 405512 | tf_op jit(solution)/shard_map/ppermute | solution.py:425
  67.6 9.3 %collective-permute-start.7 = (f32[264,128]{1,0:T(8,128)S(1)}, f32[264,128]{1,0:T(8,128)S(1)}, u32[]{:S(2)}, u32[]{:S(2)}) collective-permute-start(f32[264,128]{1,0:T(8,128)S(1)} %shard_map.40.refs_1_), channel_id=1, source_target_pairs={{0,4},{1,5},{2,6},{3,7},{4,8},{5,9},{6,10},{7,11},{8,12},{9,13},{1... | collective-permute-start | bytes 405512 | tf_op jit(solution)/shard_map/ppermute | solution.py:425
  79.9 5.3 %collective-permute-start.14 = (f32[320,256]{1,0:T(8,128)S(1)}, f32[320,256]{1,0:T(8,128)S(1)}, u32[]{:S(2)}, u32[]{:S(2)}) collective-permute-start(f32[320,256]{1,0:T(8,128)S(1)} %get-tuple-element.60.weights_ref.own_ref), channel_id=1, source_target_pairs={{0,16},{16,0},{32,48},{48,32},{64,80},{80,64},{96,112},{112,96},{1... | collective-permute-start | bytes 983048 | tf_op jit(solution)/shard_map/ppermute | solution.py:421
  80.8 12.0 %collective-permute-start.13 = (f32[320,256]{1,0:T(8,128)S(1)}, f32[320,256]{1,0:T(8,128)S(1)}, u32[]{:S(2)}, u32[]{:S(2)}) collective-permute-start(f32[320,256]{1,0:T(8,128)S(1)} %get-tuple-element.60.weights_ref.own_ref), channel_id=1, source_target_pairs={{16,32},{48,64},{80,96},{112,0},{17,33},{49,65},{81,97},{113,1},{1... | collective-permute-start | bytes 983048 | tf_op jit(solution)/shard_map/ppermute | solution.py:462
  82.9 9.9 %collective-permute-start.15 = (f32[256,128]{1,0:T(8,128)S(1)}, f32[256,128]{1,0:T(8,128)S(1)}, u32[]{:S(2)}, u32[]{:S(2)}) collective-permute-start(f32[256,128]{1,0:T(8,128)S(1)} %get-tuple-element.61), channel_id=1, source_target_pairs={{16,48},{48,80},{80,112},{112,16},{17,49},{49,81},{81,113},{113,17... | collective-permute-start | bytes 393224 | tf_op jit(solution)/shard_map/ppermute | solution.py:461
  88.0 21.1 %collective-permute-start.24 = (f32[4,400,128]{2,1,0:T(8,128)S(1)}, f32[4,400,128]{2,1,0:T(8,128)S(1)}, u32[]{:S(2)}, u32[]{:S(2)}) collective-permute-start(f32[4,400,128]{2,1,0:T(8,128)S(1)} %get-tuple-element.67.refs_3_), channel_id=1, source_target_pairs={{0,32},{16,48},{32,64},{48,80},{64,96},{80,112},{96,0},{112,16},{1... | collective-permute-start | bytes 2457608 | tf_op jit(solution)/shard_map/ppermute | solution.py:474
  96.5 6.6 %collective-permute-start.17 = (f32[128,128]{1,0:T(8,128)S(1)}, f32[128,128]{1,0:T(8,128)S(1)}, u32[]{:S(2)}, u32[]{:S(2)}) collective-permute-start(f32[128,128]{1,0:T(8,128)S(1)} %add.50), channel_id=1, source_target_pairs={{0,1},{1,2},{2,3},{3,0},{4,5},{5,6},{6,7},{7,4},{8,9},{9,10},{10,1... | collective-permute-start | bytes 196616 | tf_op jit(solution)/shard_map/ppermute | solution.py:425
  98.3 7.3 %collective-permute-start.23 = (f32[256,128]{1,0:T(8,128)S(1)}, f32[256,128]{1,0:T(8,128)S(1)}, u32[]{:S(2)}, u32[]{:S(2)}) collective-permute-start(f32[256,128]{1,0:T(8,128)S(1)} %shard_map.46), channel_id=1, source_target_pairs={{0,16},{32,48},{64,80},{96,112},{1,17},{33,49},{65,81},{97,113},{2... | collective-permute-start | bytes 393224 | tf_op jit(solution)/shard_map/ppermute | solution.py:434
  103.8 5.3 %collective-permute-start.20 = (f32[128,128]{1,0:T(8,128)S(1)}, f32[128,128]{1,0:T(8,128)S(1)}, u32[]{:S(2)}, u32[]{:S(2)}) collective-permute-start(f32[128,128]{1,0:T(8,128)S(1)} %add_add_fusion.2.refs_4_), channel_id=1, source_target_pairs={{0,4},{1,5},{2,6},{3,7},{4,8},{5,9},{6,10},{7,11},{8,12},{9,13},{1... | collective-permute-start | bytes 196616 | tf_op jit(solution)/shard_map/ppermute | solution.py:425
  111.7 5.8 %collective-permute-start.26 = (f32[320,256]{1,0:T(8,128)S(1)}, f32[320,256]{1,0:T(8,128)S(1)}, u32[]{:S(2)}, u32[]{:S(2)}) collective-permute-start(f32[320,256]{1,0:T(8,128)S(1)} %get-tuple-element.69.weights_ref.own_ref), channel_id=1, source_target_pairs={{0,16},{16,0},{32,48},{48,32},{64,80},{80,64},{96,112},{112,96},{1... | collective-permute-start | bytes 983048 | tf_op jit(solution)/shard_map/ppermute | solution.py:421
  114.0 12.0 %collective-permute-start.25 = (f32[320,256]{1,0:T(8,128)S(1)}, f32[320,256]{1,0:T(8,128)S(1)}, u32[]{:S(2)}, u32[]{:S(2)}) collective-permute-start(f32[320,256]{1,0:T(8,128)S(1)} %get-tuple-element.69.weights_ref.own_ref), channel_id=1, source_target_pairs={{16,32},{48,64},{80,96},{112,0},{17,33},{49,65},{81,97},{113,1},{1... | collective-permute-start | bytes 983048 | tf_op jit(solution)/shard_map/ppermute | solution.py:462
  115.4 10.7 %collective-permute-start.27 = (f32[256,128]{1,0:T(8,128)S(1)}, f32[256,128]{1,0:T(8,128)S(1)}, u32[]{:S(2)}, u32[]{:S(2)}) collective-permute-start(f32[256,128]{1,0:T(8,128)S(1)} %get-tuple-element.70), channel_id=1, source_target_pairs={{16,48},{48,80},{80,112},{112,16},{17,49},{49,81},{81,113},{113,17... | collective-permute-start | bytes 393224 | tf_op jit(solution)/shard_map/ppermute | solution.py:461
  120.3 23.4 %collective-permute-start.36 = (f32[4,400,128]{2,1,0:T(8,128)S(1)}, f32[4,400,128]{2,1,0:T(8,128)S(1)}, u32[]{:S(2)}, u32[]{:S(2)}) collective-permute-start(f32[4,400,128]{2,1,0:T(8,128)S(1)} %get-tuple-element.77.refs_3_), channel_id=1, source_target_pairs={{0,32},{16,48},{32,64},{48,80},{64,96},{80,112},{96,0},{112,16},{1... | collective-permute-start | bytes 2457608 | tf_op jit(solution)/shard_map/ppermute | solution.py:474
  131.2 5.6 %collective-permute-start.29 = (f32[128,128]{1,0:T(8,128)S(1)}, f32[128,128]{1,0:T(8,128)S(1)}, u32[]{:S(2)}, u32[]{:S(2)}) collective-permute-start(f32[128,128]{1,0:T(8,128)S(1)} %add.54), channel_id=1, source_target_pairs={{0,1},{1,2},{2,3},{3,0},{4,5},{5,6},{6,7},{7,4},{8,9},{9,10},{10,1... | collective-permute-start | bytes 196616 | tf_op jit(solution)/shard_map/ppermute | solution.py:425
  131.8 8.2 %collective-permute-start.35 = (f32[256,128]{1,0:T(8,128)S(1)}, f32[256,128]{1,0:T(8,128)S(1)}, u32[]{:S(2)}, u32[]{:S(2)}) collective-permute-start(f32[256,128]{1,0:T(8,128)S(1)} %shard_map.52), channel_id=1, source_target_pairs={{0,16},{32,48},{64,80},{96,112},{1,17},{33,49},{65,81},{97,113},{2... | collective-permute-start | bytes 393224 | tf_op jit(solution)/shard_map/ppermute | solution.py:434
  146.5 5.7 %collective-permute-start.38 = (f32[320,256]{1,0:T(8,128)S(1)}, f32[320,256]{1,0:T(8,128)S(1)}, u32[]{:S(2)}, u32[]{:S(2)}) collective-permute-start(f32[320,256]{1,0:T(8,128)S(1)} %get-tuple-element.79.weights_ref.own_ref), channel_id=1, source_target_pairs={{0,16},{16,0},{32,48},{48,32},{64,80},{80,64},{96,112},{112,96},{1... | collective-permute-start | bytes 983048 | tf_op jit(solution)/shard_map/ppermute | solution.py:421
  149.0 10.3 %collective-permute-start.37 = (f32[320,256]{1,0:T(8,128)S(1)}, f32[320,256]{1,0:T(8,128)S(1)}, u32[]{:S(2)}, u32[]{:S(2)}) collective-permute-start(f32[320,256]{1,0:T(8,128)S(1)} %get-tuple-element.79.weights_ref.own_ref), channel_id=1, source_target_pairs={{16,32},{48,64},{80,96},{112,0},{17,33},{49,65},{81,97},{113,1},{1... | collective-permute-start | bytes 983048 | tf_op jit(solution)/shard_map/ppermute | solution.py:462
  150.3 9.0 %collective-permute-start.39 = (f32[256,128]{1,0:T(8,128)S(1)}, f32[256,128]{1,0:T(8,128)S(1)}, u32[]{:S(2)}, u32[]{:S(2)}) collective-permute-start(f32[256,128]{1,0:T(8,128)S(1)} %get-tuple-element.80), channel_id=1, source_target_pairs={{16,48},{48,80},{80,112},{112,16},{17,49},{49,81},{81,113},{113,17... | collective-permute-start | bytes 393224 | tf_op jit(solution)/shard_map/ppermute | solution.py:461
  163.5 6.2 %collective-permute-start.41 = (f32[128,128]{1,0:T(8,128)S(1)}, f32[128,128]{1,0:T(8,128)S(1)}, u32[]{:S(2)}, u32[]{:S(2)}) collective-permute-start(f32[128,128]{1,0:T(8,128)S(1)} %add.58), channel_id=1, source_target_pairs={{0,1},{1,2},{2,3},{3,0},{4,5},{5,6},{6,7},{7,4},{8,9},{9,10},{10,1... | collective-permute-start | bytes 196616 | tf_op jit(solution)/shard_map/ppermute | solution.py:425
  170.4 10.5 %collective-permute-start.47 = (f32[4,400,128]{2,1,0:T(8,128)S(1)}, f32[4,400,128]{2,1,0:T(8,128)S(1)}, u32[]{:S(2)}, u32[]{:S(2)}) collective-permute-start(f32[4,400,128]{2,1,0:T(8,128)S(1)} %get-tuple-element.92), channel_id=1, source_target_pairs={{0,16},{16,0},{32,48},{48,32},{64,80},{80,64},{96,112},{112,96},{1... | collective-permute-start | bytes 2457608 | tf_op jit(solution)/shard_map/ppermute | solution.py:421
  171.1 9.8 %collective-permute-start.48 = (f32[4,400,128]{2,1,0:T(8,128)S(1)}, f32[4,400,128]{2,1,0:T(8,128)S(1)}, u32[]{:S(2)}, u32[]{:S(2)}) collective-permute-start(f32[4,400,128]{2,1,0:T(8,128)S(1)} %get-tuple-element.93), channel_id=1, source_target_pairs={{0,16},{16,0},{32,48},{48,32},{64,80},{80,64},{96,112},{112,96},{1... | collective-permute-start | bytes 2457608 | tf_op jit(solution)/shard_map/ppermute | solution.py:421
  172.6 5.4 %collective-permute-start.44 = (f32[128,128]{1,0:T(8,128)S(1)}, f32[128,128]{1,0:T(8,128)S(1)}, u32[]{:S(2)}, u32[]{:S(2)}) collective-permute-start(f32[128,128]{1,0:T(8,128)S(1)} %add_add_fusion.refs_3_.refs_5_), channel_id=1, source_target_pairs={{0,4},{1,5},{2,6},{3,7},{4,8},{5,9},{6,10},{7,11},{8,12},{9,13},{1... | collective-permute-start | bytes 196616 | tf_op jit(solution)/shard_map/ppermute | solution.py:425
  (19 other events, 108.0 us)

commit v10 on v9

--- a/solution.py
+++ b/solution.py
@@ -117,13 +117,13 @@
     rows = x.shape[0]
     return pl.pallas_call(
         pack_main_kernel,
-        in_specs=[pl.BlockSpec(memory_space=pltpu.SMEM), pl.BlockSpec(memory_space=pl.ANY)],
+        in_specs=[pl.BlockSpec(memory_space=pltpu.SMEM), pl.BlockSpec(memory_space=pltpu.HBM)],
         out_specs=[pl.BlockSpec(memory_space=pltpu.VMEM)] * SIDE,
         out_shape=[shape(2, 2, rows, BLOCK)] * SIDE,
         scratch_shapes=[pltpu.SemaphoreType.DMA((4 * SIDE,))],
         compiler_params=pltpu.CompilerParams(vmem_limit_bytes=VMEM_LIMIT),
         cost_estimate=pl.CostEstimate(flops=0, bytes_accessed=8 * SIDE * rows * 2 * PAIR, transcendentals=0),
-    )(info, x)
+    )(info, pltpu.with_memory_space_constraint(x, pltpu.HBM))
 
 
 def pack_ahead_kernel(info_ref, *refs):
@@ -192,8 +192,8 @@
     refs[-1][...] = (refs[0][...] + refs[1][...]) + (refs[2][...] + refs[3][...])
 
 
-def sum_parts(info, parts, before):
-    return call_whole(sum_kernel, (info, *parts), [shape(*parts[0].shape)], before, nbytes=20 * parts[0].size)[0]
+def sum_parts(info, parts):
+    return call_whole(sum_kernel, (info, *parts), [shape(*parts[0].shape)], nbytes=20 * parts[0].size)[0]
 
 
 def rotation_of(gram, x_ref, r_ref):
@@ -318,11 +318,12 @@
     cross_ref[...] = cross
 
 
-def rotate_own(info, own, other, blocks, rows, step):
+def rotate_own(info, own, other, blocks, before, rows, step):
     return call_whole(
         functools.partial(own_kernel, rows, step),
         (info, own, other, *blocks),
         [shape(SIDE, step, BLOCK)] * 3 + [shape(BLOCK, BLOCK)],
+        before,
         flops=2 * 3 * SIDE * step * 4 * BLOCK * PAIR,
         nbytes=4 * 7 * SIDE * step * BLOCK,
     )
@@ -451,8 +452,8 @@
     packed = pack_ahead(info, x, main[1:])
     ahead = [packed[0]] + [lax.ppermute(packed[k], "cols", CHIPS_ON[k]) for k in range(1, SIDE)]
     value = keep + swap_core(send)
-    value = sum_parts(info, [value] + along(value, ALONG_X), [])
-    weights, lower, gram = first_cayley(info, [value] + along(value, ALONG_Z), ahead[1:])
+    value = sum_parts(info, [value] + along(value, ALONG_X))
+    weights, lower, gram = first_cayley(info, [value] + along(value, ALONG_Z), [ahead[1], ahead[3]])
 
     own_blocks = main
     ahead_blocks = [value[None] for value in ahead]
@@ -462,7 +463,8 @@
         even = lax.ppermute(weights, "cols", ODD_TO_EVEN)
         other = swap_core(weights)
         up = project(info, gram, weights)
-        up0, up1, low1, cross = rotate_own(info, weights, other, own_blocks, rows, step)
+        before = [] if sweep_round else [ahead[2]]
+        up0, up1, low1, cross = rotate_own(info, weights, other, own_blocks, before, rows, step)
         low0, keep, send = rotate_ahead(info, even, odd, cross, up0, ahead_blocks, rows, step)
         value = keep + swap_core(send)
         value = value + sum(along(value, ALONG_X))

time: 185 us -> 184 us (level)
  starting transfers between devices: 53.6 us -> 51.7 us
  local copies, waits for them, and re-layouts: 1.89 us -> 0.01 us
    ppermute x24, waiting for transfers between devices: 37.1 us -> 39.3 us  [along(): return [lax.ppermute(value, 'rows', pairs) for pairs in shifts]]
    unnamed x4 -> x2, local copies, waits for them, and re-layouts: 1.89 us -> 0.01 us
  transfers between devices with their start and end apart: 49 -> 49, of which waited for: 28 -> 29; matrix products, arithmetic and copies ran while one was open for 0% -> 0% of each run, Pallas kernels for 12% -> 14%
where the time goes in v10:
time: 184 us
  waiting for transfers between devices  88.6 us (48%)
  starting transfers between devices  51.7 us (28%)
  Pallas kernels  42.1 us (23%)
    ppermute x24, waiting for transfers between devices, along(): return [lax.ppermute(value, 'rows', pairs) for pairs in shifts]  39.3 us
    pallas_call x20, Pallas kernels, call_whole(): pl.pallas_call(inner, in_specs=[pl.BlockSpec(memory_space=pltpu.SMEM)] +...  34.4 us
    ppermute x6, waiting for transfers between devices, body(): lax.ppermute(packed[k], 'cols', CHIPS_ON[k])  32.7 us
    ppermute x24, starting transfers between devices, along(): return [lax.ppermute(value, 'rows', pairs) for pairs in shifts]  18.7 us
    ppermute x3, waiting for transfers between devices, body(): odd = lax.ppermute(lower, 'cols', ODD_TO_ODD)  12.8 us
    ppermute x6, starting transfers between devices, body(): lax.ppermute(packed[k], 'cols', CHIPS_ON[k])  9.7 us
    ppermute x9, starting transfers between devices, swap_core(): return lax.ppermute(value, 'cols', TURN_CORE)  7.59 us
    ppermute x3, starting transfers between devices, body(): odd = lax.ppermute(lower, 'cols', ODD_TO_ODD)  7.19 us
  transfers between devices with their start and end apart: 49, of which 29 were waited for; matrix products, arithmetic and copies ran while one was open for 0% of the time, Pallas kernels for 14%

profile of v10, /device:TPU:1, one launch (start us, length us, event | category | flops | bytes accessed | tf_op | source)
XLA Modules:
  0.0 183.6 jit_solution(16722251330647611083)
XLA Ops:
  0.7 2.9 %shard_map.38 = (f32[2,2,384,128]{3,2,1,0:T(8,128)S(1)}, f32[2,2,384,128]{3,2,1,0:T(8,128)S(1)}, f32[2,2,384,128]{3,2,1,0:T(8,128)S(1)}, f32[2,2,384,128]{3,2,1,0:T(8,128)S(1)}) custom-call(s32[3]{0:T(128)S(1)} %pad_add_fusion.info_ref.refs_0_, f32[384,2048]{1,0:T(8,128)} %bitcast.10), custom_call_target="tpu_custom_call" | custom-call | bytes 6291456 | tf_op jit(solution)/shard_map/pallas_call | solution.py:118
  3.7 2.2 %collective-permute-start = (f32[2,2,384,128]{3,2,1,0:T(8,128)S(1)}, f32[2,2,384,128]{3,2,1,0:T(8,128)S(1)}, u32[]{:S(2)}, u32[]{:S(2)}) collective-permute-start(f32[2,2,384,128]{3,2,1,0:T(8,128)S(1)} %get-tuple-element.51), channel_id=1, source_target_pairs={{0,32},{16,48},{32,64},{48,80},{64,96},{80,112},{96,0},{112,16},{1... | collective-permute-start | bytes 2359304 | tf_op jit(solution)/shard_map/ppermute | solution.py:449
  5.9 2.6 %collective-permute-start.1 = (f32[2,2,384,128]{3,2,1,0:T(8,128)S(1)}, f32[2,2,384,128]{3,2,1,0:T(8,128)S(1)}, u32[]{:S(2)}, u32[]{:S(2)}) collective-permute-start(f32[2,2,384,128]{3,2,1,0:T(8,128)S(1)} %get-tuple-element.52), channel_id=1, source_target_pairs={{0,64},{16,80},{32,96},{48,112},{64,0},{80,16},{96,32},{112,48},{1... | collective-permute-start | bytes 2359304 | tf_op jit(solution)/shard_map/ppermute | solution.py:449
  9.5 14.9 %collective-permute-done.refs_1_.refs_4_ = f32[2,2,384,128]{3,2,1,0:T(8,128)S(1)} collective-permute-done((f32[2,2,384,128]{3,2,1,0:T(8,128)S(1)}, f32[2,2,384,128]{3,2,1,0:T(8,128)S(1)}, u32[]{:S(2)}, u32[]{:S(2)}) %collective-permute-start) | collective-permute-done | bytes 786464 | tf_op jit(solution)/shard_map/ppermute | solution.py:449
  24.4 17.9 %collective-permute-done.1.refs_2_.refs_5_ = f32[2,2,384,128]{3,2,1,0:T(8,128)S(1)} collective-permute-done((f32[2,2,384,128]{3,2,1,0:T(8,128)S(1)}, f32[2,2,384,128]{3,2,1,0:T(8,128)S(1)}, u32[]{:S(2)}, u32[]{:S(2)}) %collective-permute-start.1) | collective-permute-done | bytes 786464 | tf_op jit(solution)/shard_map/ppermute | solution.py:449
  42.3 1.9 %shard_map.39 = (f32[264,128]{1,0:T(8,128)S(1)}, f32[264,128]{1,0:T(8,128)S(1)}) custom-call(s32[3]{0:T(128)S(1)} %pad_add_fusion.info_ref.refs_0_, f32[2,2,384,128]{3,2,1,0:T(8,128)S(1)} %get-tuple-element.50.refs_0_.refs_3_, f32[2,2,384,128]{3,2,1,0:T(8,128)S(1)} %collective-permute-done.refs_1_.refs_4_, ...), custom_call_target="tpu_custom_call" | custom-call | flops 805306368 | bytes 3145728 | tf_op jit(solution)/shard_map/pallas_call | solution.py:80
  49.3 2.5 %collective-permute-start.6 = (f32[264,128]{1,0:T(8,128)S(1)}, f32[264,128]{1,0:T(8,128)S(1)}, u32[]{:S(2)}, u32[]{:S(2)}) collective-permute-start(f32[264,128]{1,0:T(8,128)S(1)} %add.49.refs_0_), channel_id=1, source_target_pairs={{0,3},{1,0},{2,1},{3,2},{4,7},{5,4},{6,5},{7,6},{8,11},{9,8},{10,9... | collective-permute-start | bytes 405512 | tf_op jit(solution)/shard_map/ppermute | solution.py:426
  53.0 1.9 %collective-permute-done.6.refs_3_ = f32[264,128]{1,0:T(8,128)S(1)} collective-permute-done((f32[264,128]{1,0:T(8,128)S(1)}, f32[264,128]{1,0:T(8,128)S(1)}, u32[]{:S(2)}, u32[]{:S(2)}) %collective-permute-start.6) | collective-permute-done | bytes 135200 | tf_op jit(solution)/shard_map/ppermute | solution.py:426
  54.9 2.7 %collective-permute-done.5.refs_2_ = f32[264,128]{1,0:T(8,128)S(1)} collective-permute-done((f32[264,128]{1,0:T(8,128)S(1)}, f32[264,128]{1,0:T(8,128)S(1)}, u32[]{:S(2)}, u32[]{:S(2)}) %collective-permute-start.5) | collective-permute-done | bytes 135200 | tf_op jit(solution)/shard_map/ppermute | solution.py:426
  57.6 4.1 %collective-permute-done.4.refs_1_ = f32[264,128]{1,0:T(8,128)S(1)} collective-permute-done((f32[264,128]{1,0:T(8,128)S(1)}, f32[264,128]{1,0:T(8,128)S(1)}, u32[]{:S(2)}, u32[]{:S(2)}) %collective-permute-start.4) | collective-permute-done | bytes 135200 | tf_op jit(solution)/shard_map/ppermute | solution.py:426
  62.3 3.8 %collective-permute-start.9 = (f32[264,128]{1,0:T(8,128)S(1)}, f32[264,128]{1,0:T(8,128)S(1)}, u32[]{:S(2)}, u32[]{:S(2)}) collective-permute-start(f32[264,128]{1,0:T(8,128)S(1)} %shard_map.40.refs_1_), channel_id=1, source_target_pairs={{0,12},{1,13},{2,14},{3,15},{4,0},{5,1},{6,2},{7,3},{8,4},{9,5},{1... | collective-permute-start | bytes 405512 | tf_op jit(solution)/shard_map/ppermute | solution.py:426
  67.9 3.9 %collective-permute-done.9.refs_4_ = f32[264,128]{1,0:T(8,128)S(1)} collective-permute-done((f32[264,128]{1,0:T(8,128)S(1)}, f32[264,128]{1,0:T(8,128)S(1)}, u32[]{:S(2)}, u32[]{:S(2)}) %collective-permute-start.9) | collective-permute-done | bytes 135200 | tf_op jit(solution)/shard_map/ppermute | solution.py:426
  72.0 3.4 %collective-permute-done.7.refs_2_ = f32[264,128]{1,0:T(8,128)S(1)} collective-permute-done((f32[264,128]{1,0:T(8,128)S(1)}, f32[264,128]{1,0:T(8,128)S(1)}, u32[]{:S(2)}, u32[]{:S(2)}) %collective-permute-start.7) | collective-permute-done | bytes 135200 | tf_op jit(solution)/shard_map/ppermute | solution.py:426
  75.4 3.1 %shard_map.42 = (f32[320,256]{1,0:T(8,128)S(1)}, f32[256,128]{1,0:T(8,128)S(1)}, f32[256,256]{1,0:T(8,128)S(1)}) custom-call(s32[3]{0:T(128)S(1)} %pad_add_fusion.info_ref.refs_0_, f32[264,128]{1,0:T(8,128)S(1)} %shard_map.40.refs_1_, f32[264,128]{1,0:T(8,128)S(1)} %collective-permute-done.7.refs_2_, f32[264,128]{1,0:T(8,128)S(1)} %collective-permute-done.8.refs_3_, ...), custom_call_target="tpu_custom_call" | custom-call | flops 805306368 | bytes 1048576 | tf_op jit(solution)/shard_map/pallas_call | solution.py:80
  80.9 2.9 %collective-permute-start.14 = (f32[256,128]{1,0:T(8,128)S(1)}, f32[256,128]{1,0:T(8,128)S(1)}, u32[]{:S(2)}, u32[]{:S(2)}) collective-permute-start(f32[256,128]{1,0:T(8,128)S(1)} %get-tuple-element.60), channel_id=1, source_target_pairs={{16,48},{48,80},{80,112},{112,16},{17,49},{49,81},{81,113},{113,17... | collective-permute-start | bytes 393224 | tf_op jit(solution)/shard_map/ppermute | solution.py:462
  83.9 2.8 %shard_map.44 = (f32[4,400,128]{2,1,0:T(8,128)S(1)}, f32[4,400,128]{2,1,0:T(8,128)S(1)}, f32[4,400,128]{2,1,0:T(8,128)S(1)}, f32[128,128]{1,0:T(8,128)S(1)}) custom-call(s32[3]{0:T(128)S(1)} %pad_add_fusion.info_ref.refs_0_, f32[320,256]{1,0:T(8,128)S(1)} %get-tuple-element.59.weights_ref.refs_1_, f32[320,256]{1,0:T(8,128)S(1)} %collective-permute-done.13.refs_2_.refs_3_, ...), custom_call_target="tpu_custom_call" | custom-call | flops 1258291200 | bytes 5734400 | tf_op jit(solution)/shard_map/pallas_call | solution.py:80
  87.5 3.8 %collective-permute-done.14.odd_ref = f32[256,128]{1,0:T(8,128)S(1)} collective-permute-done((f32[256,128]{1,0:T(8,128)S(1)}, f32[256,128]{1,0:T(8,128)S(1)}, u32[]{:S(2)}, u32[]{:S(2)}) %collective-permute-start.14) | collective-permute-done | bytes 131104 | tf_op jit(solution)/shard_map/ppermute | solution.py:462
  108.6 2.6 %shard_map.48 = (f32[320,256]{1,0:T(8,128)S(1)}, f32[256,128]{1,0:T(8,128)S(1)}, f32[256,256]{1,0:T(8,128)S(1)}) custom-call(s32[3]{0:T(128)S(1)} %pad_add_fusion.info_ref.refs_0_, f32[128,128]{1,0:T(8,128)S(1)} %shard_map.43.refs_1_, f32[320,256]{1,0:T(8,128)S(1)} %collective-permute-done.12.even_ref.refs_1_.refs_2_, ...), custom_call_target="tpu_custom_call" | custom-call | flops 805306368 | bytes 1048576 | tf_op jit(solution)/shard_map/pallas_call | solution.py:80
  113.9 2.4 %collective-permute-start.27 = (f32[256,128]{1,0:T(8,128)S(1)}, f32[256,128]{1,0:T(8,128)S(1)}, u32[]{:S(2)}, u32[]{:S(2)}) collective-permute-start(f32[256,128]{1,0:T(8,128)S(1)} %get-tuple-element.70), channel_id=1, source_target_pairs={{16,48},{48,80},{80,112},{112,16},{17,49},{49,81},{81,113},{113,17... | collective-permute-start | bytes 393224 | tf_op jit(solution)/shard_map/ppermute | solution.py:462
  116.3 2.8 %shard_map.50 = (f32[4,400,128]{2,1,0:T(8,128)S(1)}, f32[4,400,128]{2,1,0:T(8,128)S(1)}, f32[4,400,128]{2,1,0:T(8,128)S(1)}, f32[128,128]{1,0:T(8,128)S(1)}) custom-call(s32[3]{0:T(128)S(1)} %pad_add_fusion.info_ref.refs_0_, f32[320,256]{1,0:T(8,128)S(1)} %get-tuple-element.69.weights_ref.own_ref, f32[320,256]{1,0:T(8,128)S(1)} %collective-permute-done.26.other_ref.refs_3_, ...), custom_call_target="tpu_custom_call" | custom-call | flops 1258291200 | bytes 5734400 | tf_op jit(solution)/shard_map/pallas_call | solution.py:80
  119.9 4.6 %collective-permute-done.27.odd_ref = f32[256,128]{1,0:T(8,128)S(1)} collective-permute-done((f32[256,128]{1,0:T(8,128)S(1)}, f32[256,128]{1,0:T(8,128)S(1)}, u32[]{:S(2)}, u32[]{:S(2)}) %collective-permute-start.27) | collective-permute-done | bytes 131104 | tf_op jit(solution)/shard_map/ppermute | solution.py:462
  131.4 2.0 %collective-permute-done.30 = f32[128,128]{1,0:T(8,128)S(1)} collective-permute-done((f32[128,128]{1,0:T(8,128)S(1)}, f32[128,128]{1,0:T(8,128)S(1)}, u32[]{:S(2)}, u32[]{:S(2)}) %collective-permute-start.30) | collective-permute-done | bytes 65568 | tf_op jit(solution)/shard_map/ppermute | solution.py:426
  142.0 2.6 %shard_map.54 = (f32[320,256]{1,0:T(8,128)S(1)}, f32[256,128]{1,0:T(8,128)S(1)}, f32[256,256]{1,0:T(8,128)S(1)}) custom-call(s32[3]{0:T(128)S(1)} %pad_add_fusion.info_ref.refs_0_, f32[128,128]{1,0:T(8,128)S(1)} %shard_map.49.refs_1_, f32[320,256]{1,0:T(8,128)S(1)} %collective-permute-done.25.even_ref.refs_1_.refs_2_, ...), custom_call_target="tpu_custom_call" | custom-call | flops 805306368 | bytes 1048576 | tf_op jit(solution)/shard_map/pallas_call | solution.py:80
  144.7 2.6 %collective-permute-start.38 = (f32[320,256]{1,0:T(8,128)S(1)}, f32[320,256]{1,0:T(8,128)S(1)}, u32[]{:S(2)}, u32[]{:S(2)}) collective-permute-start(f32[320,256]{1,0:T(8,128)S(1)} %get-tuple-element.79.weights_ref.own_ref), channel_id=1, source_target_pairs={{0,16},{16,0},{32,48},{48,32},{64,80},{80,64},{96,112},{112,96},{1... | collective-permute-start | bytes 983048 | tf_op jit(solution)/shard_map/ppermute | solution.py:422
  148.6 1.9 %collective-permute-start.39 = (f32[256,128]{1,0:T(8,128)S(1)}, f32[256,128]{1,0:T(8,128)S(1)}, u32[]{:S(2)}, u32[]{:S(2)}) collective-permute-start(f32[256,128]{1,0:T(8,128)S(1)} %get-tuple-element.80), channel_id=1, source_target_pairs={{16,48},{48,80},{80,112},{112,16},{17,49},{49,81},{81,113},{113,17... | collective-permute-start | bytes 393224 | tf_op jit(solution)/shard_map/ppermute | solution.py:462
  150.5 2.8 %shard_map.56 = (f32[4,400,128]{2,1,0:T(8,128)S(1)}, f32[4,400,128]{2,1,0:T(8,128)S(1)}, f32[4,400,128]{2,1,0:T(8,128)S(1)}, f32[128,128]{1,0:T(8,128)S(1)}) custom-call(s32[3]{0:T(128)S(1)} %pad_add_fusion.info_ref.refs_0_, f32[320,256]{1,0:T(8,128)S(1)} %get-tuple-element.79.weights_ref.own_ref, f32[320,256]{1,0:T(8,128)S(1)} %collective-permute-done.38.other_ref.refs_2_, ...), custom_call_target="tpu_custom_call" | custom-call | flops 1258291200 | bytes 5734400 | tf_op jit(solution)/shard_map/pallas_call | solution.py:80
  153.3 4.3 %collective-permute-done.39.odd_ref = f32[256,128]{1,0:T(8,128)S(1)} collective-permute-done((f32[256,128]{1,0:T(8,128)S(1)}, f32[256,128]{1,0:T(8,128)S(1)}, u32[]{:S(2)}, u32[]{:S(2)}) %collective-permute-start.39) | collective-permute-done | bytes 131104 | tf_op jit(solution)/shard_map/ppermute | solution.py:462
  162.5 1.9 %collective-permute-done.43 = f32[128,128]{1,0:T(8,128)S(1)} collective-permute-done((f32[128,128]{1,0:T(8,128)S(1)}, f32[128,128]{1,0:T(8,128)S(1)}, u32[]{:S(2)}, u32[]{:S(2)}) %collective-permute-start.43) | collective-permute-done | bytes 65568 | tf_op jit(solution)/shard_map/ppermute | solution.py:426
  166.0 2.1 %collective-permute-done.41 = f32[128,128]{1,0:T(8,128)S(1)} collective-permute-done((f32[128,128]{1,0:T(8,128)S(1)}, f32[128,128]{1,0:T(8,128)S(1)}, u32[]{:S(2)}, u32[]{:S(2)}) %collective-permute-start.41) | collective-permute-done | bytes 65568 | tf_op jit(solution)/shard_map/ppermute | solution.py:426
  172.8 2.2 %collective-permute-done.45.refs_5_ = f32[128,128]{1,0:T(8,128)S(1)} collective-permute-done((f32[128,128]{1,0:T(8,128)S(1)}, f32[128,128]{1,0:T(8,128)S(1)}, u32[]{:S(2)}, u32[]{:S(2)}) %collective-permute-start.45) | collective-permute-done | bytes 65568 | tf_op jit(solution)/shard_map/ppermute | solution.py:426
  176.5 2.9 %shard_map.58 = (f32[256,256]{1,0:T(8,128)S(1)}, f32[256,128]{1,0:T(8,128)}, f32[256,256]{1,0:T(8,128)S(1)}) custom-call(s32[3]{0:T(128)S(1)} %pad_add_fusion.info_ref.refs_0_, f32[128,128]{1,0:T(8,128)S(1)} %shard_map.55.refs_0_, f32[320,256]{1,0:T(8,128)S(1)} %collective-permute-done.37.even_ref.refs_1_, ...), custom_call_target="tpu_custom_call" | custom-call | flops 805306368 | bytes 1048576 | tf_op jit(solution)/shard_map/pallas_call | solution.py:80
  179.4 4.1 %shard_map.60 = (f32[8,384,256]{2,1,0:T(8,128)}, f32[2,64,256]{2,1,0:T(8,128)}, f32[1,256]{1,0:T(1,128)}) custom-call(s32[3]{0:T(128)S(1)} %pad_add_fusion.info_ref.refs_0_, f32[256,256]{1,0:T(8,128)S(1)} %get-tuple-element.87.weights_ref, f32[256,256]{1,0:T(8,128)S(1)} %get-tuple-element.88.gram_ref, f32[4,400,128]{2,1,0:T(8,128)S(1)} %get-tuple-element.84.up0_ref.refs_1_, ...), custom_call_target="tpu_custom_call" | custom-call | flops 1258291200 | bytes 6553600 | tf_op jit(solution)/shard_map/pallas_call | solution.py:405
  (99 shorter events, 63.2 us)
Async XLA Ops:
  3.7 20.7 %collective-permute-start = (f32[2,2,384,128]{3,2,1,0:T(8,128)S(1)}, f32[2,2,384,128]{3,2,1,0:T(8,128)S(1)}, u32[]{:S(2)}, u32[]{:S(2)}) collective-permute-start(f32[2,2,384,128]{3,2,1,0:T(8,128)S(1)} %get-tuple-element.51), channel_id=1, source_target_pairs={{0,32},{16,48},{32,64},{48,80},{64,96},{80,112},{96,0},{112,16},{1... | collective-permute-start | bytes 2359304 | tf_op jit(solution)/shard_map/ppermute | solution.py:449
  5.9 36.4 %collective-permute-start.1 = (f32[2,2,384,128]{3,2,1,0:T(8,128)S(1)}, f32[2,2,384,128]{3,2,1,0:T(8,128)S(1)}, u32[]{:S(2)}, u32[]{:S(2)}) collective-permute-start(f32[2,2,384,128]{3,2,1,0:T(8,128)S(1)} %get-tuple-element.52), channel_id=1, source_target_pairs={{0,64},{16,80},{32,96},{48,112},{64,0},{80,16},{96,32},{112,48},{1... | collective-permute-start | bytes 2359304 | tf_op jit(solution)/shard_map/ppermute | solution.py:449
  8.5 33.8 %collective-permute-start.2 = (f32[2,2,384,128]{3,2,1,0:T(8,128)S(1)}, f32[2,2,384,128]{3,2,1,0:T(8,128)S(1)}, u32[]{:S(2)}, u32[]{:S(2)}) collective-permute-start(f32[2,2,384,128]{3,2,1,0:T(8,128)S(1)} %get-tuple-element.53), channel_id=1, source_target_pairs={{0,96},{16,112},{32,0},{48,16},{64,32},{80,48},{96,64},{112,80},{1... | collective-permute-start | bytes 2359304 | tf_op jit(solution)/shard_map/ppermute | solution.py:449
  46.5 20.3 %collective-permute-start.10 = (f32[2,384,128]{2,1,0:T(8,128)S(1)}, f32[2,384,128]{2,1,0:T(8,128)S(1)}, u32[]{:S(2)}, u32[]{:S(2)}) collective-permute-start(f32[2,384,128]{2,1,0:T(8,128)S(1)} %get-tuple-element.56), channel_id=1, source_target_pairs={{0,32},{16,48},{32,64},{48,80},{64,96},{80,112},{96,0},{112,16},{1... | collective-permute-start | bytes 1179656 | tf_op jit(solution)/shard_map/ppermute | solution.py:453
  47.5 20.3 %collective-permute-start.11 = (f32[2,384,128]{2,1,0:T(8,128)S(1)}, f32[2,384,128]{2,1,0:T(8,128)S(1)}, u32[]{:S(2)}, u32[]{:S(2)}) collective-permute-start(f32[2,384,128]{2,1,0:T(8,128)S(1)} %get-tuple-element.57), channel_id=1, source_target_pairs={{0,96},{16,112},{32,0},{48,16},{64,32},{80,48},{96,64},{112,80},{1... | collective-permute-start | bytes 1179656 | tf_op jit(solution)/shard_map/ppermute | solution.py:453
  49.3 5.6 %collective-permute-start.6 = (f32[264,128]{1,0:T(8,128)S(1)}, f32[264,128]{1,0:T(8,128)S(1)}, u32[]{:S(2)}, u32[]{:S(2)}) collective-permute-start(f32[264,128]{1,0:T(8,128)S(1)} %add.49.refs_0_), channel_id=1, source_target_pairs={{0,3},{1,0},{2,1},{3,2},{4,7},{5,4},{6,5},{7,6},{8,11},{9,8},{10,9... | collective-permute-start | bytes 405512 | tf_op jit(solution)/shard_map/ppermute | solution.py:426
  51.8 5.7 %collective-permute-start.5 = (f32[264,128]{1,0:T(8,128)S(1)}, f32[264,128]{1,0:T(8,128)S(1)}, u32[]{:S(2)}, u32[]{:S(2)}) collective-permute-start(f32[264,128]{1,0:T(8,128)S(1)} %add.49.refs_0_), channel_id=1, source_target_pairs={{0,2},{1,3},{2,0},{3,1},{4,6},{5,7},{6,4},{7,5},{8,10},{9,11},{10,... | collective-permute-start | bytes 405512 | tf_op jit(solution)/shard_map/ppermute | solution.py:426
  52.4 9.3 %collective-permute-start.4 = (f32[264,128]{1,0:T(8,128)S(1)}, f32[264,128]{1,0:T(8,128)S(1)}, u32[]{:S(2)}, u32[]{:S(2)}) collective-permute-start(f32[264,128]{1,0:T(8,128)S(1)} %add.49.refs_0_), channel_id=1, source_target_pairs={{0,1},{1,2},{2,3},{3,0},{4,5},{5,6},{6,7},{7,4},{8,9},{9,10},{10,1... | collective-permute-start | bytes 405512 | tf_op jit(solution)/shard_map/ppermute | solution.py:426
  62.3 9.5 %collective-permute-start.9 = (f32[264,128]{1,0:T(8,128)S(1)}, f32[264,128]{1,0:T(8,128)S(1)}, u32[]{:S(2)}, u32[]{:S(2)}) collective-permute-start(f32[264,128]{1,0:T(8,128)S(1)} %shard_map.40.refs_1_), channel_id=1, source_target_pairs={{0,12},{1,13},{2,14},{3,15},{4,0},{5,1},{6,2},{7,3},{8,4},{9,5},{1... | collective-permute-start | bytes 405512 | tf_op jit(solution)/shard_map/ppermute | solution.py:426
  66.1 5.9 %collective-permute-start.8 = (f32[264,128]{1,0:T(8,128)S(1)}, f32[264,128]{1,0:T(8,128)S(1)}, u32[]{:S(2)}, u32[]{:S(2)}) collective-permute-start(f32[264,128]{1,0:T(8,128)S(1)} %shard_map.40.refs_1_), channel_id=1, source_target_pairs={{0,8},{1,9},{2,10},{3,11},{4,12},{5,13},{6,14},{7,15},{8,0},{9,1},... | collective-permute-start | bytes 405512 | tf_op jit(solution)/shard_map/ppermute | solution.py:426
  66.1 9.3 %collective-permute-start.7 = (f32[264,128]{1,0:T(8,128)S(1)}, f32[264,128]{1,0:T(8,128)S(1)}, u32[]{:S(2)}, u32[]{:S(2)}) collective-permute-start(f32[264,128]{1,0:T(8,128)S(1)} %shard_map.40.refs_1_), channel_id=1, source_target_pairs={{0,4},{1,5},{2,6},{3,7},{4,8},{5,9},{6,10},{7,11},{8,12},{9,13},{1... | collective-permute-start | bytes 405512 | tf_op jit(solution)/shard_map/ppermute | solution.py:426
  66.8 17.0 %collective-permute-start.15 = (f32[2,384,128]{2,1,0:T(8,128)S(1)}, f32[2,384,128]{2,1,0:T(8,128)S(1)}, u32[]{:S(2)}, u32[]{:S(2)}) collective-permute-start(f32[2,384,128]{2,1,0:T(8,128)S(1)} %get-tuple-element.61), channel_id=1, source_target_pairs={{0,64},{16,80},{32,96},{48,112},{64,0},{80,16},{96,32},{112,48},{1... | collective-permute-start | bytes 1179656 | tf_op jit(solution)/shard_map/ppermute | solution.py:453
  78.5 5.4 %collective-permute-start.13 = (f32[320,256]{1,0:T(8,128)S(1)}, f32[320,256]{1,0:T(8,128)S(1)}, u32[]{:S(2)}, u32[]{:S(2)}) collective-permute-start(f32[320,256]{1,0:T(8,128)S(1)} %get-tuple-element.59.weights_ref.refs_1_), channel_id=1, source_target_pairs={{0,16},{16,0},{32,48},{48,32},{64,80},{80,64},{96,112},{112,96},{1... | collective-permute-start | bytes 983048 | tf_op jit(solution)/shard_map/ppermute | solution.py:422
  79.3 12.0 %collective-permute-start.12 = (f32[320,256]{1,0:T(8,128)S(1)}, f32[320,256]{1,0:T(8,128)S(1)}, u32[]{:S(2)}, u32[]{:S(2)}) collective-permute-start(f32[320,256]{1,0:T(8,128)S(1)} %get-tuple-element.59.weights_ref.refs_1_), channel_id=1, source_target_pairs={{16,32},{48,64},{80,96},{112,0},{17,33},{49,65},{81,97},{113,1},{1... | collective-permute-start | bytes 983048 | tf_op jit(solution)/shard_map/ppermute | solution.py:463
  80.9 10.4 %collective-permute-start.14 = (f32[256,128]{1,0:T(8,128)S(1)}, f32[256,128]{1,0:T(8,128)S(1)}, u32[]{:S(2)}, u32[]{:S(2)}) collective-permute-start(f32[256,128]{1,0:T(8,128)S(1)} %get-tuple-element.60), channel_id=1, source_target_pairs={{16,48},{48,80},{80,112},{112,16},{17,49},{49,81},{81,113},{113,17... | collective-permute-start | bytes 393224 | tf_op jit(solution)/shard_map/ppermute | solution.py:462
  86.6 22.0 %collective-permute-start.24 = (f32[4,400,128]{2,1,0:T(8,128)S(1)}, f32[4,400,128]{2,1,0:T(8,128)S(1)}, u32[]{:S(2)}, u32[]{:S(2)}) collective-permute-start(f32[4,400,128]{2,1,0:T(8,128)S(1)} %get-tuple-element.67.refs_3_), channel_id=1, source_target_pairs={{0,32},{16,48},{32,64},{48,80},{64,96},{80,112},{96,0},{112,16},{1... | collective-permute-start | bytes 2457608 | tf_op jit(solution)/shard_map/ppermute | solution.py:476
  94.6 5.3 %collective-permute-start.18 = (f32[128,128]{1,0:T(8,128)S(1)}, f32[128,128]{1,0:T(8,128)S(1)}, u32[]{:S(2)}, u32[]{:S(2)}) collective-permute-start(f32[128,128]{1,0:T(8,128)S(1)} %add.50), channel_id=1, source_target_pairs={{0,2},{1,3},{2,0},{3,1},{4,6},{5,7},{6,4},{7,5},{8,10},{9,11},{10,... | collective-permute-start | bytes 196616 | tf_op jit(solution)/shard_map/ppermute | solution.py:426
  95.0 6.8 %collective-permute-start.17 = (f32[128,128]{1,0:T(8,128)S(1)}, f32[128,128]{1,0:T(8,128)S(1)}, u32[]{:S(2)}, u32[]{:S(2)}) collective-permute-start(f32[128,128]{1,0:T(8,128)S(1)} %add.50), channel_id=1, source_target_pairs={{0,1},{1,2},{2,3},{3,0},{4,5},{5,6},{6,7},{7,4},{8,9},{9,10},{10,1... | collective-permute-start | bytes 196616 | tf_op jit(solution)/shard_map/ppermute | solution.py:426
  96.6 7.7 %collective-permute-start.23 = (f32[256,128]{1,0:T(8,128)S(1)}, f32[256,128]{1,0:T(8,128)S(1)}, u32[]{:S(2)}, u32[]{:S(2)}) collective-permute-start(f32[256,128]{1,0:T(8,128)S(1)} %shard_map.46), channel_id=1, source_target_pairs={{0,16},{32,48},{64,80},{96,112},{1,17},{33,49},{65,81},{97,113},{2... | collective-permute-start | bytes 393224 | tf_op jit(solution)/shard_map/ppermute | solution.py:435
  102.5 6.1 %collective-permute-start.20 = (f32[128,128]{1,0:T(8,128)S(1)}, f32[128,128]{1,0:T(8,128)S(1)}, u32[]{:S(2)}, u32[]{:S(2)}) collective-permute-start(f32[128,128]{1,0:T(8,128)S(1)} %add_add_fusion.2.refs_4_), channel_id=1, source_target_pairs={{0,4},{1,5},{2,6},{3,7},{4,8},{5,9},{6,10},{7,11},{8,12},{9,13},{1... | collective-permute-start | bytes 196616 | tf_op jit(solution)/shard_map/ppermute | solution.py:426
  112.6 12.0 %collective-permute-start.25 = (f32[320,256]{1,0:T(8,128)S(1)}, f32[320,256]{1,0:T(8,128)S(1)}, u32[]{:S(2)}, u32[]{:S(2)}) collective-permute-start(f32[320,256]{1,0:T(8,128)S(1)} %get-tuple-element.69.weights_ref.own_ref), channel_id=1, source_target_pairs={{16,32},{48,64},{80,96},{112,0},{17,33},{49,65},{81,97},{113,1},{1... | collective-permute-start | bytes 983048 | tf_op jit(solution)/shard_map/ppermute | solution.py:463
  113.9 10.7 %collective-permute-start.27 = (f32[256,128]{1,0:T(8,128)S(1)}, f32[256,128]{1,0:T(8,128)S(1)}, u32[]{:S(2)}, u32[]{:S(2)}) collective-permute-start(f32[256,128]{1,0:T(8,128)S(1)} %get-tuple-element.70), channel_id=1, source_target_pairs={{16,48},{48,80},{80,112},{112,16},{17,49},{49,81},{81,113},{113,17... | collective-permute-start | bytes 393224 | tf_op jit(solution)/shard_map/ppermute | solution.py:462
  119.0 23.0 %collective-permute-start.36 = (f32[4,400,128]{2,1,0:T(8,128)S(1)}, f32[4,400,128]{2,1,0:T(8,128)S(1)}, u32[]{:S(2)}, u32[]{:S(2)}) collective-permute-start(f32[4,400,128]{2,1,0:T(8,128)S(1)} %get-tuple-element.77.refs_3_), channel_id=1, source_target_pairs={{0,32},{16,48},{32,64},{48,80},{64,96},{80,112},{96,0},{112,16},{1... | collective-permute-start | bytes 2457608 | tf_op jit(solution)/shard_map/ppermute | solution.py:476
  129.5 5.8 %collective-permute-start.29 = (f32[128,128]{1,0:T(8,128)S(1)}, f32[128,128]{1,0:T(8,128)S(1)}, u32[]{:S(2)}, u32[]{:S(2)}) collective-permute-start(f32[128,128]{1,0:T(8,128)S(1)} %add.54), channel_id=1, source_target_pairs={{0,1},{1,2},{2,3},{3,0},{4,5},{5,6},{6,7},{7,4},{8,9},{9,10},{10,1... | collective-permute-start | bytes 196616 | tf_op jit(solution)/shard_map/ppermute | solution.py:426
  130.1 8.2 %collective-permute-start.35 = (f32[256,128]{1,0:T(8,128)S(1)}, f32[256,128]{1,0:T(8,128)S(1)}, u32[]{:S(2)}, u32[]{:S(2)}) collective-permute-start(f32[256,128]{1,0:T(8,128)S(1)} %shard_map.52), channel_id=1, source_target_pairs={{0,16},{32,48},{64,80},{96,112},{1,17},{33,49},{65,81},{97,113},{2... | collective-permute-start | bytes 393224 | tf_op jit(solution)/shard_map/ppermute | solution.py:435
  144.7 5.9 %collective-permute-start.38 = (f32[320,256]{1,0:T(8,128)S(1)}, f32[320,256]{1,0:T(8,128)S(1)}, u32[]{:S(2)}, u32[]{:S(2)}) collective-permute-start(f32[320,256]{1,0:T(8,128)S(1)} %get-tuple-element.79.weights_ref.own_ref), channel_id=1, source_target_pairs={{0,16},{16,0},{32,48},{48,32},{64,80},{80,64},{96,112},{112,96},{1... | collective-permute-start | bytes 983048 | tf_op jit(solution)/shard_map/ppermute | solution.py:422
  147.3 10.3 %collective-permute-start.37 = (f32[320,256]{1,0:T(8,128)S(1)}, f32[320,256]{1,0:T(8,128)S(1)}, u32[]{:S(2)}, u32[]{:S(2)}) collective-permute-start(f32[320,256]{1,0:T(8,128)S(1)} %get-tuple-element.79.weights_ref.own_ref), channel_id=1, source_target_pairs={{16,32},{48,64},{80,96},{112,0},{17,33},{49,65},{81,97},{113,1},{1... | collective-permute-start | bytes 983048 | tf_op jit(solution)/shard_map/ppermute | solution.py:463
  148.6 9.0 %collective-permute-start.39 = (f32[256,128]{1,0:T(8,128)S(1)}, f32[256,128]{1,0:T(8,128)S(1)}, u32[]{:S(2)}, u32[]{:S(2)}) collective-permute-start(f32[256,128]{1,0:T(8,128)S(1)} %get-tuple-element.80), channel_id=1, source_target_pairs={{16,48},{48,80},{80,112},{112,16},{17,49},{49,81},{81,113},{113,17... | collective-permute-start | bytes 393224 | tf_op jit(solution)/shard_map/ppermute | solution.py:462
  161.8 6.3 %collective-permute-start.41 = (f32[128,128]{1,0:T(8,128)S(1)}, f32[128,128]{1,0:T(8,128)S(1)}, u32[]{:S(2)}, u32[]{:S(2)}) collective-permute-start(f32[128,128]{1,0:T(8,128)S(1)} %add.58), channel_id=1, source_target_pairs={{0,1},{1,2},{2,3},{3,0},{4,5},{5,6},{6,7},{7,4},{8,9},{9,10},{10,1... | collective-permute-start | bytes 196616 | tf_op jit(solution)/shard_map/ppermute | solution.py:426
  168.9 10.5 %collective-permute-start.47 = (f32[4,400,128]{2,1,0:T(8,128)S(1)}, f32[4,400,128]{2,1,0:T(8,128)S(1)}, u32[]{:S(2)}, u32[]{:S(2)}) collective-permute-start(f32[4,400,128]{2,1,0:T(8,128)S(1)} %get-tuple-element.92), channel_id=1, source_target_pairs={{0,16},{16,0},{32,48},{48,32},{64,80},{80,64},{96,112},{112,96},{1... | collective-permute-start | bytes 2457608 | tf_op jit(solution)/shard_map/ppermute | solution.py:422
  169.6 9.8 %collective-permute-start.48 = (f32[4,400,128]{2,1,0:T(8,128)S(1)}, f32[4,400,128]{2,1,0:T(8,128)S(1)}, u32[]{:S(2)}, u32[]{:S(2)}) collective-permute-start(f32[4,400,128]{2,1,0:T(8,128)S(1)} %get-tuple-element.93), channel_id=1, source_target_pairs={{0,16},{16,0},{32,48},{48,32},{64,80},{80,64},{96,112},{112,96},{1... | collective-permute-start | bytes 2457608 | tf_op jit(solution)/shard_map/ppermute | solution.py:422
  170.9 5.6 %collective-permute-start.44 = (f32[128,128]{1,0:T(8,128)S(1)}, f32[128,128]{1,0:T(8,128)S(1)}, u32[]{:S(2)}, u32[]{:S(2)}) collective-permute-start(f32[128,128]{1,0:T(8,128)S(1)} %add_add_fusion.refs_3_.refs_5_), channel_id=1, source_target_pairs={{0,4},{1,5},{2,6},{3,7},{4,8},{5,9},{6,10},{7,11},{8,12},{9,13},{1... | collective-permute-start | bytes 196616 | tf_op jit(solution)/shard_map/ppermute | solution.py:426
  (18 other events, 109.0 us)
